TPU v7x, 512 devices: a whole 4x4x16 slice. The times are simulated.
512 devices in a mesh: tm: 32 (over z, core), row: 16 (over y, x).
Axes of the slice: x: 4, y: 4, z: 16, core: 2. Of those that a mesh axis runs over, the one named last changes fastest.
Arguments:
- covariance: float32 [32, 1024, 1024], P('tm', 'row'), as said below
- precision: float32 [32, 1024, 1024], P('tm', 'row'), as said below
- band_weight: float32 [32, 5, 1024], P('tm'), may hold values from -0.5 to 0.5
- band_offset: int32 [32, 5], P('tm'), may hold values from -64 to 64, as said below
- prior_mean: float32 [32, 1024], P('tm', 'row'), may hold values from -6 to 6
- innovation: float32 [32, 128], P('tm'), may hold values from -6 to 6
- seen_sites: int32 [32, 128], P('tm'), may hold values from 0 to 511, as said below
Outputs:
- smoother_gain: float32 [32, 1024, 1024], P('tm', 'row')
- smoother_shift: float32 [32, 1024], P('tm', 'row')
- smoother_spread: float32 [32, 1024, 1024], P('tm', 'row')
Inputs may be any that keep to these rules, and one draw needn't show every extreme that they name: `covariance`: each block's matrix is symmetric. `precision`: each block's matrix is symmetric. `band_offset`: the offsets of one block are distinct, and one of them has magnitude 64. `seen_sites`: the sites of one step are distinct.
All inputs are finite; a program needn't handle non-finite values.
Results may differ from a plain program's by a relative error of at most 0.0003.
Values sent between devices are 32-bit elements; how exact they have to be, the bound alone decides.
No kernel may reach another device: no remote copies, remote signals or barrier semaphores. Data moves between devices by JAX's collectives and lax.ppermute only.
A program may use at most 64 MiB of HBM per device.

v0:
```python
import jax
import jax.numpy as jnp
from jax import lax
from jax.sharding import PartitionSpec as P

NBAND = 5
REACH = 64


HIGHEST = lax.Precision.HIGHEST


def padded_2(cells, sides, width):
    for axis, dim in sides:
        count = lax.axis_size(axis)
        ends = count - 1
        head = lax.slice_in_dim(cells, 0, width, axis=dim)
        tail = lax.slice_in_dim(cells, cells.shape[dim] - width, cells.shape[dim], axis=dim)
        cells = jnp.concatenate(
            [
                lax.ppermute(tail, axis, [(i, (i + 1) % count) for i in range(ends)]),
                cells,
                lax.ppermute(head, axis, [((i + 1) % count, i) for i in range(ends)]),
            ],
            axis=dim,
        )
    return cells


def shifted(block, axis, distance):
    devices = range(lax.axis_size(axis))
    route = [(i - distance, i) for i in devices if i - distance in devices]
    return lax.ppermute(block, axis, route)


def product(left, right):
    return jnp.dot(left, right, precision=HIGHEST, preferred_element_type=jnp.float32)


def against(left, right):
    return lax.dot_general(
        left, right, (((1,), (1,)), ((), ())), precision=HIGHEST, preferred_element_type=jnp.float32
    )


def band_columns(matrix, weights, offsets):
    columns = matrix.shape[1]
    padded = jnp.pad(matrix, ((0, 0), (REACH, REACH)))
    summed = jnp.zeros(matrix.shape, jnp.float32)
    for band_index in range(NBAND):
        start_at = offsets[band_index] + REACH
        sliced = lax.dynamic_slice_in_dim(padded, start_at, columns, 1)
        summed = summed + weights[band_index][None, :] * sliced
    return summed


def body(covariance, precision, band_weight, band_offset, prior_mean, innovation, seen_sites):
    spread_rows = covariance[0]
    weights = band_weight[0]
    offsets = band_offset[0]
    local_rows = spread_rows.shape[0]
    columns = spread_rows.shape[1]
    first_local = lax.axis_index("row") * local_rows
    crossed = band_columns(spread_rows, weights, offsets)
    gain_rows = product(crossed, lax.all_gather(precision[0], "row", axis=0, tiled=True))
    matches = (seen_sites[0][:, None] == jnp.arange(columns, dtype=jnp.int32)[None, :]).astype(
        jnp.float32
    )
    pulled = product(innovation[0], matches)
    filtered = prior_mean[0] + product(spread_rows, pulled)
    rimmed = padded_2(filtered, (("row", 0),), REACH)
    local_weights = lax.dynamic_slice_in_dim(weights, first_local, local_rows, 1)
    forward = jnp.zeros((local_rows,), jnp.float32)
    for band_index in range(NBAND):
        start_at = offsets[band_index] + REACH
        forward = forward + local_weights[band_index] * lax.dynamic_slice_in_dim(
            rimmed, start_at, local_rows, 0
        )
    gain_full, forward_full = (
        lax.all_gather(gain_rows, "row", axis=0, tiled=True),
        lax.all_gather(forward, "row", axis=0, tiled=True),
    )
    spread_now = spread_rows - against(crossed, gain_full)
    shift_rows = filtered - product(gain_rows, forward_full)
    time_index = lax.axis_index("tm")
    time_count = lax.axis_size("tm")
    for stride in (1, 2):
        piece_gain, piece_shift, piece_spread = shifted(
            (gain_rows, shift_rows, spread_now), "tm", -stride
        )
        later_gain, later_shift, later_spread = (
            lax.all_gather(piece_gain, "row", axis=0, tiled=True),
            lax.all_gather(piece_shift, "row", axis=0, tiled=True),
            lax.all_gather(piece_spread, "row", axis=0, tiled=True),
        )
        merged_gain = product(gain_rows, later_gain)
        merged_shift = product(gain_rows, later_shift) + shift_rows
        merged_spread = against(product(gain_rows, later_spread), gain_full) + spread_now
        inside = time_index + stride < time_count
        if stride == 1:
            gain_full = jnp.where(inside, product(gain_full, later_gain), gain_full)
        gain_rows = jnp.where(inside, merged_gain, gain_rows)
        shift_rows = jnp.where(inside, merged_shift, shift_rows)
        spread_now = jnp.where(inside, merged_spread, spread_now)
    return (gain_rows[None], shift_rows[None], spread_now[None])


def solution(mesh):
    in_specs = (
        P("tm", "row", None),
        P("tm", "row", None),
        P("tm", None, None),
        P("tm", None),
        P("tm", "row"),
        P("tm", None),
        P("tm", None),
    )
    out_specs = (P("tm", "row", None), P("tm", "row"), P("tm", "row", None))
    return jax.shard_map(body, mesh=mesh, in_specs=in_specs, out_specs=out_specs, check_vma=False)
```

profile of v0, /device:TPU:96, one launch (start us, length us, event | category | flops | bytes accessed | tf_op | source)
XLA Modules:
  0.0 491.6 jit_solution(2502290297912747095)
XLA Ops:
  8.0 1.5 fusion.51
  16.6 1.9 fusion.27
  18.5 62.7 %all-gather.18.cloned.1.call-done = f32[1,1024,1024]{2,1,0:T(8,128)} async-done(((f32[1,64,1024]{2,1,0:T(8,128)}), f32[1,1024,1024]{2,1,0:T(8,128)}) %all-gather.18.cloned.1.call-update) | async-done | bytes 4194320 | tf_op jit(solution)/shard_map/all_gather | solution.py:65
  81.3 5.5 %fusion = f32[64,1024]{1,0:T(8,128)} fusion(f32[64,1024]{1,0:T(8,128)S(1)} %fusion.27, f32[1,1024,1024]{2,1,0:T(8,128)} %all-gather.18.cloned.1.call-done), kind=kOutput, calls=%fused_computation | convolution fusion | flops 805306368 | bytes 4718592 | tf_op jit(solution)/shard_map/dot_general | solution.py:37
  86.9 1.9 collective-permute-start
  88.8 4.2 collective-permute-done
  93.8 59.8 %all-gather.12.cloned.1.call-done = f32[1024,1024]{1,0:T(8,128)} async-done(((f32[64,1024]{1,0:T(8,128)}), f32[1024,1024]{1,0:T(8,128)}) %all-gather.12.cloned.1.call-update) | async-done | bytes 4194320 | tf_op jit(solution)/shard_map/all_gather | solution.py:80
  153.6 6.3 %convolution_subtract_fusion = f32[64,1024]{1,0:T(8,128)S(1)} fusion(f32[64,1024]{1,0:T(8,128)S(1)} %fusion.27, f32[1024,1024]{1,0:T(8,128)} %all-gather.12.cloned.1.call-done, f32[1,64,1024]{2,1,0:T(8,128)S(1)} %copy-done.4), kind=kOutput, calls=%fused_computation.10 | convolution fusion | flops 805371904 | bytes 4980736 | tf_op jit(solution)/shard_map/dot_general | solution.py:41
  159.9 1.9 collective-permute-start.6
  161.8 3.9 collective-permute-done.6
  166.5 57.4 %all-gather.8.cloned.1.call-done = f32[1024,1024]{1,0:T(8,128)} async-done(((f32[64,1024]{1,0:T(8,128)}), f32[1024,1024]{1,0:T(8,128)}) %all-gather.8.cloned.1.call-update) | async-done | bytes 4194320 | tf_op jit(solution)/shard_map/all_gather | solution.py:92
  223.9 4.8 convolution_select_fusion.1
  228.7 2.4 collective-permute-start.1
  231.1 8.8 %collective-permute-done.1 = f32[64,1024]{1,0:T(8,128)S(1)} collective-permute-done((f32[64,1024]{1,0:T(8,128)S(1)}, f32[64,1024]{1,0:T(8,128)S(1)}, u32[]{:S(2)}, u32[]{:S(2)}) %collective-permute-start.1) | collective-permute-done | bytes 262176 | tf_op jit(solution)/shard_map/ppermute | solution.py:33
  240.9 52.5 %all-gather.14.cloned.1.call-done = f32[1024,1024]{1,0:T(8,128)} async-done(((f32[64,1024]{1,0:T(8,128)}), f32[1024,1024]{1,0:T(8,128)}) %all-gather.14.cloned.1.call-update) | async-done | bytes 4194320 | tf_op jit(solution)/shard_map/all_gather | solution.py:94
  293.4 5.0 %fusion.52 = f32[64,1024]{1,0:T(8,128)S(1)} fusion(f32[64,1024]{1,0:T(8,128)S(1)} %copy-done.3, f32[1024,1024]{1,0:T(8,128)} %all-gather.14.cloned.1.call-done), kind=kOutput, calls=%fused_computation.67 | convolution fusion | flops 805306368 | bytes 4718592 | tf_op jit(solution)/shard_map/dot_general | solution.py:37
  298.4 4.1 fusion.6
  302.5 2.4 collective-permute-start.7
  304.9 8.8 %collective-permute-done.7 = f32[64,1024]{1,0:T(8,128)S(1)} collective-permute-done((f32[64,1024]{1,0:T(8,128)S(1)}, f32[64,1024]{1,0:T(8,128)S(1)}, u32[]{:S(2)}, u32[]{:S(2)}) %collective-permute-start.7) | collective-permute-done | bytes 262176 | tf_op jit(solution)/shard_map/ppermute | solution.py:33
  315.1 1.3 collective-permute-start.3
  316.4 4.5 collective-permute-start.2
  327.1 37.3 %all-reduce.1 = f32[1024]{0:T(1024)S(1)} all-reduce(f32[1024]{0:T(1024)S(1)} %fusion.37), channel_id=1, replica_groups=mesh['tm'=32,'row'=16] {'row'}, use_global_device_ids=true, to_apply=%add.1 | all-reduce | flops 1024 | bytes 8192
  364.7 2.0 collective-permute-start.4
  366.7 1.3 collective-permute-done.4
  368.1 36.0 %all-reduce.2 = f32[1024]{0:T(1024)S(1)} all-reduce(f32[1024]{0:T(1024)S(1)} %dynamic-update-slice.1), channel_id=1, replica_groups=mesh['tm'=32,'row'=16] {'row'}, use_global_device_ids=true, to_apply=%add.2 | all-reduce | flops 1024 | bytes 8192
  404.4 2.0 collective-permute-start.5
  406.4 4.7 collective-permute-done.5
  411.3 37.4 %all-reduce.3 = f32[1024]{0:T(1024)S(1)} all-reduce(f32[1024]{0:T(1024)S(1)} %dynamic-update-slice.2), channel_id=1, replica_groups=mesh['tm'=32,'row'=16] {'row'}, use_global_device_ids=true, to_apply=%add.3 | all-reduce | flops 1024 | bytes 8192
  449.5 17.5 %fusion.54 = f32[1024,1024]{1,0:T(8,128)} fusion(f32[1024,1024]{1,0:T(8,128)} %all-gather.12.cloned.1.call-done, f32[1024,1024]{1,0:T(8,128)} %all-gather.8.cloned.1.call-done), kind=kOutput, calls=%fused_computation.69 | convolution fusion | flops 12884901888 | bytes 12582912 | tf_op jit(solution)/shard_map/dot_general | solution.py:37
  467.0 5.5 %fusion.5 = f32[1,64,1024]{2,1,0:T(8,128)} fusion(f32[64,1024]{1,0:T(8,128)S(1)} %convolution_select_fusion.1, f32[1024,1024]{1,0:T(8,128)} %all-gather.10.cloned.1.call-done, pred[]{:T(512)S(6)} %lt.29), kind=kOutput, calls=%fused_computation.7 | convolution fusion | flops 805371904 | bytes 4718593 | tf_op jit(solution)/shard_map/dot_general | solution.py:37
  472.6 5.0 %fusion.53 = f32[64,1024]{1,0:T(8,128)S(1)} fusion(f32[64,1024]{1,0:T(8,128)S(1)} %convolution_select_fusion.1, f32[1024,1024]{1,0:T(8,128)} %all-gather.16.cloned.1.call-done), kind=kOutput, calls=%fused_computation.68 | convolution fusion | flops 805306368 | bytes 4718592 | tf_op jit(solution)/shard_map/dot_general | solution.py:37
  477.6 7.2 %fusion.13 = f32[1,64,1024]{2,1,0:T(8,128)} fusion(f32[64,1024]{1,0:T(8,128)S(1)} %fusion.6, f32[64,1024]{1,0:T(8,128)S(1)} %fusion.53, f32[1024,1024]{1,0:T(8,128)} %fusion.54, f32[1024,1024]{1,0:T(8,128)S(1)} %copy-done.2, pred[]{:T(512)S(6)} %lt.30, pred[]{:T(512)S(6)} %lt.29), kind=kOutput, calls=%fused_computation.13 | convolution fusion | flops 806486016 | bytes 9175042 | tf_op jit(solution)/shard_map/dot_general | solution.py:41
  (52 shorter events, 9.4 us)
Async XLA Ops:
  7.2 307.3 %copy-start = (f32[1,128]{1,0:T(1,128)S(1)}, f32[1,128]{1,0:T(1,128)}, u32[]{:S(2)}) copy-start(f32[1,128]{1,0:T(1,128)} %param.12) | copy-start | bytes 1540
  7.2 146.5 %copy-start.4 = (f32[1,64,1024]{2,1,0:T(8,128)S(1)}, f32[1,64,1024]{2,1,0:T(8,128)}, u32[]{:S(2)}) copy-start(f32[1,64,1024]{2,1,0:T(8,128)} %param.7) | copy-start | bytes 786436
  7.2 74.1 %all-gather.18.cloned.1.call-start = ((), (), s32[]{:S(2)}) async-start(), calls=%async_computation.5 | async-start | bytes 4456448 | tf_op jit(solution)/shard_map/all_gather | solution.py:65
  7.9 145.7 %all-gather.12.cloned.1.call-start = ((), (), s32[]{:S(2)}) async-start(), calls=%async_computation.2 | async-start | bytes 4456448 | tf_op jit(solution)/shard_map/all_gather | solution.py:80
  86.8 137.1 %copy-start.3 = (f32[64,1024]{1,0:T(8,128)S(1)}, f32[64,1024]{1,0:T(8,128)}, u32[]{:S(2)}) copy-start(f32[64,1024]{1,0:T(8,128)} %fusion) | copy-start | bytes 786436
  86.9 137.0 %all-gather.8.cloned.1.call-start = ((), (), s32[]{:S(2)}) async-start(), calls=%async_computation | async-start | bytes 4456448 | tf_op jit(solution)/shard_map/all_gather | solution.py:92
  86.9 6.1 %collective-permute-start = (f32[64,1024]{1,0:T(8,128)}, f32[64,1024]{1,0:T(8,128)S(1)}, u32[]{:S(2)}, u32[]{:S(2)}) collective-permute-start(f32[64,1024]{1,0:T(8,128)} %fusion), channel_id=1, source_target_pairs={{16,0},{32,16},{48,32},{64,48},{80,64},{96,80},{112,96},{128,112},... | collective-permute-start | bytes 786440 | tf_op jit(solution)/shard_map/ppermute | solution.py:33
  93.0 0.7 copy-start.7
  93.7 199.7 %all-gather.14.cloned.1.call-start = ((), (), s32[]{:S(2)}) async-start(), calls=%async_computation.3 | async-start | bytes 4456448 | tf_op jit(solution)/shard_map/all_gather | solution.py:94
  159.9 5.8 %collective-permute-start.6 = (f32[64,1024]{1,0:T(8,128)S(1)}, f32[64,1024]{1,0:T(8,128)S(1)}, u32[]{:S(2)}, u32[]{:S(2)}) collective-permute-start(f32[64,1024]{1,0:T(8,128)S(1)} %convolution_subtract_fusion), channel_id=1, source_target_pairs={{16,0},{32,16},{48,32},{64,48},{80,64},{96,80},{112,96},{128,112},... | collective-permute-start | bytes 786440 | tf_op jit(solution)/shard_map/ppermute | solution.py:33
  165.7 0.7 copy-start.8
  166.4 300.6 %all-gather.10.cloned.1.call-start = ((), (), s32[]{:S(2)}) async-start(), calls=%async_computation.1 | async-start | bytes 4456448 | tf_op jit(solution)/shard_map/all_gather | solution.py:92
  228.7 11.2 %collective-permute-start.1 = (f32[64,1024]{1,0:T(8,128)S(1)}, f32[64,1024]{1,0:T(8,128)S(1)}, u32[]{:S(2)}, u32[]{:S(2)}) collective-permute-start(f32[64,1024]{1,0:T(8,128)S(1)} %convolution_select_fusion.1), channel_id=1, source_target_pairs={{32,0},{48,16},{64,32},{80,48},{96,64},{112,80},{128,96},{144,112}... | collective-permute-start | bytes 786440 | tf_op jit(solution)/shard_map/ppermute | solution.py:33
  239.9 0.7 copy-start.5
  240.6 73.8 %copy-start.10 = (s32[1,128]{1,0:T(1,128)S(1)}, s32[1,128]{1,0:T(1,128)}, u32[]{:S(2)}) copy-start(s32[1,128]{1,0:T(1,128)} %param.13) | copy-start | bytes 1540
  240.6 74.1 %copy-start.9 = (f32[1,64]{1,0:T(1,128)S(1)}, f32[1,64]{1,0:T(1,128)}, u32[]{:S(2)}) copy-start(f32[1,64]{1,0:T(1,128)} %param.11) | copy-start | bytes 772
  240.6 231.9 %all-gather.16.cloned.1.call-start = ((), (), s32[]{:S(2)}) async-start(), calls=%async_computation.4 | async-start | bytes 4456448 | tf_op jit(solution)/shard_map/all_gather | solution.py:94
  293.4 5.0 %copy-start.1 = (f32[1024,1024]{1,0:T(8,128)S(1)}, f32[1024,1024]{1,0:T(8,128)}, u32[]{:S(2)}) copy-start(f32[1024,1024]{1,0:T(8,128)} %all-gather.12.cloned.1.call-done) | copy-start | bytes 12582916
  302.5 11.1 %collective-permute-start.7 = (f32[64,1024]{1,0:T(8,128)S(1)}, f32[64,1024]{1,0:T(8,128)S(1)}, u32[]{:S(2)}, u32[]{:S(2)}) collective-permute-start(f32[64,1024]{1,0:T(8,128)S(1)} %fusion.6), channel_id=1, source_target_pairs={{32,0},{48,16},{64,32},{80,48},{96,64},{112,80},{128,96},{144,112}... | collective-permute-start | bytes 786440 | tf_op jit(solution)/shard_map/ppermute | solution.py:33
  313.7 0.7 copy-start.6
  315.1 11.1 %collective-permute-start.3 = (f32[64]{0:T(128)S(1)}, f32[64]{0:T(128)S(1)}, u32[]{:S(2)}, u32[]{:S(2)}) collective-permute-start(f32[64]{0:T(128)S(1)} %fusion.22), channel_id=1, source_target_pairs={{1,0},{2,1},{3,2},{4,3},{5,4},{6,5},{7,6},{8,7},{9,8},{10,9},{11,1... | collective-permute-start | bytes 776 | tf_op jit(solution)/shard_map/ppermute | solution.py:23
  316.4 9.7 %collective-permute-start.2 = (f32[64]{0:T(128)S(1)}, f32[64]{0:T(128)S(1)}, u32[]{:S(2)}, u32[]{:S(2)}) collective-permute-start(f32[64]{0:T(128)S(1)} %fusion.22), channel_id=1, source_target_pairs={{0,1},{1,2},{2,3},{3,4},{4,5},{5,6},{6,7},{7,8},{8,9},{9,10},{10,1... | collective-permute-start | bytes 776 | tf_op jit(solution)/shard_map/ppermute | solution.py:21
  364.7 3.2 collective-permute-start.4
  404.4 6.7 %collective-permute-start.5 = (f32[64]{0:T(128)S(1)}, f32[64]{0:T(128)S(1)}, u32[]{:S(2)}, u32[]{:S(2)}) collective-permute-start(f32[64]{0:T(128)S(1)} %fusion.20), channel_id=1, source_target_pairs={{32,0},{48,16},{64,32},{80,48},{96,64},{112,80},{128,96},{144,112}... | collective-permute-start | bytes 776 | tf_op jit(solution)/shard_map/ppermute | solution.py:33
  472.6 5.0 %copy-start.2 = (f32[1024,1024]{1,0:T(8,128)S(1)}, f32[1024,1024]{1,0:T(8,128)}, u32[]{:S(2)}) copy-start(f32[1024,1024]{1,0:T(8,128)} %all-gather.12.cloned.1.call-done) | copy-start | bytes 12582916
Sparse Core Ops, SparseCore 0:
  11.0 70.2 all-gather.17
  87.0 66.6 all-gather.11
  157.2 66.6 all-gather.7
  226.8 66.6 all-gather.13
  296.9 66.9 all-gather.9
  366.7 66.9 all-gather.15
where the time goes:
time: 492 us
  waiting for transfers between devices  265 us (54%)
  blocking collectives  111 us (23%)
  matrix products  62.9 us (13%)
  between operations  24.6 us (5%)
  starting transfers between devices  18.8 us (4%)
  local copies, waits for them, and re-layouts  6.74 us (1%)
    unnamed x3, blocking collectives  111 us
    all_gather x1, waiting for transfers between devices, body(): lax.all_gather(precision[0], 'row', axis=0, tiled=True)  62.7 us
    all_gather x1, waiting for transfers between devices, body(): lax.all_gather(gain_rows, 'row', axis=0, tiled=True)  59.8 us
    all_gather x2, waiting for transfers between devices, body(): lax.all_gather(piece_gain, 'row', axis=0, tiled=True)  57.4 us
    all_gather x2, waiting for transfers between devices, body(): lax.all_gather(piece_spread, 'row', axis=0, tiled=True)  52.6 us
    dot_general x11, matrix products, product(): jnp.dot(left, right, precision=HIGHEST, preferred_element_type=jnp.float32)  45.4 us
    ppermute x6, waiting for transfers between devices, shifted(): return lax.ppermute(block, axis, route)  31.6 us
    dot_general x3, matrix products, against(): lax.dot_general(left, right, (((1,), (1,)), ((), ())), precision=HIGHEST,...  17.6 us
  transfers between devices with their start and end apart: 14, of which 10 were waited for; matrix products, arithmetic and copies ran while one was open for 11% of the time, Pallas kernels for 0%

commit v1 on v0

v1 whole, which is shorter than its diff:
```python
import jax
import jax.numpy as jnp
from jax import lax
from jax.sharding import Mesh, PartitionSpec as P

NBAND = 5
REACH = 64
SIDE = 4

HIGHEST = lax.Precision.HIGHEST
HIGH = lax.Precision.HIGH


def shifted(block, distance):
    count = lax.axis_size("tm")
    return lax.ppermute(block, "tm", [(i + distance, i) for i in range(count - distance)])


def swap(message, axis):
    return lax.all_to_all(message, axis, 0, 0)


def spread_out(message, axis):
    return swap(jnp.broadcast_to(message[None], (SIDE,) + message.shape), axis)


def times(left, right):
    return jnp.dot(left, right, precision=HIGH, preferred_element_type=jnp.float32)


def against(left, right):
    return lax.dot_general(
        left, right, (((1,), (1,)), ((), ())), precision=HIGH, preferred_element_type=jnp.float32
    )


def matvec(matrix, vector):
    return jnp.sum(matrix * vector[None, :], axis=1)


def band_columns(matrix, weights, offsets):
    columns = matrix.shape[-1]
    padded = jnp.pad(matrix, ((0, 0), (REACH, REACH)))
    summed = jnp.zeros(matrix.shape, jnp.float32)
    for band_index in range(NBAND):
        start_at = offsets[band_index] + REACH
        sliced = lax.dynamic_slice_in_dim(padded, start_at, columns, 1)
        summed = summed + weights[band_index][None, :] * sliced
    return summed


def swap_order(array):
    rest = array.shape[1:]
    rows = array.shape[0]
    parts = array.reshape((SIDE, SIDE, rows // (SIDE * SIDE)) + rest)
    return jnp.swapaxes(parts, 0, 1).reshape((rows,) + rest)


def swap_lanes(array):
    rows, columns = array.shape
    parts = array.reshape(rows, SIDE, SIDE, columns // (SIDE * SIDE))
    return jnp.swapaxes(parts, 1, 2).reshape(rows, columns)


def side_by_side(blocks):
    return jnp.concatenate([blocks[i] for i in range(SIDE)], axis=1)


def with_row(block, vector):
    return jnp.concatenate([block, jnp.pad(vector[None, :], ((0, 7), (0, 0)))], axis=0)


def body(covariance, precision, band_weight, band_offset, prior_mean, innovation, seen_sites):
    own = covariance[0]
    inverse = precision[0]
    weights = band_weight[0]
    offsets = band_offset[0]
    rows, columns = own.shape
    panel = SIDE * rows
    at_y = lax.axis_index("y")
    at_x = lax.axis_index("x")
    at_t = lax.axis_index("tm")
    count_t = lax.axis_size("tm")

    crossed = band_columns(own, weights, offsets)
    matches = seen_sites[0][:, None] == jnp.arange(columns, dtype=jnp.int32)[None, :]
    pulled = jnp.sum(jnp.where(matches, innovation[0][:, None], 0.0), axis=0)
    filtered = prior_mean[0] + matvec(own, pulled)

    pieces = own.reshape(rows, SIDE, SIDE, rows).transpose(2, 0, 1, 3).reshape(SIDE, rows, panel)
    message = jnp.concatenate(
        [jnp.broadcast_to(crossed[None], (SIDE, rows, columns)), pieces], axis=2
    )
    got = swap(message, "x").reshape(panel, columns + panel)
    crossed_panel = got[:, :columns]
    own_block = got[:, columns:]
    padded = jnp.pad(filtered, (0, columns - rows))
    got = spread_out(with_row(inverse, padded), "y")
    inverse_panel = got[:, :rows].reshape(panel, columns)
    filtered_mine = got[:, rows, :rows].reshape(panel)
    gain = against(crossed_panel, inverse_panel)

    crossed_mine = lax.all_gather(swap_lanes(crossed), "y", axis=0, tiled=True)
    gain_tall = lax.all_gather(gain, "y", axis=0, tiled=True)
    gain_later = shifted(gain, 1)

    got = spread_out(with_row(gain, filtered_mine), "x")
    gain_wide = side_by_side(got[:, :panel])
    filtered_all = swap_order(got[:, panel].reshape(columns))
    rimmed = jnp.pad(filtered_all, (REACH, REACH))
    forward = jnp.zeros((columns,), jnp.float32)
    for band_index in range(NBAND):
        start_at = offsets[band_index] + REACH
        forward = forward + weights[band_index] * lax.dynamic_slice_in_dim(
            rimmed, start_at, columns, 0
        )
    shift = lax.dynamic_slice_in_dim(filtered_all, at_y * panel, panel, 0) - matvec(
        gain_wide, swap_order(forward)
    )
    spread = own_block - against(gain_wide, crossed_mine)

    later = jnp.concatenate([gain_later, shifted(with_row(spread, shift), 1)], axis=0)
    got = spread_out(later, "y")
    later_gain = swap_order(got[:, :panel].reshape(columns, panel))
    later_spread = swap_order(got[:, panel : 2 * panel].reshape(columns, panel))
    later_shift = swap_order(got[:, 2 * panel].reshape(columns))
    inside = at_t + 1 < count_t
    gain_2 = jnp.where(inside, times(gain_wide, later_gain), gain)
    turned = jnp.where(inside, times(gain_wide, later_spread), 0.0)
    shift_2 = shift + jnp.where(inside, matvec(gain_wide, later_shift), 0.0)
    gain_2_later = shifted(gain_2, 2)
    part = against(swap_order(gain_tall), turned).reshape(SIDE, panel, panel)
    message = jnp.concatenate(
        [part, jnp.broadcast_to(gain_2[None], (SIDE, panel, panel))], axis=1
    )
    got = swap(message, "x")
    spread_2 = spread + jnp.sum(got[:, :panel], axis=0).T
    gain_2_wide = side_by_side(got[:, panel:])

    tall = lax.all_gather(jnp.concatenate([gain_2, gain_2_later], axis=0), "y", axis=0)
    got = spread_out(shifted(with_row(spread_2, shift_2), 2), "y")
    later_spread = swap_order(got[:, :panel].reshape(columns, panel))
    later_shift = swap_order(got[:, panel].reshape(columns))
    inside = at_t + 2 < count_t
    gain_2_tall = tall[:, :panel].reshape(columns, panel)
    later_gain = swap_order(tall[:, panel:].reshape(columns, panel))
    turned = jnp.where(inside, times(gain_2_wide, later_spread), 0.0)
    gain_4 = jnp.where(inside, times(gain_2_wide, later_gain), gain_2)
    shift_4 = shift_2 + jnp.where(inside, matvec(gain_2_wide, later_shift), 0.0)
    part = against(turned, gain_2_tall).reshape(SIDE, rows, columns)
    message = jnp.concatenate(
        [part, gain_4.reshape(SIDE, rows, panel), spread_2.reshape(SIDE, rows, panel)], axis=2
    )
    got = swap(message, "x")
    placed = swap_lanes(jnp.concatenate([got[i, :, columns : columns + panel] for i in range(SIDE)], axis=1))
    kept = swap_lanes(jnp.concatenate([got[i, :, columns + panel :] for i in range(SIDE)], axis=1))
    final_spread = jnp.sum(got[:, :, :columns], axis=0) + kept
    final_shift = lax.dynamic_slice_in_dim(shift_4, at_x * rows, rows, 0)
    return placed[None], final_shift[None], final_spread[None]


def solution(mesh):
    count = mesh.devices.shape[0]
    grid = Mesh(mesh.devices.reshape(count, SIDE, SIDE), ("tm", "y", "x"))
    row = ("y", "x")
    in_specs = (
        P("tm", row, None),
        P("tm", row, None),
        P("tm", None, None),
        P("tm", None),
        P("tm", row),
        P("tm", None),
        P("tm", None),
    )
    out_specs = (P("tm", row, None), P("tm", row), P("tm", row, None))
    return jax.shard_map(body, mesh=grid, in_specs=in_specs, out_specs=out_specs, check_vma=False)
```

time: 492 us -> 261 us (0.53)
  the two profiles are of different devices: /device:TPU:96 before, /device:TPU:32 now
where the time goes in v1:
time: 261 us; the launch traced here: 259 us
  waiting for transfers between devices  159 us (61%)
  starting transfers between devices  37 us (14%)
  local copies, waits for them, and re-layouts  23.1 us (9%)
  between operations  20.7 us (8%)
  other arithmetic  13.9 us (5%)
  matrix products  6.14 us (2%)
    all_to_all x7, waiting for transfers between devices, swap(): return lax.all_to_all(message, axis, 0, 0)  85.5 us
    all_gather x1, waiting for transfers between devices, body(): gain_tall = lax.all_gather(gain, 'y', axis=0, tiled=True)  37.9 us
    all_to_all x7, starting transfers between devices, swap(): return lax.all_to_all(message, axis, 0, 0)  28.6 us
    all_gather x1, waiting for transfers between devices, body(): crossed_mine = lax.all_gather(swap_lanes(crossed), 'y', axis=0, tiled=True)  23.8 us
    ppermute x4, waiting for transfers between devices, shifted(): lax.ppermute(block, 'tm', [(i + distance, i) for i in range(count - dista...  10.7 us
    ppermute x4, starting transfers between devices, shifted(): lax.ppermute(block, 'tm', [(i + distance, i) for i in range(count - dista...  8.25 us
  transfers between devices with their start and end apart: 14, of which 10 were waited for; matrix products, arithmetic and copies ran while one was open for 8% of the time, Pallas kernels for 0%

profile of v1, /device:TPU:32, one launch (start us, length us, event | category | flops | bytes accessed | tf_op | source)
XLA Modules:
  0.0 259.4 jit_solution(3531839173708747810)
XLA Ops:
  11.9 4.5 %all-to-all-start.1 = ((f32[4,72,1024]{2,1,0:T(8,128)}), f32[4,72,1024]{2,1,0:T(8,128)S(1)}, u32[]{:S(2)}, u32[]{:S(2)}) async-start(f32[4,72,1024]{2,1,0:T(8,128)} %broadcast_in_dim.80), calls=%async_computation.1 | async-start | bytes 2359296 | tf_op jit(solution)/shard_map/all_to_all | solution.py:20
  25.4 1.2 pad_maximum_fusion.2
  26.6 6.2 %all-to-all-done.1 = f32[4,72,1024]{2,1,0:T(8,128)S(1)} async-done(((f32[4,72,1024]{2,1,0:T(8,128)}), f32[4,72,1024]{2,1,0:T(8,128)S(1)}, u32[]{:S(2)}, u32[]{:S(2)}) %all-to-all-start.1) | async-done | bytes 1179680 | tf_op jit(solution)/shard_map/all_to_all | solution.py:20
  32.8 4.3 %all-to-all-start = ((f32[4,64,1280]{2,1,0:T(8,128)}), f32[4,64,1280]{2,1,0:T(8,128)S(1)}, u32[]{:S(2)}, u32[]{:S(2)}) async-start(f32[4,64,1280]{2,1,0:T(8,128)} %pad_maximum_fusion.2), calls=%async_computation | async-start | bytes 2621440 | tf_op jit(solution)/shard_map/all_to_all | solution.py:20
  37.9 15.9 %all-to-all-done = f32[4,64,1280]{2,1,0:T(8,128)S(1)} async-done(((f32[4,64,1280]{2,1,0:T(8,128)}), f32[4,64,1280]{2,1,0:T(8,128)S(1)}, u32[]{:S(2)}, u32[]{:S(2)}) %all-to-all-start) | async-done | bytes 1310752 | tf_op jit(solution)/shard_map/all_to_all | solution.py:20
  55.6 3.5 %all-to-all-start.2 = ((f32[4,264,256]{2,1,0:T(8,128)}), f32[4,264,256]{2,1,0:T(8,128)S(1)}, u32[]{:S(2)}, u32[]{:S(2)}) async-start(f32[4,264,256]{2,1,0:T(8,128)} %broadcast_in_dim.81), calls=%async_computation.2 | async-start | bytes 2162688 | tf_op jit(solution)/shard_map/all_to_all | solution.py:20
  60.5 2.2 reshape.154
  62.7 9.7 %all-to-all-done.2 = f32[4,264,256]{2,1,0:T(8,128)S(1)} async-done(((f32[4,264,256]{2,1,0:T(8,128)}), f32[4,264,256]{2,1,0:T(8,128)S(1)}, u32[]{:S(2)}, u32[]{:S(2)}) %all-to-all-start.2) | async-done | bytes 1081376 | tf_op jit(solution)/shard_map/all_to_all | solution.py:20
  73.2 23.8 %all-gather.7.cloned.1.call-done = f32[256,1024]{1,0:T(8,128)} async-done(((f32[64,1024]{1,0:T(8,128)}), f32[256,1024]{1,0:T(8,128)}) %all-gather.7.cloned.1.call-update) | async-done | bytes 1048592 | tf_op jit(solution)/shard_map/all_gather | solution.py:103
  97.0 1.8 convolution_subtract_fusion
  98.9 1.9 collective-permute-start.1
  100.8 2.5 collective-permute-start
  103.3 4.3 %collective-permute-done = f32[256,256]{1,0:T(8,128)S(1)} collective-permute-done((f32[256,256]{1,0:T(8,128)S(1)}, f32[256,256]{1,0:T(8,128)S(1)}, u32[]{:S(2)}, u32[]{:S(2)}) %collective-permute-start) | collective-permute-done | bytes 262176 | tf_op jit(solution)/shard_map/ppermute | solution.py:16
  107.6 1.5 broadcast_in_dim.83
  109.1 3.6 %all-to-all-start.3 = ((f32[4,520,256]{2,1,0:T(8,128)}), f32[4,520,256]{2,1,0:T(8,128)S(1)}, u32[]{:S(2)}, u32[]{:S(2)}) async-start(f32[4,520,256]{2,1,0:T(8,128)} %broadcast_in_dim.83), calls=%async_computation.3 | async-start | bytes 4259840 | tf_op jit(solution)/shard_map/all_to_all | solution.py:20
  113.5 37.9 %all-gather.5.cloned.1.call-done = f32[1024,256]{1,0:T(8,128)} async-done(((f32[256,256]{1,0:T(8,128)}), f32[1024,256]{1,0:T(8,128)}) %all-gather.5.cloned.1.call-update) | async-done | bytes 1048592 | tf_op jit(solution)/shard_map/all_gather | solution.py:104
  151.4 2.3 copy.50
  155.6 1.9 collective-permute-start.3
  158.2 1.5 pad_maximum_fusion
  159.8 4.5 %all-to-all-start.4 = ((f32[4,512,256]{2,1,0:T(8,128)}), f32[4,512,256]{2,1,0:T(8,128)}, u32[]{:S(2)}, u32[]{:S(2)}) async-start(f32[4,512,256]{2,1,0:T(8,128)} %pad_maximum_fusion), calls=%async_computation.4 | async-start | bytes 4194304 | tf_op jit(solution)/shard_map/all_to_all | solution.py:20
  164.3 1.8 pad_maximum_fusion.6
  166.5 23.1 %all-to-all-done.4 = f32[4,512,256]{2,1,0:T(8,128)} async-done(((f32[4,512,256]{2,1,0:T(8,128)}), f32[4,512,256]{2,1,0:T(8,128)}, u32[]{:S(2)}, u32[]{:S(2)}) %all-to-all-start.4) | async-done | bytes 2097184 | tf_op jit(solution)/shard_map/all_to_all | solution.py:20
  189.6 1.3 slice_reduce_fusion.1
  191.1 1.9 collective-permute-start.2
  193.1 6.4 %collective-permute-done.2 = f32[264,256]{1,0:T(8,128)S(1)} collective-permute-done((f32[264,256]{1,0:T(8,128)S(1)}, f32[264,256]{1,0:T(8,128)S(1)}, u32[]{:S(2)}, u32[]{:S(2)}) %collective-permute-start.2) | collective-permute-done | bytes 270368 | tf_op jit(solution)/shard_map/ppermute | solution.py:16
  200.5 4.0 %all-to-all-start.5 = ((f32[4,264,256]{2,1,0:T(8,128)}), f32[4,264,256]{2,1,0:T(8,128)S(1)}, u32[]{:S(2)}, u32[]{:S(2)}) async-start(f32[4,264,256]{2,1,0:T(8,128)} %broadcast_in_dim.88), calls=%async_computation.5 | async-start | bytes 2162688 | tf_op jit(solution)/shard_map/all_to_all | solution.py:20
  204.6 1.3 slice_bitcast_fusion.3
  205.9 12.7 %all-to-all-done.5 = f32[4,264,256]{2,1,0:T(8,128)S(1)} async-done(((f32[4,264,256]{2,1,0:T(8,128)}), f32[4,264,256]{2,1,0:T(8,128)S(1)}, u32[]{:S(2)}, u32[]{:S(2)}) %all-to-all-start.5) | async-done | bytes 1081376 | tf_op jit(solution)/shard_map/all_to_all | solution.py:20
  219.4 1.7 fusion.24
  223.3 1.3 pad_maximum_fusion.1
  224.6 4.3 %all-to-all-start.6 = ((f32[4,64,1536]{2,1,0:T(8,128)}), f32[4,64,1536]{2,1,0:T(8,128)S(1)}, u32[]{:S(2)}, u32[]{:S(2)}) async-start(f32[4,64,1536]{2,1,0:T(8,128)} %pad_maximum_fusion.1), calls=%async_computation.6 | async-start | bytes 3145728 | tf_op jit(solution)/shard_map/all_to_all | solution.py:20
  230.7 17.8 %all-to-all-done.6 = f32[4,64,1536]{2,1,0:T(8,128)S(1)} async-done(((f32[4,64,1536]{2,1,0:T(8,128)}), f32[4,64,1536]{2,1,0:T(8,128)S(1)}, u32[]{:S(2)}, u32[]{:S(2)}) %all-to-all-start.6) | async-done | bytes 1572896 | tf_op jit(solution)/shard_map/all_to_all | solution.py:20
  (125 shorter events, 26.2 us)
Async XLA Ops:
  10.7 5.6 %copy-start.15 = (s32[1,5]{1,0:T(1,128)S(1)}, s32[1,5]{1,0:T(1,128)}, u32[]{:S(2)}) copy-start(s32[1,5]{1,0:T(1,128)} %param.10) | copy-start | bytes 64
  10.7 12.5 %copy-start.11 = (f32[1,64,1024]{2,1,0:T(8,128)S(1)}, f32[1,64,1024]{2,1,0:T(8,128)}, u32[]{:S(2)}) copy-start(f32[1,64,1024]{2,1,0:T(8,128)} %param.7) | copy-start | bytes 786436
  11.9 21.0 %all-to-all-start.1 = ((f32[4,72,1024]{2,1,0:T(8,128)}), f32[4,72,1024]{2,1,0:T(8,128)S(1)}, u32[]{:S(2)}, u32[]{:S(2)}) async-start(f32[4,72,1024]{2,1,0:T(8,128)} %broadcast_in_dim.80), calls=%async_computation.1 | async-start | bytes 2359296 | tf_op jit(solution)/shard_map/all_to_all | solution.py:20
  16.3 7.8 %copy-start.14 = (f32[1,5,1024]{2,0,1:T(1,128)S(1)}, f32[1,5,1024]{2,0,1:T(1,128)}, u32[]{:S(2)}) copy-start(f32[1,5,1024]{2,0,1:T(1,128)} %param.9) | copy-start | bytes 61444
  24.1 2.5 copy-start.12
  24.6 0.7 copy-start.7
  32.8 21.0 %all-to-all-start = ((f32[4,64,1280]{2,1,0:T(8,128)}), f32[4,64,1280]{2,1,0:T(8,128)S(1)}, u32[]{:S(2)}, u32[]{:S(2)}) async-start(f32[4,64,1280]{2,1,0:T(8,128)} %pad_maximum_fusion.2), calls=%async_computation | async-start | bytes 2621440 | tf_op jit(solution)/shard_map/all_to_all | solution.py:20
  37.9 16.6 %copy-start.16 = (f32[1,256]{1,0:T(1,128)S(1)}, f32[1,256]{1,0:T(1,128)}, u32[]{:S(2)}) copy-start(f32[1,256]{1,0:T(1,128)} %broadcast_in_dim_reshape_squeeze.3) | copy-start | bytes 3076
  54.5 1.1 copy-start.1
  54.5 4.7 %copy-start.8 = (f32[64,1024]{1,0:T(8,128)S(1)}, f32[64,1024]{1,0:T(8,128)}, u32[]{:S(2)}) copy-start(f32[64,1024]{1,0:T(8,128)} %copy-done.7) | copy-start | bytes 786436
  55.6 16.8 %all-to-all-start.2 = ((f32[4,264,256]{2,1,0:T(8,128)}), f32[4,264,256]{2,1,0:T(8,128)S(1)}, u32[]{:S(2)}, u32[]{:S(2)}) async-start(f32[4,264,256]{2,1,0:T(8,128)} %broadcast_in_dim.81), calls=%async_computation.2 | async-start | bytes 2162688 | tf_op jit(solution)/shard_map/all_to_all | solution.py:20
  59.1 13.5 %copy-start.13 = (f32[1,1,1024]{2,0,1:T(1,128)S(1)}, f32[1,1,1024]{2,0,1:T(1,128)}, u32[]{:S(2)}) copy-start(f32[1,1,1024]{2,0,1:T(1,128)} %copy-done.12) | copy-start | bytes 12292
  59.1 37.9 %all-gather.7.cloned.1.call-start = ((), (), s32[]{:S(2)}) async-start(), calls=%async_computation.8 | async-start | bytes 1310720 | tf_op jit(solution)/shard_map/all_gather | solution.py:103
  73.2 27.6 %copy-start.2 = (f32[256,256]{1,0:T(8,128)S(1)}, f32[256,256]{1,0:T(8,128)}, u32[]{:S(2)}) copy-start(f32[256,256]{1,0:T(8,128)} %copy-done.1) | copy-start | bytes 786436
  98.9 10.3 %copy-start.9 = (f32[256,256]{1,0:T(8,128)}, f32[256,256]{1,0:T(8,128)S(1)}, u32[]{:S(2)}) copy-start(f32[256,256]{1,0:T(8,128)S(1)} %convolution_subtract_fusion) | copy-start | bytes 786436
  98.9 8.7 %collective-permute-start.1 = (f32[264,256]{1,0:T(8,128)S(1)}, f32[264,256]{1,0:T(8,128)S(1)}, u32[]{:S(2)}, u32[]{:S(2)}) collective-permute-start(f32[264,256]{1,0:T(8,128)S(1)} %select_maximum_fusion.2), channel_id=1, source_target_pairs={{16,0},{32,16},{48,32},{64,48},{80,64},{96,80},{112,96},{128,112},... | collective-permute-start | bytes 811016 | tf_op jit(solution)/shard_map/ppermute | solution.py:16
  100.8 6.8 %collective-permute-start = (f32[256,256]{1,0:T(8,128)S(1)}, f32[256,256]{1,0:T(8,128)S(1)}, u32[]{:S(2)}, u32[]{:S(2)}) collective-permute-start(f32[256,256]{1,0:T(8,128)S(1)} %copy-done.2), channel_id=1, source_target_pairs={{16,0},{32,16},{48,32},{64,48},{80,64},{96,80},{112,96},{128,112},... | collective-permute-start | bytes 786440 | tf_op jit(solution)/shard_map/ppermute | solution.py:16
  109.1 44.5 %all-to-all-start.3 = ((f32[4,520,256]{2,1,0:T(8,128)}), f32[4,520,256]{2,1,0:T(8,128)S(1)}, u32[]{:S(2)}, u32[]{:S(2)}) async-start(f32[4,520,256]{2,1,0:T(8,128)} %broadcast_in_dim.83), calls=%async_computation.3 | async-start | bytes 4259840 | tf_op jit(solution)/shard_map/all_to_all | solution.py:20
  112.7 38.6 %all-gather.5.cloned.1.call-start = ((), (), s32[]{:S(2)}) async-start(), calls=%async_computation.7 | async-start | bytes 1310720 | tf_op jit(solution)/shard_map/all_gather | solution.py:104
  154.0 1.0 copy-start.3
  154.6 2.9 %copy-start = (f32[4,4,64,256]{3,2,1,0:T(8,128)S(1)}, f32[4,4,64,256]{3,2,1,0:T(8,128)}, u32[]{:S(2)}) copy-start(f32[4,4,64,256]{3,2,1,0:T(8,128)} %copy.50) | copy-start | bytes 3145732
  155.6 8.8 %copy-start.5 = (f32[256,256]{1,0:T(8,128)}, f32[256,256]{1,0:T(8,128)S(1)}, u32[]{:S(2)}) copy-start(f32[256,256]{1,0:T(8,128)S(1)} %convolution_select_fusion.2) | copy-start | bytes 786436
  155.6 8.7 %collective-permute-start.3 = (f32[256,256]{1,0:T(8,128)S(1)}, f32[256,256]{1,0:T(8,128)}, u32[]{:S(2)}, u32[]{:S(2)}) collective-permute-start(f32[256,256]{1,0:T(8,128)S(1)} %convolution_select_fusion.2), channel_id=1, source_target_pairs={{32,0},{48,16},{64,32},{80,48},{96,64},{112,80},{128,96},{144,112}... | collective-permute-start | bytes 786440 | tf_op jit(solution)/shard_map/ppermute | solution.py:16
  159.8 29.8 %all-to-all-start.4 = ((f32[4,512,256]{2,1,0:T(8,128)}), f32[4,512,256]{2,1,0:T(8,128)}, u32[]{:S(2)}, u32[]{:S(2)}) async-start(f32[4,512,256]{2,1,0:T(8,128)} %pad_maximum_fusion), calls=%async_computation.4 | async-start | bytes 4194304 | tf_op jit(solution)/shard_map/all_to_all | solution.py:20
  164.2 55.1 %all-gather.9.cloned.1.call-start = ((), (), s32[]{:S(2)}) async-start(), calls=%async_computation.9 | async-start | bytes 2621440 | tf_op jit(solution)/shard_map/all_gather | solution.py:140
  166.1 24.9 %copy-start.10 = (f32[256,256]{1,0:T(8,128)S(1)}, f32[256,256]{1,0:T(8,128)}, u32[]{:S(2)}) copy-start(f32[256,256]{1,0:T(8,128)} %copy-done.9) | copy-start | bytes 786436
  191.1 8.4 %collective-permute-start.2 = (f32[264,256]{1,0:T(8,128)S(1)}, f32[264,256]{1,0:T(8,128)S(1)}, u32[]{:S(2)}, u32[]{:S(2)}) collective-permute-start(f32[264,256]{1,0:T(8,128)S(1)} %select_maximum_fusion.1), channel_id=1, source_target_pairs={{32,0},{48,16},{64,32},{80,48},{96,64},{112,80},{128,96},{144,112}... | collective-permute-start | bytes 811016 | tf_op jit(solution)/shard_map/ppermute | solution.py:16
  200.5 18.0 %all-to-all-start.5 = ((f32[4,264,256]{2,1,0:T(8,128)}), f32[4,264,256]{2,1,0:T(8,128)S(1)}, u32[]{:S(2)}, u32[]{:S(2)}) async-start(f32[4,264,256]{2,1,0:T(8,128)} %broadcast_in_dim.88), calls=%async_computation.5 | async-start | bytes 2162688 | tf_op jit(solution)/shard_map/all_to_all | solution.py:20
  205.9 15.3 %copy-start.4 = (f32[256,256]{1,0:T(8,128)}, f32[256,256]{1,0:T(8,128)S(1)}, u32[]{:S(2)}) copy-start(f32[256,256]{1,0:T(8,128)S(1)} %get-tuple-element.10) | copy-start | bytes 786436
  221.1 1.0 copy-start.6
  224.6 24.0 %all-to-all-start.6 = ((f32[4,64,1536]{2,1,0:T(8,128)}), f32[4,64,1536]{2,1,0:T(8,128)S(1)}, u32[]{:S(2)}, u32[]{:S(2)}) async-start(f32[4,64,1536]{2,1,0:T(8,128)} %pad_maximum_fusion.1), calls=%async_computation.6 | async-start | bytes 3145728 | tf_op jit(solution)/shard_map/all_to_all | solution.py:20
Sparse Core Ops, SparseCore 0:
  62.8 34.1 all-gather.6
  116.3 35.0 all-gather.4
  167.2 40.4 all-gather.8

commit v2 on v1

v2 whole, which is shorter than its diff:
```python
import jax
import jax.numpy as jnp
from jax import lax
from jax.experimental import pallas as pl
from jax.experimental.pallas import tpu as pltpu
from jax.sharding import Mesh, PartitionSpec as P

NBAND = 5
SIDE = 4

HIGHEST = lax.Precision.HIGHEST
F32 = jnp.float32


def dot(left, right):
    return jnp.dot(left, right, precision=HIGHEST, preferred_element_type=F32)


def dot_t(left, right):
    return lax.dot_general(
        left, right, (((1,), (1,)), ((), ())), precision=HIGHEST, preferred_element_type=F32
    )


def vector_times(row, matrix):
    return dot_t(jnp.broadcast_to(row, (8, row.shape[1])), matrix)[0:1]


def swap_lanes(array):
    width = array.shape[1] // (SIDE * SIDE)
    low = lax.broadcasted_iota(jnp.int32, (array.shape[0], 2 * width), 1) < width
    blocks = []
    for b in range(SIDE):
        for half in range(SIDE // 2):
            ends = []
            for side in range(2):
                at = (2 * half + side) * SIDE + b
                block = array[:, (at // 2) * 2 * width : (at // 2 + 1) * 2 * width]
                if at % 2 != side:
                    block = pltpu.roll(block, width, 1)
                ends.append(block)
            blocks.append(jnp.where(low, ends[0], ends[1]))
    return jnp.concatenate(blocks, axis=1)


def bands(array, weights, offset_at):
    columns = array.shape[1]
    lane = lax.broadcasted_iota(jnp.int32, (1, columns), 1)
    total = jnp.zeros(array.shape, F32)
    for b in range(NBAND):
        offset = offset_at(b)
        source = lane + offset
        weight = jnp.where((source >= 0) & (source < columns), weights[b : b + 1], 0.0)
        total = total + weight * pltpu.roll(array, lax.rem(columns - offset, columns), 1)
    return total


def bands_row(row, weights, offset_at):
    return bands(jnp.broadcast_to(row, (8, row.shape[1])), weights, offset_at)[0:1]


def wide(ref, rows):
    return jnp.concatenate([ref[i, 0:rows, :] for i in range(SIDE)], axis=1)


def place_tall(pieces, firsts, at_y, out_ref, row0=0):
    chunk = 64
    for piece, step in zip(pieces, firsts):
        source = lax.rem(at_y + SIDE - step, SIDE)
        for b in range(SIDE):
            out_ref[pl.ds(pl.multiple_of(b * SIDE * chunk + source * chunk, chunk), chunk), :] = piece[
                row0 + b * chunk : row0 + (b + 1) * chunk, :
            ]


STEPS = (0, 1, 3, 2)


def prepare(offsets, own, inverse, weights, prior, innovation, sites, x_out, y_out):
    rows, columns = own.shape
    panel = SIDE * rows
    matrix = own[...]
    crossed = bands(matrix, weights[...], lambda b: offsets[0, b])
    state = lax.broadcasted_iota(jnp.int32, (columns, sites.shape[1]), 0)
    matches = (state == sites[...]).astype(F32)
    pulled = vector_times(innovation[...], matches)
    filtered = prior[...] + vector_times(pulled, matrix)
    own_swapped = swap_lanes(matrix)
    crossed_swapped = swap_lanes(crossed)
    for i in range(SIDE):
        x_out[i, :, 0:columns] = crossed
        x_out[i, :, columns : columns + panel] = own_swapped[:, i * panel : (i + 1) * panel]
        x_out[i, :, columns + panel :] = crossed_swapped[:, i * panel : (i + 1) * panel]
    y_out[0:rows, :] = inverse[...]
    y_out[rows:, :] = jnp.zeros((8, columns), F32)
    y_out[rows : rows + 1, 0:rows] = filtered


def first_gain(where, x_in, p0, p1, p2, p3, gain_out, x_out, inverse):
    rows = x_in.shape[1]
    columns = p0.shape[1]
    at_y = where[0]
    filtered = [None] * SIDE
    for piece, step in zip((p0, p1, p2, p3), STEPS):
        source = lax.rem(at_y + SIDE - step, SIDE)
        inverse[pl.ds(pl.multiple_of(source * rows, rows), rows), :] = piece[0:rows, :]
        inverse[pl.ds(pl.multiple_of(SIDE * rows + 8 * source, 8), 8), :] = piece[rows:, :]
    crossed = jnp.concatenate([x_in[i, :, 0:columns] for i in range(SIDE)], axis=0)
    gain = dot_t(crossed, inverse[0 : SIDE * rows, :])
    gain_out[...] = gain
    tail = jnp.concatenate(
        [inverse[SIDE * rows + 8 * i : SIDE * rows + 8 * i + 1, 0:rows] for i in range(SIDE)], axis=1
    )
    tail = jnp.broadcast_to(tail, (8, SIDE * rows))
    for i in range(SIDE):
        x_out[i, 0 : SIDE * rows, :] = gain
        x_out[i, SIDE * rows :, :] = tail


def second_gain(
    where, offsets, weights, gain, x_in, e0, e1, e2, e3, c0, c1, c2, c3,
    gain_out, x_out, shift_out, c_out, tall,
):
    panel = gain.shape[0]
    rows = panel // SIDE
    at_y = where[0]
    gain_wide = wide(x_in, panel)
    filtered = jnp.concatenate([x_in[i, panel : panel + 1, :] for i in range(SIDE)], axis=1)
    natural = swap_lanes(jnp.broadcast_to(filtered, (8, filtered.shape[1])))
    forward = swap_lanes(bands(natural, weights[...], lambda b: offsets[0, b]))
    mine = jnp.zeros((1, panel), F32)
    for i in range(SIDE):
        mine = mine + jnp.where(at_y == i, natural[0:1, i * panel : (i + 1) * panel], 0.0)
    shift_out[...] = jnp.broadcast_to(mine - vector_times(forward[0:1], gain_wide), (8, panel))
    place_tall((e0, e1, e2, e3), STEPS, at_y, tall)
    gain_2 = jnp.where(where[2] == 1, dot(gain_wide, tall[...]), gain[...])
    gain_out[...] = gain_2
    for i in range(SIDE):
        x_out[i] = gain_2
    for piece, step in zip((c0, c1, c2, c3), STEPS):
        source = lax.rem(at_y + SIDE - step, SIDE)
        c_out[pl.ds(pl.multiple_of(source * rows, rows), rows), :] = piece[...]
    c_out[panel : panel + NBAND, :] = weights[...]
    c_out[panel + NBAND : panel + NBAND + 1, :] = filtered
    c_out[panel + NBAND + 1 : panel + NBAND + 2, :] = forward[0:1]
    lane = lax.broadcasted_iota(jnp.int32, (1, c_out.shape[1]), 1)
    held = jnp.zeros((1, c_out.shape[1]), jnp.int32)
    for b in range(NBAND):
        held = jnp.where(lane == b, offsets[0, b], held)
    c_out[panel + NBAND + 2 : panel + NBAND + 3, :] = held.astype(F32)


def first_spread(
    where, offsets, c_in, gain_in, gain_2_in, first_in, e0, e1, e2, e3, shift,
    part_out, shift_out, tall,
):
    panel = e0.shape[0]
    columns = c_in.shape[1]
    rows = panel // SIDE
    at_y = where[0]
    later = c_in[0:panel, :]
    crossed = bands(later, c_in[panel : panel + NBAND, :], lambda b: offsets[b])
    gain_wide = wide(gain_in, panel)
    gain_2_wide = wide(gain_2_in, panel)
    turned = dot_t(gain_wide, swap_lanes(later)) - dot_t(gain_2_wide, swap_lanes(crossed))
    filtered = c_in[panel + NBAND : panel + NBAND + 1, :]
    forward = c_in[panel + NBAND + 1 : panel + NBAND + 2, :]
    moved = vector_times(filtered, gain_wide) - vector_times(forward, gain_2_wide)
    inside = where[2] == 1
    shift_out[...] = shift[...] + jnp.where(inside, moved, 0.0)
    mine = jnp.concatenate([first_in[i, :, columns + panel :] for i in range(SIDE)], axis=0)
    turned = jnp.where(inside, turned, 0.0) - mine
    place_tall((e0, e1, e2, e3), STEPS, at_y, tall)
    for i in range(SIDE):
        part_out[i] = dot_t(tall[i * panel : (i + 1) * panel, :], turned)


def join_spread(parts, first_in, shift, out):
    panel = parts.shape[1]
    columns = first_in.shape[2] - 2 * panel
    total = (parts[0] + parts[1]) + (parts[2] + parts[3])
    mine = jnp.concatenate(
        [first_in[i, :, columns : columns + panel] for i in range(SIDE)], axis=0
    )
    out[0:panel, :] = mine + total.T
    out[panel:, :] = shift[...]


def second_spread(
    where, gain_2, gain_2_in, spread, y_in, a0, a1, a2, a3, x_out, shift_out, tall, later_tall,
):
    panel = gain_2.shape[0]
    rows = panel // SIDE
    columns = SIDE * panel
    at_y = where[0]
    inside = where[3] == 1
    gain_2_wide = wide(gain_2_in, panel)
    for i in range(SIDE):
        for b in range(SIDE):
            tall[b * panel + i * rows : b * panel + (i + 1) * rows, :] = y_in[
                i, b * rows : (b + 1) * rows, :
            ]
    turned = jnp.where(inside, dot(gain_2_wide, tall[...]), 0.0)
    shifts = jnp.concatenate([y_in[i, panel : panel + 8, :] for i in range(SIDE)], axis=1)
    moved = vector_times(swap_lanes(shifts)[0:1], gain_2_wide)
    shift_out[...] = spread[panel:, :] + jnp.where(inside, moved, 0.0)
    place_tall((a0, a1, a2, a3), STEPS, at_y, later_tall, panel)
    gain_4 = jnp.where(inside, dot(gain_2_wide, later_tall[...]), gain_2[...])
    for i in range(SIDE):
        x_out[i, :, columns : columns + panel] = gain_4[i * rows : (i + 1) * rows]
        x_out[i, :, columns + panel :] = spread[i * rows : (i + 1) * rows, :]
    for piece, step in zip((a0, a1, a2, a3), STEPS):
        source = lax.rem(at_y + SIDE - step, SIDE)
        tall[pl.ds(pl.multiple_of(source * panel, panel), panel), :] = piece[0:panel, :]
    part = dot_t(turned, tall[...])
    for i in range(SIDE):
        x_out[i, :, 0:columns] = part[i * rows : (i + 1) * rows]


def finish(x_in, gain_out, spread_out):
    rows, columns = gain_out.shape
    panel = SIDE * rows
    gain_out[...] = swap_lanes(
        jnp.concatenate([x_in[i, :, columns : columns + panel] for i in range(SIDE)], axis=1)
    )
    kept = swap_lanes(jnp.concatenate([x_in[i, :, columns + panel :] for i in range(SIDE)], axis=1))
    total = (x_in[0, :, 0:columns] + x_in[1, :, 0:columns]) + (
        x_in[2, :, 0:columns] + x_in[3, :, 0:columns]
    )
    spread_out[...] = total + kept


VMEM = pl.BlockSpec(memory_space=pltpu.VMEM)
SMEM = pl.BlockSpec(memory_space=pltpu.SMEM)


def call(kernel, scalars, arrays, outs, scratch=(), flops=0):
    shapes = [jax.ShapeDtypeStruct(s, F32) for s in outs]
    size = sum(a.size for a in arrays) + sum(s.size for s in shapes)
    return pl.pallas_call(
        kernel,
        out_shape=shapes,
        in_specs=[SMEM] * len(scalars) + [VMEM] * len(arrays),
        out_specs=[VMEM] * len(outs),
        scratch_shapes=[pltpu.VMEM(s, F32) for s in scratch],
        compiler_params=pltpu.CompilerParams(vmem_limit_bytes=40 * 2**20),
        cost_estimate=pl.CostEstimate(flops=flops, bytes_accessed=4 * size, transcendentals=0),
    )(*scalars, *arrays)


def shifted(block, distance):
    count = lax.axis_size("tm")
    return lax.ppermute(block, "tm", [(i + distance, i) for i in range(count - distance)])


def swap(message, axis):
    return lax.all_to_all(message, axis, 0, 0)


def ring(block, axis):
    pieces = [block]
    for step in STEPS[1:]:
        pieces.append(lax.ppermute(block, axis, [(i, (i + step) % SIDE) for i in range(SIDE)]))
    return pieces


def ring_shifted(block, distance):
    count = lax.axis_size("tm")
    pieces = []
    for step in STEPS:
        route = [
            ((i + distance) * SIDE + j, i * SIDE + (j + step) % SIDE)
            for i in range(count - distance)
            for j in range(SIDE)
        ]
        pieces.append(lax.ppermute(block, ("tm", "y"), route))
    return pieces


def body(covariance, precision, band_weight, band_offset, prior_mean, innovation, seen_sites):
    own = covariance[0]
    inverse = precision[0]
    weights = band_weight[0]
    rows, columns = own.shape
    panel = SIDE * rows
    at_t = lax.axis_index("tm")
    count_t = lax.axis_size("tm")
    at_x = lax.axis_index("x")
    where = jnp.stack(
        [
            lax.axis_index("y").astype(jnp.int32),
            at_x.astype(jnp.int32),
            (at_t + 1 < count_t).astype(jnp.int32),
            (at_t + 2 < count_t).astype(jnp.int32),
        ]
    )
    unit = 2 * panel * panel * columns

    x_message, y_message = call(
        prepare,
        (band_offset,),
        (own, inverse, weights, prior_mean, innovation, seen_sites),
        ((SIDE, rows, columns + 2 * panel), (rows + 8, columns)),
    )
    first_in = swap(x_message, "x")
    inverse_pieces = ring(y_message, "y")
    own_pieces = ring(own, "y")
    gain, x_message = call(
        first_gain,
        (where,),
        (first_in, *inverse_pieces),
        ((panel, panel), (SIDE, panel + 8, panel)),
        ((panel + 32, columns),),
        unit,
    )
    gain_in = swap(x_message, "x")
    later_pieces = ring_shifted(gain, 1)
    gain_2, x_message, shift, c_message = call(
        second_gain,
        (where, band_offset),
        (weights, gain, gain_in, *later_pieces, *own_pieces),
        ((panel, panel), (SIDE, panel, panel), (8, panel), (panel + 8, columns)),
        ((columns, panel),),
        unit,
    )
    gain_2_in = swap(x_message, "x")
    gain_pieces = ring(gain, "y")
    gain_2_later = shifted(gain_2, 2)
    c_in = shifted(c_message, 1)
    next_offsets = c_in[panel + NBAND + 2, 0:8].astype(jnp.int32)
    part, shift_2 = call(
        first_spread,
        (where, next_offsets),
        (c_in, gain_in, gain_2_in, first_in, *gain_pieces, shift),
        ((SIDE, panel, panel), (8, panel)),
        ((columns, panel),),
        3 * unit,
    )
    parts = swap(part, "x")
    gain_2_pieces = ring(jnp.concatenate([gain_2, gain_2_later], axis=0), "y")
    (spread_2,) = call(join_spread, (), (parts, first_in, shift_2), ((panel + 8, panel),))
    later = shifted(spread_2, 2)
    y_in = swap(jnp.broadcast_to(later[None], (SIDE, panel + 8, panel)), "y")
    x_message, shift_4 = call(
        second_spread,
        (where,),
        (gain_2, gain_2_in, spread_2, y_in, *gain_2_pieces),
        ((SIDE, rows, columns + 2 * panel), (8, panel)),
        ((columns, panel), (columns, panel)),
        3 * unit,
    )
    last_in = swap(x_message, "x")
    final_gain, final_spread = call(finish, (), (last_in,), ((rows, columns), (rows, columns)))
    final_shift = lax.dynamic_slice_in_dim(shift_4[0], at_x * rows, rows, 0)
    return final_gain[None], final_shift[None], final_spread[None]


def solution(mesh):
    count = mesh.devices.shape[0]
    grid = Mesh(mesh.devices.reshape(count, SIDE, SIDE), ("tm", "y", "x"))
    row = ("y", "x")
    in_specs = (
        P("tm", row, None),
        P("tm", row, None),
        P("tm", None, None),
        P("tm", None),
        P("tm", row),
        P("tm", None),
        P("tm", None),
    )
    out_specs = (P("tm", row, None), P("tm", row), P("tm", row, None))
    return jax.shard_map(body, mesh=grid, in_specs=in_specs, out_specs=out_specs, check_vma=False)
```

time: 261 us -> 221 us (0.85)
  the two profiles are of different devices: /device:TPU:32 before, /device:TPU:224 now
where the time goes in v2:
time: 221 us; the launch traced here: 219 us
  starting transfers between devices  87 us (39%)
  waiting for transfers between devices  62.3 us (28%)
  local copies, waits for them, and re-layouts  27.5 us (12%)
  Pallas kernels  23.3 us (11%)
  blocking collectives  17.6 us (8%)
    ppermute x12, starting transfers between devices, ring(): lax.ppermute(block, axis, [(i, (i + step) % SIDE) for i in range(SIDE)])  43.7 us
    ppermute x12, waiting for transfers between devices, ring(): lax.ppermute(block, axis, [(i, (i + step) % SIDE) for i in range(SIDE)])  35.9 us
    unnamed x66, local copies, waits for them, and re-layouts  25.8 us
    all_to_all x5, starting transfers between devices, swap(): return lax.all_to_all(message, axis, 0, 0)  23.6 us
    pallas_call x7, Pallas kernels, call(): pl.pallas_call(kernel, out_shape=shapes, in_specs=[SMEM] * len(scalars) +...  23.3 us
    all_to_all x1, blocking collectives, swap(): return lax.all_to_all(message, axis, 0, 0)  17.6 us
    all_to_all x5, waiting for transfers between devices, swap(): return lax.all_to_all(message, axis, 0, 0)  15.1 us
    ppermute x4, starting transfers between devices, ring_shifted(): pieces.append(lax.ppermute(block, ('tm', 'y'), route))  10.3 us
  transfers between devices with their start and end apart: 24, of which 11 were waited for; matrix products, arithmetic and copies ran while one was open for 1% of the time, Pallas kernels for 0%

profile of v2, /device:TPU:224, one launch (start us, length us, event | category | flops | bytes accessed | tf_op | source)
XLA Modules:
  0.0 219.4 jit_solution(14080124707204994187)
XLA Ops:
  5.9 2.7 %shard_map.94 = (f32[4,64,1536]{2,1,0:T(8,128)}, f32[72,1024]{1,0:T(8,128)S(1)}) custom-call(s32[1,5]{1,0:T(1,128)S(1)} %copy-done.27, f32[64,1024]{1,0:T(8,128)S(1)} %bitcast.13, f32[64,1024]{1,0:T(8,128)S(1)} %bitcast.20, f32[5,1024]{1,0:T(8,128)S(1)} %bitcast.18, f32[1,64]{1,0:T(1,128)S(1)} %copy-done.29, f32[1,128]{1,0:T(1,128)S(1)} %copy-done.30, ...), custom_call_target="tpu_custom_call" | custom-call | bytes 2413824 | tf_op jit(solution)/shard_map/pallas_call | solution.py:240
  8.6 4.3 %all-to-all-start = ((f32[4,64,1536]{2,1,0:T(8,128)}), f32[4,64,1536]{2,1,0:T(8,128)S(1)}, u32[]{:S(2)}, u32[]{:S(2)}) async-start(f32[4,64,1536]{2,1,0:T(8,128)} %get-tuple-element.17), calls=%async_computation | async-start | bytes 3145728 | tf_op jit(solution)/shard_map/all_to_all | solution.py:257
  12.9 3.5 %collective-permute-start = (f32[72,1024]{1,0:T(8,128)S(1)}, f32[72,1024]{1,0:T(8,128)S(1)}, u32[]{:S(2)}, u32[]{:S(2)}) collective-permute-start(f32[72,1024]{1,0:T(8,128)S(1)} %get-tuple-element.18.p0), channel_id=1, source_target_pairs={{0,4},{4,8},{8,12},{12,0},{1,5},{5,9},{9,13},{13,1},{2,6},{6,10},{... | collective-permute-start | bytes 884744 | tf_op jit(solution)/shard_map/ppermute | solution.py:263
  16.4 3.6 %collective-permute-start.1 = (f32[72,1024]{1,0:T(8,128)S(1)}, f32[72,1024]{1,0:T(8,128)S(1)}, u32[]{:S(2)}, u32[]{:S(2)}) collective-permute-start(f32[72,1024]{1,0:T(8,128)S(1)} %get-tuple-element.18.p0), channel_id=1, source_target_pairs={{0,12},{4,0},{8,4},{12,8},{1,13},{5,1},{9,5},{13,9},{2,14},{6,2},{... | collective-permute-start | bytes 884744 | tf_op jit(solution)/shard_map/ppermute | solution.py:263
  20.0 3.9 %collective-permute-start.2 = (f32[72,1024]{1,0:T(8,128)S(1)}, f32[72,1024]{1,0:T(8,128)S(1)}, u32[]{:S(2)}, u32[]{:S(2)}) collective-permute-start(f32[72,1024]{1,0:T(8,128)S(1)} %get-tuple-element.18.p0), channel_id=1, source_target_pairs={{0,8},{4,12},{8,0},{12,4},{1,9},{5,13},{9,1},{13,5},{2,10},{6,14},... | collective-permute-start | bytes 884744 | tf_op jit(solution)/shard_map/ppermute | solution.py:263
  24.5 3.7 %collective-permute-done.1.p2 = f32[72,1024]{1,0:T(8,128)S(1)} collective-permute-done((f32[72,1024]{1,0:T(8,128)S(1)}, f32[72,1024]{1,0:T(8,128)S(1)}, u32[]{:S(2)}, u32[]{:S(2)}) %collective-permute-start.1) | collective-permute-done | bytes 294944 | tf_op jit(solution)/shard_map/ppermute | solution.py:263
  28.2 3.8 %collective-permute-done.2.p3 = f32[72,1024]{1,0:T(8,128)S(1)} collective-permute-done((f32[72,1024]{1,0:T(8,128)S(1)}, f32[72,1024]{1,0:T(8,128)S(1)}, u32[]{:S(2)}, u32[]{:S(2)}) %collective-permute-start.2) | collective-permute-done | bytes 294944 | tf_op jit(solution)/shard_map/ppermute | solution.py:263
  36.5 3.6 %all-to-all-start.1 = ((f32[4,264,256]{2,1,0:T(8,128)}), f32[4,264,256]{2,1,0:T(8,128)S(1)}, u32[]{:S(2)}, u32[]{:S(2)}) async-start(f32[4,264,256]{2,1,0:T(8,128)} %copy-done), calls=%async_computation.1 | async-start | bytes 2162688 | tf_op jit(solution)/shard_map/all_to_all | solution.py:257
  40.2 4.3 %collective-permute-start.7 = (f32[64,1024]{1,0:T(8,128)S(1)}, f32[64,1024]{1,0:T(8,128)S(1)}, u32[]{:S(2)}, u32[]{:S(2)}) collective-permute-start(f32[64,1024]{1,0:T(8,128)S(1)} %bitcast.14), channel_id=1, source_target_pairs={{0,4},{4,8},{8,12},{12,0},{1,5},{5,9},{9,13},{13,1},{2,6},{6,10},{... | collective-permute-start | bytes 786440 | tf_op jit(solution)/shard_map/ppermute | solution.py:263
  47.2 3.9 %collective-permute-start.9 = (f32[64,1024]{1,0:T(8,128)S(1)}, f32[64,1024]{1,0:T(8,128)S(1)}, u32[]{:S(2)}, u32[]{:S(2)}) collective-permute-start(f32[64,1024]{1,0:T(8,128)S(1)} %bitcast.16), channel_id=1, source_target_pairs={{0,8},{4,12},{8,0},{12,4},{1,9},{5,13},{9,1},{13,5},{2,10},{6,14},... | collective-permute-start | bytes 786440 | tf_op jit(solution)/shard_map/ppermute | solution.py:263
  56.1 4.0 %collective-permute-start.5 = (f32[256,256]{1,0:T(8,128)S(1)}, f32[256,256]{1,0:T(8,128)S(1)}, u32[]{:S(2)}, u32[]{:S(2)}) collective-permute-start(f32[256,256]{1,0:T(8,128)S(1)} %get-tuple-element.19.gain.e0), channel_id=1, source_target_pairs={{16,12},{20,0},{24,4},{28,8},{32,28},{36,16},{40,20},{44,24},{48,4... | collective-permute-start | bytes 786440 | tf_op jit(solution)/shard_map/ppermute | solution.py:276
  65.7 4.3 %collective-permute-done.6.e3 = f32[256,256]{1,0:T(8,128)S(1)} collective-permute-done((f32[256,256]{1,0:T(8,128)S(1)}, f32[256,256]{1,0:T(8,128)S(1)}, u32[]{:S(2)}, u32[]{:S(2)}) %collective-permute-start.6) | collective-permute-done | bytes 262176 | tf_op jit(solution)/shard_map/ppermute | solution.py:276
  77.4 3.6 %shard_map.96 = (f32[256,256]{1,0:T(8,128)S(1)}, f32[4,256,256]{2,1,0:T(8,128)S(1)}, f32[8,256]{1,0:T(8,128)S(1)}, f32[264,1024]{1,0:T(8,128)}) custom-call(s32[4]{0:T(128)S(1)} %pad_add_fusion.where, s32[1,5]{1,0:T(1,128)S(1)} %copy-done.28, f32[5,1024]{1,0:T(8,128)S(1)} %bitcast.19, f32[256,256]{1,0:T(8,128)S(1)} %get-tuple-element.19.gain.e0, ...), custom_call_target="tpu_custom_call" | custom-call | flops 134217728 | bytes 5861376 | tf_op jit(solution)/shard_map/pallas_call | solution.py:240
  81.9 4.6 %collective-permute-start.10 = (f32[264,1024]{1,0:T(8,128)}, f32[264,1024]{1,0:T(8,128)}, u32[]{:S(2)}, u32[]{:S(2)}) collective-permute-start(f32[264,1024]{1,0:T(8,128)} %get-tuple-element.23), channel_id=1, source_target_pairs={{16,0},{32,16},{48,32},{64,48},{80,64},{96,80},{112,96},{128,112},... | collective-permute-start | bytes 3244040 | tf_op jit(solution)/shard_map/ppermute | solution.py:253
  86.5 4.8 %all-to-all-start.2 = ((f32[4,256,256]{2,1,0:T(8,128)}), f32[4,256,256]{2,1,0:T(8,128)}, u32[]{:S(2)}, u32[]{:S(2)}) async-start(f32[4,256,256]{2,1,0:T(8,128)} %copy-done.3), calls=%async_computation.2 | async-start | bytes 2097152 | tf_op jit(solution)/shard_map/all_to_all | solution.py:257
  91.3 3.4 %collective-permute-start.11 = (f32[256,256]{1,0:T(8,128)S(1)}, f32[256,256]{1,0:T(8,128)S(1)}, u32[]{:S(2)}, u32[]{:S(2)}) collective-permute-start(f32[256,256]{1,0:T(8,128)S(1)} %get-tuple-element.19.gain.e0), channel_id=1, source_target_pairs={{0,4},{4,8},{8,12},{12,0},{1,5},{5,9},{9,13},{13,1},{2,6},{6,10},{... | collective-permute-start | bytes 786440 | tf_op jit(solution)/shard_map/ppermute | solution.py:263
  94.7 3.6 %collective-permute-start.12 = (f32[256,256]{1,0:T(8,128)S(1)}, f32[256,256]{1,0:T(8,128)S(1)}, u32[]{:S(2)}, u32[]{:S(2)}) collective-permute-start(f32[256,256]{1,0:T(8,128)S(1)} %get-tuple-element.19.gain.e0), channel_id=1, source_target_pairs={{0,12},{4,0},{8,4},{12,8},{1,13},{5,1},{9,5},{13,9},{2,14},{6,2},{... | collective-permute-start | bytes 786440 | tf_op jit(solution)/shard_map/ppermute | solution.py:263
  98.3 3.5 %collective-permute-start.13 = (f32[256,256]{1,0:T(8,128)S(1)}, f32[256,256]{1,0:T(8,128)S(1)}, u32[]{:S(2)}, u32[]{:S(2)}) collective-permute-start(f32[256,256]{1,0:T(8,128)S(1)} %get-tuple-element.19.gain.e0), channel_id=1, source_target_pairs={{0,8},{4,12},{8,0},{12,4},{1,9},{5,13},{9,1},{13,5},{2,10},{6,14},... | collective-permute-start | bytes 786440 | tf_op jit(solution)/shard_map/ppermute | solution.py:263
  103.0 6.8 %collective-permute-done.12.e2 = f32[256,256]{1,0:T(8,128)S(1)} collective-permute-done((f32[256,256]{1,0:T(8,128)S(1)}, f32[256,256]{1,0:T(8,128)S(1)}, u32[]{:S(2)}, u32[]{:S(2)}) %collective-permute-start.12) | collective-permute-done | bytes 262176 | tf_op jit(solution)/shard_map/ppermute | solution.py:263
  113.2 8.1 %shard_map.97 = (f32[4,256,256]{2,1,0:T(8,128)S(1)}, f32[8,256]{1,0:T(8,128)S(1)}) custom-call(s32[4]{0:T(128)S(1)} %pad_add_fusion.where, s32[8]{0:T(128)S(1)} %fusion.offsets, f32[264,1024]{1,0:T(8,128)} %collective-permute-done.10.c_in, f32[4,264,256]{2,1,0:T(8,128)S(1)} %all-to-all-done.1.x_in.gain_in, f32[4,256,256]{2,1,0:T(8,128)} %all-to-all-done.2.gain_2_in, ...), custom_call_target="tpu_custom_call" | custom-call | flops 402653184 | bytes 6897664 | tf_op jit(solution)/shard_map/pallas_call | solution.py:240
  121.2 17.6 %all_to_all.30.parts = f32[4,256,256]{2,1,0:T(8,128)S(1)} all-to-all(f32[4,256,256]{2,1,0:T(8,128)S(1)} %get-tuple-element.25), channel_id=1, replica_groups=mesh['tm'=32,'y'=4,'x'=4] {'x'}, dimensions={0} | all-to-all | bytes 2097152 | tf_op jit(solution)/shard_map/all_to_all | solution.py:257
  138.9 2.8 %collective-permute-start.14 = (f32[264,256]{1,0:T(8,128)S(1)}, f32[264,256]{1,0:T(8,128)S(1)}, u32[]{:S(2)}, u32[]{:S(2)}) collective-permute-start(f32[264,256]{1,0:T(8,128)S(1)} %shard_map.98.spread), channel_id=1, source_target_pairs={{32,0},{48,16},{64,32},{80,48},{96,64},{112,80},{128,96},{144,112}... | collective-permute-start | bytes 811016 | tf_op jit(solution)/shard_map/ppermute | solution.py:253
  143.8 7.0 %collective-permute-done.14 = f32[264,256]{1,0:T(8,128)S(1)} collective-permute-done((f32[264,256]{1,0:T(8,128)S(1)}, f32[264,256]{1,0:T(8,128)S(1)}, u32[]{:S(2)}, u32[]{:S(2)}) %collective-permute-start.14) | collective-permute-done | bytes 270368 | tf_op jit(solution)/shard_map/ppermute | solution.py:253
  151.8 7.3 %all-to-all-start.4 = ((f32[4,264,256]{2,1,0:T(8,128)}), f32[4,264,256]{2,1,0:T(8,128)S(1)}, u32[]{:S(2)}, u32[]{:S(2)}) async-start(f32[4,264,256]{2,1,0:T(8,128)} %broadcast_in_dim.6), calls=%async_computation.4 | async-start | bytes 2162688 | tf_op jit(solution)/shard_map/all_to_all | solution.py:257
  159.2 3.9 %collective-permute-start.16 = (f32[512,256]{1,0:T(8,128)S(1)}, f32[512,256]{1,0:T(8,128)S(1)}, u32[]{:S(2)}, u32[]{:S(2)}) collective-permute-start(f32[512,256]{1,0:T(8,128)S(1)} %constant_dynamic-update-slice_fusion.a0), channel_id=1, source_target_pairs={{0,4},{4,8},{8,12},{12,0},{1,5},{5,9},{9,13},{13,1},{2,6},{6,10},{... | collective-permute-start | bytes 1572872 | tf_op jit(solution)/shard_map/ppermute | solution.py:263
  163.2 3.1 %collective-permute-start.17 = (f32[512,256]{1,0:T(8,128)S(1)}, f32[512,256]{1,0:T(8,128)S(1)}, u32[]{:S(2)}, u32[]{:S(2)}) collective-permute-start(f32[512,256]{1,0:T(8,128)S(1)} %constant_dynamic-update-slice_fusion.a0), channel_id=1, source_target_pairs={{0,12},{4,0},{8,4},{12,8},{1,13},{5,1},{9,5},{13,9},{2,14},{6,2},{... | collective-permute-start | bytes 1572872 | tf_op jit(solution)/shard_map/ppermute | solution.py:263
  166.3 4.2 %collective-permute-start.18 = (f32[512,256]{1,0:T(8,128)S(1)}, f32[512,256]{1,0:T(8,128)S(1)}, u32[]{:S(2)}, u32[]{:S(2)}) collective-permute-start(f32[512,256]{1,0:T(8,128)S(1)} %constant_dynamic-update-slice_fusion.a0), channel_id=1, source_target_pairs={{0,8},{4,12},{8,0},{12,4},{1,9},{5,13},{9,1},{13,5},{2,10},{6,14},... | collective-permute-start | bytes 1572872 | tf_op jit(solution)/shard_map/ppermute | solution.py:263
  170.5 15.3 %collective-permute-done.16.a1 = f32[512,256]{1,0:T(8,128)S(1)} collective-permute-done((f32[512,256]{1,0:T(8,128)S(1)}, f32[512,256]{1,0:T(8,128)S(1)}, u32[]{:S(2)}, u32[]{:S(2)}) %collective-permute-start.16) | collective-permute-done | bytes 524320 | tf_op jit(solution)/shard_map/ppermute | solution.py:263
  186.6 5.2 %collective-permute-done.18.a3 = f32[512,256]{1,0:T(8,128)S(1)} collective-permute-done((f32[512,256]{1,0:T(8,128)S(1)}, f32[512,256]{1,0:T(8,128)S(1)}, u32[]{:S(2)}, u32[]{:S(2)}) %collective-permute-start.18) | collective-permute-done | bytes 524320 | tf_op jit(solution)/shard_map/ppermute | solution.py:263
  194.7 6.1 %shard_map.99 = (f32[4,64,1536]{2,1,0:T(8,128)}, f32[8,256]{1,0:T(8,128)S(1)}) custom-call(s32[4]{0:T(128)S(1)} %pad_add_fusion.where, f32[256,256]{1,0:T(8,128)S(1)} %get-tuple-element.21.gain_2, f32[4,256,256]{2,1,0:T(8,128)} %all-to-all-done.2.gain_2_in, f32[264,256]{1,0:T(8,128)S(1)} %shard_map.98.spread, f32[4,264,256]{2,1,0:T(8,128)S(1)} %all-to-all-done.4.y_in, ...), custom_call_target="tpu_custom_call" | custom-call | flops 402653184 | bytes 6340608 | tf_op jit(solution)/shard_map/pallas_call | solution.py:240
  200.8 3.6 %all-to-all-start.5 = ((f32[4,64,1536]{2,1,0:T(8,128)}), f32[4,64,1536]{2,1,0:T(8,128)S(1)}, u32[]{:S(2)}, u32[]{:S(2)}) async-start(f32[4,64,1536]{2,1,0:T(8,128)} %get-tuple-element.27), calls=%async_computation.5 | async-start | bytes 3145728 | tf_op jit(solution)/shard_map/all_to_all | solution.py:257
  205.0 13.5 %all-to-all-done.5.x_in = f32[4,64,1536]{2,1,0:T(8,128)S(1)} async-done(((f32[4,64,1536]{2,1,0:T(8,128)}), f32[4,64,1536]{2,1,0:T(8,128)S(1)}, u32[]{:S(2)}, u32[]{:S(2)}) %all-to-all-start.5) | async-done | bytes 1572896 | tf_op jit(solution)/shard_map/all_to_all | solution.py:257
  (96 shorter events, 44.9 us)
Async XLA Ops:
  8.6 25.0 %all-to-all-start = ((f32[4,64,1536]{2,1,0:T(8,128)}), f32[4,64,1536]{2,1,0:T(8,128)S(1)}, u32[]{:S(2)}, u32[]{:S(2)}) async-start(f32[4,64,1536]{2,1,0:T(8,128)} %get-tuple-element.17), calls=%async_computation | async-start | bytes 3145728 | tf_op jit(solution)/shard_map/all_to_all | solution.py:257
  12.9 11.6 %collective-permute-start = (f32[72,1024]{1,0:T(8,128)S(1)}, f32[72,1024]{1,0:T(8,128)S(1)}, u32[]{:S(2)}, u32[]{:S(2)}) collective-permute-start(f32[72,1024]{1,0:T(8,128)S(1)} %get-tuple-element.18.p0), channel_id=1, source_target_pairs={{0,4},{4,8},{8,12},{12,0},{1,5},{5,9},{9,13},{13,1},{2,6},{6,10},{... | collective-permute-start | bytes 884744 | tf_op jit(solution)/shard_map/ppermute | solution.py:263
  16.4 11.8 %collective-permute-start.1 = (f32[72,1024]{1,0:T(8,128)S(1)}, f32[72,1024]{1,0:T(8,128)S(1)}, u32[]{:S(2)}, u32[]{:S(2)}) collective-permute-start(f32[72,1024]{1,0:T(8,128)S(1)} %get-tuple-element.18.p0), channel_id=1, source_target_pairs={{0,12},{4,0},{8,4},{12,8},{1,13},{5,1},{9,5},{13,9},{2,14},{6,2},{... | collective-permute-start | bytes 884744 | tf_op jit(solution)/shard_map/ppermute | solution.py:263
  20.0 12.1 %collective-permute-start.2 = (f32[72,1024]{1,0:T(8,128)S(1)}, f32[72,1024]{1,0:T(8,128)S(1)}, u32[]{:S(2)}, u32[]{:S(2)}) collective-permute-start(f32[72,1024]{1,0:T(8,128)S(1)} %get-tuple-element.18.p0), channel_id=1, source_target_pairs={{0,8},{4,12},{8,0},{12,4},{1,9},{5,13},{9,1},{13,5},{2,10},{6,14},... | collective-permute-start | bytes 884744 | tf_op jit(solution)/shard_map/ppermute | solution.py:263
  35.5 1.0 copy-start
  36.5 3.7 %copy-start.2 = (f32[1,64,1024]{2,1,0:T(8,128)S(1)}, f32[1,64,1024]{2,1,0:T(8,128)}, u32[]{:S(2)}) copy-start(f32[1,64,1024]{2,1,0:T(8,128)} %param.7) | copy-start | bytes 786436
  36.5 34.2 %copy-start.28 = (s32[1,5]{1,0:T(1,128)S(1)}, s32[1,5]{1,0:T(1,128)}, u32[]{:S(2)}) copy-start(s32[1,5]{1,0:T(1,128)} %offsets.3) | copy-start | bytes 64
  36.5 34.2 %all-to-all-start.1 = ((f32[4,264,256]{2,1,0:T(8,128)}), f32[4,264,256]{2,1,0:T(8,128)S(1)}, u32[]{:S(2)}, u32[]{:S(2)}) async-start(f32[4,264,256]{2,1,0:T(8,128)} %copy-done), calls=%async_computation.1 | async-start | bytes 2162688 | tf_op jit(solution)/shard_map/all_to_all | solution.py:257
  40.2 15.2 %collective-permute-start.7 = (f32[64,1024]{1,0:T(8,128)S(1)}, f32[64,1024]{1,0:T(8,128)S(1)}, u32[]{:S(2)}, u32[]{:S(2)}) collective-permute-start(f32[64,1024]{1,0:T(8,128)S(1)} %bitcast.14), channel_id=1, source_target_pairs={{0,4},{4,8},{8,12},{12,0},{1,5},{5,9},{9,13},{13,1},{2,6},{6,10},{... | collective-permute-start | bytes 786440 | tf_op jit(solution)/shard_map/ppermute | solution.py:263
  44.5 15.6 %collective-permute-start.8 = (f32[64,1024]{1,0:T(8,128)S(1)}, f32[64,1024]{1,0:T(8,128)S(1)}, u32[]{:S(2)}, u32[]{:S(2)}) collective-permute-start(f32[64,1024]{1,0:T(8,128)S(1)} %bitcast.15), channel_id=1, source_target_pairs={{0,12},{4,0},{8,4},{12,8},{1,13},{5,1},{9,5},{13,9},{2,14},{6,2},{... | collective-permute-start | bytes 786440 | tf_op jit(solution)/shard_map/ppermute | solution.py:263
  47.2 15.7 %collective-permute-start.9 = (f32[64,1024]{1,0:T(8,128)S(1)}, f32[64,1024]{1,0:T(8,128)S(1)}, u32[]{:S(2)}, u32[]{:S(2)}) collective-permute-start(f32[64,1024]{1,0:T(8,128)S(1)} %bitcast.16), channel_id=1, source_target_pairs={{0,8},{4,12},{8,0},{12,4},{1,9},{5,13},{9,1},{13,5},{2,10},{6,14},... | collective-permute-start | bytes 786440 | tf_op jit(solution)/shard_map/ppermute | solution.py:263
  51.1 12.5 %collective-permute-start.3 = (f32[256,256]{1,0:T(8,128)S(1)}, f32[256,256]{1,0:T(8,128)S(1)}, u32[]{:S(2)}, u32[]{:S(2)}) collective-permute-start(f32[256,256]{1,0:T(8,128)S(1)} %get-tuple-element.19.gain.e0), channel_id=1, source_target_pairs={{16,0},{20,4},{24,8},{28,12},{32,16},{36,20},{40,24},{44,28},{48,3... | collective-permute-start | bytes 786440 | tf_op jit(solution)/shard_map/ppermute | solution.py:276
  53.1 11.2 %collective-permute-start.4 = (f32[256,256]{1,0:T(8,128)S(1)}, f32[256,256]{1,0:T(8,128)S(1)}, u32[]{:S(2)}, u32[]{:S(2)}) collective-permute-start(f32[256,256]{1,0:T(8,128)S(1)} %get-tuple-element.19.gain.e0), channel_id=1, source_target_pairs={{16,4},{20,8},{24,12},{28,0},{32,20},{36,24},{40,28},{44,16},{48,3... | collective-permute-start | bytes 786440 | tf_op jit(solution)/shard_map/ppermute | solution.py:276
  56.1 8.9 %collective-permute-start.5 = (f32[256,256]{1,0:T(8,128)S(1)}, f32[256,256]{1,0:T(8,128)S(1)}, u32[]{:S(2)}, u32[]{:S(2)}) collective-permute-start(f32[256,256]{1,0:T(8,128)S(1)} %get-tuple-element.19.gain.e0), channel_id=1, source_target_pairs={{16,12},{20,0},{24,4},{28,8},{32,28},{36,16},{40,20},{44,24},{48,4... | collective-permute-start | bytes 786440 | tf_op jit(solution)/shard_map/ppermute | solution.py:276
  60.8 9.2 %collective-permute-start.6 = (f32[256,256]{1,0:T(8,128)S(1)}, f32[256,256]{1,0:T(8,128)S(1)}, u32[]{:S(2)}, u32[]{:S(2)}) collective-permute-start(f32[256,256]{1,0:T(8,128)S(1)} %get-tuple-element.19.gain.e0), channel_id=1, source_target_pairs={{16,8},{20,12},{24,0},{28,4},{32,24},{36,28},{40,16},{44,20},{48,4... | collective-permute-start | bytes 786440 | tf_op jit(solution)/shard_map/ppermute | solution.py:276
  70.7 1.0 copy-start.9
  80.9 1.0 copy-start.3
  81.9 19.9 %collective-permute-start.10 = (f32[264,1024]{1,0:T(8,128)}, f32[264,1024]{1,0:T(8,128)}, u32[]{:S(2)}, u32[]{:S(2)}) collective-permute-start(f32[264,1024]{1,0:T(8,128)} %get-tuple-element.23), channel_id=1, source_target_pairs={{16,0},{32,16},{48,32},{64,48},{80,64},{96,80},{112,96},{128,112},... | collective-permute-start | bytes 3244040 | tf_op jit(solution)/shard_map/ppermute | solution.py:253
  86.5 24.7 %all-to-all-start.2 = ((f32[4,256,256]{2,1,0:T(8,128)}), f32[4,256,256]{2,1,0:T(8,128)}, u32[]{:S(2)}, u32[]{:S(2)}) async-start(f32[4,256,256]{2,1,0:T(8,128)} %copy-done.3), calls=%async_computation.2 | async-start | bytes 2097152 | tf_op jit(solution)/shard_map/all_to_all | solution.py:257
  91.3 11.7 %collective-permute-start.11 = (f32[256,256]{1,0:T(8,128)S(1)}, f32[256,256]{1,0:T(8,128)S(1)}, u32[]{:S(2)}, u32[]{:S(2)}) collective-permute-start(f32[256,256]{1,0:T(8,128)S(1)} %get-tuple-element.19.gain.e0), channel_id=1, source_target_pairs={{0,4},{4,8},{8,12},{12,0},{1,5},{5,9},{9,13},{13,1},{2,6},{6,10},{... | collective-permute-start | bytes 786440 | tf_op jit(solution)/shard_map/ppermute | solution.py:263
  94.7 15.1 %collective-permute-start.12 = (f32[256,256]{1,0:T(8,128)S(1)}, f32[256,256]{1,0:T(8,128)S(1)}, u32[]{:S(2)}, u32[]{:S(2)}) collective-permute-start(f32[256,256]{1,0:T(8,128)S(1)} %get-tuple-element.19.gain.e0), channel_id=1, source_target_pairs={{0,12},{4,0},{8,4},{12,8},{1,13},{5,1},{9,5},{13,9},{2,14},{6,2},{... | collective-permute-start | bytes 786440 | tf_op jit(solution)/shard_map/ppermute | solution.py:263
  98.3 12.2 %collective-permute-start.13 = (f32[256,256]{1,0:T(8,128)S(1)}, f32[256,256]{1,0:T(8,128)S(1)}, u32[]{:S(2)}, u32[]{:S(2)}) collective-permute-start(f32[256,256]{1,0:T(8,128)S(1)} %get-tuple-element.19.gain.e0), channel_id=1, source_target_pairs={{0,8},{4,12},{8,0},{12,4},{1,9},{5,13},{9,1},{13,5},{2,10},{6,14},... | collective-permute-start | bytes 786440 | tf_op jit(solution)/shard_map/ppermute | solution.py:263
  111.3 1.0 copy-start.23
  138.9 11.8 %collective-permute-start.14 = (f32[264,256]{1,0:T(8,128)S(1)}, f32[264,256]{1,0:T(8,128)S(1)}, u32[]{:S(2)}, u32[]{:S(2)}) collective-permute-start(f32[264,256]{1,0:T(8,128)S(1)} %shard_map.98.spread), channel_id=1, source_target_pairs={{32,0},{48,16},{64,32},{80,48},{96,64},{112,80},{128,96},{144,112}... | collective-permute-start | bytes 811016 | tf_op jit(solution)/shard_map/ppermute | solution.py:253
  141.8 17.5 %collective-permute-start.15 = (f32[256,256]{1,0:T(8,128)S(1)}, f32[256,256]{1,0:T(8,128)S(1)}, u32[]{:S(2)}, u32[]{:S(2)}) collective-permute-start(f32[256,256]{1,0:T(8,128)S(1)} %get-tuple-element.21.gain_2), channel_id=1, source_target_pairs={{32,0},{48,16},{64,32},{80,48},{96,64},{112,80},{128,96},{144,112}... | collective-permute-start | bytes 786440 | tf_op jit(solution)/shard_map/ppermute | solution.py:253
  151.8 40.8 %all-to-all-start.4 = ((f32[4,264,256]{2,1,0:T(8,128)}), f32[4,264,256]{2,1,0:T(8,128)S(1)}, u32[]{:S(2)}, u32[]{:S(2)}) async-start(f32[4,264,256]{2,1,0:T(8,128)} %broadcast_in_dim.6), calls=%async_computation.4 | async-start | bytes 2162688 | tf_op jit(solution)/shard_map/all_to_all | solution.py:257
  159.2 26.6 %collective-permute-start.16 = (f32[512,256]{1,0:T(8,128)S(1)}, f32[512,256]{1,0:T(8,128)S(1)}, u32[]{:S(2)}, u32[]{:S(2)}) collective-permute-start(f32[512,256]{1,0:T(8,128)S(1)} %constant_dynamic-update-slice_fusion.a0), channel_id=1, source_target_pairs={{0,4},{4,8},{8,12},{12,0},{1,5},{5,9},{9,13},{13,1},{2,6},{6,10},{... | collective-permute-start | bytes 1572872 | tf_op jit(solution)/shard_map/ppermute | solution.py:263
  163.2 22.6 %collective-permute-start.17 = (f32[512,256]{1,0:T(8,128)S(1)}, f32[512,256]{1,0:T(8,128)S(1)}, u32[]{:S(2)}, u32[]{:S(2)}) collective-permute-start(f32[512,256]{1,0:T(8,128)S(1)} %constant_dynamic-update-slice_fusion.a0), channel_id=1, source_target_pairs={{0,12},{4,0},{8,4},{12,8},{1,13},{5,1},{9,5},{13,9},{2,14},{6,2},{... | collective-permute-start | bytes 1572872 | tf_op jit(solution)/shard_map/ppermute | solution.py:263
  166.3 25.5 %collective-permute-start.18 = (f32[512,256]{1,0:T(8,128)S(1)}, f32[512,256]{1,0:T(8,128)S(1)}, u32[]{:S(2)}, u32[]{:S(2)}) collective-permute-start(f32[512,256]{1,0:T(8,128)S(1)} %constant_dynamic-update-slice_fusion.a0), channel_id=1, source_target_pairs={{0,8},{4,12},{8,0},{12,4},{1,9},{5,13},{9,1},{13,5},{2,10},{6,14},... | collective-permute-start | bytes 1572872 | tf_op jit(solution)/shard_map/ppermute | solution.py:263
  192.6 1.0 copy-start.5
  193.7 1.0 copy-start.7
  200.8 17.7 %all-to-all-start.5 = ((f32[4,64,1536]{2,1,0:T(8,128)}), f32[4,64,1536]{2,1,0:T(8,128)S(1)}, u32[]{:S(2)}, u32[]{:S(2)}) async-start(f32[4,64,1536]{2,1,0:T(8,128)} %get-tuple-element.27), calls=%async_computation.5 | async-start | bytes 3145728 | tf_op jit(solution)/shard_map/all_to_all | solution.py:257
  (24 other events, 19.1 us)

commit v3 on v2

--- a/solution.py
+++ b/solution.py
@@ -1,3 +1,5 @@
+import math
+
 import jax
 import jax.numpy as jnp
 from jax import lax
@@ -12,18 +14,36 @@
 F32 = jnp.float32
 
 
+def halves(array):
+    high = array.astype(jnp.bfloat16)
+    return high, (array - high.astype(F32)).astype(jnp.bfloat16)
+
+
+def three(left, right, contract):
+    def one(first, second):
+        return lax.dot_general(first, second, (contract, ((), ())), preferred_element_type=F32)
+
+    left_high, left_low = left
+    right_high, right_low = right
+    return one(left_high, right_high) + (one(left_high, right_low) + one(left_low, right_high))
+
+
 def dot(left, right):
-    return jnp.dot(left, right, precision=HIGHEST, preferred_element_type=F32)
+    return three(halves(left), halves(right), ((1,), (0,)))
 
 
 def dot_t(left, right):
+    return three(halves(left), halves(right), ((1,), (1,)))
+
+
+def exact_dot_t(left, right):
     return lax.dot_general(
         left, right, (((1,), (1,)), ((), ())), precision=HIGHEST, preferred_element_type=F32
     )
 
 
 def vector_times(row, matrix):
-    return dot_t(jnp.broadcast_to(row, (8, row.shape[1])), matrix)[0:1]
+    return exact_dot_t(jnp.broadcast_to(row, (8, row.shape[1])), matrix)[0:1]
 
 
 def swap_lanes(array):
@@ -118,11 +138,10 @@
 
 
 def second_gain(
-    where, offsets, weights, gain, x_in, e0, e1, e2, e3, c0, c1, c2, c3,
+    where, offsets, weights, gain, x_in, e0, e1, e2, e3, own_panel,
     gain_out, x_out, shift_out, c_out, tall,
 ):
     panel = gain.shape[0]
-    rows = panel // SIDE
     at_y = where[0]
     gain_wide = wide(x_in, panel)
     filtered = jnp.concatenate([x_in[i, panel : panel + 1, :] for i in range(SIDE)], axis=1)
@@ -137,9 +156,7 @@
     gain_out[...] = gain_2
     for i in range(SIDE):
         x_out[i] = gain_2
-    for piece, step in zip((c0, c1, c2, c3), STEPS):
-        source = lax.rem(at_y + SIDE - step, SIDE)
-        c_out[pl.ds(pl.multiple_of(source * rows, rows), rows), :] = piece[...]
+    c_out[0:panel, :] = own_panel[...]
     c_out[panel : panel + NBAND, :] = weights[...]
     c_out[panel + NBAND : panel + NBAND + 1, :] = filtered
     c_out[panel + NBAND + 1 : panel + NBAND + 2, :] = forward[0:1]
@@ -186,6 +203,11 @@
     out[panel:, :] = shift[...]
 
 
+def four_times(block, p1, p2, p3, out):
+    for i in range(SIDE):
+        out[i] = block[...]
+
+
 def second_spread(
     where, gain_2, gain_2_in, spread, y_in, a0, a1, a2, a3, x_out, shift_out, tall, later_tall,
 ):
@@ -230,22 +252,27 @@
     spread_out[...] = total + kept
 
 
-VMEM = pl.BlockSpec(memory_space=pltpu.VMEM)
+WHOLE = pl.BlockSpec()
+UNREAD = pl.BlockSpec(memory_space=pl.ANY)
 SMEM = pl.BlockSpec(memory_space=pltpu.SMEM)
 
 
-def call(kernel, scalars, arrays, outs, scratch=(), flops=0):
-    shapes = [jax.ShapeDtypeStruct(s, F32) for s in outs]
-    size = sum(a.size for a in arrays) + sum(s.size for s in shapes)
+def far(*arrays):
+    return [pltpu.with_memory_space_constraint(a, pltpu.HBM) for a in arrays]
+
+
+def call(kernel, scalars, arrays, outs, scratch=(), flops=0, unread=()):
+    shapes = [pltpu.HBM(s, F32) if len(s) == 3 else jax.ShapeDtypeStruct(s, F32) for s in outs]
+    size = sum(a.size for a in arrays) + sum(math.prod(s) for s in outs)
     return pl.pallas_call(
         kernel,
         out_shape=shapes,
-        in_specs=[SMEM] * len(scalars) + [VMEM] * len(arrays),
-        out_specs=[VMEM] * len(outs),
+        in_specs=[SMEM] * len(scalars) + [WHOLE] * len(arrays) + [UNREAD] * len(unread),
+        out_specs=[WHOLE] * len(outs),
         scratch_shapes=[pltpu.VMEM(s, F32) for s in scratch],
-        compiler_params=pltpu.CompilerParams(vmem_limit_bytes=40 * 2**20),
+        compiler_params=pltpu.CompilerParams(vmem_limit_bytes=24 * 2**20),
         cost_estimate=pl.CostEstimate(flops=flops, bytes_accessed=4 * size, transcendentals=0),
-    )(*scalars, *arrays)
+    )(*scalars, *arrays, *unread)
 
 
 def shifted(block, distance):
@@ -299,12 +326,12 @@
     x_message, y_message = call(
         prepare,
         (band_offset,),
-        (own, inverse, weights, prior_mean, innovation, seen_sites),
+        far(own, inverse, weights, prior_mean, innovation, seen_sites),
         ((SIDE, rows, columns + 2 * panel), (rows + 8, columns)),
     )
     first_in = swap(x_message, "x")
     inverse_pieces = ring(y_message, "y")
-    own_pieces = ring(own, "y")
+    own_panel = lax.all_gather(own, "y", axis=0, tiled=True)
     gain, x_message = call(
         first_gain,
         (where,),
@@ -318,7 +345,7 @@
     gain_2, x_message, shift, c_message = call(
         second_gain,
         (where, band_offset),
-        (weights, gain, gain_in, *later_pieces, *own_pieces),
+        (*far(weights), gain, gain_in, *far(*later_pieces, own_panel)),
         ((panel, panel), (SIDE, panel, panel), (8, panel), (panel + 8, columns)),
         ((columns, panel),),
         unit,
@@ -331,7 +358,7 @@
     part, shift_2 = call(
         first_spread,
         (where, next_offsets),
-        (c_in, gain_in, gain_2_in, first_in, *gain_pieces, shift),
+        (c_in, gain_in, gain_2_in, first_in, gain, *far(*gain_pieces[1:]), shift),
         ((SIDE, panel, panel), (8, panel)),
         ((columns, panel),),
         3 * unit,
@@ -340,7 +367,10 @@
     gain_2_pieces = ring(jnp.concatenate([gain_2, gain_2_later], axis=0), "y")
     (spread_2,) = call(join_spread, (), (parts, first_in, shift_2), ((panel + 8, panel),))
     later = shifted(spread_2, 2)
-    y_in = swap(jnp.broadcast_to(later[None], (SIDE, panel + 8, panel)), "y")
+    (y_message,) = call(
+        four_times, (), (later,), ((SIDE, panel + 8, panel),), unread=gain_2_pieces[1:]
+    )
+    y_in = swap(y_message, "y")
     x_message, shift_4 = call(
         second_spread,
         (where,),

time: 221 us -> 200 us (0.905)
  the two profiles are of different devices: /device:TPU:224 before, /device:TPU:2 now
where the time goes in v3:
time: 200 us; the launch traced here: 199 us
  waiting for transfers between devices  68.4 us (34%)
  starting transfers between devices  66.6 us (33%)
  Pallas kernels  25.4 us (13%)
  blocking collectives  18 us (9%)
  between operations  14.2 us (7%)
  local copies, waits for them, and re-layouts  5.5 us (3%)
    ppermute x9, waiting for transfers between devices, ring(): lax.ppermute(block, axis, [(i, (i + step) % SIDE) for i in range(SIDE)])  31.9 us
    ppermute x9, starting transfers between devices, ring(): lax.ppermute(block, axis, [(i, (i + step) % SIDE) for i in range(SIDE)])  28.8 us
    all_to_all x5, starting transfers between devices, swap(): return lax.all_to_all(message, axis, 0, 0)  28.8 us
    pallas_call x8, Pallas kernels, call(): pl.pallas_call(kernel, out_shape=shapes, in_specs=[SMEM] * len(scalars) +...  25.4 us
    all_to_all x1, blocking collectives, swap(): return lax.all_to_all(message, axis, 0, 0)  18 us
    ppermute x4, waiting for transfers between devices, ring_shifted(): pieces.append(lax.ppermute(block, ('tm', 'y'), route))  14.5 us
    all_to_all x5, waiting for transfers between devices, swap(): return lax.all_to_all(message, axis, 0, 0)  14.2 us
    ppermute x3, waiting for transfers between devices, shifted(): lax.ppermute(block, 'tm', [(i + distance, i) for i in range(count - dista...  7.23 us
  transfers between devices with their start and end apart: 22, of which 11 were waited for; matrix products, arithmetic and copies ran while one was open for 1% of the time, Pallas kernels for 1%

profile of v3, /device:TPU:2, one launch (start us, length us, event | category | flops | bytes accessed | tf_op | source)
XLA Modules:
  0.0 199.0 jit_solution(15848405404252753617)
XLA Ops:
  7.2 1.3 copy.12
  9.2 3.1 %shard_map.94 = (f32[4,64,1536]{2,1,0:T(8,128)}, f32[72,1024]{1,0:T(8,128)S(1)}) custom-call(s32[1,5]{1,0:T(1,128)S(1)} %copy-done, f32[64,1024]{1,0:T(8,128)} %bitcast.15, f32[64,1024]{1,0:T(8,128)} %bitcast.18, f32[5,1024]{1,0:T(8,128)} %bitcast.16, f32[1,64]{1,0:T(1,128)} %prior.1, f32[1,128]{1,0:T(1,128)} %innovation.1, s32[1,128]{1,0:T(1,128)} %sites.1), custom_call_target="tpu_custom_call" | custom-call | bytes 2413824 | tf_op jit(solution)/shard_map/pallas_call | solution.py:267
  12.3 9.4 %all-to-all-start = ((f32[4,64,1536]{2,1,0:T(8,128)}), f32[4,64,1536]{2,1,0:T(8,128)S(1)}, u32[]{:S(2)}, u32[]{:S(2)}) async-start(f32[4,64,1536]{2,1,0:T(8,128)} %get-tuple-element.17), calls=%async_computation | async-start | bytes 3145728 | tf_op jit(solution)/shard_map/all_to_all | solution.py:284
  22.5 1.9 collective-permute-start
  24.4 5.1 %collective-permute-start.1 = (f32[72,1024]{1,0:T(8,128)S(1)}, f32[72,1024]{1,0:T(8,128)S(1)}, u32[]{:S(2)}, u32[]{:S(2)}) collective-permute-start(f32[72,1024]{1,0:T(8,128)S(1)} %get-tuple-element.18.p0), channel_id=1, source_target_pairs={{0,12},{4,0},{8,4},{12,8},{1,13},{5,1},{9,5},{13,9},{2,14},{6,2},{... | collective-permute-start | bytes 884744 | tf_op jit(solution)/shard_map/ppermute | solution.py:290
  29.5 1.9 collective-permute-start.2
  31.5 3.9 %collective-permute-done.p1 = f32[72,1024]{1,0:T(8,128)S(1)} collective-permute-done((f32[72,1024]{1,0:T(8,128)S(1)}, f32[72,1024]{1,0:T(8,128)S(1)}, u32[]{:S(2)}, u32[]{:S(2)}) %collective-permute-start) | collective-permute-done | bytes 294944 | tf_op jit(solution)/shard_map/ppermute | solution.py:290
  35.4 2.7 %collective-permute-done.1.p2 = f32[72,1024]{1,0:T(8,128)S(1)} collective-permute-done((f32[72,1024]{1,0:T(8,128)S(1)}, f32[72,1024]{1,0:T(8,128)S(1)}, u32[]{:S(2)}, u32[]{:S(2)}) %collective-permute-start.1) | collective-permute-done | bytes 294944 | tf_op jit(solution)/shard_map/ppermute | solution.py:290
  38.1 1.5 collective-permute-done.2.p3
  39.6 2.3 %shard_map.95 = (f32[256,256]{1,0:T(8,128)S(1)}, f32[4,264,256]{2,1,0:T(8,128)}) custom-call(s32[4]{0:T(128)S(1)} %pad_add_fusion.where, f32[4,64,1536]{2,1,0:T(8,128)S(1)} %all-to-all-done.x_in.first_in, f32[72,1024]{1,0:T(8,128)S(1)} %get-tuple-element.18.p0, f32[72,1024]{1,0:T(8,128)S(1)} %collective-permute-done.p1, ...), custom_call_target="tpu_custom_call" | custom-call | flops 134217728 | bytes 4096000 | tf_op jit(solution)/shard_map/pallas_call | solution.py:267
  42.0 4.9 %all-to-all-start.1 = ((f32[4,264,256]{2,1,0:T(8,128)}), f32[4,264,256]{2,1,0:T(8,128)S(1)}, u32[]{:S(2)}, u32[]{:S(2)}) async-start(f32[4,264,256]{2,1,0:T(8,128)} %get-tuple-element.20), calls=%async_computation.1 | async-start | bytes 2162688 | tf_op jit(solution)/shard_map/all_to_all | solution.py:284
  52.1 14.4 %collective-permute-done.4.e1 = f32[256,256]{1,0:T(8,128)S(1)} collective-permute-done((f32[256,256]{1,0:T(8,128)S(1)}, f32[256,256]{1,0:T(8,128)S(1)}, u32[]{:S(2)}, u32[]{:S(2)}) %collective-permute-start.4) | collective-permute-done | bytes 262176 | tf_op jit(solution)/shard_map/ppermute | solution.py:303
  67.4 4.6 %shard_map.96 = (f32[256,256]{1,0:T(8,128)S(1)}, f32[4,256,256]{2,1,0:T(8,128)}, f32[8,256]{1,0:T(8,128)S(1)}, f32[264,1024]{1,0:T(8,128)}) custom-call(s32[4]{0:T(128)S(1)} %pad_add_fusion.where, s32[1,5]{1,0:T(1,128)S(1)} %copy-done.1, f32[5,1024]{1,0:T(8,128)} %bitcast.17, f32[256,256]{1,0:T(8,128)S(1)} %get-tuple-element.19.gain.e0, ...), custom_call_target="tpu_custom_call" | custom-call | flops 134217728 | bytes 5861376 | tf_op jit(solution)/shard_map/pallas_call | solution.py:267
  73.3 4.8 %all-to-all-start.2 = ((f32[4,256,256]{2,1,0:T(8,128)}), f32[4,256,256]{2,1,0:T(8,128)}, u32[]{:S(2)}, u32[]{:S(2)}) async-start(f32[4,256,256]{2,1,0:T(8,128)} %get-tuple-element.22), calls=%async_computation.2 | async-start | bytes 2097152 | tf_op jit(solution)/shard_map/all_to_all | solution.py:284
  78.1 3.1 %collective-permute-start.8 = (f32[256,256]{1,0:T(8,128)S(1)}, f32[256,256]{1,0:T(8,128)S(1)}, u32[]{:S(2)}, u32[]{:S(2)}) collective-permute-start(f32[256,256]{1,0:T(8,128)S(1)} %get-tuple-element.19.gain.e0), channel_id=1, source_target_pairs={{0,4},{4,8},{8,12},{12,0},{1,5},{5,9},{9,13},{13,1},{2,6},{6,10},{... | collective-permute-start | bytes 786440 | tf_op jit(solution)/shard_map/ppermute | solution.py:290
  81.2 3.9 %collective-permute-start.9 = (f32[256,256]{1,0:T(8,128)S(1)}, f32[256,256]{1,0:T(8,128)S(1)}, u32[]{:S(2)}, u32[]{:S(2)}) collective-permute-start(f32[256,256]{1,0:T(8,128)S(1)} %get-tuple-element.19.gain.e0), channel_id=1, source_target_pairs={{0,12},{4,0},{8,4},{12,8},{1,13},{5,1},{9,5},{13,9},{2,14},{6,2},{... | collective-permute-start | bytes 786440 | tf_op jit(solution)/shard_map/ppermute | solution.py:290
  85.2 2.0 collective-permute-start.10
  87.9 2.2 %collective-permute-done.8.e1 = f32[256,256]{1,0:T(8,128)S(1)} collective-permute-done((f32[256,256]{1,0:T(8,128)S(1)}, f32[256,256]{1,0:T(8,128)S(1)}, u32[]{:S(2)}, u32[]{:S(2)}) %collective-permute-start.8) | collective-permute-done | bytes 262176 | tf_op jit(solution)/shard_map/ppermute | solution.py:290
  90.0 6.8 %collective-permute-done.9.e2 = f32[256,256]{1,0:T(8,128)S(1)} collective-permute-done((f32[256,256]{1,0:T(8,128)S(1)}, f32[256,256]{1,0:T(8,128)S(1)}, u32[]{:S(2)}, u32[]{:S(2)}) %collective-permute-start.9) | collective-permute-done | bytes 262176 | tf_op jit(solution)/shard_map/ppermute | solution.py:290
  97.6 7.9 %shard_map.97 = (f32[4,256,256]{2,1,0:T(8,128)}, f32[8,256]{1,0:T(8,128)S(1)}) custom-call(s32[4]{0:T(128)S(1)} %pad_add_fusion.where, s32[8]{0:T(128)S(1)} %fusion.offsets, f32[264,1024]{1,0:T(8,128)} %collective-permute-done.7.c_in, f32[4,264,256]{2,1,0:T(8,128)S(1)} %all-to-all-done.1.x_in.gain_in, f32[4,256,256]{2,1,0:T(8,128)} %all-to-all-done.2.gain_2_in, ...), custom_call_target="tpu_custom_call" | custom-call | flops 402653184 | bytes 6897664 | tf_op jit(solution)/shard_map/pallas_call | solution.py:267
  105.5 4.8 %all-to-all-start.3 = ((f32[4,256,256]{2,1,0:T(8,128)}), f32[4,256,256]{2,1,0:T(8,128)S(1)}, u32[]{:S(2)}, u32[]{:S(2)}) async-start(f32[4,256,256]{2,1,0:T(8,128)} %get-tuple-element.25), calls=%async_computation.3 | async-start | bytes 2097152 | tf_op jit(solution)/shard_map/all_to_all | solution.py:284
  112.3 7.2 %collective-permute-done.12 = f32[256,256]{1,0:T(8,128)S(1)} collective-permute-done((f32[256,256]{1,0:T(8,128)S(1)}, f32[256,256]{1,0:T(8,128)S(1)}, u32[]{:S(2)}, u32[]{:S(2)}) %collective-permute-start.12) | collective-permute-done | bytes 262176 | tf_op jit(solution)/shard_map/ppermute | solution.py:280
  120.2 4.6 %collective-permute-start.13 = (f32[512,256]{1,0:T(8,128)}, f32[512,256]{1,0:T(8,128)S(1)}, u32[]{:S(2)}, u32[]{:S(2)}) collective-permute-start(f32[512,256]{1,0:T(8,128)} %constant_dynamic-update-slice_fusion.a0), channel_id=1, source_target_pairs={{0,4},{4,8},{8,12},{12,0},{1,5},{5,9},{9,13},{13,1},{2,6},{6,10},{... | collective-permute-start | bytes 1572872 | tf_op jit(solution)/shard_map/ppermute | solution.py:290
  124.9 2.8 %collective-permute-start.14 = (f32[512,256]{1,0:T(8,128)}, f32[512,256]{1,0:T(8,128)}, u32[]{:S(2)}, u32[]{:S(2)}) collective-permute-start(f32[512,256]{1,0:T(8,128)} %constant_dynamic-update-slice_fusion.a0), channel_id=1, source_target_pairs={{0,12},{4,0},{8,4},{12,8},{1,13},{5,1},{9,5},{13,9},{2,14},{6,2},{... | collective-permute-start | bytes 1572872 | tf_op jit(solution)/shard_map/ppermute | solution.py:290
  127.7 3.4 %collective-permute-start.15 = (f32[512,256]{1,0:T(8,128)}, f32[512,256]{1,0:T(8,128)}, u32[]{:S(2)}, u32[]{:S(2)}) collective-permute-start(f32[512,256]{1,0:T(8,128)} %constant_dynamic-update-slice_fusion.a0), channel_id=1, source_target_pairs={{0,8},{4,12},{8,0},{12,4},{1,9},{5,13},{9,1},{13,5},{2,10},{6,14},... | collective-permute-start | bytes 1572872 | tf_op jit(solution)/shard_map/ppermute | solution.py:290
  132.6 5.4 %collective-permute-done.13.p1.a1 = f32[512,256]{1,0:T(8,128)S(1)} collective-permute-done((f32[512,256]{1,0:T(8,128)}, f32[512,256]{1,0:T(8,128)S(1)}, u32[]{:S(2)}, u32[]{:S(2)}) %collective-permute-start.13) | collective-permute-done | bytes 524320 | tf_op jit(solution)/shard_map/ppermute | solution.py:290
  137.9 4.0 %collective-permute-done.14.p2.a2 = f32[512,256]{1,0:T(8,128)} collective-permute-done((f32[512,256]{1,0:T(8,128)}, f32[512,256]{1,0:T(8,128)}, u32[]{:S(2)}, u32[]{:S(2)}) %collective-permute-start.14) | collective-permute-done | bytes 524320 | tf_op jit(solution)/shard_map/ppermute | solution.py:290
  141.9 5.4 %collective-permute-done.15.p3.a3 = f32[512,256]{1,0:T(8,128)} collective-permute-done((f32[512,256]{1,0:T(8,128)}, f32[512,256]{1,0:T(8,128)}, u32[]{:S(2)}, u32[]{:S(2)}) %collective-permute-start.15) | collective-permute-done | bytes 524320 | tf_op jit(solution)/shard_map/ppermute | solution.py:290
  148.4 18.0 %all_to_all.30.y_in = f32[4,264,256]{2,1,0:T(8,128)S(1)} all-to-all(f32[4,264,256]{2,1,0:T(8,128)} %shard_map.99), channel_id=1, replica_groups=mesh['tm'=32,'y'=4,'x'=4] {'y'}, dimensions={0} | all-to-all | bytes 2162688 | tf_op jit(solution)/shard_map/all_to_all | solution.py:284
  166.4 5.3 %shard_map.100 = (f32[4,64,1536]{2,1,0:T(8,128)}, f32[8,256]{1,0:T(8,128)S(1)}) custom-call(s32[4]{0:T(128)S(1)} %pad_add_fusion.where, f32[256,256]{1,0:T(8,128)S(1)} %get-tuple-element.21.gain_2, f32[4,256,256]{2,1,0:T(8,128)} %all-to-all-done.2.gain_2_in, f32[264,256]{1,0:T(8,128)S(1)} %shard_map.98.spread, f32[4,264,256]{2,1,0:T(8,128)S(1)} %all_to_all.30.y_in, ...), custom_call_target="tpu_custom_call" | custom-call | flops 402653184 | bytes 6340608 | tf_op jit(solution)/shard_map/pallas_call | solution.py:267
  171.7 4.8 %all-to-all-start.5 = ((f32[4,64,1536]{2,1,0:T(8,128)}), f32[4,64,1536]{2,1,0:T(8,128)S(1)}, u32[]{:S(2)}, u32[]{:S(2)}) async-start(f32[4,64,1536]{2,1,0:T(8,128)} %get-tuple-element.27), calls=%async_computation.5 | async-start | bytes 3145728 | tf_op jit(solution)/shard_map/all_to_all | solution.py:284
  177.1 14.1 %all-to-all-done.5.x_in = f32[4,64,1536]{2,1,0:T(8,128)S(1)} async-done(((f32[4,64,1536]{2,1,0:T(8,128)}), f32[4,64,1536]{2,1,0:T(8,128)S(1)}, u32[]{:S(2)}, u32[]{:S(2)}) %all-to-all-start.5) | async-done | bytes 1572896 | tf_op jit(solution)/shard_map/all_to_all | solution.py:284
  (43 shorter events, 16.8 us)
Async XLA Ops:
  8.5 0.7 copy-start
  12.3 27.4 %all-to-all-start = ((f32[4,64,1536]{2,1,0:T(8,128)}), f32[4,64,1536]{2,1,0:T(8,128)S(1)}, u32[]{:S(2)}, u32[]{:S(2)}) async-start(f32[4,64,1536]{2,1,0:T(8,128)} %get-tuple-element.17), calls=%async_computation | async-start | bytes 3145728 | tf_op jit(solution)/shard_map/all_to_all | solution.py:284
  21.7 45.6 %all-gather.3.cloned.1.call-start = ((), (), s32[]{:S(2)}) async-start(), calls=%async_computation.6 | async-start | bytes 1310720 | tf_op jit(solution)/shard_map/all_gather | solution.py:334
  22.5 13.0 %collective-permute-start = (f32[72,1024]{1,0:T(8,128)S(1)}, f32[72,1024]{1,0:T(8,128)S(1)}, u32[]{:S(2)}, u32[]{:S(2)}) collective-permute-start(f32[72,1024]{1,0:T(8,128)S(1)} %get-tuple-element.18.p0), channel_id=1, source_target_pairs={{0,4},{4,8},{8,12},{12,0},{1,5},{5,9},{9,13},{13,1},{2,6},{6,10},{... | collective-permute-start | bytes 884744 | tf_op jit(solution)/shard_map/ppermute | solution.py:290
  24.4 13.7 %collective-permute-start.1 = (f32[72,1024]{1,0:T(8,128)S(1)}, f32[72,1024]{1,0:T(8,128)S(1)}, u32[]{:S(2)}, u32[]{:S(2)}) collective-permute-start(f32[72,1024]{1,0:T(8,128)S(1)} %get-tuple-element.18.p0), channel_id=1, source_target_pairs={{0,12},{4,0},{8,4},{12,8},{1,13},{5,1},{9,5},{13,9},{2,14},{6,2},{... | collective-permute-start | bytes 884744 | tf_op jit(solution)/shard_map/ppermute | solution.py:290
  29.5 10.1 %collective-permute-start.2 = (f32[72,1024]{1,0:T(8,128)S(1)}, f32[72,1024]{1,0:T(8,128)S(1)}, u32[]{:S(2)}, u32[]{:S(2)}) collective-permute-start(f32[72,1024]{1,0:T(8,128)S(1)} %get-tuple-element.18.p0), channel_id=1, source_target_pairs={{0,8},{4,12},{8,0},{12,4},{1,9},{5,13},{9,1},{13,5},{2,10},{6,14},... | collective-permute-start | bytes 884744 | tf_op jit(solution)/shard_map/ppermute | solution.py:290
  42.0 25.4 %copy-start.1 = (s32[1,5]{1,0:T(1,128)S(1)}, s32[1,5]{1,0:T(1,128)}, u32[]{:S(2)}) copy-start(s32[1,5]{1,0:T(1,128)} %offsets.3) | copy-start | bytes 64
  42.0 25.3 %all-to-all-start.1 = ((f32[4,264,256]{2,1,0:T(8,128)}), f32[4,264,256]{2,1,0:T(8,128)S(1)}, u32[]{:S(2)}, u32[]{:S(2)}) async-start(f32[4,264,256]{2,1,0:T(8,128)} %get-tuple-element.20), calls=%async_computation.1 | async-start | bytes 2162688 | tf_op jit(solution)/shard_map/all_to_all | solution.py:284
  46.9 5.2 %collective-permute-start.3 = (f32[256,256]{1,0:T(8,128)S(1)}, f32[256,256]{1,0:T(8,128)S(1)}, u32[]{:S(2)}, u32[]{:S(2)}) collective-permute-start(f32[256,256]{1,0:T(8,128)S(1)} %get-tuple-element.19.gain.e0), channel_id=1, source_target_pairs={{16,0},{20,4},{24,8},{28,12},{32,16},{36,20},{40,24},{44,28},{48,3... | collective-permute-start | bytes 786440 | tf_op jit(solution)/shard_map/ppermute | solution.py:303
  48.2 18.4 %collective-permute-start.4 = (f32[256,256]{1,0:T(8,128)S(1)}, f32[256,256]{1,0:T(8,128)S(1)}, u32[]{:S(2)}, u32[]{:S(2)}) collective-permute-start(f32[256,256]{1,0:T(8,128)S(1)} %get-tuple-element.19.gain.e0), channel_id=1, source_target_pairs={{16,4},{20,8},{24,12},{28,0},{32,20},{36,24},{40,28},{44,16},{48,3... | collective-permute-start | bytes 786440 | tf_op jit(solution)/shard_map/ppermute | solution.py:303
  49.5 17.1 %collective-permute-start.5 = (f32[256,256]{1,0:T(8,128)S(1)}, f32[256,256]{1,0:T(8,128)S(1)}, u32[]{:S(2)}, u32[]{:S(2)}) collective-permute-start(f32[256,256]{1,0:T(8,128)S(1)} %get-tuple-element.19.gain.e0), channel_id=1, source_target_pairs={{16,12},{20,0},{24,4},{28,8},{32,28},{36,16},{40,20},{44,24},{48,4... | collective-permute-start | bytes 786440 | tf_op jit(solution)/shard_map/ppermute | solution.py:303
  50.8 16.5 %collective-permute-start.6 = (f32[256,256]{1,0:T(8,128)S(1)}, f32[256,256]{1,0:T(8,128)}, u32[]{:S(2)}, u32[]{:S(2)}) collective-permute-start(f32[256,256]{1,0:T(8,128)S(1)} %get-tuple-element.19.gain.e0), channel_id=1, source_target_pairs={{16,8},{20,12},{24,0},{28,4},{32,24},{36,28},{40,16},{44,20},{48,4... | collective-permute-start | bytes 786440 | tf_op jit(solution)/shard_map/ppermute | solution.py:303
  52.1 15.3 %copy-start.2 = (f32[256,256]{1,0:T(8,128)}, f32[256,256]{1,0:T(8,128)S(1)}, u32[]{:S(2)}) copy-start(f32[256,256]{1,0:T(8,128)S(1)} %collective-permute-done.3.e0) | copy-start | bytes 786436
  66.6 0.8 copy-start.3
  66.6 0.7 copy-start.5
  72.0 15.2 %collective-permute-start.7 = (f32[264,1024]{1,0:T(8,128)}, f32[264,1024]{1,0:T(8,128)}, u32[]{:S(2)}, u32[]{:S(2)}) collective-permute-start(f32[264,1024]{1,0:T(8,128)} %get-tuple-element.23), channel_id=1, source_target_pairs={{16,0},{32,16},{48,32},{64,48},{80,64},{96,80},{112,96},{128,112},... | collective-permute-start | bytes 3244040 | tf_op jit(solution)/shard_map/ppermute | solution.py:280
  73.3 24.3 %all-to-all-start.2 = ((f32[4,256,256]{2,1,0:T(8,128)}), f32[4,256,256]{2,1,0:T(8,128)}, u32[]{:S(2)}, u32[]{:S(2)}) async-start(f32[4,256,256]{2,1,0:T(8,128)} %get-tuple-element.22), calls=%async_computation.2 | async-start | bytes 2097152 | tf_op jit(solution)/shard_map/all_to_all | solution.py:284
  78.1 11.9 %collective-permute-start.8 = (f32[256,256]{1,0:T(8,128)S(1)}, f32[256,256]{1,0:T(8,128)S(1)}, u32[]{:S(2)}, u32[]{:S(2)}) collective-permute-start(f32[256,256]{1,0:T(8,128)S(1)} %get-tuple-element.19.gain.e0), channel_id=1, source_target_pairs={{0,4},{4,8},{8,12},{12,0},{1,5},{5,9},{9,13},{13,1},{2,6},{6,10},{... | collective-permute-start | bytes 786440 | tf_op jit(solution)/shard_map/ppermute | solution.py:290
  81.2 15.6 %collective-permute-start.9 = (f32[256,256]{1,0:T(8,128)S(1)}, f32[256,256]{1,0:T(8,128)S(1)}, u32[]{:S(2)}, u32[]{:S(2)}) collective-permute-start(f32[256,256]{1,0:T(8,128)S(1)} %get-tuple-element.19.gain.e0), channel_id=1, source_target_pairs={{0,12},{4,0},{8,4},{12,8},{1,13},{5,1},{9,5},{13,9},{2,14},{6,2},{... | collective-permute-start | bytes 786440 | tf_op jit(solution)/shard_map/ppermute | solution.py:290
  85.2 12.4 %collective-permute-start.10 = (f32[256,256]{1,0:T(8,128)S(1)}, f32[256,256]{1,0:T(8,128)}, u32[]{:S(2)}, u32[]{:S(2)}) collective-permute-start(f32[256,256]{1,0:T(8,128)S(1)} %get-tuple-element.19.gain.e0), channel_id=1, source_target_pairs={{0,8},{4,12},{8,0},{12,4},{1,9},{5,13},{9,1},{13,5},{2,10},{6,14},... | collective-permute-start | bytes 786440 | tf_op jit(solution)/shard_map/ppermute | solution.py:290
  90.0 7.5 %copy-start.4 = (f32[256,256]{1,0:T(8,128)}, f32[256,256]{1,0:T(8,128)S(1)}, u32[]{:S(2)}) copy-start(f32[256,256]{1,0:T(8,128)S(1)} %collective-permute-done.8.e1) | copy-start | bytes 786436
  96.9 0.7 copy-start.6
  105.5 25.6 %all-to-all-start.3 = ((f32[4,256,256]{2,1,0:T(8,128)}), f32[4,256,256]{2,1,0:T(8,128)S(1)}, u32[]{:S(2)}, u32[]{:S(2)}) async-start(f32[4,256,256]{2,1,0:T(8,128)} %get-tuple-element.25), calls=%async_computation.3 | async-start | bytes 2097152 | tf_op jit(solution)/shard_map/all_to_all | solution.py:284
  110.3 9.2 %collective-permute-start.12 = (f32[256,256]{1,0:T(8,128)S(1)}, f32[256,256]{1,0:T(8,128)S(1)}, u32[]{:S(2)}, u32[]{:S(2)}) collective-permute-start(f32[256,256]{1,0:T(8,128)S(1)} %get-tuple-element.21.gain_2), channel_id=1, source_target_pairs={{32,0},{48,16},{64,32},{80,48},{96,64},{112,80},{128,96},{144,112}... | collective-permute-start | bytes 786440 | tf_op jit(solution)/shard_map/ppermute | solution.py:280
  120.2 17.7 %collective-permute-start.13 = (f32[512,256]{1,0:T(8,128)}, f32[512,256]{1,0:T(8,128)S(1)}, u32[]{:S(2)}, u32[]{:S(2)}) collective-permute-start(f32[512,256]{1,0:T(8,128)} %constant_dynamic-update-slice_fusion.a0), channel_id=1, source_target_pairs={{0,4},{4,8},{8,12},{12,0},{1,5},{5,9},{9,13},{13,1},{2,6},{6,10},{... | collective-permute-start | bytes 1572872 | tf_op jit(solution)/shard_map/ppermute | solution.py:290
  124.9 17.1 %collective-permute-start.14 = (f32[512,256]{1,0:T(8,128)}, f32[512,256]{1,0:T(8,128)}, u32[]{:S(2)}, u32[]{:S(2)}) collective-permute-start(f32[512,256]{1,0:T(8,128)} %constant_dynamic-update-slice_fusion.a0), channel_id=1, source_target_pairs={{0,12},{4,0},{8,4},{12,8},{1,13},{5,1},{9,5},{13,9},{2,14},{6,2},{... | collective-permute-start | bytes 1572872 | tf_op jit(solution)/shard_map/ppermute | solution.py:290
  127.7 19.6 %collective-permute-start.15 = (f32[512,256]{1,0:T(8,128)}, f32[512,256]{1,0:T(8,128)}, u32[]{:S(2)}, u32[]{:S(2)}) collective-permute-start(f32[512,256]{1,0:T(8,128)} %constant_dynamic-update-slice_fusion.a0), channel_id=1, source_target_pairs={{0,8},{4,12},{8,0},{12,4},{1,9},{5,13},{9,1},{13,5},{2,10},{6,14},... | collective-permute-start | bytes 1572872 | tf_op jit(solution)/shard_map/ppermute | solution.py:290
  131.3 16.1 %collective-permute-start.11 = (f32[264,256]{1,0:T(8,128)S(1)}, f32[264,256]{1,0:T(8,128)S(1)}, u32[]{:S(2)}, u32[]{:S(2)}) collective-permute-start(f32[264,256]{1,0:T(8,128)S(1)} %shard_map.98.spread), channel_id=1, source_target_pairs={{32,0},{48,16},{64,32},{80,48},{96,64},{112,80},{128,96},{144,112}... | collective-permute-start | bytes 811016 | tf_op jit(solution)/shard_map/ppermute | solution.py:280
  171.7 19.5 %all-to-all-start.5 = ((f32[4,64,1536]{2,1,0:T(8,128)}), f32[4,64,1536]{2,1,0:T(8,128)S(1)}, u32[]{:S(2)}, u32[]{:S(2)}) async-start(f32[4,64,1536]{2,1,0:T(8,128)} %get-tuple-element.27), calls=%async_computation.5 | async-start | bytes 3145728 | tf_op jit(solution)/shard_map/all_to_all | solution.py:284
Sparse Core Ops, SparseCore 0:
  24.7 32.6 all-gather.2

commit v4 on v3

v4 whole, which is shorter than its diff:
```python
import math

import jax
import jax.numpy as jnp
from jax import lax
from jax.experimental import pallas as pl
from jax.experimental.pallas import tpu as pltpu
from jax.sharding import Mesh, PartitionSpec as P

NBAND = 5
SIDE = 4

HIGHEST = lax.Precision.HIGHEST
F32 = jnp.float32


def halves(array):
    high = array.astype(jnp.bfloat16)
    return high, (array - high.astype(F32)).astype(jnp.bfloat16)


def three(left, right, contract):
    def one(first, second):
        return lax.dot_general(first, second, (contract, ((), ())), preferred_element_type=F32)

    left_high, left_low = left
    right_high, right_low = right
    return one(left_high, right_high) + (one(left_high, right_low) + one(left_low, right_high))


def dot_t(left, right):
    return three(halves(left), halves(right), ((1,), (1,)))


def exact_dot_t(left, right):
    return lax.dot_general(
        left, right, (((1,), (1,)), ((), ())), precision=HIGHEST, preferred_element_type=F32
    )


def vector_times(row, matrix):
    return exact_dot_t(jnp.broadcast_to(row, (8, row.shape[1])), matrix)[0:1]


def row_times(row, matrix_halves):
    whole = jnp.broadcast_to(row, (8, row.shape[1]))
    return three(halves(whole), matrix_halves, ((1,), (1,)))[0:1]


LANES = 128


def tiles(array):
    return [array[:, i : i + LANES] for i in range(0, array.shape[1], LANES)]


def low_lanes(rows, width):
    return lax.broadcasted_iota(jnp.int32, (rows, LANES), 1) < width


def swap_tiles(blocks):
    width = LANES // 2
    low = low_lanes(blocks[0].shape[0], width)
    rolled = [pltpu.roll(block, width, 1) for block in blocks]
    out = []
    for b in range(SIDE):
        for half in range(SIDE // 2):
            ends = []
            for side in range(2):
                at = (2 * half + side) * SIDE + b
                ends.append((blocks if at % 2 == side else rolled)[at // 2])
            out.append(jnp.where(low, ends[0], ends[1]))
    return out


def swap_lanes(array):
    return jnp.concatenate(swap_tiles(tiles(array)), axis=1)


def band_tiles(blocks, weights, offset_at):
    rows = blocks[0].shape[0]
    width = LANES // 2
    low = low_lanes(rows, width)
    zero = jnp.zeros((rows, LANES), F32)
    turned = [zero] + [pltpu.roll(block, width, 1) for block in blocks] + [zero]
    moved = [jnp.where(low, turned[i], turned[i + 1]) for i in range(len(blocks) + 1)]
    totals = [zero] * len(blocks)
    for b in range(NBAND):
        distance = offset_at(b) + width
        near = low_lanes(rows, LANES - distance)
        back = lax.rem(LANES - distance, LANES)
        rolled = [pltpu.roll(block, back, 1) for block in moved]
        for i in range(len(blocks)):
            weight = weights[b : b + 1, i * LANES : (i + 1) * LANES]
            totals[i] = totals[i] + weight * jnp.where(near, rolled[i], rolled[i + 1])
    return totals


def bands(array, weights, offset_at):
    return jnp.concatenate(band_tiles(tiles(array), weights, offset_at), axis=1)


def wide(ref, rows):
    return jnp.concatenate([ref[i, 0:rows, :] for i in range(SIDE)], axis=1)


STEPS = (0, 1, 3, 2)


def sources(pieces, at):
    return [(piece, lax.rem(at + SIDE - step, SIDE)) for piece, step in zip(pieces, STEPS)]


def place_tall(pieces, at_y, out_ref, row0=0):
    panel = out_ref.shape[0] // SIDE
    chunk = panel // SIDE
    for piece, source in sources(pieces, at_y):
        for b in range(SIDE):
            out_ref[pl.ds(pl.multiple_of(b * panel + source * chunk, chunk), chunk), :] = piece[
                row0 + b * chunk : row0 + (b + 1) * chunk, :
            ]


def prepare(offsets, own, inverse, weights, prior, innovation, sites, crossed_out, y_out):
    rows, columns = own.shape
    matrix = own[...]
    crossed_out[...] = bands(matrix, weights[...], lambda b: offsets[0, b])
    state = lax.broadcasted_iota(jnp.int32, (columns, sites.shape[1]), 0)
    matches = (state == sites[...]).astype(F32)
    pulled = vector_times(innovation[...], matches)
    filtered = prior[...] + vector_times(pulled, matrix)
    for i in range(SIDE):
        y_out[i, 0:rows, :] = inverse[...]
        y_out[i, rows : 2 * rows, :] = matrix
        y_out[i, 2 * rows :, :] = jnp.zeros((8, columns), F32)
        y_out[i, 2 * rows : 2 * rows + 1, 0:rows] = filtered


def place_rows(pieces, at, out):
    rows = pieces[0].shape[0]
    for piece, source in sources(pieces, at):
        out[pl.ds(pl.multiple_of(source * rows, rows), rows), :] = piece[...]


def first_gain(where, y_in, x0, x1, x2, x3, gain_out, x_out, crossed):
    rows = x0.shape[0]
    panel = SIDE * rows
    place_rows((x0, x1, x2, x3), where[1], crossed)
    inverse = jnp.concatenate([y_in[i, 0:rows, :] for i in range(SIDE)], axis=0)
    gain = dot_t(crossed[...], inverse)
    gain_out[...] = gain
    tail = jnp.concatenate(
        [y_in[i, 2 * rows : 2 * rows + 1, 0:rows] for i in range(SIDE)], axis=1
    )
    tail = jnp.broadcast_to(tail, (8, panel))
    for i in range(SIDE):
        x_out[i, 0:panel, :] = gain
        x_out[i, panel:, :] = tail


def cut_blocks(where, y_in, x0, x1, x2, x3, out, crossed):
    rows = x0.shape[0]
    panel = SIDE * rows
    place_rows((x0, x1, x2, x3), where[1], crossed)
    at_y = pl.multiple_of(where[0] * panel, panel)
    own = jnp.concatenate(
        [y_in[i, rows : 2 * rows, pl.ds(at_y, panel)] for i in range(SIDE)], axis=0
    )
    out[0:panel, :] = own.T
    odd = lax.rem(where[1], 2)
    at_x = lax.div(where[1], 2) * LANES
    low = low_lanes(panel, rows)
    parts = []
    for i in range(SIDE):
        part = crossed[:, pl.ds(pl.multiple_of(i * panel + at_x, LANES), LANES)]
        turn = odd if i % 2 == 0 else 1 - odd
        parts.append(pltpu.roll(part, turn * rows, 1))
    out[panel:, 0:LANES] = jnp.where(low, parts[0], parts[1])
    out[panel:, LANES:] = jnp.where(low, parts[2], parts[3])


def second_gain(
    where, offsets, weights, gain, x_in, e0, e1, e2, e3, y_in,
    gain_out, x_out, shift_out, c_out, high_out, low_out, tall,
):
    panel = gain.shape[0]
    rows = panel // SIDE
    at_y = where[0]
    gain_wide = halves(wide(x_in, panel))
    high_out[...] = gain_wide[0]
    low_out[...] = gain_wide[1]
    place_tall((e0, e1, e2, e3), at_y, tall)
    product = three(gain_wide, halves(tall[...]), ((1,), (0,)))
    gain_2 = jnp.where(where[2] == 1, product, gain[...])
    gain_out[...] = gain_2
    for i in range(SIDE):
        x_out[i] = gain_2
    filtered = jnp.concatenate([x_in[i, panel : panel + 8, :] for i in range(SIDE)], axis=1)
    natural = swap_lanes(filtered)
    forward = swap_lanes(bands(natural, weights[...], lambda b: offsets[0, b]))
    mine = jnp.zeros((1, panel), F32)
    for i in range(SIDE):
        mine = mine + jnp.where(at_y == i, natural[0:1, i * panel : (i + 1) * panel], 0.0)
    shift_out[...] = jnp.broadcast_to(mine - row_times(forward[0:1], gain_wide), (8, panel))
    for i in range(SIDE):
        c_out[i * rows : (i + 1) * rows, :] = y_in[i, rows : 2 * rows, :]
    c_out[panel : panel + NBAND, :] = weights[...]
    c_out[panel + NBAND : panel + NBAND + 1, :] = filtered[0:1]
    c_out[panel + NBAND + 1 : panel + NBAND + 2, :] = forward[0:1]
    lane = lax.broadcasted_iota(jnp.int32, (1, c_out.shape[1]), 1)
    held = jnp.zeros((1, c_out.shape[1]), jnp.int32)
    for b in range(NBAND):
        held = jnp.where(lane == b, offsets[0, b], held)
    c_out[panel + NBAND + 2 : panel + NBAND + 3, :] = held.astype(F32)


def later_inputs(offsets, c_in, rows_out, own_high, own_low, crossed_high, crossed_low):
    panel = own_high.shape[0]
    step = 16
    weights = c_in[panel : panel + NBAND, :]

    def put(at, blocks, high_out, low_out):
        for i, block in enumerate(swap_tiles(blocks)):
            high, low = halves(block)
            high_out[pl.ds(at, step), i * LANES : (i + 1) * LANES] = high
            low_out[pl.ds(at, step), i * LANES : (i + 1) * LANES] = low

    def one(index, carry):
        at = pl.multiple_of(index * step, step)
        blocks = tiles(c_in[pl.ds(at, step), :])
        put(at, blocks, own_high, own_low)
        put(at, band_tiles(blocks, weights, lambda b: offsets[b]), crossed_high, crossed_low)
        return carry

    lax.fori_loop(0, panel // step, one, 0)
    rows_out[...] = c_in[panel:, :]


def first_spread(
    where, wide_high, wide_low, gain_2_in, own_high, own_low, crossed_high, crossed_low,
    later_rows, blocks, e0, e1, e2, e3, shift, gain_2, gain_2_later,
    part_out, shift_out, pair_out, high_out, low_out, tall,
):
    panel = e0.shape[0]
    at_y = where[0]
    pair_out[0:panel, :] = gain_2[...]
    pair_out[panel:, :] = gain_2_later[...]
    gain_wide = (wide_high[...], wide_low[...])
    gain_2_wide = halves(wide(gain_2_in, panel))
    high_out[...] = gain_2_wide[0]
    low_out[...] = gain_2_wide[1]
    across = ((1,), (1,))
    turned = three(gain_wide, (own_high[...], own_low[...]), across) - three(
        gain_2_wide, (crossed_high[...], crossed_low[...]), across
    )
    moved = row_times(later_rows[NBAND : NBAND + 1, :], gain_wide) - row_times(
        later_rows[NBAND + 1 : NBAND + 2, :], gain_2_wide
    )
    inside = where[2] == 1
    shift_out[...] = shift[...] + jnp.where(inside, moved, 0.0)
    turned = halves(jnp.where(inside, turned, 0.0) - blocks[panel:, :])
    place_tall((e0, e1, e2, e3), at_y, tall)
    for i in range(SIDE):
        part_out[i] = three(halves(tall[i * panel : (i + 1) * panel, :]), turned, across)


def join_spread(parts, blocks, shift, out):
    panel = parts.shape[1]
    total = (parts[0] + parts[1]) + (parts[2] + parts[3])
    out[0:panel, :] = blocks[0:panel, :] + total.T
    out[panel:, :] = shift[...]


def four_times(block, p1, p2, p3, out):
    for i in range(SIDE):
        out[i] = block[...]


def second_spread(
    where, gain_2, wide_high, wide_low, spread, y_in, a0, a1, a2, a3,
    x_out, shift_out, tall, later_tall,
):
    panel = gain_2.shape[0]
    rows = panel // SIDE
    columns = SIDE * panel
    at_y = where[0]
    inside = where[3] == 1
    gain_2_wide = (wide_high[...], wide_low[...])
    for i in range(SIDE):
        for b in range(SIDE):
            tall[b * panel + i * rows : b * panel + (i + 1) * rows, :] = y_in[
                i, b * rows : (b + 1) * rows, :
            ]
    along = ((1,), (0,))
    turned = halves(jnp.where(inside, three(gain_2_wide, halves(tall[...]), along), 0.0))
    shifts = jnp.concatenate([y_in[i, panel : panel + 8, :] for i in range(SIDE)], axis=1)
    moved = row_times(swap_lanes(shifts)[0:1], gain_2_wide)
    shift_out[...] = spread[panel:, :] + jnp.where(inside, moved, 0.0)
    pieces = (a0, a1, a2, a3)
    place_tall(pieces, at_y, later_tall, panel)
    gain_4 = jnp.where(inside, three(gain_2_wide, halves(later_tall[...]), along), gain_2[...])
    for i in range(SIDE):
        x_out[i, :, columns : columns + panel] = gain_4[i * rows : (i + 1) * rows]
        x_out[i, :, columns + panel :] = spread[i * rows : (i + 1) * rows, :]
    for piece, source in sources(pieces, at_y):
        tall[pl.ds(pl.multiple_of(source * panel, panel), panel), :] = piece[0:panel, :]
    part = three(turned, halves(tall[...]), ((1,), (1,)))
    for i in range(SIDE):
        x_out[i, :, 0:columns] = part[i * rows : (i + 1) * rows]


def finish(x_in, gain_out, spread_out):
    rows, columns = gain_out.shape
    panel = SIDE * rows
    gain_out[...] = swap_lanes(
        jnp.concatenate([x_in[i, :, columns : columns + panel] for i in range(SIDE)], axis=1)
    )
    kept = swap_lanes(jnp.concatenate([x_in[i, :, columns + panel :] for i in range(SIDE)], axis=1))
    total = (x_in[0, :, 0:columns] + x_in[1, :, 0:columns]) + (
        x_in[2, :, 0:columns] + x_in[3, :, 0:columns]
    )
    spread_out[...] = total + kept


WHOLE = pl.BlockSpec()
UNREAD = pl.BlockSpec(memory_space=pl.ANY)
SMEM = pl.BlockSpec(memory_space=pltpu.SMEM)


def far(*arrays):
    return [pltpu.with_memory_space_constraint(a, pltpu.HBM) for a in arrays]


def call(kernel, scalars, arrays, outs, scratch=(), flops=0, unread=(), coarse=()):
    shapes = [pltpu.HBM(s, F32) for s in outs] + [pltpu.HBM(s, jnp.bfloat16) for s in coarse]
    size = sum(a.size for a in arrays) + sum(math.prod(s) for s in outs)
    return pl.pallas_call(
        kernel,
        out_shape=shapes,
        in_specs=[SMEM] * len(scalars) + [WHOLE] * len(arrays) + [UNREAD] * len(unread),
        out_specs=[WHOLE] * len(shapes),
        scratch_shapes=[pltpu.VMEM(s, F32) for s in scratch],
        compiler_params=pltpu.CompilerParams(vmem_limit_bytes=24 * 2**20),
        cost_estimate=pl.CostEstimate(flops=flops, bytes_accessed=4 * size, transcendentals=0),
    )(*scalars, *arrays, *unread)


def shifted(block, distance):
    count = lax.axis_size("tm")
    return lax.ppermute(block, "tm", [(i + distance, i) for i in range(count - distance)])


def swap(message, axis):
    return lax.all_to_all(message, axis, 0, 0)


def ring(block, axis):
    pieces = [block]
    for step in STEPS[1:]:
        pieces.append(lax.ppermute(block, axis, [(i, (i + step) % SIDE) for i in range(SIDE)]))
    return pieces


def ring_shifted(block, distance):
    count = lax.axis_size("tm")
    pieces = []
    for step in STEPS:
        route = [
            ((i + distance) * SIDE + j, i * SIDE + (j + step) % SIDE)
            for i in range(count - distance)
            for j in range(SIDE)
        ]
        pieces.append(lax.ppermute(block, ("tm", "y"), route))
    return pieces


def body(covariance, precision, band_weight, band_offset, prior_mean, innovation, seen_sites):
    own = covariance[0]
    inverse = precision[0]
    weights = band_weight[0]
    rows, columns = own.shape
    panel = SIDE * rows
    at_t = lax.axis_index("tm")
    count_t = lax.axis_size("tm")
    at_x = lax.axis_index("x")
    where = jnp.stack(
        [
            lax.axis_index("y").astype(jnp.int32),
            at_x.astype(jnp.int32),
            (at_t + 1 < count_t).astype(jnp.int32),
            (at_t + 2 < count_t).astype(jnp.int32),
        ]
    )
    unit = 2 * panel * panel * columns

    crossed, y_message = call(
        prepare,
        (band_offset,),
        far(own, inverse, weights, prior_mean, innovation, seen_sites),
        ((rows, columns), (SIDE, 2 * rows + 8, columns)),
    )
    y_in = swap(y_message, "y")
    crossed_pieces = ring(crossed, "x")
    gain, x_message = call(
        first_gain,
        (where,),
        (y_in, *far(*crossed_pieces)),
        ((panel, panel), (SIDE, panel + 8, panel)),
        ((panel, columns),),
        unit,
    )
    gain_in = swap(x_message, "x")
    later_pieces = ring_shifted(gain, 1)
    (blocks,) = call(
        cut_blocks, (where,), (y_in, *far(*crossed_pieces)), ((2 * panel, panel),), ((panel, columns),)
    )
    gain_2, x_message, shift, c_message, wide_high, wide_low = call(
        second_gain,
        (where, band_offset),
        (*far(weights, gain), gain_in, *far(*later_pieces), y_in),
        ((panel, panel), (SIDE, panel, panel), (8, panel), (panel + 8, columns)),
        ((columns, panel),),
        unit,
        coarse=((panel, columns),) * 2,
    )
    gain_2_in = swap(x_message, "x")
    gain_pieces = ring(gain, "y")
    gain_2_later = shifted(gain_2, 2)
    c_in = shifted(c_message, 1)
    next_offsets = c_in[panel + NBAND + 2, 0:8].astype(jnp.int32)
    later_rows, *later_halves = call(
        later_inputs, (next_offsets,), far(c_in), ((8, columns),), coarse=((panel, columns),) * 4
    )
    part, shift_2, gain_2_pair, wide_high, wide_low = call(
        first_spread,
        (where,),
        (
            *far(wide_high, wide_low), gain_2_in, *far(*later_halves, later_rows, blocks),
            *far(gain, *gain_pieces[1:], shift, gain_2, gain_2_later),
        ),
        ((SIDE, panel, panel), (8, panel), (2 * panel, panel)),
        ((columns, panel),),
        3 * unit,
        coarse=((panel, columns),) * 2,
    )
    parts = swap(part, "x")
    gain_2_pieces = ring(gain_2_pair, "y")
    (spread_2,) = call(join_spread, (), (parts, *far(blocks, shift_2)), ((panel + 8, panel),))
    later = shifted(spread_2, 2)
    (y_message,) = call(
        four_times, (), (later,), ((SIDE, panel + 8, panel),), unread=gain_2_pieces[1:]
    )
    y_in = swap(y_message, "y")
    x_message, shift_4 = call(
        second_spread,
        (where,),
        (*far(gain_2, wide_high, wide_low, spread_2), y_in, *far(*gain_2_pieces)),
        ((SIDE, rows, columns + 2 * panel), (8, panel)),
        ((columns, panel), (columns, panel)),
        3 * unit,
    )
    last_in = swap(x_message, "x")
    final_gain, final_spread = call(finish, (), (last_in,), ((rows, columns), (rows, columns)))
    final_shift = lax.dynamic_slice_in_dim(shift_4[0], at_x * rows, rows, 0)
    return final_gain[None], final_shift[None], final_spread[None]


def solution(mesh):
    count = mesh.devices.shape[0]
    grid = Mesh(mesh.devices.reshape(count, SIDE, SIDE), ("tm", "y", "x"))
    row = ("y", "x")
    in_specs = (
        P("tm", row, None),
        P("tm", row, None),
        P("tm", None, None),
        P("tm", None),
        P("tm", row),
        P("tm", None),
        P("tm", None),
    )
    out_specs = (P("tm", row, None), P("tm", row), P("tm", row, None))
    return jax.shard_map(body, mesh=grid, in_specs=in_specs, out_specs=out_specs, check_vma=False)
```

time: 200 us -> 191 us (0.955)
  the two profiles are of different devices: /device:TPU:2 before, /device:TPU:384 now
where the time goes in v4:
time: 191 us; the launch traced here: 190 us
  starting transfers between devices  75.7 us (40%)
  waiting for transfers between devices  54.3 us (28%)
  Pallas kernels  35.3 us (18%)
  blocking collectives  17.1 us (9%)
  local copies, waits for them, and re-layouts  5.64 us (3%)
    pallas_call x10, Pallas kernels, call(): pl.pallas_call(kernel, out_shape=shapes, in_specs=[SMEM] * len(scalars) +...  35.3 us
    ppermute x9, starting transfers between devices, ring(): lax.ppermute(block, axis, [(i, (i + step) % SIDE) for i in range(SIDE)])  30.4 us
    all_to_all x5, waiting for transfers between devices, swap(): return lax.all_to_all(message, axis, 0, 0)  28.8 us
    all_to_all x5, starting transfers between devices, swap(): return lax.all_to_all(message, axis, 0, 0)  23 us
    all_to_all x1, blocking collectives, swap(): return lax.all_to_all(message, axis, 0, 0)  17.1 us
    ppermute x9, waiting for transfers between devices, ring(): lax.ppermute(block, axis, [(i, (i + step) % SIDE) for i in range(SIDE)])  15.9 us
    ppermute x4, starting transfers between devices, ring_shifted(): pieces.append(lax.ppermute(block, ('tm', 'y'), route))  12.3 us
    ppermute x3, starting transfers between devices, shifted(): lax.ppermute(block, 'tm', [(i + distance, i) for i in range(count - dista...  10 us
  transfers between devices with their start and end apart: 21, of which 9 were waited for; matrix products, arithmetic and copies ran while one was open for 1% of the time, Pallas kernels for 6%

profile of v4, /device:TPU:384, one launch (start us, length us, event | category | flops | bytes accessed | tf_op | source)
XLA Modules:
  0.0 189.7 jit_solution(7812625173441682493)
XLA Ops:
  2.6 3.4 %shard_map.94 = (f32[64,1024]{1,0:T(8,128)}, f32[4,136,1024]{2,1,0:T(8,128)}) custom-call(s32[1,5]{1,0:T(1,128)S(1)} %copy-done.3, f32[64,1024]{1,0:T(8,128)} %bitcast.15, f32[64,1024]{1,0:T(8,128)} %bitcast.16, f32[5,1024]{1,0:T(8,128)} %bitcast.13, f32[1,64]{1,0:T(1,128)} %prior.1, f32[1,128]{1,0:T(1,128)} %innovation.1, s32[1,128]{1,0:T(1,128)} %sites.1), custom_call_target="tpu_custom_call" | custom-call | bytes 3036416 | tf_op jit(solution)/shard_map/pallas_call | solution.py:337
  6.0 4.6 %all-to-all-start = ((f32[4,136,1024]{2,1,0:T(8,128)}), f32[4,136,1024]{2,1,0:T(8,128)S(1)}, u32[]{:S(2)}, u32[]{:S(2)}) async-start(f32[4,136,1024]{2,1,0:T(8,128)} %get-tuple-element.27), calls=%async_computation | async-start | bytes 4456448 | tf_op jit(solution)/shard_map/all_to_all | solution.py:354
  10.6 3.4 %collective-permute-start = (f32[64,1024]{1,0:T(8,128)S(1)}, f32[64,1024]{1,0:T(8,128)S(1)}, u32[]{:S(2)}, u32[]{:S(2)}) collective-permute-start(f32[64,1024]{1,0:T(8,128)S(1)} %copy-done.6), channel_id=1, source_target_pairs={{0,1},{1,2},{2,3},{3,0},{4,5},{5,6},{6,7},{7,4},{8,9},{9,10},{10,1... | collective-permute-start | bytes 786440 | tf_op jit(solution)/shard_map/ppermute | solution.py:360
  14.0 3.7 %collective-permute-start.1 = (f32[64,1024]{1,0:T(8,128)S(1)}, f32[64,1024]{1,0:T(8,128)S(1)}, u32[]{:S(2)}, u32[]{:S(2)}) collective-permute-start(f32[64,1024]{1,0:T(8,128)S(1)} %copy-done.6), channel_id=1, source_target_pairs={{0,3},{1,0},{2,1},{3,2},{4,7},{5,4},{6,5},{7,6},{8,11},{9,8},{10,9... | collective-permute-start | bytes 786440 | tf_op jit(solution)/shard_map/ppermute | solution.py:360
  17.7 3.7 %collective-permute-start.2 = (f32[64,1024]{1,0:T(8,128)S(1)}, f32[64,1024]{1,0:T(8,128)S(1)}, u32[]{:S(2)}, u32[]{:S(2)}) collective-permute-start(f32[64,1024]{1,0:T(8,128)S(1)} %copy-done.6), channel_id=1, source_target_pairs={{0,2},{1,3},{2,0},{3,1},{4,6},{5,7},{6,4},{7,5},{8,10},{9,11},{10,... | collective-permute-start | bytes 786440 | tf_op jit(solution)/shard_map/ppermute | solution.py:360
  21.5 6.8 %collective-permute-done.1.x2 = f32[64,1024]{1,0:T(8,128)S(1)} collective-permute-done((f32[64,1024]{1,0:T(8,128)S(1)}, f32[64,1024]{1,0:T(8,128)S(1)}, u32[]{:S(2)}, u32[]{:S(2)}) %collective-permute-start.1) | collective-permute-done | bytes 262176 | tf_op jit(solution)/shard_map/ppermute | solution.py:360
  28.3 10.0 %all-to-all-done.y_in = f32[4,136,1024]{2,1,0:T(8,128)S(1)} async-done(((f32[4,136,1024]{2,1,0:T(8,128)}), f32[4,136,1024]{2,1,0:T(8,128)S(1)}, u32[]{:S(2)}, u32[]{:S(2)}) %all-to-all-start) | async-done | bytes 2228256 | tf_op jit(solution)/shard_map/all_to_all | solution.py:354
  38.4 3.1 %shard_map.95 = (f32[256,256]{1,0:T(8,128)}, f32[4,264,256]{2,1,0:T(8,128)}) custom-call(s32[4]{0:T(128)S(1)} %pad_add_fusion.where, f32[4,136,1024]{2,1,0:T(8,128)S(1)} %all-to-all-done.y_in, f32[64,1024]{1,0:T(8,128)} %get-tuple-element.28.x0, f32[64,1024]{1,0:T(8,128)} %copy-done.7, f32[64,1024]{1,0:T(8,128)} %copy-done.8, f32[64,1024]{1,0:T(8,128)} %copy-done.9), custom_call_target="tpu_custom_call" | custom-call | flops 134217728 | bytes 4620288 | tf_op jit(solution)/shard_map/pallas_call | solution.py:337
  41.5 4.4 %all-to-all-start.1 = ((f32[4,264,256]{2,1,0:T(8,128)}), f32[4,264,256]{2,1,0:T(8,128)S(1)}, u32[]{:S(2)}, u32[]{:S(2)}) async-start(f32[4,264,256]{2,1,0:T(8,128)} %get-tuple-element.30), calls=%async_computation.1 | async-start | bytes 2162688 | tf_op jit(solution)/shard_map/all_to_all | solution.py:354
  48.0 4.1 %collective-permute-start.4 = (f32[256,256]{1,0:T(8,128)}, f32[256,256]{1,0:T(8,128)S(1)}, u32[]{:S(2)}, u32[]{:S(2)}) collective-permute-start(f32[256,256]{1,0:T(8,128)} %get-tuple-element.29.gain.e0), channel_id=1, source_target_pairs={{16,4},{20,8},{24,12},{28,0},{32,20},{36,24},{40,28},{44,16},{48,3... | collective-permute-start | bytes 786440 | tf_op jit(solution)/shard_map/ppermute | solution.py:373
  52.1 4.2 %collective-permute-start.5 = (f32[256,256]{1,0:T(8,128)}, f32[256,256]{1,0:T(8,128)S(1)}, u32[]{:S(2)}, u32[]{:S(2)}) collective-permute-start(f32[256,256]{1,0:T(8,128)} %get-tuple-element.29.gain.e0), channel_id=1, source_target_pairs={{16,12},{20,0},{24,4},{28,8},{32,28},{36,16},{40,20},{44,24},{48,4... | collective-permute-start | bytes 786440 | tf_op jit(solution)/shard_map/ppermute | solution.py:373
  59.9 5.3 %collective-permute-done.5.e2 = f32[256,256]{1,0:T(8,128)S(1)} collective-permute-done((f32[256,256]{1,0:T(8,128)}, f32[256,256]{1,0:T(8,128)S(1)}, u32[]{:S(2)}, u32[]{:S(2)}) %collective-permute-start.5) | collective-permute-done | bytes 262176 | tf_op jit(solution)/shard_map/ppermute | solution.py:373
  65.9 2.7 %collective-permute-done.6.e3 = f32[256,256]{1,0:T(8,128)} collective-permute-done((f32[256,256]{1,0:T(8,128)}, f32[256,256]{1,0:T(8,128)}, u32[]{:S(2)}, u32[]{:S(2)}) %collective-permute-start.6) | collective-permute-done | bytes 262176 | tf_op jit(solution)/shard_map/ppermute | solution.py:373
  68.6 4.1 %shard_map.96 = (f32[256,256]{1,0:T(8,128)}, f32[4,256,256]{2,1,0:T(8,128)}, f32[8,256]{1,0:T(8,128)}, f32[264,1024]{1,0:T(8,128)}, bf16[256,1024]{1,0:T(8,128)(2,1)}, /*index=5*/bf16[256,1024]{1,0:T(8,128)(2,1)}) custom-call(s32[4]{0:T(128)S(1)} %pad_add_fusion.where, s32[1,5]{1,0:T(1,128)S(1)} %copy-done.4, f32[5,1024]{1,0:T(8,128)} %bitcast.14, ...), custom_call_target="tpu_custom_call" | custom-call | flops 134217728 | bytes 7041024 | tf_op jit(solution)/shard_map/pallas_call | solution.py:337
  72.7 3.6 %collective-permute-start.7 = (f32[264,1024]{1,0:T(8,128)}, f32[264,1024]{1,0:T(8,128)}, u32[]{:S(2)}, u32[]{:S(2)}) collective-permute-start(f32[264,1024]{1,0:T(8,128)} %get-tuple-element.35), channel_id=1, source_target_pairs={{16,0},{32,16},{48,32},{64,48},{80,64},{96,80},{112,96},{128,112},... | collective-permute-start | bytes 3244040 | tf_op jit(solution)/shard_map/ppermute | solution.py:350
  76.3 4.8 %all-to-all-start.2 = ((f32[4,256,256]{2,1,0:T(8,128)}), f32[4,256,256]{2,1,0:T(8,128)S(1)}, u32[]{:S(2)}, u32[]{:S(2)}) async-start(f32[4,256,256]{2,1,0:T(8,128)} %get-tuple-element.34), calls=%async_computation.2 | async-start | bytes 2097152 | tf_op jit(solution)/shard_map/all_to_all | solution.py:354
  83.1 5.1 %collective-permute-start.9 = (f32[256,256]{1,0:T(8,128)}, f32[256,256]{1,0:T(8,128)S(1)}, u32[]{:S(2)}, u32[]{:S(2)}) collective-permute-start(f32[256,256]{1,0:T(8,128)} %get-tuple-element.29.gain.e0), channel_id=1, source_target_pairs={{0,12},{4,0},{8,4},{12,8},{1,13},{5,1},{9,5},{13,9},{2,14},{6,2},{... | collective-permute-start | bytes 786440 | tf_op jit(solution)/shard_map/ppermute | solution.py:360
  88.2 2.4 %collective-permute-start.10 = (f32[256,256]{1,0:T(8,128)}, f32[256,256]{1,0:T(8,128)S(1)}, u32[]{:S(2)}, u32[]{:S(2)}) collective-permute-start(f32[256,256]{1,0:T(8,128)} %get-tuple-element.29.gain.e0), channel_id=1, source_target_pairs={{0,8},{4,12},{8,0},{12,4},{1,9},{5,13},{9,1},{13,5},{2,10},{6,14},... | collective-permute-start | bytes 786440 | tf_op jit(solution)/shard_map/ppermute | solution.py:360
  90.6 3.5 %collective-permute-start.11 = (f32[256,256]{1,0:T(8,128)S(1)}, f32[256,256]{1,0:T(8,128)}, u32[]{:S(2)}, u32[]{:S(2)}) collective-permute-start(f32[256,256]{1,0:T(8,128)S(1)} %copy-done.5), channel_id=1, source_target_pairs={{32,0},{48,16},{64,32},{80,48},{96,64},{112,80},{128,96},{144,112}... | collective-permute-start | bytes 786440 | tf_op jit(solution)/shard_map/ppermute | solution.py:350
  97.2 7.5 %shard_map.97 = (f32[8,1024]{1,0:T(8,128)}, bf16[256,1024]{1,0:T(8,128)(2,1)}, bf16[256,1024]{1,0:T(8,128)(2,1)}, bf16[256,1024]{1,0:T(8,128)(2,1)}, bf16[256,1024]{1,0:T(8,128)(2,1)}) custom-call(s32[8]{0:T(128)S(1)} %fusion.offsets, f32[264,1024]{1,0:T(8,128)} %collective-permute-done.7.c_in), custom_call_target="tpu_custom_call" | custom-call | bytes 1114112 | tf_op jit(solution)/shard_map/pallas_call | solution.py:337
  106.2 5.8 %shard_map.99 = (f32[4,256,256]{2,1,0:T(8,128)}, f32[8,256]{1,0:T(8,128)}, f32[512,256]{1,0:T(8,128)}, bf16[256,1024]{1,0:T(8,128)(2,1)}, bf16[256,1024]{1,0:T(8,128)(2,1)}) custom-call(s32[4]{0:T(128)S(1)} %pad_add_fusion.where, bf16[256,1024]{1,0:T(8,128)(2,1)} %get-tuple-element.32.wide_high, bf16[256,1024]{1,0:T(8,128)(2,1)} %get-tuple-element.33.wide_low, ...), custom_call_target="tpu_custom_call" | custom-call | flops 402653184 | bytes 11059200 | tf_op jit(solution)/shard_map/pallas_call | solution.py:337
  112.0 4.9 %all-to-all-start.3 = ((f32[4,256,256]{2,1,0:T(8,128)}), f32[4,256,256]{2,1,0:T(8,128)S(1)}, u32[]{:S(2)}, u32[]{:S(2)}) async-start(f32[4,256,256]{2,1,0:T(8,128)} %get-tuple-element.44), calls=%async_computation.3 | async-start | bytes 2097152 | tf_op jit(solution)/shard_map/all_to_all | solution.py:354
  116.9 3.3 %collective-permute-start.13 = (f32[512,256]{1,0:T(8,128)S(1)}, f32[512,256]{1,0:T(8,128)S(1)}, u32[]{:S(2)}, u32[]{:S(2)}) collective-permute-start(f32[512,256]{1,0:T(8,128)S(1)} %copy-done.10), channel_id=1, source_target_pairs={{0,4},{4,8},{8,12},{12,0},{1,5},{5,9},{9,13},{13,1},{2,6},{6,10},{... | collective-permute-start | bytes 1572872 | tf_op jit(solution)/shard_map/ppermute | solution.py:360
  120.2 3.7 %collective-permute-start.14 = (f32[512,256]{1,0:T(8,128)S(1)}, f32[512,256]{1,0:T(8,128)S(1)}, u32[]{:S(2)}, u32[]{:S(2)}) collective-permute-start(f32[512,256]{1,0:T(8,128)S(1)} %copy-done.10), channel_id=1, source_target_pairs={{0,12},{4,0},{8,4},{12,8},{1,13},{5,1},{9,5},{13,9},{2,14},{6,2},{... | collective-permute-start | bytes 1572872 | tf_op jit(solution)/shard_map/ppermute | solution.py:360
  124.0 3.2 %collective-permute-start.15 = (f32[512,256]{1,0:T(8,128)S(1)}, f32[512,256]{1,0:T(8,128)S(1)}, u32[]{:S(2)}, u32[]{:S(2)}) collective-permute-start(f32[512,256]{1,0:T(8,128)S(1)} %copy-done.10), channel_id=1, source_target_pairs={{0,8},{4,12},{8,0},{12,4},{1,9},{5,13},{9,1},{13,5},{2,10},{6,14},... | collective-permute-start | bytes 1572872 | tf_op jit(solution)/shard_map/ppermute | solution.py:360
  127.1 4.1 %all-to-all-done.3.parts = f32[4,256,256]{2,1,0:T(8,128)S(1)} async-done(((f32[4,256,256]{2,1,0:T(8,128)}), f32[4,256,256]{2,1,0:T(8,128)S(1)}, u32[]{:S(2)}, u32[]{:S(2)}) %all-to-all-start.3) | async-done | bytes 1048608 | tf_op jit(solution)/shard_map/all_to_all | solution.py:354
  133.1 2.9 %collective-permute-start.12 = (f32[264,256]{1,0:T(8,128)}, f32[264,256]{1,0:T(8,128)S(1)}, u32[]{:S(2)}, u32[]{:S(2)}) collective-permute-start(f32[264,256]{1,0:T(8,128)} %shard_map.100.spread), channel_id=1, source_target_pairs={{32,0},{48,16},{64,32},{80,48},{96,64},{112,80},{128,96},{144,112}... | collective-permute-start | bytes 811016 | tf_op jit(solution)/shard_map/ppermute | solution.py:350
  136.0 7.8 %collective-permute-done.13.p1.a1 = f32[512,256]{1,0:T(8,128)S(1)} collective-permute-done((f32[512,256]{1,0:T(8,128)S(1)}, f32[512,256]{1,0:T(8,128)S(1)}, u32[]{:S(2)}, u32[]{:S(2)}) %collective-permute-start.13) | collective-permute-done | bytes 524320 | tf_op jit(solution)/shard_map/ppermute | solution.py:360
  146.4 17.1 %all_to_all.30.y_in = f32[4,264,256]{2,1,0:T(8,128)S(1)} all-to-all(f32[4,264,256]{2,1,0:T(8,128)} %shard_map.101), channel_id=1, replica_groups=mesh['tm'=32,'y'=4,'x'=4] {'y'}, dimensions={0} | all-to-all | bytes 2162688 | tf_op jit(solution)/shard_map/all_to_all | solution.py:354
  163.6 5.1 %shard_map.102 = (f32[4,64,1536]{2,1,0:T(8,128)}, f32[8,256]{1,0:T(8,128)}) custom-call(s32[4]{0:T(128)S(1)} %pad_add_fusion.where, f32[256,256]{1,0:T(8,128)} %get-tuple-element.31.gain_2, bf16[256,1024]{1,0:T(8,128)(2,1)} %get-tuple-element.42.wide_high, bf16[256,1024]{1,0:T(8,128)(2,1)} %get-tuple-element.43.wide_low, f32[264,256]{1,0:T(8,128)} %shard_map.100.spread, ...), custom_call_target="tpu_custom_call" | custom-call | flops 402653184 | bytes 7389184 | tf_op jit(solution)/shard_map/pallas_call | solution.py:337
  168.7 4.2 %all-to-all-start.5 = ((f32[4,64,1536]{2,1,0:T(8,128)}), f32[4,64,1536]{2,1,0:T(8,128)S(1)}, u32[]{:S(2)}, u32[]{:S(2)}) async-start(f32[4,64,1536]{2,1,0:T(8,128)} %get-tuple-element.47), calls=%async_computation.5 | async-start | bytes 3145728 | tf_op jit(solution)/shard_map/all_to_all | solution.py:354
  174.2 14.6 %all-to-all-done.5.x_in = f32[4,64,1536]{2,1,0:T(8,128)S(1)} async-done(((f32[4,64,1536]{2,1,0:T(8,128)}), f32[4,64,1536]{2,1,0:T(8,128)S(1)}, u32[]{:S(2)}, u32[]{:S(2)}) %all-to-all-start.5) | async-done | bytes 1572896 | tf_op jit(solution)/shard_map/all_to_all | solution.py:354
  (60 shorter events, 21.6 us)
Async XLA Ops:
  6.0 4.6 %copy-start.6 = (f32[64,1024]{1,0:T(8,128)S(1)}, f32[64,1024]{1,0:T(8,128)}, u32[]{:S(2)}) copy-start(f32[64,1024]{1,0:T(8,128)} %get-tuple-element.28.x0) | copy-start | bytes 786436
  6.0 32.3 %all-to-all-start = ((f32[4,136,1024]{2,1,0:T(8,128)}), f32[4,136,1024]{2,1,0:T(8,128)S(1)}, u32[]{:S(2)}, u32[]{:S(2)}) async-start(f32[4,136,1024]{2,1,0:T(8,128)} %get-tuple-element.27), calls=%async_computation | async-start | bytes 4456448 | tf_op jit(solution)/shard_map/all_to_all | solution.py:354
  10.6 10.9 %collective-permute-start = (f32[64,1024]{1,0:T(8,128)S(1)}, f32[64,1024]{1,0:T(8,128)S(1)}, u32[]{:S(2)}, u32[]{:S(2)}) collective-permute-start(f32[64,1024]{1,0:T(8,128)S(1)} %copy-done.6), channel_id=1, source_target_pairs={{0,1},{1,2},{2,3},{3,0},{4,5},{5,6},{6,7},{7,4},{8,9},{9,10},{10,1... | collective-permute-start | bytes 786440 | tf_op jit(solution)/shard_map/ppermute | solution.py:360
  14.0 14.3 %collective-permute-start.1 = (f32[64,1024]{1,0:T(8,128)S(1)}, f32[64,1024]{1,0:T(8,128)S(1)}, u32[]{:S(2)}, u32[]{:S(2)}) collective-permute-start(f32[64,1024]{1,0:T(8,128)S(1)} %copy-done.6), channel_id=1, source_target_pairs={{0,3},{1,0},{2,1},{3,2},{4,7},{5,4},{6,5},{7,6},{8,11},{9,8},{10,9... | collective-permute-start | bytes 786440 | tf_op jit(solution)/shard_map/ppermute | solution.py:360
  17.7 10.6 %collective-permute-start.2 = (f32[64,1024]{1,0:T(8,128)S(1)}, f32[64,1024]{1,0:T(8,128)S(1)}, u32[]{:S(2)}, u32[]{:S(2)}) collective-permute-start(f32[64,1024]{1,0:T(8,128)S(1)} %copy-done.6), channel_id=1, source_target_pairs={{0,2},{1,3},{2,0},{3,1},{4,6},{5,7},{6,4},{7,5},{8,10},{9,11},{10,... | collective-permute-start | bytes 786440 | tf_op jit(solution)/shard_map/ppermute | solution.py:360
  21.5 16.9 %copy-start.7 = (f32[64,1024]{1,0:T(8,128)}, f32[64,1024]{1,0:T(8,128)S(1)}, u32[]{:S(2)}) copy-start(f32[64,1024]{1,0:T(8,128)S(1)} %collective-permute-done.x1) | copy-start | bytes 786436
  28.3 10.1 %copy-start.8 = (f32[64,1024]{1,0:T(8,128)}, f32[64,1024]{1,0:T(8,128)S(1)}, u32[]{:S(2)}) copy-start(f32[64,1024]{1,0:T(8,128)S(1)} %collective-permute-done.1.x2) | copy-start | bytes 786436
  28.3 10.0 %copy-start.9 = (f32[64,1024]{1,0:T(8,128)}, f32[64,1024]{1,0:T(8,128)S(1)}, u32[]{:S(2)}) copy-start(f32[64,1024]{1,0:T(8,128)S(1)} %collective-permute-done.2.x3) | copy-start | bytes 786436
  41.5 27.1 %copy-start.4 = (s32[1,5]{1,0:T(1,128)S(1)}, s32[1,5]{1,0:T(1,128)}, u32[]{:S(2)}) copy-start(s32[1,5]{1,0:T(1,128)} %offsets.3) | copy-start | bytes 64
  41.5 27.1 %all-to-all-start.1 = ((f32[4,264,256]{2,1,0:T(8,128)}), f32[4,264,256]{2,1,0:T(8,128)S(1)}, u32[]{:S(2)}, u32[]{:S(2)}) async-start(f32[4,264,256]{2,1,0:T(8,128)} %get-tuple-element.30), calls=%async_computation.1 | async-start | bytes 2162688 | tf_op jit(solution)/shard_map/all_to_all | solution.py:354
  45.9 12.3 %collective-permute-start.3 = (f32[256,256]{1,0:T(8,128)}, f32[256,256]{1,0:T(8,128)S(1)}, u32[]{:S(2)}, u32[]{:S(2)}) collective-permute-start(f32[256,256]{1,0:T(8,128)} %get-tuple-element.29.gain.e0), channel_id=1, source_target_pairs={{16,0},{20,4},{24,8},{28,12},{32,16},{36,20},{40,24},{44,28},{48,3... | collective-permute-start | bytes 786440 | tf_op jit(solution)/shard_map/ppermute | solution.py:373
  48.0 11.9 %collective-permute-start.4 = (f32[256,256]{1,0:T(8,128)}, f32[256,256]{1,0:T(8,128)S(1)}, u32[]{:S(2)}, u32[]{:S(2)}) collective-permute-start(f32[256,256]{1,0:T(8,128)} %get-tuple-element.29.gain.e0), channel_id=1, source_target_pairs={{16,4},{20,8},{24,12},{28,0},{32,20},{36,24},{40,28},{44,16},{48,3... | collective-permute-start | bytes 786440 | tf_op jit(solution)/shard_map/ppermute | solution.py:373
  52.1 13.1 %collective-permute-start.5 = (f32[256,256]{1,0:T(8,128)}, f32[256,256]{1,0:T(8,128)S(1)}, u32[]{:S(2)}, u32[]{:S(2)}) collective-permute-start(f32[256,256]{1,0:T(8,128)} %get-tuple-element.29.gain.e0), channel_id=1, source_target_pairs={{16,12},{20,0},{24,4},{28,8},{32,28},{36,16},{40,20},{44,24},{48,4... | collective-permute-start | bytes 786440 | tf_op jit(solution)/shard_map/ppermute | solution.py:373
  56.3 12.3 %collective-permute-start.6 = (f32[256,256]{1,0:T(8,128)}, f32[256,256]{1,0:T(8,128)}, u32[]{:S(2)}, u32[]{:S(2)}) collective-permute-start(f32[256,256]{1,0:T(8,128)} %get-tuple-element.29.gain.e0), channel_id=1, source_target_pairs={{16,8},{20,12},{24,0},{28,4},{32,24},{36,28},{40,16},{44,20},{48,4... | collective-permute-start | bytes 786440 | tf_op jit(solution)/shard_map/ppermute | solution.py:373
  58.2 7.0 %copy-start.14 = (f32[256,256]{1,0:T(8,128)}, f32[256,256]{1,0:T(8,128)S(1)}, u32[]{:S(2)}) copy-start(f32[256,256]{1,0:T(8,128)S(1)} %collective-permute-done.3.e0) | copy-start | bytes 786436
  59.9 5.3 %copy-start.15 = (f32[256,256]{1,0:T(8,128)}, f32[256,256]{1,0:T(8,128)S(1)}, u32[]{:S(2)}) copy-start(f32[256,256]{1,0:T(8,128)S(1)} %collective-permute-done.4.e1) | copy-start | bytes 786436
  72.7 17.9 %copy-start.5 = (f32[256,256]{1,0:T(8,128)S(1)}, f32[256,256]{1,0:T(8,128)}, u32[]{:S(2)}) copy-start(f32[256,256]{1,0:T(8,128)} %get-tuple-element.31.gain_2) | copy-start | bytes 786436
  72.7 23.7 %collective-permute-start.7 = (f32[264,1024]{1,0:T(8,128)}, f32[264,1024]{1,0:T(8,128)}, u32[]{:S(2)}, u32[]{:S(2)}) collective-permute-start(f32[264,1024]{1,0:T(8,128)} %get-tuple-element.35), channel_id=1, source_target_pairs={{16,0},{32,16},{48,32},{64,48},{80,64},{96,80},{112,96},{128,112},... | collective-permute-start | bytes 3244040 | tf_op jit(solution)/shard_map/ppermute | solution.py:350
  76.3 29.8 %all-to-all-start.2 = ((f32[4,256,256]{2,1,0:T(8,128)}), f32[4,256,256]{2,1,0:T(8,128)S(1)}, u32[]{:S(2)}, u32[]{:S(2)}) async-start(f32[4,256,256]{2,1,0:T(8,128)} %get-tuple-element.34), calls=%async_computation.2 | async-start | bytes 2097152 | tf_op jit(solution)/shard_map/all_to_all | solution.py:354
  81.2 23.5 %collective-permute-start.8 = (f32[256,256]{1,0:T(8,128)}, f32[256,256]{1,0:T(8,128)S(1)}, u32[]{:S(2)}, u32[]{:S(2)}) collective-permute-start(f32[256,256]{1,0:T(8,128)} %get-tuple-element.29.gain.e0), channel_id=1, source_target_pairs={{0,4},{4,8},{8,12},{12,0},{1,5},{5,9},{9,13},{13,1},{2,6},{6,10},{... | collective-permute-start | bytes 786440 | tf_op jit(solution)/shard_map/ppermute | solution.py:360
  83.1 21.6 %collective-permute-start.9 = (f32[256,256]{1,0:T(8,128)}, f32[256,256]{1,0:T(8,128)S(1)}, u32[]{:S(2)}, u32[]{:S(2)}) collective-permute-start(f32[256,256]{1,0:T(8,128)} %get-tuple-element.29.gain.e0), channel_id=1, source_target_pairs={{0,12},{4,0},{8,4},{12,8},{1,13},{5,1},{9,5},{13,9},{2,14},{6,2},{... | collective-permute-start | bytes 786440 | tf_op jit(solution)/shard_map/ppermute | solution.py:360
  88.2 16.5 %collective-permute-start.10 = (f32[256,256]{1,0:T(8,128)}, f32[256,256]{1,0:T(8,128)S(1)}, u32[]{:S(2)}, u32[]{:S(2)}) collective-permute-start(f32[256,256]{1,0:T(8,128)} %get-tuple-element.29.gain.e0), channel_id=1, source_target_pairs={{0,8},{4,12},{8,0},{12,4},{1,9},{5,13},{9,1},{13,5},{2,10},{6,14},... | collective-permute-start | bytes 786440 | tf_op jit(solution)/shard_map/ppermute | solution.py:360
  90.6 15.5 %collective-permute-start.11 = (f32[256,256]{1,0:T(8,128)S(1)}, f32[256,256]{1,0:T(8,128)}, u32[]{:S(2)}, u32[]{:S(2)}) collective-permute-start(f32[256,256]{1,0:T(8,128)S(1)} %copy-done.5), channel_id=1, source_target_pairs={{32,0},{48,16},{64,32},{80,48},{96,64},{112,80},{128,96},{144,112}... | collective-permute-start | bytes 786440 | tf_op jit(solution)/shard_map/ppermute | solution.py:350
  112.0 4.9 %copy-start.10 = (f32[512,256]{1,0:T(8,128)S(1)}, f32[512,256]{1,0:T(8,128)}, u32[]{:S(2)}) copy-start(f32[512,256]{1,0:T(8,128)} %get-tuple-element.46.a0) | copy-start | bytes 1572868
  112.0 19.3 %all-to-all-start.3 = ((f32[4,256,256]{2,1,0:T(8,128)}), f32[4,256,256]{2,1,0:T(8,128)S(1)}, u32[]{:S(2)}, u32[]{:S(2)}) async-start(f32[4,256,256]{2,1,0:T(8,128)} %get-tuple-element.44), calls=%async_computation.3 | async-start | bytes 2097152 | tf_op jit(solution)/shard_map/all_to_all | solution.py:354
  116.9 27.0 %collective-permute-start.13 = (f32[512,256]{1,0:T(8,128)S(1)}, f32[512,256]{1,0:T(8,128)S(1)}, u32[]{:S(2)}, u32[]{:S(2)}) collective-permute-start(f32[512,256]{1,0:T(8,128)S(1)} %copy-done.10), channel_id=1, source_target_pairs={{0,4},{4,8},{8,12},{12,0},{1,5},{5,9},{9,13},{13,1},{2,6},{6,10},{... | collective-permute-start | bytes 1572872 | tf_op jit(solution)/shard_map/ppermute | solution.py:360
  120.2 24.9 %collective-permute-start.14 = (f32[512,256]{1,0:T(8,128)S(1)}, f32[512,256]{1,0:T(8,128)S(1)}, u32[]{:S(2)}, u32[]{:S(2)}) collective-permute-start(f32[512,256]{1,0:T(8,128)S(1)} %copy-done.10), channel_id=1, source_target_pairs={{0,12},{4,0},{8,4},{12,8},{1,13},{5,1},{9,5},{13,9},{2,14},{6,2},{... | collective-permute-start | bytes 1572872 | tf_op jit(solution)/shard_map/ppermute | solution.py:360
  124.0 21.1 %collective-permute-start.15 = (f32[512,256]{1,0:T(8,128)S(1)}, f32[512,256]{1,0:T(8,128)S(1)}, u32[]{:S(2)}, u32[]{:S(2)}) collective-permute-start(f32[512,256]{1,0:T(8,128)S(1)} %copy-done.10), channel_id=1, source_target_pairs={{0,8},{4,12},{8,0},{12,4},{1,9},{5,13},{9,1},{13,5},{2,10},{6,14},... | collective-permute-start | bytes 1572872 | tf_op jit(solution)/shard_map/ppermute | solution.py:360
  133.1 12.0 %collective-permute-start.12 = (f32[264,256]{1,0:T(8,128)}, f32[264,256]{1,0:T(8,128)S(1)}, u32[]{:S(2)}, u32[]{:S(2)}) collective-permute-start(f32[264,256]{1,0:T(8,128)} %shard_map.100.spread), channel_id=1, source_target_pairs={{32,0},{48,16},{64,32},{80,48},{96,64},{112,80},{128,96},{144,112}... | collective-permute-start | bytes 811016 | tf_op jit(solution)/shard_map/ppermute | solution.py:350
  143.9 2.4 %copy-start = (f32[512,256]{1,0:T(8,128)}, f32[512,256]{1,0:T(8,128)S(1)}, u32[]{:S(2)}) copy-start(f32[512,256]{1,0:T(8,128)S(1)} %collective-permute-done.13.p1.a1) | copy-start | bytes 1572868
  145.1 1.3 copy-start.2
  168.7 20.1 %all-to-all-start.5 = ((f32[4,64,1536]{2,1,0:T(8,128)}), f32[4,64,1536]{2,1,0:T(8,128)S(1)}, u32[]{:S(2)}, u32[]{:S(2)}) async-start(f32[4,64,1536]{2,1,0:T(8,128)} %get-tuple-element.47), calls=%async_computation.5 | async-start | bytes 3145728 | tf_op jit(solution)/shard_map/all_to_all | solution.py:354
  (6 other events, 4.7 us)

commit v5 on v4

--- a/solution.py
+++ b/solution.py
@@ -121,19 +121,29 @@
             ]
 
 
-def prepare(offsets, own, inverse, weights, prior, innovation, sites, crossed_out, y_out):
+def first_message(offsets, own, inverse, weights, prior, innovation, sites, y_out, c_out):
     rows, columns = own.shape
     matrix = own[...]
-    crossed_out[...] = bands(matrix, weights[...], lambda b: offsets[0, b])
     state = lax.broadcasted_iota(jnp.int32, (columns, sites.shape[1]), 0)
     matches = (state == sites[...]).astype(F32)
     pulled = vector_times(innovation[...], matches)
     filtered = prior[...] + vector_times(pulled, matrix)
     for i in range(SIDE):
         y_out[i, 0:rows, :] = inverse[...]
-        y_out[i, rows : 2 * rows, :] = matrix
-        y_out[i, 2 * rows :, :] = jnp.zeros((8, columns), F32)
-        y_out[i, 2 * rows : 2 * rows + 1, 0:rows] = filtered
+        y_out[i, rows:, :] = jnp.zeros((8, columns), F32)
+        y_out[i, rows : rows + 1, 0:rows] = filtered
+    c_out[0:rows, :] = matrix
+    c_out[rows:, :] = jnp.zeros((8, columns), F32)
+    c_out[rows : rows + NBAND, :] = weights[...]
+    lane = lax.broadcasted_iota(jnp.int32, (1, columns), 1)
+    held = jnp.zeros((1, columns), jnp.int32)
+    for b in range(NBAND):
+        held = jnp.where(lane == b, offsets[0, b], held)
+    c_out[rows + NBAND : rows + NBAND + 1, :] = held.astype(F32)
+
+
+def cross(offsets, own, weights, crossed_out):
+    crossed_out[...] = bands(own[...], weights[...], lambda b: offsets[0, b])
 
 
 def place_rows(pieces, at, out):
@@ -142,49 +152,41 @@
         out[pl.ds(pl.multiple_of(source * rows, rows), rows), :] = piece[...]
 
 
-def first_gain(where, y_in, x0, x1, x2, x3, gain_out, x_out, crossed):
+def pick_chunks(ref, at_x):
+    panel = ref.shape[0]
+    odd = lax.rem(at_x, 2)
+    base = lax.div(at_x, 2) * LANES
+    low = low_lanes(panel, LANES // 2)
+    parts = []
+    for i in range(SIDE):
+        part = ref[:, pl.ds(pl.multiple_of(i * panel + base, LANES), LANES)]
+        turn = odd if i % 2 == 0 else 1 - odd
+        parts.append(pltpu.roll(part, turn * (LANES // 2), 1))
+    return jnp.where(low, parts[0], parts[1]), jnp.where(low, parts[2], parts[3])
+
+
+def first_gain(where, y_in, x0, x1, x2, x3, gain_out, block_out, x_out, crossed):
     rows = x0.shape[0]
     panel = SIDE * rows
     place_rows((x0, x1, x2, x3), where[1], crossed)
     inverse = jnp.concatenate([y_in[i, 0:rows, :] for i in range(SIDE)], axis=0)
     gain = dot_t(crossed[...], inverse)
     gain_out[...] = gain
-    tail = jnp.concatenate(
-        [y_in[i, 2 * rows : 2 * rows + 1, 0:rows] for i in range(SIDE)], axis=1
-    )
+    tail = jnp.concatenate([y_in[i, rows : rows + 1, 0:rows] for i in range(SIDE)], axis=1)
     tail = jnp.broadcast_to(tail, (8, panel))
     for i in range(SIDE):
         x_out[i, 0:panel, :] = gain
         x_out[i, panel:, :] = tail
-
-
-def cut_blocks(where, y_in, x0, x1, x2, x3, out, crossed):
-    rows = x0.shape[0]
-    panel = SIDE * rows
-    place_rows((x0, x1, x2, x3), where[1], crossed)
-    at_y = pl.multiple_of(where[0] * panel, panel)
-    own = jnp.concatenate(
-        [y_in[i, rows : 2 * rows, pl.ds(at_y, panel)] for i in range(SIDE)], axis=0
-    )
-    out[0:panel, :] = own.T
-    odd = lax.rem(where[1], 2)
-    at_x = lax.div(where[1], 2) * LANES
-    low = low_lanes(panel, rows)
-    parts = []
-    for i in range(SIDE):
-        part = crossed[:, pl.ds(pl.multiple_of(i * panel + at_x, LANES), LANES)]
-        turn = odd if i % 2 == 0 else 1 - odd
-        parts.append(pltpu.roll(part, turn * rows, 1))
-    out[panel:, 0:LANES] = jnp.where(low, parts[0], parts[1])
-    out[panel:, LANES:] = jnp.where(low, parts[2], parts[3])
+    first, second = pick_chunks(crossed, where[1])
+    block_out[:, 0:LANES] = first
+    block_out[:, LANES:] = second
 
 
 def second_gain(
-    where, offsets, weights, gain, x_in, e0, e1, e2, e3, y_in,
-    gain_out, x_out, shift_out, c_out, high_out, low_out, tall,
+    where, offsets, weights, gain, x_in, e0, e1, e2, e3, u1, u2, u3, u4,
+    gain_out, x_out, shift_out, rows_out, high_out, low_out, tall,
 ):
     panel = gain.shape[0]
-    rows = panel // SIDE
     at_y = where[0]
     gain_wide = halves(wide(x_in, panel))
     high_out[...] = gain_wide[0]
@@ -202,45 +204,38 @@
     for i in range(SIDE):
         mine = mine + jnp.where(at_y == i, natural[0:1, i * panel : (i + 1) * panel], 0.0)
     shift_out[...] = jnp.broadcast_to(mine - row_times(forward[0:1], gain_wide), (8, panel))
-    for i in range(SIDE):
-        c_out[i * rows : (i + 1) * rows, :] = y_in[i, rows : 2 * rows, :]
-    c_out[panel : panel + NBAND, :] = weights[...]
-    c_out[panel + NBAND : panel + NBAND + 1, :] = filtered[0:1]
-    c_out[panel + NBAND + 1 : panel + NBAND + 2, :] = forward[0:1]
-    lane = lax.broadcasted_iota(jnp.int32, (1, c_out.shape[1]), 1)
-    held = jnp.zeros((1, c_out.shape[1]), jnp.int32)
-    for b in range(NBAND):
-        held = jnp.where(lane == b, offsets[0, b], held)
-    c_out[panel + NBAND + 2 : panel + NBAND + 3, :] = held.astype(F32)
-
-
-def later_inputs(offsets, c_in, rows_out, own_high, own_low, crossed_high, crossed_low):
-    panel = own_high.shape[0]
+    rows_out[0:4, :] = filtered[0:4]
+    rows_out[4:, :] = forward[0:4]
+
+
+def later_inputs(offsets, piece, own_high, own_low, crossed_high, crossed_low):
+    rows = own_high.shape[0]
     step = 16
-    weights = c_in[panel : panel + NBAND, :]
+    weights = piece[rows : rows + NBAND, :]
 
     def put(at, blocks, high_out, low_out):
         for i, block in enumerate(swap_tiles(blocks)):
             high, low = halves(block)
-            high_out[pl.ds(at, step), i * LANES : (i + 1) * LANES] = high
-            low_out[pl.ds(at, step), i * LANES : (i + 1) * LANES] = low
-
-    def one(index, carry):
-        at = pl.multiple_of(index * step, step)
-        blocks = tiles(c_in[pl.ds(at, step), :])
+            high_out[at : at + step, i * LANES : (i + 1) * LANES] = high
+            low_out[at : at + step, i * LANES : (i + 1) * LANES] = low
+
+    for at in range(0, rows, step):
+        blocks = tiles(piece[at : at + step, :])
         put(at, blocks, own_high, own_low)
         put(at, band_tiles(blocks, weights, lambda b: offsets[b]), crossed_high, crossed_low)
-        return carry
-
-    lax.fori_loop(0, panel // step, one, 0)
-    rows_out[...] = c_in[panel:, :]
 
 
 def first_spread(
-    where, wide_high, wide_low, gain_2_in, own_high, own_low, crossed_high, crossed_low,
-    later_rows, blocks, e0, e1, e2, e3, shift, gain_2, gain_2_later,
-    part_out, shift_out, pair_out, high_out, low_out, tall,
+    where, wide_high, wide_low, gain_2_in,
+    later_rows, block, own, e0, e1, e2, e3, shift, gain_2, gain_2_later,
+    h0, h1, h2, h3, l0, l1, l2, l3, g0, g1, g2, g3, k0, k1, k2, k3,
+    part_out, shift_out, pair_out, high_out, low_out,
+    tall, own_high, own_low, crossed_high, crossed_low,
 ):
+    place_rows((h0, h1, h2, h3), where[0], own_high)
+    place_rows((l0, l1, l2, l3), where[0], own_low)
+    place_rows((g0, g1, g2, g3), where[0], crossed_high)
+    place_rows((k0, k1, k2, k3), where[0], crossed_low)
     panel = e0.shape[0]
     at_y = where[0]
     pair_out[0:panel, :] = gain_2[...]
@@ -253,25 +248,29 @@
     turned = three(gain_wide, (own_high[...], own_low[...]), across) - three(
         gain_2_wide, (crossed_high[...], crossed_low[...]), across
     )
-    moved = row_times(later_rows[NBAND : NBAND + 1, :], gain_wide) - row_times(
-        later_rows[NBAND + 1 : NBAND + 2, :], gain_2_wide
+    moved = row_times(later_rows[0:1, :], gain_wide) - row_times(
+        later_rows[4:5, :], gain_2_wide
     )
     inside = where[2] == 1
     shift_out[...] = shift[...] + jnp.where(inside, moved, 0.0)
-    turned = halves(jnp.where(inside, turned, 0.0) - blocks[panel:, :])
+    turned = halves(jnp.where(inside, turned, 0.0) - block[...])
     place_tall((e0, e1, e2, e3), at_y, tall)
+    twice = jnp.concatenate(swap_tiles(tiles(jnp.concatenate([own[...]] * 2, axis=0))), axis=1)
+    mine = low_lanes(panel, LANES // 2) == (lax.rem(where[1], 2) == 0)
+    at_x = pl.multiple_of(lax.div(where[1], 2) * LANES, LANES)
     for i in range(SIDE):
         part_out[i] = three(halves(tall[i * panel : (i + 1) * panel, :]), turned, across)
-
-
-def join_spread(parts, blocks, shift, out):
+        turned_own = twice[:, i * panel : (i + 1) * panel].T
+        part_out[i, :, pl.ds(at_x, LANES)] += jnp.where(mine, turned_own, 0.0)
+
+
+def join_spread(parts, shift, out):
     panel = parts.shape[1]
-    total = (parts[0] + parts[1]) + (parts[2] + parts[3])
-    out[0:panel, :] = blocks[0:panel, :] + total.T
+    out[0:panel, :] = ((parts[0] + parts[1]) + (parts[2] + parts[3])).T
     out[panel:, :] = shift[...]
 
 
-def four_times(block, p1, p2, p3, out):
+def four_times(block, p1, p2, out):
     for i in range(SIDE):
         out[i] = block[...]
 
@@ -301,25 +300,31 @@
     gain_4 = jnp.where(inside, three(gain_2_wide, halves(later_tall[...]), along), gain_2[...])
     for i in range(SIDE):
         x_out[i, :, columns : columns + panel] = gain_4[i * rows : (i + 1) * rows]
-        x_out[i, :, columns + panel :] = spread[i * rows : (i + 1) * rows, :]
     for piece, source in sources(pieces, at_y):
         tall[pl.ds(pl.multiple_of(source * panel, panel), panel), :] = piece[0:panel, :]
     part = three(turned, halves(tall[...]), ((1,), (1,)))
     for i in range(SIDE):
         x_out[i, :, 0:columns] = part[i * rows : (i + 1) * rows]
+    odd = lax.rem(where[1], 2)
+    base = lax.div(where[1], 2) * LANES
+    mine = low_lanes(panel, LANES // 2) == (odd == 0)
+    for c in range(SIDE):
+        kept = spread[0:panel, (c // 2) * LANES : (c // 2 + 1) * LANES]
+        turn = odd if c % 2 == 0 else 1 - odd
+        kept = jnp.where(mine, pltpu.roll(kept, turn * (LANES // 2), 1), 0.0)
+        at = pl.multiple_of(c * panel + base, LANES)
+        for i in range(SIDE):
+            x_out[i, :, pl.ds(at, LANES)] += kept[i * rows : (i + 1) * rows]
 
 
 def finish(x_in, gain_out, spread_out):
-    rows, columns = gain_out.shape
-    panel = SIDE * rows
+    columns = gain_out.shape[1]
     gain_out[...] = swap_lanes(
-        jnp.concatenate([x_in[i, :, columns : columns + panel] for i in range(SIDE)], axis=1)
-    )
-    kept = swap_lanes(jnp.concatenate([x_in[i, :, columns + panel :] for i in range(SIDE)], axis=1))
-    total = (x_in[0, :, 0:columns] + x_in[1, :, 0:columns]) + (
+        jnp.concatenate([x_in[i, :, columns:] for i in range(SIDE)], axis=1)
+    )
+    spread_out[...] = (x_in[0, :, 0:columns] + x_in[1, :, 0:columns]) + (
         x_in[2, :, 0:columns] + x_in[3, :, 0:columns]
     )
-    spread_out[...] = total + kept
 
 
 WHOLE = pl.BlockSpec()
@@ -339,7 +344,7 @@
         out_shape=shapes,
         in_specs=[SMEM] * len(scalars) + [WHOLE] * len(arrays) + [UNREAD] * len(unread),
         out_specs=[WHOLE] * len(shapes),
-        scratch_shapes=[pltpu.VMEM(s, F32) for s in scratch],
+        scratch_shapes=[pltpu.VMEM(s[:2], *(s[2:] or (F32,))) for s in scratch],
         compiler_params=pltpu.CompilerParams(vmem_limit_bytes=24 * 2**20),
         cost_estimate=pl.CostEstimate(flops=flops, bytes_accessed=4 * size, transcendentals=0),
     )(*scalars, *arrays, *unread)
@@ -393,69 +398,72 @@
     )
     unit = 2 * panel * panel * columns
 
-    crossed, y_message = call(
-        prepare,
+    y_message, c_message = call(
+        first_message,
         (band_offset,),
         far(own, inverse, weights, prior_mean, innovation, seen_sites),
-        ((rows, columns), (SIDE, 2 * rows + 8, columns)),
+        ((SIDE, rows + 8, columns), (rows + 8, columns)),
     )
     y_in = swap(y_message, "y")
+    (crossed,) = call(cross, (band_offset,), far(own, weights), ((rows, columns),))
     crossed_pieces = ring(crossed, "x")
-    gain, x_message = call(
+    c_later = shifted(c_message, 1)
+    gain, crossed_block, x_message = call(
         first_gain,
         (where,),
         (y_in, *far(*crossed_pieces)),
-        ((panel, panel), (SIDE, panel + 8, panel)),
+        ((panel, panel), (panel, panel), (SIDE, panel + 8, panel)),
         ((panel, columns),),
         unit,
     )
     gain_in = swap(x_message, "x")
     later_pieces = ring_shifted(gain, 1)
-    (blocks,) = call(
-        cut_blocks, (where,), (y_in, *far(*crossed_pieces)), ((2 * panel, panel),), ((panel, columns),)
-    )
-    gain_2, x_message, shift, c_message, wide_high, wide_low = call(
+    gain_pieces = ring(gain, "y")
+    c_pieces = ring(c_later, "y")
+    next_offsets = c_later[rows + NBAND, 0:8].astype(jnp.int32)
+    gain_2, x_message, shift, rows_message, wide_high, wide_low = call(
         second_gain,
         (where, band_offset),
-        (*far(weights, gain), gain_in, *far(*later_pieces), y_in),
-        ((panel, panel), (SIDE, panel, panel), (8, panel), (panel + 8, columns)),
+        (*far(weights, gain), gain_in, *far(*later_pieces)),
+        ((panel, panel), (SIDE, panel, panel), (8, panel), (8, columns)),
         ((columns, panel),),
         unit,
+        unread=(*gain_pieces[1:], c_later),
         coarse=((panel, columns),) * 2,
     )
     gain_2_in = swap(x_message, "x")
-    gain_pieces = ring(gain, "y")
     gain_2_later = shifted(gain_2, 2)
-    c_in = shifted(c_message, 1)
-    next_offsets = c_in[panel + NBAND + 2, 0:8].astype(jnp.int32)
-    later_rows, *later_halves = call(
-        later_inputs, (next_offsets,), far(c_in), ((8, columns),), coarse=((panel, columns),) * 4
-    )
+    later_rows = shifted(rows_message, 1)
+    later_halves = [
+        call(later_inputs, (next_offsets,), far(piece), (), coarse=((rows, columns),) * 4)
+        for piece in c_pieces
+    ]
+    later_halves = [half for halves_of in zip(*later_halves) for half in halves_of]
     part, shift_2, gain_2_pair, wide_high, wide_low = call(
         first_spread,
         (where,),
         (
-            *far(wide_high, wide_low), gain_2_in, *far(*later_halves, later_rows, blocks),
-            *far(gain, *gain_pieces[1:], shift, gain_2, gain_2_later),
+            *far(wide_high, wide_low), gain_2_in, *far(later_rows, crossed_block),
+            *far(own, gain, *gain_pieces[1:], shift, gain_2, gain_2_later, *later_halves),
         ),
         ((SIDE, panel, panel), (8, panel), (2 * panel, panel)),
-        ((columns, panel),),
+        ((columns, panel),) + ((panel, columns, jnp.bfloat16),) * 4,
         3 * unit,
         coarse=((panel, columns),) * 2,
     )
     parts = swap(part, "x")
     gain_2_pieces = ring(gain_2_pair, "y")
-    (spread_2,) = call(join_spread, (), (parts, *far(blocks, shift_2)), ((panel + 8, panel),))
+    (spread_2,) = call(join_spread, (), (parts, *far(shift_2)), ((panel + 8, panel),))
     later = shifted(spread_2, 2)
     (y_message,) = call(
-        four_times, (), (later,), ((SIDE, panel + 8, panel),), unread=gain_2_pieces[1:]
+        four_times, (), (later,), ((SIDE, panel + 8, panel),), unread=gain_2_pieces[1:3]
     )
     y_in = swap(y_message, "y")
     x_message, shift_4 = call(
         second_spread,
         (where,),
         (*far(gain_2, wide_high, wide_low, spread_2), y_in, *far(*gain_2_pieces)),
-        ((SIDE, rows, columns + 2 * panel), (8, panel)),
+        ((SIDE, rows, columns + panel), (8, panel)),
         ((columns, panel), (columns, panel)),
         3 * unit,
     )

time: 191 us -> 207 us (1.084)
  the two profiles are of different devices: /device:TPU:384 before, /device:TPU:192 now
where the time goes in v5:
time: 207 us; the launch traced here: 205 us
  starting transfers between devices  86.9 us (42%)
  waiting for transfers between devices  71.9 us (35%)
  Pallas kernels  37.2 us (18%)
  local copies, waits for them, and re-layouts  8.34 us (4%)
    ppermute x12, starting transfers between devices, ring(): lax.ppermute(block, axis, [(i, (i + step) % SIDE) for i in range(SIDE)])  43.2 us
    ppermute x12, waiting for transfers between devices, ring(): lax.ppermute(block, axis, [(i, (i + step) % SIDE) for i in range(SIDE)])  38.5 us
    pallas_call x13, Pallas kernels, call(): pl.pallas_call(kernel, out_shape=shapes, in_specs=[SMEM] * len(scalars) +...  37.2 us
    all_to_all x6, starting transfers between devices, swap(): return lax.all_to_all(message, axis, 0, 0)  25.4 us
    all_to_all x6, waiting for transfers between devices, swap(): return lax.all_to_all(message, axis, 0, 0)  24.4 us
    ppermute x4, starting transfers between devices, ring_shifted(): pieces.append(lax.ppermute(block, ('tm', 'y'), route))  10.1 us
    ppermute x4, starting transfers between devices, shifted(): lax.ppermute(block, 'tm', [(i + distance, i) for i in range(count - dista...  8.21 us
    ppermute x4, waiting for transfers between devices, shifted(): lax.ppermute(block, 'tm', [(i + distance, i) for i in range(count - dista...  7.14 us
  transfers between devices with their start and end apart: 26, of which 12 were waited for; matrix products, arithmetic and copies ran while one was open for 1% of the time, Pallas kernels for 7%

profile of v5, /device:TPU:192, one launch (start us, length us, event | category | flops | bytes accessed | tf_op | source)
XLA Modules:
  0.0 205.5 jit_solution(7323802516075670973)
XLA Ops:
  2.6 2.9 %shard_map.94 = (f32[4,72,1024]{2,1,0:T(8,128)}, f32[72,1024]{1,0:T(8,128)}) custom-call(s32[1,5]{1,0:T(1,128)S(1)} %copy-done.6, f32[64,1024]{1,0:T(8,128)} %bitcast.13, f32[64,1024]{1,0:T(8,128)} %bitcast.19, f32[5,1024]{1,0:T(8,128)} %bitcast.16, f32[1,64]{1,0:T(1,128)} %prior.1, f32[1,128]{1,0:T(1,128)} %innovation.1, s32[1,128]{1,0:T(1,128)} %sites.1), custom_call_target="tpu_custom_call" | custom-call | bytes 2020608 | tf_op jit(solution)/shard_map/pallas_call | solution.py:342
  5.5 4.6 %all-to-all-start = ((f32[4,72,1024]{2,1,0:T(8,128)}), f32[4,72,1024]{2,1,0:T(8,128)S(1)}, u32[]{:S(2)}, u32[]{:S(2)}) async-start(f32[4,72,1024]{2,1,0:T(8,128)} %get-tuple-element.39), calls=%async_computation | async-start | bytes 2359296 | tf_op jit(solution)/shard_map/all_to_all | solution.py:359
  12.3 4.9 %collective-permute-start.2 = (f32[64,1024]{1,0:T(8,128)}, f32[64,1024]{1,0:T(8,128)S(1)}, u32[]{:S(2)}, u32[]{:S(2)}) collective-permute-start(f32[64,1024]{1,0:T(8,128)} %shard_map.95.x0), channel_id=1, source_target_pairs={{0,2},{1,3},{2,0},{3,1},{4,6},{5,7},{6,4},{7,5},{8,10},{9,11},{10,... | collective-permute-start | bytes 786440 | tf_op jit(solution)/shard_map/ppermute | solution.py:365
  17.2 3.0 %collective-permute-start.1 = (f32[64,1024]{1,0:T(8,128)}, f32[64,1024]{1,0:T(8,128)S(1)}, u32[]{:S(2)}, u32[]{:S(2)}) collective-permute-start(f32[64,1024]{1,0:T(8,128)} %shard_map.95.x0), channel_id=1, source_target_pairs={{0,3},{1,0},{2,1},{3,2},{4,7},{5,4},{6,5},{7,6},{8,11},{9,8},{10,9... | collective-permute-start | bytes 786440 | tf_op jit(solution)/shard_map/ppermute | solution.py:365
  20.3 2.8 %collective-permute-start = (f32[64,1024]{1,0:T(8,128)}, f32[64,1024]{1,0:T(8,128)S(1)}, u32[]{:S(2)}, u32[]{:S(2)}) collective-permute-start(f32[64,1024]{1,0:T(8,128)} %shard_map.95.x0), channel_id=1, source_target_pairs={{0,1},{1,2},{2,3},{3,0},{4,5},{5,6},{6,7},{7,4},{8,9},{9,10},{10,1... | collective-permute-start | bytes 786440 | tf_op jit(solution)/shard_map/ppermute | solution.py:365
  23.7 5.7 %collective-permute-done.1.x2 = f32[64,1024]{1,0:T(8,128)S(1)} collective-permute-done((f32[64,1024]{1,0:T(8,128)}, f32[64,1024]{1,0:T(8,128)S(1)}, u32[]{:S(2)}, u32[]{:S(2)}) %collective-permute-start.1) | collective-permute-done | bytes 262176 | tf_op jit(solution)/shard_map/ppermute | solution.py:365
  31.5 3.1 %shard_map.96 = (f32[256,256]{1,0:T(8,128)}, f32[256,256]{1,0:T(8,128)}, f32[4,264,256]{2,1,0:T(8,128)}) custom-call(s32[4]{0:T(128)S(1)} %pad_add_fusion.where, f32[4,72,1024]{2,1,0:T(8,128)S(1)} %all-to-all-done.y_in, f32[64,1024]{1,0:T(8,128)} %shard_map.95.x0, f32[64,1024]{1,0:T(8,128)} %copy-done.18, f32[64,1024]{1,0:T(8,128)} %copy-done.17, ...), custom_call_target="tpu_custom_call" | custom-call | flops 134217728 | bytes 3833856 | tf_op jit(solution)/shard_map/pallas_call | solution.py:342
  34.6 3.6 %all-to-all-start.1 = ((f32[4,264,256]{2,1,0:T(8,128)}), f32[4,264,256]{2,1,0:T(8,128)S(1)}, u32[]{:S(2)}, u32[]{:S(2)}) async-start(f32[4,264,256]{2,1,0:T(8,128)} %get-tuple-element.41), calls=%async_computation.1 | async-start | bytes 2162688 | tf_op jit(solution)/shard_map/all_to_all | solution.py:359
  40.2 5.2 %collective-permute-start.9 = (f32[256,256]{1,0:T(8,128)S(1)}, f32[256,256]{1,0:T(8,128)S(1)}, u32[]{:S(2)}, u32[]{:S(2)}) collective-permute-start(f32[256,256]{1,0:T(8,128)S(1)} %copy-done.9), channel_id=1, source_target_pairs={{0,8},{4,12},{8,0},{12,4},{1,9},{5,13},{9,1},{13,5},{2,10},{6,14},... | collective-permute-start | bytes 786440 | tf_op jit(solution)/shard_map/ppermute | solution.py:365
  45.4 3.1 %collective-permute-start.8 = (f32[256,256]{1,0:T(8,128)S(1)}, f32[256,256]{1,0:T(8,128)S(1)}, u32[]{:S(2)}, u32[]{:S(2)}) collective-permute-start(f32[256,256]{1,0:T(8,128)S(1)} %copy-done.9), channel_id=1, source_target_pairs={{0,12},{4,0},{8,4},{12,8},{1,13},{5,1},{9,5},{13,9},{2,14},{6,2},{... | collective-permute-start | bytes 786440 | tf_op jit(solution)/shard_map/ppermute | solution.py:365
  48.5 2.8 %collective-permute-start.7 = (f32[256,256]{1,0:T(8,128)S(1)}, f32[256,256]{1,0:T(8,128)S(1)}, u32[]{:S(2)}, u32[]{:S(2)}) collective-permute-start(f32[256,256]{1,0:T(8,128)S(1)} %copy-done.9), channel_id=1, source_target_pairs={{0,4},{4,8},{8,12},{12,0},{1,5},{5,9},{9,13},{13,1},{2,6},{6,10},{... | collective-permute-start | bytes 786440 | tf_op jit(solution)/shard_map/ppermute | solution.py:365
  53.2 4.4 %collective-permute-start.5 = (f32[256,256]{1,0:T(8,128)S(1)}, f32[256,256]{1,0:T(8,128)S(1)}, u32[]{:S(2)}, u32[]{:S(2)}) collective-permute-start(f32[256,256]{1,0:T(8,128)S(1)} %copy-done.9), channel_id=1, source_target_pairs={{16,12},{20,0},{24,4},{28,8},{32,28},{36,16},{40,20},{44,24},{48,4... | collective-permute-start | bytes 786440 | tf_op jit(solution)/shard_map/ppermute | solution.py:378
  59.6 4.7 %collective-permute-done.8.u2.e2 = f32[256,256]{1,0:T(8,128)S(1)} collective-permute-done((f32[256,256]{1,0:T(8,128)S(1)}, f32[256,256]{1,0:T(8,128)S(1)}, u32[]{:S(2)}, u32[]{:S(2)}) %collective-permute-start.8) | collective-permute-done | bytes 262176 | tf_op jit(solution)/shard_map/ppermute | solution.py:365
  66.2 3.0 %collective-permute-done.7.u1.e1 = f32[256,256]{1,0:T(8,128)S(1)} collective-permute-done((f32[256,256]{1,0:T(8,128)S(1)}, f32[256,256]{1,0:T(8,128)S(1)}, u32[]{:S(2)}, u32[]{:S(2)}) %collective-permute-start.7) | collective-permute-done | bytes 262176 | tf_op jit(solution)/shard_map/ppermute | solution.py:365
  71.7 3.5 %shard_map.97 = (f32[256,256]{1,0:T(8,128)}, f32[4,256,256]{2,1,0:T(8,128)}, f32[8,256]{1,0:T(8,128)}, f32[8,1024]{1,0:T(8,128)}, bf16[256,1024]{1,0:T(8,128)(2,1)}, /*index=5*/bf16[256,1024]{1,0:T(8,128)(2,1)}) custom-call(s32[4]{0:T(128)S(1)} %pad_add_fusion.where, s32[1,5]{1,0:T(1,128)S(1)} %copy-done.7, f32[5,1024]{1,0:T(8,128)} %bitcast.18, ...), custom_call_target="tpu_custom_call" | custom-call | flops 134217728 | bytes 3764224 | tf_op jit(solution)/shard_map/pallas_call | solution.py:342
  75.2 4.9 %all-to-all-start.2 = ((f32[4,256,256]{2,1,0:T(8,128)}), f32[4,256,256]{2,1,0:T(8,128)S(1)}, u32[]{:S(2)}, u32[]{:S(2)}) async-start(f32[4,256,256]{2,1,0:T(8,128)} %get-tuple-element.46), calls=%async_computation.2 | async-start | bytes 2097152 | tf_op jit(solution)/shard_map/all_to_all | solution.py:359
  80.1 3.4 %collective-permute-start.15 = (f32[72,1024]{1,0:T(8,128)S(1)}, f32[72,1024]{1,0:T(8,128)S(1)}, u32[]{:S(2)}, u32[]{:S(2)}) collective-permute-start(f32[72,1024]{1,0:T(8,128)S(1)} %collective-permute-done.10.u4.piece), channel_id=1, source_target_pairs={{0,8},{4,12},{8,0},{12,4},{1,9},{5,13},{9,1},{13,5},{2,10},{6,14},... | collective-permute-start | bytes 884744 | tf_op jit(solution)/shard_map/ppermute | solution.py:365
  83.5 3.2 %collective-permute-start.14 = (f32[72,1024]{1,0:T(8,128)S(1)}, f32[72,1024]{1,0:T(8,128)S(1)}, u32[]{:S(2)}, u32[]{:S(2)}) collective-permute-start(f32[72,1024]{1,0:T(8,128)S(1)} %collective-permute-done.10.u4.piece), channel_id=1, source_target_pairs={{0,12},{4,0},{8,4},{12,8},{1,13},{5,1},{9,5},{13,9},{2,14},{6,2},{... | collective-permute-start | bytes 884744 | tf_op jit(solution)/shard_map/ppermute | solution.py:365
  93.7 2.7 %shard_map.98 = (bf16[64,1024]{1,0:T(8,128)(2,1)}, bf16[64,1024]{1,0:T(8,128)(2,1)}, bf16[64,1024]{1,0:T(8,128)(2,1)}, bf16[64,1024]{1,0:T(8,128)(2,1)}) custom-call(s32[8]{0:T(128)S(1)} %fusion.offsets, f32[72,1024]{1,0:T(8,128)} %copy-done.2), custom_call_target="tpu_custom_call" | custom-call | bytes 294912 | tf_op jit(solution)/shard_map/pallas_call | solution.py:342
  97.1 2.7 %shard_map.101 = (bf16[64,1024]{1,0:T(8,128)(2,1)}, bf16[64,1024]{1,0:T(8,128)(2,1)}, bf16[64,1024]{1,0:T(8,128)(2,1)}, bf16[64,1024]{1,0:T(8,128)(2,1)}) custom-call(s32[8]{0:T(128)S(1)} %fusion.offsets, f32[72,1024]{1,0:T(8,128)} %copy-done.14), custom_call_target="tpu_custom_call" | custom-call | bytes 294912 | tf_op jit(solution)/shard_map/pallas_call | solution.py:342
  103.8 2.7 %shard_map.99 = (bf16[64,1024]{1,0:T(8,128)(2,1)}, bf16[64,1024]{1,0:T(8,128)(2,1)}, bf16[64,1024]{1,0:T(8,128)(2,1)}, bf16[64,1024]{1,0:T(8,128)(2,1)}) custom-call(s32[8]{0:T(128)S(1)} %fusion.offsets, f32[72,1024]{1,0:T(8,128)} %copy-done.12), custom_call_target="tpu_custom_call" | custom-call | bytes 294912 | tf_op jit(solution)/shard_map/pallas_call | solution.py:342
  107.2 6.2 %shard_map.102 = (f32[4,256,256]{2,1,0:T(8,128)}, f32[8,256]{1,0:T(8,128)}, f32[512,256]{1,0:T(8,128)}, bf16[256,1024]{1,0:T(8,128)(2,1)}, bf16[256,1024]{1,0:T(8,128)(2,1)}) custom-call(s32[4]{0:T(128)S(1)} %pad_add_fusion.where, bf16[256,1024]{1,0:T(8,128)(2,1)} %get-tuple-element.44.wide_high, bf16[256,1024]{1,0:T(8,128)(2,1)} %get-tuple-element.45.wide_low, ...), custom_call_target="tpu_custom_call" | custom-call | flops 402653184 | bytes 11059200 | tf_op jit(solution)/shard_map/pallas_call | solution.py:342
  113.4 4.7 %all-to-all-start.3 = ((f32[4,256,256]{2,1,0:T(8,128)}), f32[4,256,256]{2,1,0:T(8,128)S(1)}, u32[]{:S(2)}, u32[]{:S(2)}) async-start(f32[4,256,256]{2,1,0:T(8,128)} %get-tuple-element.68), calls=%async_computation.3 | async-start | bytes 2097152 | tf_op jit(solution)/shard_map/all_to_all | solution.py:359
  118.1 4.8 %collective-permute-start.18 = (f32[512,256]{1,0:T(8,128)S(1)}, f32[512,256]{1,0:T(8,128)S(1)}, u32[]{:S(2)}, u32[]{:S(2)}) collective-permute-start(f32[512,256]{1,0:T(8,128)S(1)} %copy-done.10), channel_id=1, source_target_pairs={{0,12},{4,0},{8,4},{12,8},{1,13},{5,1},{9,5},{13,9},{2,14},{6,2},{... | collective-permute-start | bytes 1572872 | tf_op jit(solution)/shard_map/ppermute | solution.py:365
  124.9 8.9 %all-to-all-done.3.parts = f32[4,256,256]{2,1,0:T(8,128)S(1)} async-done(((f32[4,256,256]{2,1,0:T(8,128)}), f32[4,256,256]{2,1,0:T(8,128)S(1)}, u32[]{:S(2)}, u32[]{:S(2)}) %all-to-all-start.3) | async-done | bytes 1048608 | tf_op jit(solution)/shard_map/all_to_all | solution.py:359
  139.4 7.1 %collective-permute-done.16.block = f32[264,256]{1,0:T(8,128)S(1)} collective-permute-done((f32[264,256]{1,0:T(8,128)}, f32[264,256]{1,0:T(8,128)S(1)}, u32[]{:S(2)}, u32[]{:S(2)}) %collective-permute-start.16) | collective-permute-done | bytes 270368 | tf_op jit(solution)/shard_map/ppermute | solution.py:355
  147.7 4.1 %all-to-all-start.4 = ((f32[4,264,256]{2,1,0:T(8,128)}), f32[4,264,256]{2,1,0:T(8,128)S(1)}, u32[]{:S(2)}, u32[]{:S(2)}) async-start(f32[4,264,256]{2,1,0:T(8,128)} %shard_map.104), calls=%async_computation.4 | async-start | bytes 2162688 | tf_op jit(solution)/shard_map/all_to_all | solution.py:359
  151.7 5.4 %collective-permute-start.19 = (f32[512,256]{1,0:T(8,128)S(1)}, f32[512,256]{1,0:T(8,128)S(1)}, u32[]{:S(2)}, u32[]{:S(2)}) collective-permute-start(f32[512,256]{1,0:T(8,128)S(1)} %copy-done.10), channel_id=1, source_target_pairs={{0,8},{4,12},{8,0},{12,4},{1,9},{5,13},{9,1},{13,5},{2,10},{6,14},... | collective-permute-start | bytes 1572872 | tf_op jit(solution)/shard_map/ppermute | solution.py:365
  157.2 21.1 %collective-permute-done.19.a3 = f32[512,256]{1,0:T(8,128)S(1)} collective-permute-done((f32[512,256]{1,0:T(8,128)S(1)}, f32[512,256]{1,0:T(8,128)S(1)}, u32[]{:S(2)}, u32[]{:S(2)}) %collective-permute-start.19) | collective-permute-done | bytes 524320 | tf_op jit(solution)/shard_map/ppermute | solution.py:365
  179.1 5.1 %shard_map.105 = (f32[4,64,1280]{2,1,0:T(8,128)}, f32[8,256]{1,0:T(8,128)}) custom-call(s32[4]{0:T(128)S(1)} %pad_add_fusion.where, f32[256,256]{1,0:T(8,128)} %get-tuple-element.43.gain_2, bf16[256,1024]{1,0:T(8,128)(2,1)} %get-tuple-element.66.wide_high, bf16[256,1024]{1,0:T(8,128)(2,1)} %get-tuple-element.67.wide_low, f32[264,256]{1,0:T(8,128)} %shard_map.103.spread, ...), custom_call_target="tpu_custom_call" | custom-call | flops 402653184 | bytes 7127040 | tf_op jit(solution)/shard_map/pallas_call | solution.py:342
  184.2 3.5 %all-to-all-start.5 = ((f32[4,64,1280]{2,1,0:T(8,128)}), f32[4,64,1280]{2,1,0:T(8,128)S(1)}, u32[]{:S(2)}, u32[]{:S(2)}) async-start(f32[4,64,1280]{2,1,0:T(8,128)} %get-tuple-element.71), calls=%async_computation.5 | async-start | bytes 2621440 | tf_op jit(solution)/shard_map/all_to_all | solution.py:359
  189.0 15.5 %all-to-all-done.5.x_in = f32[4,64,1280]{2,1,0:T(8,128)S(1)} async-done(((f32[4,64,1280]{2,1,0:T(8,128)}), f32[4,64,1280]{2,1,0:T(8,128)S(1)}, u32[]{:S(2)}, u32[]{:S(2)}) %all-to-all-start.5) | async-done | bytes 1310752 | tf_op jit(solution)/shard_map/all_to_all | solution.py:359
  (88 shorter events, 41.2 us)
Async XLA Ops:
  5.5 25.3 %all-to-all-start = ((f32[4,72,1024]{2,1,0:T(8,128)}), f32[4,72,1024]{2,1,0:T(8,128)S(1)}, u32[]{:S(2)}, u32[]{:S(2)}) async-start(f32[4,72,1024]{2,1,0:T(8,128)} %get-tuple-element.39), calls=%async_computation | async-start | bytes 2359296 | tf_op jit(solution)/shard_map/all_to_all | solution.py:359
  12.3 11.4 %collective-permute-start.2 = (f32[64,1024]{1,0:T(8,128)}, f32[64,1024]{1,0:T(8,128)S(1)}, u32[]{:S(2)}, u32[]{:S(2)}) collective-permute-start(f32[64,1024]{1,0:T(8,128)} %shard_map.95.x0), channel_id=1, source_target_pairs={{0,2},{1,3},{2,0},{3,1},{4,6},{5,7},{6,4},{7,5},{8,10},{9,11},{10,... | collective-permute-start | bytes 786440 | tf_op jit(solution)/shard_map/ppermute | solution.py:365
  17.2 12.1 %collective-permute-start.1 = (f32[64,1024]{1,0:T(8,128)}, f32[64,1024]{1,0:T(8,128)S(1)}, u32[]{:S(2)}, u32[]{:S(2)}) collective-permute-start(f32[64,1024]{1,0:T(8,128)} %shard_map.95.x0), channel_id=1, source_target_pairs={{0,3},{1,0},{2,1},{3,2},{4,7},{5,4},{6,5},{7,6},{8,11},{9,8},{10,9... | collective-permute-start | bytes 786440 | tf_op jit(solution)/shard_map/ppermute | solution.py:365
  20.3 10.5 %collective-permute-start = (f32[64,1024]{1,0:T(8,128)}, f32[64,1024]{1,0:T(8,128)S(1)}, u32[]{:S(2)}, u32[]{:S(2)}) collective-permute-start(f32[64,1024]{1,0:T(8,128)} %shard_map.95.x0), channel_id=1, source_target_pairs={{0,1},{1,2},{2,3},{3,0},{4,5},{5,6},{6,7},{7,4},{8,9},{9,10},{10,1... | collective-permute-start | bytes 786440 | tf_op jit(solution)/shard_map/ppermute | solution.py:365
  34.6 36.3 %all-to-all-start.1 = ((f32[4,264,256]{2,1,0:T(8,128)}), f32[4,264,256]{2,1,0:T(8,128)S(1)}, u32[]{:S(2)}, u32[]{:S(2)}) async-start(f32[4,264,256]{2,1,0:T(8,128)} %get-tuple-element.41), calls=%async_computation.1 | async-start | bytes 2162688 | tf_op jit(solution)/shard_map/all_to_all | solution.py:359
  38.3 14.9 %collective-permute-start.10 = (f32[72,1024]{1,0:T(8,128)S(1)}, f32[72,1024]{1,0:T(8,128)S(1)}, u32[]{:S(2)}, u32[]{:S(2)}) collective-permute-start(f32[72,1024]{1,0:T(8,128)S(1)} %copy-done.23), channel_id=1, source_target_pairs={{16,0},{32,16},{48,32},{64,48},{80,64},{96,80},{112,96},{128,112},... | collective-permute-start | bytes 884744 | tf_op jit(solution)/shard_map/ppermute | solution.py:355
  40.2 17.4 %collective-permute-start.9 = (f32[256,256]{1,0:T(8,128)S(1)}, f32[256,256]{1,0:T(8,128)S(1)}, u32[]{:S(2)}, u32[]{:S(2)}) collective-permute-start(f32[256,256]{1,0:T(8,128)S(1)} %copy-done.9), channel_id=1, source_target_pairs={{0,8},{4,12},{8,0},{12,4},{1,9},{5,13},{9,1},{13,5},{2,10},{6,14},... | collective-permute-start | bytes 786440 | tf_op jit(solution)/shard_map/ppermute | solution.py:365
  45.4 18.9 %collective-permute-start.8 = (f32[256,256]{1,0:T(8,128)S(1)}, f32[256,256]{1,0:T(8,128)S(1)}, u32[]{:S(2)}, u32[]{:S(2)}) collective-permute-start(f32[256,256]{1,0:T(8,128)S(1)} %copy-done.9), channel_id=1, source_target_pairs={{0,12},{4,0},{8,4},{12,8},{1,13},{5,1},{9,5},{13,9},{2,14},{6,2},{... | collective-permute-start | bytes 786440 | tf_op jit(solution)/shard_map/ppermute | solution.py:365
  48.5 20.7 %collective-permute-start.7 = (f32[256,256]{1,0:T(8,128)S(1)}, f32[256,256]{1,0:T(8,128)S(1)}, u32[]{:S(2)}, u32[]{:S(2)}) collective-permute-start(f32[256,256]{1,0:T(8,128)S(1)} %copy-done.9), channel_id=1, source_target_pairs={{0,4},{4,8},{8,12},{12,0},{1,5},{5,9},{9,13},{13,1},{2,6},{6,10},{... | collective-permute-start | bytes 786440 | tf_op jit(solution)/shard_map/ppermute | solution.py:365
  51.3 17.9 %collective-permute-start.6 = (f32[256,256]{1,0:T(8,128)S(1)}, f32[256,256]{1,0:T(8,128)S(1)}, u32[]{:S(2)}, u32[]{:S(2)}) collective-permute-start(f32[256,256]{1,0:T(8,128)S(1)} %copy-done.9), channel_id=1, source_target_pairs={{16,8},{20,12},{24,0},{28,4},{32,24},{36,28},{40,16},{44,20},{48,4... | collective-permute-start | bytes 786440 | tf_op jit(solution)/shard_map/ppermute | solution.py:378
  53.2 40.5 %copy-start.2 = (f32[72,1024]{1,0:T(8,128)}, f32[72,1024]{1,0:T(8,128)S(1)}, u32[]{:S(2)}) copy-start(f32[72,1024]{1,0:T(8,128)S(1)} %collective-permute-done.10.u4.piece) | copy-start | bytes 884740
  53.2 16.3 %collective-permute-start.5 = (f32[256,256]{1,0:T(8,128)S(1)}, f32[256,256]{1,0:T(8,128)S(1)}, u32[]{:S(2)}, u32[]{:S(2)}) collective-permute-start(f32[256,256]{1,0:T(8,128)S(1)} %copy-done.9), channel_id=1, source_target_pairs={{16,12},{20,0},{24,4},{28,8},{32,28},{36,16},{40,20},{44,24},{48,4... | collective-permute-start | bytes 786440 | tf_op jit(solution)/shard_map/ppermute | solution.py:378
  57.6 17.6 %copy-start.3 = (f32[256,256]{1,0:T(8,128)}, f32[256,256]{1,0:T(8,128)S(1)}, u32[]{:S(2)}) copy-start(f32[256,256]{1,0:T(8,128)S(1)} %collective-permute-done.9.u3.e3) | copy-start | bytes 786436
  57.6 13.3 %collective-permute-start.4 = (f32[256,256]{1,0:T(8,128)S(1)}, f32[256,256]{1,0:T(8,128)S(1)}, u32[]{:S(2)}, u32[]{:S(2)}) collective-permute-start(f32[256,256]{1,0:T(8,128)S(1)} %copy-done.9), channel_id=1, source_target_pairs={{16,4},{20,8},{24,12},{28,0},{32,20},{36,24},{40,28},{44,16},{48,3... | collective-permute-start | bytes 786440 | tf_op jit(solution)/shard_map/ppermute | solution.py:378
  64.3 10.9 %copy-start.4 = (f32[256,256]{1,0:T(8,128)}, f32[256,256]{1,0:T(8,128)S(1)}, u32[]{:S(2)}) copy-start(f32[256,256]{1,0:T(8,128)S(1)} %collective-permute-done.8.u2.e2) | copy-start | bytes 786436
  64.3 6.7 %collective-permute-start.3 = (f32[256,256]{1,0:T(8,128)S(1)}, f32[256,256]{1,0:T(8,128)}, u32[]{:S(2)}, u32[]{:S(2)}) collective-permute-start(f32[256,256]{1,0:T(8,128)S(1)} %copy-done.9), channel_id=1, source_target_pairs={{16,0},{20,4},{24,8},{28,12},{32,16},{36,20},{40,24},{44,28},{48,3... | collective-permute-start | bytes 786440 | tf_op jit(solution)/shard_map/ppermute | solution.py:378
  75.2 14.1 %copy-start.8 = (f32[256,256]{1,0:T(8,128)S(1)}, f32[256,256]{1,0:T(8,128)}, u32[]{:S(2)}) copy-start(f32[256,256]{1,0:T(8,128)} %get-tuple-element.43.gain_2) | copy-start | bytes 786436
  75.2 16.2 %copy-start.24 = (f32[8,1024]{1,0:T(8,128)S(1)}, f32[8,1024]{1,0:T(8,128)}, u32[]{:S(2)}) copy-start(f32[8,1024]{1,0:T(8,128)} %get-tuple-element.47) | copy-start | bytes 98308
  75.2 31.3 %all-to-all-start.2 = ((f32[4,256,256]{2,1,0:T(8,128)}), f32[4,256,256]{2,1,0:T(8,128)S(1)}, u32[]{:S(2)}, u32[]{:S(2)}) async-start(f32[4,256,256]{2,1,0:T(8,128)} %get-tuple-element.46), calls=%async_computation.2 | async-start | bytes 2097152 | tf_op jit(solution)/shard_map/all_to_all | solution.py:359
  80.1 16.3 %collective-permute-start.15 = (f32[72,1024]{1,0:T(8,128)S(1)}, f32[72,1024]{1,0:T(8,128)S(1)}, u32[]{:S(2)}, u32[]{:S(2)}) collective-permute-start(f32[72,1024]{1,0:T(8,128)S(1)} %collective-permute-done.10.u4.piece), channel_id=1, source_target_pairs={{0,8},{4,12},{8,0},{12,4},{1,9},{5,13},{9,1},{13,5},{2,10},{6,14},... | collective-permute-start | bytes 884744 | tf_op jit(solution)/shard_map/ppermute | solution.py:365
  83.5 16.3 %collective-permute-start.14 = (f32[72,1024]{1,0:T(8,128)S(1)}, f32[72,1024]{1,0:T(8,128)S(1)}, u32[]{:S(2)}, u32[]{:S(2)}) collective-permute-start(f32[72,1024]{1,0:T(8,128)S(1)} %collective-permute-done.10.u4.piece), channel_id=1, source_target_pairs={{0,12},{4,0},{8,4},{12,8},{1,13},{5,1},{9,5},{13,9},{2,14},{6,2},{... | collective-permute-start | bytes 884744 | tf_op jit(solution)/shard_map/ppermute | solution.py:365
  86.7 16.4 %collective-permute-start.13 = (f32[72,1024]{1,0:T(8,128)S(1)}, f32[72,1024]{1,0:T(8,128)S(1)}, u32[]{:S(2)}, u32[]{:S(2)}) collective-permute-start(f32[72,1024]{1,0:T(8,128)S(1)} %collective-permute-done.10.u4.piece), channel_id=1, source_target_pairs={{0,4},{4,8},{8,12},{12,0},{1,5},{5,9},{9,13},{13,1},{2,6},{6,10},{... | collective-permute-start | bytes 884744 | tf_op jit(solution)/shard_map/ppermute | solution.py:365
  89.4 17.1 %collective-permute-start.12 = (f32[256,256]{1,0:T(8,128)S(1)}, f32[256,256]{1,0:T(8,128)S(1)}, u32[]{:S(2)}, u32[]{:S(2)}) collective-permute-start(f32[256,256]{1,0:T(8,128)S(1)} %copy-done.8), channel_id=1, source_target_pairs={{32,0},{48,16},{64,32},{80,48},{96,64},{112,80},{128,96},{144,112}... | collective-permute-start | bytes 786440 | tf_op jit(solution)/shard_map/ppermute | solution.py:355
  91.4 15.1 %collective-permute-start.11 = (f32[8,1024]{1,0:T(8,128)S(1)}, f32[8,1024]{1,0:T(8,128)S(1)}, u32[]{:S(2)}, u32[]{:S(2)}) collective-permute-start(f32[8,1024]{1,0:T(8,128)S(1)} %copy-done.24), channel_id=1, source_target_pairs={{16,0},{32,16},{48,32},{64,48},{80,64},{96,80},{112,96},{128,112},... | collective-permute-start | bytes 98312 | tf_op jit(solution)/shard_map/ppermute | solution.py:355
  113.4 20.3 %all-to-all-start.3 = ((f32[4,256,256]{2,1,0:T(8,128)}), f32[4,256,256]{2,1,0:T(8,128)S(1)}, u32[]{:S(2)}, u32[]{:S(2)}) async-start(f32[4,256,256]{2,1,0:T(8,128)} %get-tuple-element.68), calls=%async_computation.3 | async-start | bytes 2097152 | tf_op jit(solution)/shard_map/all_to_all | solution.py:359
  118.1 19.2 %collective-permute-start.18 = (f32[512,256]{1,0:T(8,128)S(1)}, f32[512,256]{1,0:T(8,128)S(1)}, u32[]{:S(2)}, u32[]{:S(2)}) collective-permute-start(f32[512,256]{1,0:T(8,128)S(1)} %copy-done.10), channel_id=1, source_target_pairs={{0,12},{4,0},{8,4},{12,8},{1,13},{5,1},{9,5},{13,9},{2,14},{6,2},{... | collective-permute-start | bytes 1572872 | tf_op jit(solution)/shard_map/ppermute | solution.py:365
  122.9 16.5 %collective-permute-start.17 = (f32[512,256]{1,0:T(8,128)S(1)}, f32[512,256]{1,0:T(8,128)S(1)}, u32[]{:S(2)}, u32[]{:S(2)}) collective-permute-start(f32[512,256]{1,0:T(8,128)S(1)} %copy-done.10), channel_id=1, source_target_pairs={{0,4},{4,8},{8,12},{12,0},{1,5},{5,9},{9,13},{13,1},{2,6},{6,10},{... | collective-permute-start | bytes 1572872 | tf_op jit(solution)/shard_map/ppermute | solution.py:365
  135.3 11.2 %collective-permute-start.16 = (f32[264,256]{1,0:T(8,128)}, f32[264,256]{1,0:T(8,128)S(1)}, u32[]{:S(2)}, u32[]{:S(2)}) collective-permute-start(f32[264,256]{1,0:T(8,128)} %shard_map.103.spread), channel_id=1, source_target_pairs={{32,0},{48,16},{64,32},{80,48},{96,64},{112,80},{128,96},{144,112}... | collective-permute-start | bytes 811016 | tf_op jit(solution)/shard_map/ppermute | solution.py:355
  137.3 10.3 %copy-start = (f32[512,256]{1,0:T(8,128)}, f32[512,256]{1,0:T(8,128)S(1)}, u32[]{:S(2)}) copy-start(f32[512,256]{1,0:T(8,128)S(1)} %collective-permute-done.18.p2.a2) | copy-start | bytes 1572868
  147.7 30.6 %all-to-all-start.4 = ((f32[4,264,256]{2,1,0:T(8,128)}), f32[4,264,256]{2,1,0:T(8,128)S(1)}, u32[]{:S(2)}, u32[]{:S(2)}) async-start(f32[4,264,256]{2,1,0:T(8,128)} %shard_map.104), calls=%async_computation.4 | async-start | bytes 2162688 | tf_op jit(solution)/shard_map/all_to_all | solution.py:359
  151.7 26.5 %collective-permute-start.19 = (f32[512,256]{1,0:T(8,128)S(1)}, f32[512,256]{1,0:T(8,128)S(1)}, u32[]{:S(2)}, u32[]{:S(2)}) collective-permute-start(f32[512,256]{1,0:T(8,128)S(1)} %copy-done.10), channel_id=1, source_target_pairs={{0,8},{4,12},{8,0},{12,4},{1,9},{5,13},{9,1},{13,5},{2,10},{6,14},... | collective-permute-start | bytes 1572872 | tf_op jit(solution)/shard_map/ppermute | solution.py:365
  184.2 20.3 %all-to-all-start.5 = ((f32[4,64,1280]{2,1,0:T(8,128)}), f32[4,64,1280]{2,1,0:T(8,128)S(1)}, u32[]{:S(2)}, u32[]{:S(2)}) async-start(f32[4,64,1280]{2,1,0:T(8,128)} %get-tuple-element.71), calls=%async_computation.5 | async-start | bytes 2621440 | tf_op jit(solution)/shard_map/all_to_all | solution.py:359
  (19 other events, 51.0 us)

commit v6 on v5

--- a/solution.py
+++ b/solution.py
@@ -121,29 +121,19 @@
             ]
 
 
-def first_message(offsets, own, inverse, weights, prior, innovation, sites, y_out, c_out):
+def prepare(offsets, own, inverse, weights, prior, innovation, sites, crossed_out, y_out):
     rows, columns = own.shape
     matrix = own[...]
+    crossed_out[...] = bands(matrix, weights[...], lambda b: offsets[0, b])
     state = lax.broadcasted_iota(jnp.int32, (columns, sites.shape[1]), 0)
     matches = (state == sites[...]).astype(F32)
     pulled = vector_times(innovation[...], matches)
     filtered = prior[...] + vector_times(pulled, matrix)
     for i in range(SIDE):
         y_out[i, 0:rows, :] = inverse[...]
-        y_out[i, rows:, :] = jnp.zeros((8, columns), F32)
-        y_out[i, rows : rows + 1, 0:rows] = filtered
-    c_out[0:rows, :] = matrix
-    c_out[rows:, :] = jnp.zeros((8, columns), F32)
-    c_out[rows : rows + NBAND, :] = weights[...]
-    lane = lax.broadcasted_iota(jnp.int32, (1, columns), 1)
-    held = jnp.zeros((1, columns), jnp.int32)
-    for b in range(NBAND):
-        held = jnp.where(lane == b, offsets[0, b], held)
-    c_out[rows + NBAND : rows + NBAND + 1, :] = held.astype(F32)
-
-
-def cross(offsets, own, weights, crossed_out):
-    crossed_out[...] = bands(own[...], weights[...], lambda b: offsets[0, b])
+        y_out[i, rows : 2 * rows, :] = matrix
+        y_out[i, 2 * rows :, :] = jnp.zeros((8, columns), F32)
+        y_out[i, 2 * rows : 2 * rows + 1, 0:rows] = filtered
 
 
 def place_rows(pieces, at, out):
@@ -165,14 +155,18 @@
     return jnp.where(low, parts[0], parts[1]), jnp.where(low, parts[2], parts[3])
 
 
-def first_gain(where, y_in, x0, x1, x2, x3, gain_out, block_out, x_out, crossed):
+def first_gain(
+    where, offsets, y_in, x0, x1, x2, x3, weights, gain_out, block_out, c_out, x_out, crossed
+):
     rows = x0.shape[0]
     panel = SIDE * rows
     place_rows((x0, x1, x2, x3), where[1], crossed)
     inverse = jnp.concatenate([y_in[i, 0:rows, :] for i in range(SIDE)], axis=0)
     gain = dot_t(crossed[...], inverse)
     gain_out[...] = gain
-    tail = jnp.concatenate([y_in[i, rows : rows + 1, 0:rows] for i in range(SIDE)], axis=1)
+    tail = jnp.concatenate(
+        [y_in[i, 2 * rows : 2 * rows + 1, 0:rows] for i in range(SIDE)], axis=1
+    )
     tail = jnp.broadcast_to(tail, (8, panel))
     for i in range(SIDE):
         x_out[i, 0:panel, :] = gain
@@ -180,10 +174,18 @@
     first, second = pick_chunks(crossed, where[1])
     block_out[:, 0:LANES] = first
     block_out[:, LANES:] = second
+    for i in range(SIDE):
+        c_out[i * rows : (i + 1) * rows, :] = y_in[i, rows : 2 * rows, :]
+    lane = lax.broadcasted_iota(jnp.int32, (1, c_out.shape[1]), 1)
+    held = jnp.zeros((1, c_out.shape[1]), jnp.int32)
+    for b in range(NBAND):
+        held = jnp.where(lane == b, offsets[0, b], held)
+    c_out[panel:, :] = jnp.broadcast_to(held.astype(F32), (8, c_out.shape[1]))
+    c_out[panel : panel + NBAND, :] = weights[...]
 
 
 def second_gain(
-    where, offsets, weights, gain, x_in, e0, e1, e2, e3, u1, u2, u3, u4,
+    where, offsets, weights, gain, x_in, e0, e1, e2, e3, unread,
     gain_out, x_out, shift_out, rows_out, high_out, low_out, tall,
 ):
     panel = gain.shape[0]
@@ -208,34 +210,44 @@
     rows_out[4:, :] = forward[0:4]
 
 
-def later_inputs(offsets, piece, own_high, own_low, crossed_high, crossed_low):
-    rows = own_high.shape[0]
-    step = 16
-    weights = piece[rows : rows + NBAND, :]
-
-    def put(at, blocks, high_out, low_out):
+def later_inputs(offsets, c_in, own_high, own_low, crossed_high, crossed_low):
+    panel, columns = own_high.shape
+    matrix = c_in[0:panel, :]
+    weights = c_in[panel : panel + NBAND, :]
+    high, low = halves(matrix)
+    reach = 3 * LANES
+    ahead = (
+        lax.broadcasted_iota(jnp.int32, (reach, LANES), 0)
+        - lax.broadcasted_iota(jnp.int32, (reach, LANES), 1)
+        - LANES
+    )
+    count = columns // LANES
+    crossed = []
+    for i in range(count):
+        first = max(i - 1, 0)
+        last = min(i + 2, count)
+        spread = jnp.zeros((reach, LANES), F32)
+        for b in range(NBAND):
+            weight = weights[b : b + 1, i * LANES : (i + 1) * LANES]
+            spread = spread + jnp.where(ahead == offsets[b], weight, 0.0)
+        spread = spread[(first - i + 1) * LANES : (last - i + 1) * LANES]
+        lanes = slice(first * LANES, last * LANES)
+        crossed.append(three((high[:, lanes], low[:, lanes]), halves(spread), ((1,), (0,))))
+    for blocks, high_out, low_out in (
+        (tiles(matrix), own_high, own_low),
+        (crossed, crossed_high, crossed_low),
+    ):
         for i, block in enumerate(swap_tiles(blocks)):
             high, low = halves(block)
-            high_out[at : at + step, i * LANES : (i + 1) * LANES] = high
-            low_out[at : at + step, i * LANES : (i + 1) * LANES] = low
-
-    for at in range(0, rows, step):
-        blocks = tiles(piece[at : at + step, :])
-        put(at, blocks, own_high, own_low)
-        put(at, band_tiles(blocks, weights, lambda b: offsets[b]), crossed_high, crossed_low)
+            high_out[:, i * LANES : (i + 1) * LANES] = high
+            low_out[:, i * LANES : (i + 1) * LANES] = low
 
 
 def first_spread(
-    where, wide_high, wide_low, gain_2_in,
+    where, wide_high, wide_low, gain_2_in, own_high, own_low, crossed_high, crossed_low,
     later_rows, block, own, e0, e1, e2, e3, shift, gain_2, gain_2_later,
-    h0, h1, h2, h3, l0, l1, l2, l3, g0, g1, g2, g3, k0, k1, k2, k3,
-    part_out, shift_out, pair_out, high_out, low_out,
-    tall, own_high, own_low, crossed_high, crossed_low,
+    part_out, shift_out, pair_out, high_out, low_out, tall,
 ):
-    place_rows((h0, h1, h2, h3), where[0], own_high)
-    place_rows((l0, l1, l2, l3), where[0], own_low)
-    place_rows((g0, g1, g2, g3), where[0], crossed_high)
-    place_rows((k0, k1, k2, k3), where[0], crossed_low)
     panel = e0.shape[0]
     at_y = where[0]
     pair_out[0:panel, :] = gain_2[...]
@@ -270,7 +282,7 @@
     out[panel:, :] = shift[...]
 
 
-def four_times(block, p1, p2, out):
+def four_times(block, p1, p2, p3, out):
     for i in range(SIDE):
         out[i] = block[...]
 
@@ -344,7 +356,7 @@
         out_shape=shapes,
         in_specs=[SMEM] * len(scalars) + [WHOLE] * len(arrays) + [UNREAD] * len(unread),
         out_specs=[WHOLE] * len(shapes),
-        scratch_shapes=[pltpu.VMEM(s[:2], *(s[2:] or (F32,))) for s in scratch],
+        scratch_shapes=[pltpu.VMEM(s, F32) for s in scratch],
         compiler_params=pltpu.CompilerParams(vmem_limit_bytes=24 * 2**20),
         cost_estimate=pl.CostEstimate(flops=flops, bytes_accessed=4 * size, transcendentals=0),
     )(*scalars, *arrays, *unread)
@@ -398,29 +410,26 @@
     )
     unit = 2 * panel * panel * columns
 
-    y_message, c_message = call(
-        first_message,
+    crossed, y_message = call(
+        prepare,
         (band_offset,),
         far(own, inverse, weights, prior_mean, innovation, seen_sites),
-        ((SIDE, rows + 8, columns), (rows + 8, columns)),
+        ((rows, columns), (SIDE, 2 * rows + 8, columns)),
     )
     y_in = swap(y_message, "y")
-    (crossed,) = call(cross, (band_offset,), far(own, weights), ((rows, columns),))
     crossed_pieces = ring(crossed, "x")
-    c_later = shifted(c_message, 1)
-    gain, crossed_block, x_message = call(
+    gain, crossed_block, c_message, x_message = call(
         first_gain,
-        (where,),
-        (y_in, *far(*crossed_pieces)),
-        ((panel, panel), (panel, panel), (SIDE, panel + 8, panel)),
+        (where, band_offset),
+        (y_in, *far(*crossed_pieces, weights)),
+        ((panel, panel), (panel, panel), (panel + 8, columns), (SIDE, panel + 8, panel)),
         ((panel, columns),),
         unit,
     )
     gain_in = swap(x_message, "x")
     later_pieces = ring_shifted(gain, 1)
-    gain_pieces = ring(gain, "y")
-    c_pieces = ring(c_later, "y")
-    next_offsets = c_later[rows + NBAND, 0:8].astype(jnp.int32)
+    c_in = shifted(c_message, 1)
+    next_offsets = c_in[panel + NBAND, 0:8].astype(jnp.int32)
     gain_2, x_message, shift, rows_message, wide_high, wide_low = call(
         second_gain,
         (where, band_offset),
@@ -428,26 +437,25 @@
         ((panel, panel), (SIDE, panel, panel), (8, panel), (8, columns)),
         ((columns, panel),),
         unit,
-        unread=(*gain_pieces[1:], c_later),
+        unread=(c_in,),
         coarse=((panel, columns),) * 2,
     )
     gain_2_in = swap(x_message, "x")
+    gain_pieces = ring(gain, "y")
     gain_2_later = shifted(gain_2, 2)
     later_rows = shifted(rows_message, 1)
-    later_halves = [
-        call(later_inputs, (next_offsets,), far(piece), (), coarse=((rows, columns),) * 4)
-        for piece in c_pieces
-    ]
-    later_halves = [half for halves_of in zip(*later_halves) for half in halves_of]
+    later_halves = call(
+        later_inputs, (next_offsets,), far(c_in), (), coarse=((panel, columns),) * 4
+    )
     part, shift_2, gain_2_pair, wide_high, wide_low = call(
         first_spread,
         (where,),
         (
-            *far(wide_high, wide_low), gain_2_in, *far(later_rows, crossed_block),
-            *far(own, gain, *gain_pieces[1:], shift, gain_2, gain_2_later, *later_halves),
+            *far(wide_high, wide_low), gain_2_in, *far(*later_halves, later_rows, crossed_block),
+            *far(own, gain, *gain_pieces[1:], shift, gain_2, gain_2_later),
         ),
         ((SIDE, panel, panel), (8, panel), (2 * panel, panel)),
-        ((columns, panel),) + ((panel, columns, jnp.bfloat16),) * 4,
+        ((columns, panel),),
         3 * unit,
         coarse=((panel, columns),) * 2,
     )
@@ -456,7 +464,7 @@
     (spread_2,) = call(join_spread, (), (parts, *far(shift_2)), ((panel + 8, panel),))
     later = shifted(spread_2, 2)
     (y_message,) = call(
-        four_times, (), (later,), ((SIDE, panel + 8, panel),), unread=gain_2_pieces[1:3]
+        four_times, (), (later,), ((SIDE, panel + 8, panel),), unread=gain_2_pieces[1:]
     )
     y_in = swap(y_message, "y")
     x_message, shift_4 = call(

time: 207 us -> 189 us (0.913)
  the two profiles are of different devices: /device:TPU:192 before, /device:TPU:224 now
where the time goes in v6:
time: 189 us; the launch traced here: 187 us
  starting transfers between devices  70.9 us (38%)
  waiting for transfers between devices  61.6 us (33%)
  Pallas kernels  29.5 us (16%)
  blocking collectives  19.4 us (10%)
  local copies, waits for them, and re-layouts  4.75 us (3%)
    all_to_all x5, waiting for transfers between devices, swap(): return lax.all_to_all(message, axis, 0, 0)  33.1 us
    pallas_call x9, Pallas kernels, call(): pl.pallas_call(kernel, out_shape=shapes, in_specs=[SMEM] * len(scalars) +...  29.5 us
    ppermute x9, starting transfers between devices, ring(): lax.ppermute(block, axis, [(i, (i + step) % SIDE) for i in range(SIDE)])  29.1 us
    all_to_all x5, starting transfers between devices, swap(): return lax.all_to_all(message, axis, 0, 0)  23.3 us
    all_to_all x1, blocking collectives, swap(): return lax.all_to_all(message, axis, 0, 0)  19.4 us
    ppermute x9, waiting for transfers between devices, ring(): lax.ppermute(block, axis, [(i, (i + step) % SIDE) for i in range(SIDE)])  16.8 us
    ppermute x4, starting transfers between devices, ring_shifted(): pieces.append(lax.ppermute(block, ('tm', 'y'), route))  10.2 us
    ppermute x4, waiting for transfers between devices, ring_shifted(): pieces.append(lax.ppermute(block, ('tm', 'y'), route))  9.5 us
  transfers between devices with their start and end apart: 22, of which 14 were waited for; matrix products, arithmetic and copies ran while one was open for 1% of the time, Pallas kernels for 3%

profile of v6, /device:TPU:224, one launch (start us, length us, event | category | flops | bytes accessed | tf_op | source)
XLA Modules:
  0.0 187.3 jit_solution(2611375731682041358)
XLA Ops:
  2.6 3.3 %shard_map.94 = (f32[64,1024]{1,0:T(8,128)}, f32[4,136,1024]{2,1,0:T(8,128)}) custom-call(s32[1,5]{1,0:T(1,128)S(1)} %copy-done.4, f32[64,1024]{1,0:T(8,128)} %bitcast.13, f32[64,1024]{1,0:T(8,128)} %bitcast.18, f32[5,1024]{1,0:T(8,128)} %bitcast.15, f32[1,64]{1,0:T(1,128)} %prior.1, f32[1,128]{1,0:T(1,128)} %innovation.1, s32[1,128]{1,0:T(1,128)} %sites.1), custom_call_target="tpu_custom_call" | custom-call | bytes 3036416 | tf_op jit(solution)/shard_map/pallas_call | solution.py:354
  5.9 4.6 %all-to-all-start = ((f32[4,136,1024]{2,1,0:T(8,128)}), f32[4,136,1024]{2,1,0:T(8,128)S(1)}, u32[]{:S(2)}, u32[]{:S(2)}) async-start(f32[4,136,1024]{2,1,0:T(8,128)} %get-tuple-element.28), calls=%async_computation | async-start | bytes 4456448 | tf_op jit(solution)/shard_map/all_to_all | solution.py:371
  10.5 4.9 %collective-permute-start.2 = (f32[64,1024]{1,0:T(8,128)S(1)}, f32[64,1024]{1,0:T(8,128)S(1)}, u32[]{:S(2)}, u32[]{:S(2)}) collective-permute-start(f32[64,1024]{1,0:T(8,128)S(1)} %copy-done.10), channel_id=1, source_target_pairs={{0,2},{1,3},{2,0},{3,1},{4,6},{5,7},{6,4},{7,5},{8,10},{9,11},{10,... | collective-permute-start | bytes 786440 | tf_op jit(solution)/shard_map/ppermute | solution.py:377
  15.5 3.0 %collective-permute-start.1 = (f32[64,1024]{1,0:T(8,128)S(1)}, f32[64,1024]{1,0:T(8,128)S(1)}, u32[]{:S(2)}, u32[]{:S(2)}) collective-permute-start(f32[64,1024]{1,0:T(8,128)S(1)} %copy-done.10), channel_id=1, source_target_pairs={{0,3},{1,0},{2,1},{3,2},{4,7},{5,4},{6,5},{7,6},{8,11},{9,8},{10,9... | collective-permute-start | bytes 786440 | tf_op jit(solution)/shard_map/ppermute | solution.py:377
  18.5 2.8 %collective-permute-start = (f32[64,1024]{1,0:T(8,128)S(1)}, f32[64,1024]{1,0:T(8,128)S(1)}, u32[]{:S(2)}, u32[]{:S(2)}) collective-permute-start(f32[64,1024]{1,0:T(8,128)S(1)} %copy-done.10), channel_id=1, source_target_pairs={{0,1},{1,2},{2,3},{3,0},{4,5},{5,6},{6,7},{7,4},{8,9},{9,10},{10,1... | collective-permute-start | bytes 786440 | tf_op jit(solution)/shard_map/ppermute | solution.py:377
  21.7 5.7 %collective-permute-done.1.x2 = f32[64,1024]{1,0:T(8,128)S(1)} collective-permute-done((f32[64,1024]{1,0:T(8,128)S(1)}, f32[64,1024]{1,0:T(8,128)S(1)}, u32[]{:S(2)}, u32[]{:S(2)}) %collective-permute-start.1) | collective-permute-done | bytes 262176 | tf_op jit(solution)/shard_map/ppermute | solution.py:377
  28.8 9.4 %all-to-all-done.y_in = f32[4,136,1024]{2,1,0:T(8,128)S(1)} async-done(((f32[4,136,1024]{2,1,0:T(8,128)}), f32[4,136,1024]{2,1,0:T(8,128)S(1)}, u32[]{:S(2)}, u32[]{:S(2)}) %all-to-all-start) | async-done | bytes 2228256 | tf_op jit(solution)/shard_map/all_to_all | solution.py:371
  38.3 3.4 %shard_map.95 = (f32[256,256]{1,0:T(8,128)}, f32[256,256]{1,0:T(8,128)}, f32[264,1024]{1,0:T(8,128)}, f32[4,264,256]{2,1,0:T(8,128)}) custom-call(s32[4]{0:T(128)S(1)} %pad_add_fusion.where, s32[1,5]{1,0:T(1,128)S(1)} %copy-done.5, f32[4,136,1024]{2,1,0:T(8,128)S(1)} %all-to-all-done.y_in, f32[64,1024]{1,0:T(8,128)} %get-tuple-element.29.x0, ...), custom_call_target="tpu_custom_call" | custom-call | flops 134217728 | bytes 5984256 | tf_op jit(solution)/shard_map/pallas_call | solution.py:354
  43.7 4.4 %all-to-all-start.1 = ((f32[4,264,256]{2,1,0:T(8,128)}), f32[4,264,256]{2,1,0:T(8,128)S(1)}, u32[]{:S(2)}, u32[]{:S(2)}) async-start(f32[4,264,256]{2,1,0:T(8,128)} %get-tuple-element.31), calls=%async_computation.1 | async-start | bytes 2162688 | tf_op jit(solution)/shard_map/all_to_all | solution.py:371
  50.0 4.4 %collective-permute-start.5 = (f32[256,256]{1,0:T(8,128)S(1)}, f32[256,256]{1,0:T(8,128)S(1)}, u32[]{:S(2)}, u32[]{:S(2)}) collective-permute-start(f32[256,256]{1,0:T(8,128)S(1)} %copy-done.7), channel_id=1, source_target_pairs={{16,12},{20,0},{24,4},{28,8},{32,28},{36,16},{40,20},{44,24},{48,4... | collective-permute-start | bytes 786440 | tf_op jit(solution)/shard_map/ppermute | solution.py:390
  59.4 2.8 %collective-permute-done.5.e2 = f32[256,256]{1,0:T(8,128)S(1)} collective-permute-done((f32[256,256]{1,0:T(8,128)S(1)}, f32[256,256]{1,0:T(8,128)S(1)}, u32[]{:S(2)}, u32[]{:S(2)}) %collective-permute-start.5) | collective-permute-done | bytes 262176 | tf_op jit(solution)/shard_map/ppermute | solution.py:390
  62.2 3.6 %collective-permute-done.4.e1 = f32[256,256]{1,0:T(8,128)S(1)} collective-permute-done((f32[256,256]{1,0:T(8,128)S(1)}, f32[256,256]{1,0:T(8,128)S(1)}, u32[]{:S(2)}, u32[]{:S(2)}) %collective-permute-start.4) | collective-permute-done | bytes 262176 | tf_op jit(solution)/shard_map/ppermute | solution.py:390
  68.5 3.9 %shard_map.96 = (f32[256,256]{1,0:T(8,128)}, f32[4,256,256]{2,1,0:T(8,128)}, f32[8,256]{1,0:T(8,128)}, f32[8,1024]{1,0:T(8,128)}, bf16[256,1024]{1,0:T(8,128)(2,1)}, /*index=5*/bf16[256,1024]{1,0:T(8,128)(2,1)}) custom-call(s32[4]{0:T(128)S(1)} %pad_add_fusion.where, s32[1,5]{1,0:T(1,128)S(1)} %copy-done.5, f32[5,1024]{1,0:T(8,128)} %bitcast.17, ...), custom_call_target="tpu_custom_call" | custom-call | flops 134217728 | bytes 3764224 | tf_op jit(solution)/shard_map/pallas_call | solution.py:354
  72.4 4.5 %all-to-all-start.2 = ((f32[4,256,256]{2,1,0:T(8,128)}), f32[4,256,256]{2,1,0:T(8,128)S(1)}, u32[]{:S(2)}, u32[]{:S(2)}) async-start(f32[4,256,256]{2,1,0:T(8,128)} %get-tuple-element.36), calls=%async_computation.2 | async-start | bytes 2097152 | tf_op jit(solution)/shard_map/all_to_all | solution.py:371
  76.9 4.0 %collective-permute-start.11 = (f32[256,256]{1,0:T(8,128)S(1)}, f32[256,256]{1,0:T(8,128)S(1)}, u32[]{:S(2)}, u32[]{:S(2)}) collective-permute-start(f32[256,256]{1,0:T(8,128)S(1)} %copy-done.8), channel_id=1, source_target_pairs={{0,8},{4,12},{8,0},{12,4},{1,9},{5,13},{9,1},{13,5},{2,10},{6,14},... | collective-permute-start | bytes 786440 | tf_op jit(solution)/shard_map/ppermute | solution.py:377
  80.9 3.0 %collective-permute-start.10 = (f32[256,256]{1,0:T(8,128)S(1)}, f32[256,256]{1,0:T(8,128)S(1)}, u32[]{:S(2)}, u32[]{:S(2)}) collective-permute-start(f32[256,256]{1,0:T(8,128)S(1)} %copy-done.8), channel_id=1, source_target_pairs={{0,12},{4,0},{8,4},{12,8},{1,13},{5,1},{9,5},{13,9},{2,14},{6,2},{... | collective-permute-start | bytes 786440 | tf_op jit(solution)/shard_map/ppermute | solution.py:377
  83.9 2.8 %collective-permute-start.9 = (f32[256,256]{1,0:T(8,128)S(1)}, f32[256,256]{1,0:T(8,128)S(1)}, u32[]{:S(2)}, u32[]{:S(2)}) collective-permute-start(f32[256,256]{1,0:T(8,128)S(1)} %copy-done.8), channel_id=1, source_target_pairs={{0,4},{4,8},{8,12},{12,0},{1,5},{5,9},{9,13},{13,1},{2,6},{6,10},{... | collective-permute-start | bytes 786440 | tf_op jit(solution)/shard_map/ppermute | solution.py:377
  86.7 2.0 %collective-permute-start.12 = (f32[256,256]{1,0:T(8,128)S(1)}, f32[256,256]{1,0:T(8,128)}, u32[]{:S(2)}, u32[]{:S(2)}) collective-permute-start(f32[256,256]{1,0:T(8,128)S(1)} %copy-done.6), channel_id=1, source_target_pairs={{32,0},{48,16},{64,32},{80,48},{96,64},{112,80},{128,96},{144,112}... | collective-permute-start | bytes 786440 | tf_op jit(solution)/shard_map/ppermute | solution.py:367
  88.8 2.6 %collective-permute-start.8 = (f32[8,1024]{1,0:T(8,128)S(1)}, f32[8,1024]{1,0:T(8,128)S(1)}, u32[]{:S(2)}, u32[]{:S(2)}) collective-permute-start(f32[8,1024]{1,0:T(8,128)S(1)} %copy-done.22), channel_id=1, source_target_pairs={{16,0},{32,16},{48,32},{64,48},{80,64},{96,80},{112,96},{128,112},... | collective-permute-start | bytes 98312 | tf_op jit(solution)/shard_map/ppermute | solution.py:367
  91.4 4.2 %shard_map.97 = (bf16[256,1024]{1,0:T(8,128)(2,1)}, bf16[256,1024]{1,0:T(8,128)(2,1)}, bf16[256,1024]{1,0:T(8,128)(2,1)}, bf16[256,1024]{1,0:T(8,128)(2,1)}) custom-call(s32[8]{0:T(128)S(1)} %fusion.offsets, f32[264,1024]{1,0:T(8,128)} %copy-done), custom_call_target="tpu_custom_call" | custom-call | bytes 1081344 | tf_op jit(solution)/shard_map/pallas_call | solution.py:354
  96.4 2.1 %collective-permute-done.12.gain_2_later = f32[256,256]{1,0:T(8,128)} collective-permute-done((f32[256,256]{1,0:T(8,128)S(1)}, f32[256,256]{1,0:T(8,128)}, u32[]{:S(2)}, u32[]{:S(2)}) %collective-permute-start.12) | collective-permute-done | bytes 262176 | tf_op jit(solution)/shard_map/ppermute | solution.py:367
  98.5 6.0 %shard_map.98 = (f32[4,256,256]{2,1,0:T(8,128)}, f32[8,256]{1,0:T(8,128)}, f32[512,256]{1,0:T(8,128)}, bf16[256,1024]{1,0:T(8,128)(2,1)}, bf16[256,1024]{1,0:T(8,128)(2,1)}) custom-call(s32[4]{0:T(128)S(1)} %pad_add_fusion.where, bf16[256,1024]{1,0:T(8,128)(2,1)} %get-tuple-element.34.wide_high, bf16[256,1024]{1,0:T(8,128)(2,1)} %get-tuple-element.35.wide_low, ...), custom_call_target="tpu_custom_call" | custom-call | flops 402653184 | bytes 11059200 | tf_op jit(solution)/shard_map/pallas_call | solution.py:354
  104.6 5.3 %all-to-all-start.3 = ((f32[4,256,256]{2,1,0:T(8,128)}), f32[4,256,256]{2,1,0:T(8,128)S(1)}, u32[]{:S(2)}, u32[]{:S(2)}) async-start(f32[4,256,256]{2,1,0:T(8,128)} %get-tuple-element.46), calls=%async_computation.3 | async-start | bytes 2097152 | tf_op jit(solution)/shard_map/all_to_all | solution.py:371
  109.8 2.7 %collective-permute-start.16 = (f32[512,256]{1,0:T(8,128)S(1)}, f32[512,256]{1,0:T(8,128)S(1)}, u32[]{:S(2)}, u32[]{:S(2)}) collective-permute-start(f32[512,256]{1,0:T(8,128)S(1)} %copy-done.9), channel_id=1, source_target_pairs={{0,8},{4,12},{8,0},{12,4},{1,9},{5,13},{9,1},{13,5},{2,10},{6,14},... | collective-permute-start | bytes 1572872 | tf_op jit(solution)/shard_map/ppermute | solution.py:377
  112.5 3.8 %collective-permute-start.15 = (f32[512,256]{1,0:T(8,128)S(1)}, f32[512,256]{1,0:T(8,128)S(1)}, u32[]{:S(2)}, u32[]{:S(2)}) collective-permute-start(f32[512,256]{1,0:T(8,128)S(1)} %copy-done.9), channel_id=1, source_target_pairs={{0,12},{4,0},{8,4},{12,8},{1,13},{5,1},{9,5},{13,9},{2,14},{6,2},{... | collective-permute-start | bytes 1572872 | tf_op jit(solution)/shard_map/ppermute | solution.py:377
  116.3 2.0 %collective-permute-start.14 = (f32[512,256]{1,0:T(8,128)S(1)}, f32[512,256]{1,0:T(8,128)S(1)}, u32[]{:S(2)}, u32[]{:S(2)}) collective-permute-start(f32[512,256]{1,0:T(8,128)S(1)} %copy-done.9), channel_id=1, source_target_pairs={{0,4},{4,8},{8,12},{12,0},{1,5},{5,9},{9,13},{13,1},{2,6},{6,10},{... | collective-permute-start | bytes 1572872 | tf_op jit(solution)/shard_map/ppermute | solution.py:377
  118.4 7.7 %all-to-all-done.3.parts = f32[4,256,256]{2,1,0:T(8,128)S(1)} async-done(((f32[4,256,256]{2,1,0:T(8,128)}), f32[4,256,256]{2,1,0:T(8,128)S(1)}, u32[]{:S(2)}, u32[]{:S(2)}) %all-to-all-start.3) | async-done | bytes 1048608 | tf_op jit(solution)/shard_map/all_to_all | solution.py:371
  129.5 8.6 %collective-permute-done.15.p2.a2 = f32[512,256]{1,0:T(8,128)S(1)} collective-permute-done((f32[512,256]{1,0:T(8,128)S(1)}, f32[512,256]{1,0:T(8,128)S(1)}, u32[]{:S(2)}, u32[]{:S(2)}) %collective-permute-start.15) | collective-permute-done | bytes 524320 | tf_op jit(solution)/shard_map/ppermute | solution.py:377
  140.1 19.4 %all_to_all.30.y_in = f32[4,264,256]{2,1,0:T(8,128)S(1)} all-to-all(f32[4,264,256]{2,1,0:T(8,128)} %shard_map.100), channel_id=1, replica_groups=mesh['tm'=32,'y'=4,'x'=4] {'y'}, dimensions={0} | all-to-all | bytes 2162688 | tf_op jit(solution)/shard_map/all_to_all | solution.py:371
  159.5 5.1 %shard_map.101 = (f32[4,64,1280]{2,1,0:T(8,128)}, f32[8,256]{1,0:T(8,128)}) custom-call(s32[4]{0:T(128)S(1)} %pad_add_fusion.where, f32[256,256]{1,0:T(8,128)} %get-tuple-element.33.gain_2, bf16[256,1024]{1,0:T(8,128)(2,1)} %get-tuple-element.44.wide_high, bf16[256,1024]{1,0:T(8,128)(2,1)} %get-tuple-element.45.wide_low, f32[264,256]{1,0:T(8,128)} %shard_map.99.spread, ...), custom_call_target="tpu_custom_call" | custom-call | flops 402653184 | bytes 7127040 | tf_op jit(solution)/shard_map/pallas_call | solution.py:354
  164.6 4.5 %all-to-all-start.5 = ((f32[4,64,1280]{2,1,0:T(8,128)}), f32[4,64,1280]{2,1,0:T(8,128)S(1)}, u32[]{:S(2)}, u32[]{:S(2)}) async-start(f32[4,64,1280]{2,1,0:T(8,128)} %get-tuple-element.49), calls=%async_computation.5 | async-start | bytes 2621440 | tf_op jit(solution)/shard_map/all_to_all | solution.py:371
  170.4 16.0 %all-to-all-done.5.x_in = f32[4,64,1280]{2,1,0:T(8,128)S(1)} async-done(((f32[4,64,1280]{2,1,0:T(8,128)}), f32[4,64,1280]{2,1,0:T(8,128)S(1)}, u32[]{:S(2)}, u32[]{:S(2)}) %all-to-all-start.5) | async-done | bytes 1310752 | tf_op jit(solution)/shard_map/all_to_all | solution.py:371
  (73 shorter events, 23.7 us)
Async XLA Ops:
  5.9 32.3 %copy-start.5 = (s32[1,5]{1,0:T(1,128)S(1)}, s32[1,5]{1,0:T(1,128)}, u32[]{:S(2)}) copy-start(s32[1,5]{1,0:T(1,128)} %offsets.5) | copy-start | bytes 64
  5.9 32.3 %all-to-all-start = ((f32[4,136,1024]{2,1,0:T(8,128)}), f32[4,136,1024]{2,1,0:T(8,128)S(1)}, u32[]{:S(2)}, u32[]{:S(2)}) async-start(f32[4,136,1024]{2,1,0:T(8,128)} %get-tuple-element.28), calls=%async_computation | async-start | bytes 4456448 | tf_op jit(solution)/shard_map/all_to_all | solution.py:371
  10.5 11.2 %collective-permute-start.2 = (f32[64,1024]{1,0:T(8,128)S(1)}, f32[64,1024]{1,0:T(8,128)S(1)}, u32[]{:S(2)}, u32[]{:S(2)}) collective-permute-start(f32[64,1024]{1,0:T(8,128)S(1)} %copy-done.10), channel_id=1, source_target_pairs={{0,2},{1,3},{2,0},{3,1},{4,6},{5,7},{6,4},{7,5},{8,10},{9,11},{10,... | collective-permute-start | bytes 786440 | tf_op jit(solution)/shard_map/ppermute | solution.py:377
  15.5 11.9 %collective-permute-start.1 = (f32[64,1024]{1,0:T(8,128)S(1)}, f32[64,1024]{1,0:T(8,128)S(1)}, u32[]{:S(2)}, u32[]{:S(2)}) collective-permute-start(f32[64,1024]{1,0:T(8,128)S(1)} %copy-done.10), channel_id=1, source_target_pairs={{0,3},{1,0},{2,1},{3,2},{4,7},{5,4},{6,5},{7,6},{8,11},{9,8},{10,9... | collective-permute-start | bytes 786440 | tf_op jit(solution)/shard_map/ppermute | solution.py:377
  18.5 10.3 %collective-permute-start = (f32[64,1024]{1,0:T(8,128)S(1)}, f32[64,1024]{1,0:T(8,128)S(1)}, u32[]{:S(2)}, u32[]{:S(2)}) collective-permute-start(f32[64,1024]{1,0:T(8,128)S(1)} %copy-done.10), channel_id=1, source_target_pairs={{0,1},{1,2},{2,3},{3,0},{4,5},{5,6},{6,7},{7,4},{8,9},{9,10},{10,1... | collective-permute-start | bytes 786440 | tf_op jit(solution)/shard_map/ppermute | solution.py:377
  21.7 16.6 %copy-start.11 = (f32[64,1024]{1,0:T(8,128)}, f32[64,1024]{1,0:T(8,128)S(1)}, u32[]{:S(2)}) copy-start(f32[64,1024]{1,0:T(8,128)S(1)} %collective-permute-done.2.x3) | copy-start | bytes 786436
  27.4 10.9 %copy-start.12 = (f32[64,1024]{1,0:T(8,128)}, f32[64,1024]{1,0:T(8,128)S(1)}, u32[]{:S(2)}) copy-start(f32[64,1024]{1,0:T(8,128)S(1)} %collective-permute-done.1.x2) | copy-start | bytes 786436
  28.8 9.4 %copy-start.13 = (f32[64,1024]{1,0:T(8,128)}, f32[64,1024]{1,0:T(8,128)S(1)}, u32[]{:S(2)}) copy-start(f32[64,1024]{1,0:T(8,128)S(1)} %collective-permute-done.x1) | copy-start | bytes 786436
  41.7 26.1 %collective-permute-start.7 = (f32[264,1024]{1,0:T(8,128)}, f32[264,1024]{1,0:T(8,128)S(1)}, u32[]{:S(2)}, u32[]{:S(2)}) collective-permute-start(f32[264,1024]{1,0:T(8,128)} %get-tuple-element.32), channel_id=1, source_target_pairs={{16,0},{32,16},{48,32},{64,48},{80,64},{96,80},{112,96},{128,112},... | collective-permute-start | bytes 3244040 | tf_op jit(solution)/shard_map/ppermute | solution.py:367
  43.7 24.1 %all-to-all-start.1 = ((f32[4,264,256]{2,1,0:T(8,128)}), f32[4,264,256]{2,1,0:T(8,128)S(1)}, u32[]{:S(2)}, u32[]{:S(2)}) async-start(f32[4,264,256]{2,1,0:T(8,128)} %get-tuple-element.31), calls=%async_computation.1 | async-start | bytes 2162688 | tf_op jit(solution)/shard_map/all_to_all | solution.py:371
  48.1 11.3 %collective-permute-start.6 = (f32[256,256]{1,0:T(8,128)S(1)}, f32[256,256]{1,0:T(8,128)S(1)}, u32[]{:S(2)}, u32[]{:S(2)}) collective-permute-start(f32[256,256]{1,0:T(8,128)S(1)} %copy-done.7), channel_id=1, source_target_pairs={{16,8},{20,12},{24,0},{28,4},{32,24},{36,28},{40,16},{44,20},{48,4... | collective-permute-start | bytes 786440 | tf_op jit(solution)/shard_map/ppermute | solution.py:390
  50.0 12.2 %collective-permute-start.5 = (f32[256,256]{1,0:T(8,128)S(1)}, f32[256,256]{1,0:T(8,128)S(1)}, u32[]{:S(2)}, u32[]{:S(2)}) collective-permute-start(f32[256,256]{1,0:T(8,128)S(1)} %copy-done.7), channel_id=1, source_target_pairs={{16,12},{20,0},{24,4},{28,8},{32,28},{36,16},{40,20},{44,24},{48,4... | collective-permute-start | bytes 786440 | tf_op jit(solution)/shard_map/ppermute | solution.py:390
  54.4 11.4 %collective-permute-start.4 = (f32[256,256]{1,0:T(8,128)S(1)}, f32[256,256]{1,0:T(8,128)S(1)}, u32[]{:S(2)}, u32[]{:S(2)}) collective-permute-start(f32[256,256]{1,0:T(8,128)S(1)} %copy-done.7), channel_id=1, source_target_pairs={{16,4},{20,8},{24,12},{28,0},{32,20},{36,24},{40,28},{44,16},{48,3... | collective-permute-start | bytes 786440 | tf_op jit(solution)/shard_map/ppermute | solution.py:390
  56.3 11.4 %collective-permute-start.3 = (f32[256,256]{1,0:T(8,128)S(1)}, f32[256,256]{1,0:T(8,128)S(1)}, u32[]{:S(2)}, u32[]{:S(2)}) collective-permute-start(f32[256,256]{1,0:T(8,128)S(1)} %copy-done.7), channel_id=1, source_target_pairs={{16,0},{20,4},{24,8},{28,12},{32,16},{36,20},{40,24},{44,28},{48,3... | collective-permute-start | bytes 786440 | tf_op jit(solution)/shard_map/ppermute | solution.py:390
  59.4 8.4 %copy-start.17 = (f32[256,256]{1,0:T(8,128)}, f32[256,256]{1,0:T(8,128)S(1)}, u32[]{:S(2)}) copy-start(f32[256,256]{1,0:T(8,128)S(1)} %collective-permute-done.6.e3) | copy-start | bytes 786436
  62.2 5.6 %copy-start.18 = (f32[256,256]{1,0:T(8,128)}, f32[256,256]{1,0:T(8,128)S(1)}, u32[]{:S(2)}) copy-start(f32[256,256]{1,0:T(8,128)S(1)} %collective-permute-done.5.e2) | copy-start | bytes 786436
  68.5 22.9 %copy-start = (f32[264,1024]{1,0:T(8,128)}, f32[264,1024]{1,0:T(8,128)S(1)}, u32[]{:S(2)}) copy-start(f32[264,1024]{1,0:T(8,128)S(1)} %collective-permute-done.7.unread.c_in) | copy-start | bytes 3244036
  72.4 14.3 %copy-start.6 = (f32[256,256]{1,0:T(8,128)S(1)}, f32[256,256]{1,0:T(8,128)}, u32[]{:S(2)}) copy-start(f32[256,256]{1,0:T(8,128)} %get-tuple-element.33.gain_2) | copy-start | bytes 786436
  72.4 16.4 %copy-start.22 = (f32[8,1024]{1,0:T(8,128)S(1)}, f32[8,1024]{1,0:T(8,128)}, u32[]{:S(2)}) copy-start(f32[8,1024]{1,0:T(8,128)} %get-tuple-element.41) | copy-start | bytes 98308
  72.4 26.1 %all-to-all-start.2 = ((f32[4,256,256]{2,1,0:T(8,128)}), f32[4,256,256]{2,1,0:T(8,128)S(1)}, u32[]{:S(2)}, u32[]{:S(2)}) async-start(f32[4,256,256]{2,1,0:T(8,128)} %get-tuple-element.36), calls=%async_computation.2 | async-start | bytes 2097152 | tf_op jit(solution)/shard_map/all_to_all | solution.py:371
  76.9 18.7 %collective-permute-start.11 = (f32[256,256]{1,0:T(8,128)S(1)}, f32[256,256]{1,0:T(8,128)S(1)}, u32[]{:S(2)}, u32[]{:S(2)}) collective-permute-start(f32[256,256]{1,0:T(8,128)S(1)} %copy-done.8), channel_id=1, source_target_pairs={{0,8},{4,12},{8,0},{12,4},{1,9},{5,13},{9,1},{13,5},{2,10},{6,14},... | collective-permute-start | bytes 786440 | tf_op jit(solution)/shard_map/ppermute | solution.py:377
  80.9 14.8 %collective-permute-start.10 = (f32[256,256]{1,0:T(8,128)S(1)}, f32[256,256]{1,0:T(8,128)S(1)}, u32[]{:S(2)}, u32[]{:S(2)}) collective-permute-start(f32[256,256]{1,0:T(8,128)S(1)} %copy-done.8), channel_id=1, source_target_pairs={{0,12},{4,0},{8,4},{12,8},{1,13},{5,1},{9,5},{13,9},{2,14},{6,2},{... | collective-permute-start | bytes 786440 | tf_op jit(solution)/shard_map/ppermute | solution.py:377
  83.9 11.7 %collective-permute-start.9 = (f32[256,256]{1,0:T(8,128)S(1)}, f32[256,256]{1,0:T(8,128)S(1)}, u32[]{:S(2)}, u32[]{:S(2)}) collective-permute-start(f32[256,256]{1,0:T(8,128)S(1)} %copy-done.8), channel_id=1, source_target_pairs={{0,4},{4,8},{8,12},{12,0},{1,5},{5,9},{9,13},{13,1},{2,6},{6,10},{... | collective-permute-start | bytes 786440 | tf_op jit(solution)/shard_map/ppermute | solution.py:377
  86.7 11.8 %collective-permute-start.12 = (f32[256,256]{1,0:T(8,128)S(1)}, f32[256,256]{1,0:T(8,128)}, u32[]{:S(2)}, u32[]{:S(2)}) collective-permute-start(f32[256,256]{1,0:T(8,128)S(1)} %copy-done.6), channel_id=1, source_target_pairs={{32,0},{48,16},{64,32},{80,48},{96,64},{112,80},{128,96},{144,112}... | collective-permute-start | bytes 786440 | tf_op jit(solution)/shard_map/ppermute | solution.py:367
  88.8 6.9 %collective-permute-start.8 = (f32[8,1024]{1,0:T(8,128)S(1)}, f32[8,1024]{1,0:T(8,128)S(1)}, u32[]{:S(2)}, u32[]{:S(2)}) collective-permute-start(f32[8,1024]{1,0:T(8,128)S(1)} %copy-done.22), channel_id=1, source_target_pairs={{16,0},{32,16},{48,32},{64,48},{80,64},{96,80},{112,96},{128,112},... | collective-permute-start | bytes 98312 | tf_op jit(solution)/shard_map/ppermute | solution.py:367
  104.6 21.5 %all-to-all-start.3 = ((f32[4,256,256]{2,1,0:T(8,128)}), f32[4,256,256]{2,1,0:T(8,128)S(1)}, u32[]{:S(2)}, u32[]{:S(2)}) async-start(f32[4,256,256]{2,1,0:T(8,128)} %get-tuple-element.46), calls=%async_computation.3 | async-start | bytes 2097152 | tf_op jit(solution)/shard_map/all_to_all | solution.py:371
  109.8 19.7 %collective-permute-start.16 = (f32[512,256]{1,0:T(8,128)S(1)}, f32[512,256]{1,0:T(8,128)S(1)}, u32[]{:S(2)}, u32[]{:S(2)}) collective-permute-start(f32[512,256]{1,0:T(8,128)S(1)} %copy-done.9), channel_id=1, source_target_pairs={{0,8},{4,12},{8,0},{12,4},{1,9},{5,13},{9,1},{13,5},{2,10},{6,14},... | collective-permute-start | bytes 1572872 | tf_op jit(solution)/shard_map/ppermute | solution.py:377
  112.5 25.6 %collective-permute-start.15 = (f32[512,256]{1,0:T(8,128)S(1)}, f32[512,256]{1,0:T(8,128)S(1)}, u32[]{:S(2)}, u32[]{:S(2)}) collective-permute-start(f32[512,256]{1,0:T(8,128)S(1)} %copy-done.9), channel_id=1, source_target_pairs={{0,12},{4,0},{8,4},{12,8},{1,13},{5,1},{9,5},{13,9},{2,14},{6,2},{... | collective-permute-start | bytes 1572872 | tf_op jit(solution)/shard_map/ppermute | solution.py:377
  116.3 22.6 %collective-permute-start.14 = (f32[512,256]{1,0:T(8,128)S(1)}, f32[512,256]{1,0:T(8,128)S(1)}, u32[]{:S(2)}, u32[]{:S(2)}) collective-permute-start(f32[512,256]{1,0:T(8,128)S(1)} %copy-done.9), channel_id=1, source_target_pairs={{0,4},{4,8},{8,12},{12,0},{1,5},{5,9},{9,13},{13,1},{2,6},{6,10},{... | collective-permute-start | bytes 1572872 | tf_op jit(solution)/shard_map/ppermute | solution.py:377
  127.6 11.5 %collective-permute-start.13 = (f32[264,256]{1,0:T(8,128)}, f32[264,256]{1,0:T(8,128)S(1)}, u32[]{:S(2)}, u32[]{:S(2)}) collective-permute-start(f32[264,256]{1,0:T(8,128)} %shard_map.99.spread), channel_id=1, source_target_pairs={{32,0},{48,16},{64,32},{80,48},{96,64},{112,80},{128,96},{144,112}... | collective-permute-start | bytes 811016 | tf_op jit(solution)/shard_map/ppermute | solution.py:367
  129.5 10.6 %copy-start.1 = (f32[512,256]{1,0:T(8,128)}, f32[512,256]{1,0:T(8,128)S(1)}, u32[]{:S(2)}) copy-start(f32[512,256]{1,0:T(8,128)S(1)} %collective-permute-done.16.p3.a3) | copy-start | bytes 1572868
  164.6 21.7 %all-to-all-start.5 = ((f32[4,64,1280]{2,1,0:T(8,128)}), f32[4,64,1280]{2,1,0:T(8,128)S(1)}, u32[]{:S(2)}, u32[]{:S(2)}) async-start(f32[4,64,1280]{2,1,0:T(8,128)} %get-tuple-element.49), calls=%async_computation.5 | async-start | bytes 2621440 | tf_op jit(solution)/shard_map/all_to_all | solution.py:371
  (13 other events, 34.1 us)

commit v7 on v6

--- a/solution.py
+++ b/solution.py
@@ -378,19 +378,6 @@
     return pieces
 
 
-def ring_shifted(block, distance):
-    count = lax.axis_size("tm")
-    pieces = []
-    for step in STEPS:
-        route = [
-            ((i + distance) * SIDE + j, i * SIDE + (j + step) % SIDE)
-            for i in range(count - distance)
-            for j in range(SIDE)
-        ]
-        pieces.append(lax.ppermute(block, ("tm", "y"), route))
-    return pieces
-
-
 def body(covariance, precision, band_weight, band_offset, prior_mean, innovation, seen_sites):
     own = covariance[0]
     inverse = precision[0]
@@ -427,9 +414,12 @@
         unit,
     )
     gain_in = swap(x_message, "x")
-    later_pieces = ring_shifted(gain, 1)
+    later_pieces = ring(shifted(gain, 1), "y")
     c_in = shifted(c_message, 1)
     next_offsets = c_in[panel + NBAND, 0:8].astype(jnp.int32)
+    later_halves = call(
+        later_inputs, (next_offsets,), far(c_in), (), coarse=((panel, columns),) * 4
+    )
     gain_2, x_message, shift, rows_message, wide_high, wide_low = call(
         second_gain,
         (where, band_offset),
@@ -437,16 +427,13 @@
         ((panel, panel), (SIDE, panel, panel), (8, panel), (8, columns)),
         ((columns, panel),),
         unit,
-        unread=(c_in,),
+        unread=(later_halves[0],),
         coarse=((panel, columns),) * 2,
     )
     gain_2_in = swap(x_message, "x")
     gain_pieces = ring(gain, "y")
     gain_2_later = shifted(gain_2, 2)
     later_rows = shifted(rows_message, 1)
-    later_halves = call(
-        later_inputs, (next_offsets,), far(c_in), (), coarse=((panel, columns),) * 4
-    )
     part, shift_2, gain_2_pair, wide_high, wide_low = call(
         first_spread,
         (where,),

time: 189 us -> 197 us (1.042)
  waiting for transfers between devices: 61.6 us -> 65.6 us
  local copies, waits for them, and re-layouts: 4.75 us -> 6.86 us
  starting transfers between devices: 70.9 us -> 72.9 us
    ppermute x9 -> x12, starting transfers between devices: 29.1 us -> 39.8 us  [ring(): lax.ppermute(block, axis, [(i, (i + step) % SIDE) for i in range(SIDE)])]
    ppermute x4 -> x0, starting transfers between devices: 10.2 us -> none  [ring_shifted(): pieces.append(lax.ppermute(block, ('tm', 'y'), route))]
    ppermute x4 -> x0, waiting for transfers between devices: 9.5 us -> none  [ring_shifted(): pieces.append(lax.ppermute(block, ('tm', 'y'), route))]
    ppermute x4 -> x5, waiting for transfers between devices: 2.24 us -> 11.7 us  [shifted(): lax.ppermute(block, 'tm', [(i + distance, i) for i in range(count - dista...]
    ppermute x9 -> x12, waiting for transfers between devices: 16.8 us -> 24.5 us  [ring(): lax.ppermute(block, axis, [(i, (i + step) % SIDE) for i in range(SIDE)])]
    all_to_all x5, waiting for transfers between devices: 33.1 us -> 29.4 us  [swap(): return lax.all_to_all(message, axis, 0, 0)]
    unnamed x47 -> x51, local copies, waits for them, and re-layouts: 3.47 us -> 5.58 us
    ppermute x4 -> x5, starting transfers between devices: 8.43 us -> 10.1 us  [shifted(): lax.ppermute(block, 'tm', [(i + distance, i) for i in range(count - dista...]
  transfers between devices with their start and end apart: 22 -> 22, of which waited for: 14 -> 13; matrix products, arithmetic and copies ran while one was open for 1% -> 1% of each run, Pallas kernels for 3% -> 3%
where the time goes in v7:
time: 197 us; the launch traced here: 195 us
  starting transfers between devices  72.9 us (37%)
  waiting for transfers between devices  65.6 us (33%)
  Pallas kernels  29.3 us (15%)
  blocking collectives  19.5 us (10%)
  local copies, waits for them, and re-layouts  6.86 us (3%)
    ppermute x12, starting transfers between devices, ring(): lax.ppermute(block, axis, [(i, (i + step) % SIDE) for i in range(SIDE)])  39.8 us
    all_to_all x5, waiting for transfers between devices, swap(): return lax.all_to_all(message, axis, 0, 0)  29.4 us
    pallas_call x9, Pallas kernels, call(): pl.pallas_call(kernel, out_shape=shapes, in_specs=[SMEM] * len(scalars) +...  29.3 us
    ppermute x12, waiting for transfers between devices, ring(): lax.ppermute(block, axis, [(i, (i + step) % SIDE) for i in range(SIDE)])  24.5 us
    all_to_all x5, starting transfers between devices, swap(): return lax.all_to_all(message, axis, 0, 0)  22.9 us
    all_to_all x1, blocking collectives, swap(): return lax.all_to_all(message, axis, 0, 0)  19.5 us
    ppermute x5, waiting for transfers between devices, shifted(): lax.ppermute(block, 'tm', [(i + distance, i) for i in range(count - dista...  11.7 us
    ppermute x5, starting transfers between devices, shifted(): lax.ppermute(block, 'tm', [(i + distance, i) for i in range(count - dista...  10.1 us
  transfers between devices with their start and end apart: 22, of which 13 were waited for; matrix products, arithmetic and copies ran while one was open for 1% of the time, Pallas kernels for 3%

profile of v7, /device:TPU:224, one launch (start us, length us, event | category | flops | bytes accessed | tf_op | source)
XLA Modules:
  0.0 195.3 jit_solution(17227284635480350756)
XLA Ops:
  2.6 3.3 %shard_map.94 = (f32[64,1024]{1,0:T(8,128)}, f32[4,136,1024]{2,1,0:T(8,128)}) custom-call(s32[1,5]{1,0:T(1,128)S(1)} %copy-done.4, f32[64,1024]{1,0:T(8,128)} %bitcast.13, f32[64,1024]{1,0:T(8,128)} %bitcast.18, f32[5,1024]{1,0:T(8,128)} %bitcast.15, f32[1,64]{1,0:T(1,128)} %prior.1, f32[1,128]{1,0:T(1,128)} %innovation.1, s32[1,128]{1,0:T(1,128)} %sites.1), custom_call_target="tpu_custom_call" | custom-call | bytes 3036416 | tf_op jit(solution)/shard_map/pallas_call | solution.py:354
  6.0 4.6 %all-to-all-start = ((f32[4,136,1024]{2,1,0:T(8,128)}), f32[4,136,1024]{2,1,0:T(8,128)S(1)}, u32[]{:S(2)}, u32[]{:S(2)}) async-start(f32[4,136,1024]{2,1,0:T(8,128)} %get-tuple-element.28), calls=%async_computation | async-start | bytes 4456448 | tf_op jit(solution)/shard_map/all_to_all | solution.py:371
  10.6 4.9 %collective-permute-start.2 = (f32[64,1024]{1,0:T(8,128)S(1)}, f32[64,1024]{1,0:T(8,128)S(1)}, u32[]{:S(2)}, u32[]{:S(2)}) collective-permute-start(f32[64,1024]{1,0:T(8,128)S(1)} %copy-done.11), channel_id=1, source_target_pairs={{0,2},{1,3},{2,0},{3,1},{4,6},{5,7},{6,4},{7,5},{8,10},{9,11},{10,... | collective-permute-start | bytes 786440 | tf_op jit(solution)/shard_map/ppermute | solution.py:377
  15.5 3.0 %collective-permute-start.1 = (f32[64,1024]{1,0:T(8,128)S(1)}, f32[64,1024]{1,0:T(8,128)S(1)}, u32[]{:S(2)}, u32[]{:S(2)}) collective-permute-start(f32[64,1024]{1,0:T(8,128)S(1)} %copy-done.11), channel_id=1, source_target_pairs={{0,3},{1,0},{2,1},{3,2},{4,7},{5,4},{6,5},{7,6},{8,11},{9,8},{10,9... | collective-permute-start | bytes 786440 | tf_op jit(solution)/shard_map/ppermute | solution.py:377
  18.6 2.8 %collective-permute-start = (f32[64,1024]{1,0:T(8,128)S(1)}, f32[64,1024]{1,0:T(8,128)S(1)}, u32[]{:S(2)}, u32[]{:S(2)}) collective-permute-start(f32[64,1024]{1,0:T(8,128)S(1)} %copy-done.11), channel_id=1, source_target_pairs={{0,1},{1,2},{2,3},{3,0},{4,5},{5,6},{6,7},{7,4},{8,9},{9,10},{10,1... | collective-permute-start | bytes 786440 | tf_op jit(solution)/shard_map/ppermute | solution.py:377
  21.7 5.7 %collective-permute-done.1.x2 = f32[64,1024]{1,0:T(8,128)S(1)} collective-permute-done((f32[64,1024]{1,0:T(8,128)S(1)}, f32[64,1024]{1,0:T(8,128)S(1)}, u32[]{:S(2)}, u32[]{:S(2)}) %collective-permute-start.1) | collective-permute-done | bytes 262176 | tf_op jit(solution)/shard_map/ppermute | solution.py:377
  28.9 9.4 %all-to-all-done.y_in = f32[4,136,1024]{2,1,0:T(8,128)S(1)} async-done(((f32[4,136,1024]{2,1,0:T(8,128)}), f32[4,136,1024]{2,1,0:T(8,128)S(1)}, u32[]{:S(2)}, u32[]{:S(2)}) %all-to-all-start) | async-done | bytes 2228256 | tf_op jit(solution)/shard_map/all_to_all | solution.py:371
  38.3 3.5 %shard_map.95 = (f32[256,256]{1,0:T(8,128)}, f32[256,256]{1,0:T(8,128)}, f32[264,1024]{1,0:T(8,128)}, f32[4,264,256]{2,1,0:T(8,128)}) custom-call(s32[4]{0:T(128)S(1)} %pad_add_fusion.where, s32[1,5]{1,0:T(1,128)S(1)} %copy-done.5, f32[4,136,1024]{2,1,0:T(8,128)S(1)} %all-to-all-done.y_in, f32[64,1024]{1,0:T(8,128)} %get-tuple-element.29.x0, ...), custom_call_target="tpu_custom_call" | custom-call | flops 134217728 | bytes 5984256 | tf_op jit(solution)/shard_map/pallas_call | solution.py:354
  43.7 4.4 %all-to-all-start.1 = ((f32[4,264,256]{2,1,0:T(8,128)}), f32[4,264,256]{2,1,0:T(8,128)S(1)}, u32[]{:S(2)}, u32[]{:S(2)}) async-start(f32[4,264,256]{2,1,0:T(8,128)} %get-tuple-element.31), calls=%async_computation.1 | async-start | bytes 2162688 | tf_op jit(solution)/shard_map/all_to_all | solution.py:371
  50.1 9.3 %collective-permute-done.3.e0 = f32[256,256]{1,0:T(8,128)S(1)} collective-permute-done((f32[256,256]{1,0:T(8,128)S(1)}, f32[256,256]{1,0:T(8,128)S(1)}, u32[]{:S(2)}, u32[]{:S(2)}) %collective-permute-start.3) | collective-permute-done | bytes 262176 | tf_op jit(solution)/shard_map/ppermute | solution.py:367
  59.4 2.5 %collective-permute-start.6 = (f32[256,256]{1,0:T(8,128)S(1)}, f32[256,256]{1,0:T(8,128)S(1)}, u32[]{:S(2)}, u32[]{:S(2)}) collective-permute-start(f32[256,256]{1,0:T(8,128)S(1)} %collective-permute-done.3.e0), channel_id=1, source_target_pairs={{0,8},{4,12},{8,0},{12,4},{1,9},{5,13},{9,1},{13,5},{2,10},{6,14},... | collective-permute-start | bytes 786440 | tf_op jit(solution)/shard_map/ppermute | solution.py:377
  61.8 4.6 %collective-permute-start.5 = (f32[256,256]{1,0:T(8,128)S(1)}, f32[256,256]{1,0:T(8,128)S(1)}, u32[]{:S(2)}, u32[]{:S(2)}) collective-permute-start(f32[256,256]{1,0:T(8,128)S(1)} %collective-permute-done.3.e0), channel_id=1, source_target_pairs={{0,12},{4,0},{8,4},{12,8},{1,13},{5,1},{9,5},{13,9},{2,14},{6,2},{... | collective-permute-start | bytes 786440 | tf_op jit(solution)/shard_map/ppermute | solution.py:377
  69.4 4.2 %shard_map.96 = (bf16[256,1024]{1,0:T(8,128)(2,1)}, bf16[256,1024]{1,0:T(8,128)(2,1)}, bf16[256,1024]{1,0:T(8,128)(2,1)}, bf16[256,1024]{1,0:T(8,128)(2,1)}) custom-call(s32[8]{0:T(128)S(1)} %fusion.offsets, f32[264,1024]{1,0:T(8,128)} %copy-done.6), custom_call_target="tpu_custom_call" | custom-call | bytes 1081344 | tf_op jit(solution)/shard_map/pallas_call | solution.py:354
  74.2 2.3 %collective-permute-done.4.e1 = f32[256,256]{1,0:T(8,128)S(1)} collective-permute-done((f32[256,256]{1,0:T(8,128)S(1)}, f32[256,256]{1,0:T(8,128)S(1)}, u32[]{:S(2)}, u32[]{:S(2)}) %collective-permute-start.4) | collective-permute-done | bytes 262176 | tf_op jit(solution)/shard_map/ppermute | solution.py:377
  78.2 3.5 %shard_map.97 = (f32[256,256]{1,0:T(8,128)}, f32[4,256,256]{2,1,0:T(8,128)}, f32[8,256]{1,0:T(8,128)}, f32[8,1024]{1,0:T(8,128)}, bf16[256,1024]{1,0:T(8,128)(2,1)}, /*index=5*/bf16[256,1024]{1,0:T(8,128)(2,1)}) custom-call(s32[4]{0:T(128)S(1)} %pad_add_fusion.where, s32[1,5]{1,0:T(1,128)S(1)} %copy-done.5, f32[5,1024]{1,0:T(8,128)} %bitcast.17, ...), custom_call_target="tpu_custom_call" | custom-call | flops 134217728 | bytes 3764224 | tf_op jit(solution)/shard_map/pallas_call | solution.py:354
  81.8 4.7 %all-to-all-start.2 = ((f32[4,256,256]{2,1,0:T(8,128)}), f32[4,256,256]{2,1,0:T(8,128)S(1)}, u32[]{:S(2)}, u32[]{:S(2)}) async-start(f32[4,256,256]{2,1,0:T(8,128)} %get-tuple-element.37), calls=%async_computation.2 | async-start | bytes 2097152 | tf_op jit(solution)/shard_map/all_to_all | solution.py:371
  86.5 2.4 %collective-permute-start.11 = (f32[256,256]{1,0:T(8,128)S(1)}, f32[256,256]{1,0:T(8,128)S(1)}, u32[]{:S(2)}, u32[]{:S(2)}) collective-permute-start(f32[256,256]{1,0:T(8,128)S(1)} %copy-done.9), channel_id=1, source_target_pairs={{0,8},{4,12},{8,0},{12,4},{1,9},{5,13},{9,1},{13,5},{2,10},{6,14},... | collective-permute-start | bytes 786440 | tf_op jit(solution)/shard_map/ppermute | solution.py:377
  88.9 5.0 %collective-permute-start.10 = (f32[256,256]{1,0:T(8,128)S(1)}, f32[256,256]{1,0:T(8,128)S(1)}, u32[]{:S(2)}, u32[]{:S(2)}) collective-permute-start(f32[256,256]{1,0:T(8,128)S(1)} %copy-done.9), channel_id=1, source_target_pairs={{0,12},{4,0},{8,4},{12,8},{1,13},{5,1},{9,5},{13,9},{2,14},{6,2},{... | collective-permute-start | bytes 786440 | tf_op jit(solution)/shard_map/ppermute | solution.py:377
  95.9 2.4 %collective-permute-start.12 = (f32[256,256]{1,0:T(8,128)S(1)}, f32[256,256]{1,0:T(8,128)S(1)}, u32[]{:S(2)}, u32[]{:S(2)}) collective-permute-start(f32[256,256]{1,0:T(8,128)S(1)} %copy-done.7), channel_id=1, source_target_pairs={{32,0},{48,16},{64,32},{80,48},{96,64},{112,80},{128,96},{144,112}... | collective-permute-start | bytes 786440 | tf_op jit(solution)/shard_map/ppermute | solution.py:367
  100.3 2.7 %collective-permute-done.10.e2 = f32[256,256]{1,0:T(8,128)S(1)} collective-permute-done((f32[256,256]{1,0:T(8,128)S(1)}, f32[256,256]{1,0:T(8,128)S(1)}, u32[]{:S(2)}, u32[]{:S(2)}) %collective-permute-start.10) | collective-permute-done | bytes 262176 | tf_op jit(solution)/shard_map/ppermute | solution.py:377
  104.8 2.4 %collective-permute-done.12.gain_2_later = f32[256,256]{1,0:T(8,128)S(1)} collective-permute-done((f32[256,256]{1,0:T(8,128)S(1)}, f32[256,256]{1,0:T(8,128)S(1)}, u32[]{:S(2)}, u32[]{:S(2)}) %collective-permute-start.12) | collective-permute-done | bytes 262176 | tf_op jit(solution)/shard_map/ppermute | solution.py:367
  107.8 6.0 %shard_map.98 = (f32[4,256,256]{2,1,0:T(8,128)}, f32[8,256]{1,0:T(8,128)}, f32[512,256]{1,0:T(8,128)}, bf16[256,1024]{1,0:T(8,128)(2,1)}, bf16[256,1024]{1,0:T(8,128)(2,1)}) custom-call(s32[4]{0:T(128)S(1)} %pad_add_fusion.where, bf16[256,1024]{1,0:T(8,128)(2,1)} %get-tuple-element.35.wide_high, bf16[256,1024]{1,0:T(8,128)(2,1)} %get-tuple-element.36.wide_low, ...), custom_call_target="tpu_custom_call" | custom-call | flops 402653184 | bytes 11059200 | tf_op jit(solution)/shard_map/pallas_call | solution.py:354
  113.9 4.7 %all-to-all-start.3 = ((f32[4,256,256]{2,1,0:T(8,128)}), f32[4,256,256]{2,1,0:T(8,128)S(1)}, u32[]{:S(2)}, u32[]{:S(2)}) async-start(f32[4,256,256]{2,1,0:T(8,128)} %get-tuple-element.46), calls=%async_computation.3 | async-start | bytes 2097152 | tf_op jit(solution)/shard_map/all_to_all | solution.py:371
  118.5 5.0 %collective-permute-start.16 = (f32[512,256]{1,0:T(8,128)S(1)}, f32[512,256]{1,0:T(8,128)S(1)}, u32[]{:S(2)}, u32[]{:S(2)}) collective-permute-start(f32[512,256]{1,0:T(8,128)S(1)} %copy-done.10), channel_id=1, source_target_pairs={{0,8},{4,12},{8,0},{12,4},{1,9},{5,13},{9,1},{13,5},{2,10},{6,14},... | collective-permute-start | bytes 1572872 | tf_op jit(solution)/shard_map/ppermute | solution.py:377
  123.5 2.8 %collective-permute-start.15 = (f32[512,256]{1,0:T(8,128)S(1)}, f32[512,256]{1,0:T(8,128)S(1)}, u32[]{:S(2)}, u32[]{:S(2)}) collective-permute-start(f32[512,256]{1,0:T(8,128)S(1)} %copy-done.10), channel_id=1, source_target_pairs={{0,12},{4,0},{8,4},{12,8},{1,13},{5,1},{9,5},{13,9},{2,14},{6,2},{... | collective-permute-start | bytes 1572872 | tf_op jit(solution)/shard_map/ppermute | solution.py:377
  126.3 3.0 %collective-permute-start.14 = (f32[512,256]{1,0:T(8,128)S(1)}, f32[512,256]{1,0:T(8,128)S(1)}, u32[]{:S(2)}, u32[]{:S(2)}) collective-permute-start(f32[512,256]{1,0:T(8,128)S(1)} %copy-done.10), channel_id=1, source_target_pairs={{0,4},{4,8},{8,12},{12,0},{1,5},{5,9},{9,13},{13,1},{2,6},{6,10},{... | collective-permute-start | bytes 1572872 | tf_op jit(solution)/shard_map/ppermute | solution.py:377
  129.4 4.6 %all-to-all-done.3.parts = f32[4,256,256]{2,1,0:T(8,128)S(1)} async-done(((f32[4,256,256]{2,1,0:T(8,128)}), f32[4,256,256]{2,1,0:T(8,128)S(1)}, u32[]{:S(2)}, u32[]{:S(2)}) %all-to-all-start.3) | async-done | bytes 1048608 | tf_op jit(solution)/shard_map/all_to_all | solution.py:371
  137.5 9.7 %collective-permute-done.15.p2.a2 = f32[512,256]{1,0:T(8,128)S(1)} collective-permute-done((f32[512,256]{1,0:T(8,128)S(1)}, f32[512,256]{1,0:T(8,128)S(1)}, u32[]{:S(2)}, u32[]{:S(2)}) %collective-permute-start.15) | collective-permute-done | bytes 524320 | tf_op jit(solution)/shard_map/ppermute | solution.py:377
  148.6 19.5 %all_to_all.30.y_in = f32[4,264,256]{2,1,0:T(8,128)S(1)} all-to-all(f32[4,264,256]{2,1,0:T(8,128)} %shard_map.100), channel_id=1, replica_groups=mesh['tm'=32,'y'=4,'x'=4] {'y'}, dimensions={0} | all-to-all | bytes 2162688 | tf_op jit(solution)/shard_map/all_to_all | solution.py:371
  168.1 5.1 %shard_map.101 = (f32[4,64,1280]{2,1,0:T(8,128)}, f32[8,256]{1,0:T(8,128)}) custom-call(s32[4]{0:T(128)S(1)} %pad_add_fusion.where, f32[256,256]{1,0:T(8,128)} %get-tuple-element.34.gain_2, bf16[256,1024]{1,0:T(8,128)(2,1)} %get-tuple-element.44.wide_high, bf16[256,1024]{1,0:T(8,128)(2,1)} %get-tuple-element.45.wide_low, f32[264,256]{1,0:T(8,128)} %shard_map.99.spread, ...), custom_call_target="tpu_custom_call" | custom-call | flops 402653184 | bytes 7127040 | tf_op jit(solution)/shard_map/pallas_call | solution.py:354
  173.2 4.5 %all-to-all-start.5 = ((f32[4,64,1280]{2,1,0:T(8,128)}), f32[4,64,1280]{2,1,0:T(8,128)S(1)}, u32[]{:S(2)}, u32[]{:S(2)}) async-start(f32[4,64,1280]{2,1,0:T(8,128)} %get-tuple-element.49), calls=%async_computation.5 | async-start | bytes 2621440 | tf_op jit(solution)/shard_map/all_to_all | solution.py:371
  179.0 15.3 %all-to-all-done.5.x_in = f32[4,64,1280]{2,1,0:T(8,128)S(1)} async-done(((f32[4,64,1280]{2,1,0:T(8,128)}), f32[4,64,1280]{2,1,0:T(8,128)S(1)}, u32[]{:S(2)}, u32[]{:S(2)}) %all-to-all-start.5) | async-done | bytes 1310752 | tf_op jit(solution)/shard_map/all_to_all | solution.py:371
  (77 shorter events, 26.2 us)
Async XLA Ops:
  6.0 32.3 %copy-start.5 = (s32[1,5]{1,0:T(1,128)S(1)}, s32[1,5]{1,0:T(1,128)}, u32[]{:S(2)}) copy-start(s32[1,5]{1,0:T(1,128)} %offsets.5) | copy-start | bytes 64
  6.0 32.3 %all-to-all-start = ((f32[4,136,1024]{2,1,0:T(8,128)}), f32[4,136,1024]{2,1,0:T(8,128)S(1)}, u32[]{:S(2)}, u32[]{:S(2)}) async-start(f32[4,136,1024]{2,1,0:T(8,128)} %get-tuple-element.28), calls=%async_computation | async-start | bytes 4456448 | tf_op jit(solution)/shard_map/all_to_all | solution.py:371
  10.6 11.2 %collective-permute-start.2 = (f32[64,1024]{1,0:T(8,128)S(1)}, f32[64,1024]{1,0:T(8,128)S(1)}, u32[]{:S(2)}, u32[]{:S(2)}) collective-permute-start(f32[64,1024]{1,0:T(8,128)S(1)} %copy-done.11), channel_id=1, source_target_pairs={{0,2},{1,3},{2,0},{3,1},{4,6},{5,7},{6,4},{7,5},{8,10},{9,11},{10,... | collective-permute-start | bytes 786440 | tf_op jit(solution)/shard_map/ppermute | solution.py:377
  15.5 11.9 %collective-permute-start.1 = (f32[64,1024]{1,0:T(8,128)S(1)}, f32[64,1024]{1,0:T(8,128)S(1)}, u32[]{:S(2)}, u32[]{:S(2)}) collective-permute-start(f32[64,1024]{1,0:T(8,128)S(1)} %copy-done.11), channel_id=1, source_target_pairs={{0,3},{1,0},{2,1},{3,2},{4,7},{5,4},{6,5},{7,6},{8,11},{9,8},{10,9... | collective-permute-start | bytes 786440 | tf_op jit(solution)/shard_map/ppermute | solution.py:377
  18.6 10.3 %collective-permute-start = (f32[64,1024]{1,0:T(8,128)S(1)}, f32[64,1024]{1,0:T(8,128)S(1)}, u32[]{:S(2)}, u32[]{:S(2)}) collective-permute-start(f32[64,1024]{1,0:T(8,128)S(1)} %copy-done.11), channel_id=1, source_target_pairs={{0,1},{1,2},{2,3},{3,0},{4,5},{5,6},{6,7},{7,4},{8,9},{9,10},{10,1... | collective-permute-start | bytes 786440 | tf_op jit(solution)/shard_map/ppermute | solution.py:377
  21.7 16.6 %copy-start.12 = (f32[64,1024]{1,0:T(8,128)}, f32[64,1024]{1,0:T(8,128)S(1)}, u32[]{:S(2)}) copy-start(f32[64,1024]{1,0:T(8,128)S(1)} %collective-permute-done.2.x3) | copy-start | bytes 786436
  27.4 10.9 %copy-start.13 = (f32[64,1024]{1,0:T(8,128)}, f32[64,1024]{1,0:T(8,128)S(1)}, u32[]{:S(2)}) copy-start(f32[64,1024]{1,0:T(8,128)S(1)} %collective-permute-done.1.x2) | copy-start | bytes 786436
  28.9 9.4 %copy-start.14 = (f32[64,1024]{1,0:T(8,128)}, f32[64,1024]{1,0:T(8,128)S(1)}, u32[]{:S(2)}) copy-start(f32[64,1024]{1,0:T(8,128)S(1)} %collective-permute-done.x1) | copy-start | bytes 786436
  41.8 26.6 %collective-permute-start.7 = (f32[264,1024]{1,0:T(8,128)}, f32[264,1024]{1,0:T(8,128)S(1)}, u32[]{:S(2)}, u32[]{:S(2)}) collective-permute-start(f32[264,1024]{1,0:T(8,128)} %get-tuple-element.32), channel_id=1, source_target_pairs={{16,0},{32,16},{48,32},{64,48},{80,64},{96,80},{112,96},{128,112},... | collective-permute-start | bytes 3244040 | tf_op jit(solution)/shard_map/ppermute | solution.py:367
  43.7 32.8 %all-to-all-start.1 = ((f32[4,264,256]{2,1,0:T(8,128)}), f32[4,264,256]{2,1,0:T(8,128)S(1)}, u32[]{:S(2)}, u32[]{:S(2)}) async-start(f32[4,264,256]{2,1,0:T(8,128)} %get-tuple-element.31), calls=%async_computation.1 | async-start | bytes 2162688 | tf_op jit(solution)/shard_map/all_to_all | solution.py:371
  48.1 11.2 %collective-permute-start.3 = (f32[256,256]{1,0:T(8,128)S(1)}, f32[256,256]{1,0:T(8,128)S(1)}, u32[]{:S(2)}, u32[]{:S(2)}) collective-permute-start(f32[256,256]{1,0:T(8,128)S(1)} %copy-done.8), channel_id=1, source_target_pairs={{16,0},{32,16},{48,32},{64,48},{80,64},{96,80},{112,96},{128,112},... | collective-permute-start | bytes 786440 | tf_op jit(solution)/shard_map/ppermute | solution.py:367
  59.4 17.1 %copy-start.19 = (f32[256,256]{1,0:T(8,128)}, f32[256,256]{1,0:T(8,128)S(1)}, u32[]{:S(2)}) copy-start(f32[256,256]{1,0:T(8,128)S(1)} %collective-permute-done.3.e0) | copy-start | bytes 786436
  59.4 14.2 %collective-permute-start.6 = (f32[256,256]{1,0:T(8,128)S(1)}, f32[256,256]{1,0:T(8,128)S(1)}, u32[]{:S(2)}, u32[]{:S(2)}) collective-permute-start(f32[256,256]{1,0:T(8,128)S(1)} %collective-permute-done.3.e0), channel_id=1, source_target_pairs={{0,8},{4,12},{8,0},{12,4},{1,9},{5,13},{9,1},{13,5},{2,10},{6,14},... | collective-permute-start | bytes 786440 | tf_op jit(solution)/shard_map/ppermute | solution.py:377
  61.8 12.3 %collective-permute-start.5 = (f32[256,256]{1,0:T(8,128)S(1)}, f32[256,256]{1,0:T(8,128)S(1)}, u32[]{:S(2)}, u32[]{:S(2)}) collective-permute-start(f32[256,256]{1,0:T(8,128)S(1)} %collective-permute-done.3.e0), channel_id=1, source_target_pairs={{0,12},{4,0},{8,4},{12,8},{1,13},{5,1},{9,5},{13,9},{2,14},{6,2},{... | collective-permute-start | bytes 786440 | tf_op jit(solution)/shard_map/ppermute | solution.py:377
  66.4 10.1 %collective-permute-start.4 = (f32[256,256]{1,0:T(8,128)S(1)}, f32[256,256]{1,0:T(8,128)S(1)}, u32[]{:S(2)}, u32[]{:S(2)}) collective-permute-start(f32[256,256]{1,0:T(8,128)S(1)} %collective-permute-done.3.e0), channel_id=1, source_target_pairs={{0,4},{4,8},{8,12},{12,0},{1,5},{5,9},{9,13},{13,1},{2,6},{6,10},{... | collective-permute-start | bytes 786440 | tf_op jit(solution)/shard_map/ppermute | solution.py:377
  81.8 4.7 %copy-start.9 = (f32[256,256]{1,0:T(8,128)S(1)}, f32[256,256]{1,0:T(8,128)}, u32[]{:S(2)}) copy-start(f32[256,256]{1,0:T(8,128)} %get-tuple-element.30.gain.e0) | copy-start | bytes 786436
  81.8 14.1 %copy-start.7 = (f32[256,256]{1,0:T(8,128)S(1)}, f32[256,256]{1,0:T(8,128)}, u32[]{:S(2)}) copy-start(f32[256,256]{1,0:T(8,128)} %get-tuple-element.34.gain_2) | copy-start | bytes 786436
  81.8 16.5 %copy-start.24 = (f32[8,1024]{1,0:T(8,128)S(1)}, f32[8,1024]{1,0:T(8,128)}, u32[]{:S(2)}) copy-start(f32[8,1024]{1,0:T(8,128)} %get-tuple-element.41) | copy-start | bytes 98308
  81.8 25.3 %all-to-all-start.2 = ((f32[4,256,256]{2,1,0:T(8,128)}), f32[4,256,256]{2,1,0:T(8,128)S(1)}, u32[]{:S(2)}, u32[]{:S(2)}) async-start(f32[4,256,256]{2,1,0:T(8,128)} %get-tuple-element.37), calls=%async_computation.2 | async-start | bytes 2097152 | tf_op jit(solution)/shard_map/all_to_all | solution.py:371
  86.5 13.7 %collective-permute-start.11 = (f32[256,256]{1,0:T(8,128)S(1)}, f32[256,256]{1,0:T(8,128)S(1)}, u32[]{:S(2)}, u32[]{:S(2)}) collective-permute-start(f32[256,256]{1,0:T(8,128)S(1)} %copy-done.9), channel_id=1, source_target_pairs={{0,8},{4,12},{8,0},{12,4},{1,9},{5,13},{9,1},{13,5},{2,10},{6,14},... | collective-permute-start | bytes 786440 | tf_op jit(solution)/shard_map/ppermute | solution.py:377
  88.9 14.1 %collective-permute-start.10 = (f32[256,256]{1,0:T(8,128)S(1)}, f32[256,256]{1,0:T(8,128)S(1)}, u32[]{:S(2)}, u32[]{:S(2)}) collective-permute-start(f32[256,256]{1,0:T(8,128)S(1)} %copy-done.9), channel_id=1, source_target_pairs={{0,12},{4,0},{8,4},{12,8},{1,13},{5,1},{9,5},{13,9},{2,14},{6,2},{... | collective-permute-start | bytes 786440 | tf_op jit(solution)/shard_map/ppermute | solution.py:377
  93.9 10.8 %collective-permute-start.9 = (f32[256,256]{1,0:T(8,128)S(1)}, f32[256,256]{1,0:T(8,128)S(1)}, u32[]{:S(2)}, u32[]{:S(2)}) collective-permute-start(f32[256,256]{1,0:T(8,128)S(1)} %copy-done.9), channel_id=1, source_target_pairs={{0,4},{4,8},{8,12},{12,0},{1,5},{5,9},{9,13},{13,1},{2,6},{6,10},{... | collective-permute-start | bytes 786440 | tf_op jit(solution)/shard_map/ppermute | solution.py:377
  95.9 11.3 %collective-permute-start.12 = (f32[256,256]{1,0:T(8,128)S(1)}, f32[256,256]{1,0:T(8,128)S(1)}, u32[]{:S(2)}, u32[]{:S(2)}) collective-permute-start(f32[256,256]{1,0:T(8,128)S(1)} %copy-done.7), channel_id=1, source_target_pairs={{32,0},{48,16},{64,32},{80,48},{96,64},{112,80},{128,96},{144,112}... | collective-permute-start | bytes 786440 | tf_op jit(solution)/shard_map/ppermute | solution.py:367
  98.3 6.4 %collective-permute-start.8 = (f32[8,1024]{1,0:T(8,128)S(1)}, f32[8,1024]{1,0:T(8,128)S(1)}, u32[]{:S(2)}, u32[]{:S(2)}) collective-permute-start(f32[8,1024]{1,0:T(8,128)S(1)} %copy-done.24), channel_id=1, source_target_pairs={{16,0},{32,16},{48,32},{64,48},{80,64},{96,80},{112,96},{128,112},... | collective-permute-start | bytes 98312 | tf_op jit(solution)/shard_map/ppermute | solution.py:367
  100.3 6.9 %copy-start.15 = (f32[256,256]{1,0:T(8,128)}, f32[256,256]{1,0:T(8,128)S(1)}, u32[]{:S(2)}) copy-start(f32[256,256]{1,0:T(8,128)S(1)} %collective-permute-done.11.e3) | copy-start | bytes 786436
  113.9 20.1 %all-to-all-start.3 = ((f32[4,256,256]{2,1,0:T(8,128)}), f32[4,256,256]{2,1,0:T(8,128)S(1)}, u32[]{:S(2)}, u32[]{:S(2)}) async-start(f32[4,256,256]{2,1,0:T(8,128)} %get-tuple-element.46), calls=%async_computation.3 | async-start | bytes 2097152 | tf_op jit(solution)/shard_map/all_to_all | solution.py:371
  118.5 18.9 %collective-permute-start.16 = (f32[512,256]{1,0:T(8,128)S(1)}, f32[512,256]{1,0:T(8,128)S(1)}, u32[]{:S(2)}, u32[]{:S(2)}) collective-permute-start(f32[512,256]{1,0:T(8,128)S(1)} %copy-done.10), channel_id=1, source_target_pairs={{0,8},{4,12},{8,0},{12,4},{1,9},{5,13},{9,1},{13,5},{2,10},{6,14},... | collective-permute-start | bytes 1572872 | tf_op jit(solution)/shard_map/ppermute | solution.py:377
  123.5 23.7 %collective-permute-start.15 = (f32[512,256]{1,0:T(8,128)S(1)}, f32[512,256]{1,0:T(8,128)S(1)}, u32[]{:S(2)}, u32[]{:S(2)}) collective-permute-start(f32[512,256]{1,0:T(8,128)S(1)} %copy-done.10), channel_id=1, source_target_pairs={{0,12},{4,0},{8,4},{12,8},{1,13},{5,1},{9,5},{13,9},{2,14},{6,2},{... | collective-permute-start | bytes 1572872 | tf_op jit(solution)/shard_map/ppermute | solution.py:377
  126.3 20.9 %collective-permute-start.14 = (f32[512,256]{1,0:T(8,128)S(1)}, f32[512,256]{1,0:T(8,128)S(1)}, u32[]{:S(2)}, u32[]{:S(2)}) collective-permute-start(f32[512,256]{1,0:T(8,128)S(1)} %copy-done.10), channel_id=1, source_target_pairs={{0,4},{4,8},{8,12},{12,0},{1,5},{5,9},{9,13},{13,1},{2,6},{6,10},{... | collective-permute-start | bytes 1572872 | tf_op jit(solution)/shard_map/ppermute | solution.py:377
  135.5 11.7 %collective-permute-start.13 = (f32[264,256]{1,0:T(8,128)}, f32[264,256]{1,0:T(8,128)S(1)}, u32[]{:S(2)}, u32[]{:S(2)}) collective-permute-start(f32[264,256]{1,0:T(8,128)} %shard_map.99.spread), channel_id=1, source_target_pairs={{32,0},{48,16},{64,32},{80,48},{96,64},{112,80},{128,96},{144,112}... | collective-permute-start | bytes 811016 | tf_op jit(solution)/shard_map/ppermute | solution.py:367
  137.5 10.9 %copy-start.1 = (f32[512,256]{1,0:T(8,128)}, f32[512,256]{1,0:T(8,128)S(1)}, u32[]{:S(2)}) copy-start(f32[512,256]{1,0:T(8,128)S(1)} %collective-permute-done.16.p3.a3) | copy-start | bytes 1572868
  173.2 21.1 %all-to-all-start.5 = ((f32[4,64,1280]{2,1,0:T(8,128)}), f32[4,64,1280]{2,1,0:T(8,128)S(1)}, u32[]{:S(2)}, u32[]{:S(2)}) async-start(f32[4,64,1280]{2,1,0:T(8,128)} %get-tuple-element.49), calls=%async_computation.5 | async-start | bytes 2621440 | tf_op jit(solution)/shard_map/all_to_all | solution.py:371
  (15 other events, 34.6 us)

commit v8 on v6

--- a/solution.py
+++ b/solution.py
@@ -155,9 +155,7 @@
     return jnp.where(low, parts[0], parts[1]), jnp.where(low, parts[2], parts[3])
 
 
-def first_gain(
-    where, offsets, y_in, x0, x1, x2, x3, weights, gain_out, block_out, c_out, x_out, crossed
-):
+def first_gain(where, y_in, x0, x1, x2, x3, gain_out, block_out, x_out, crossed):
     rows = x0.shape[0]
     panel = SIDE * rows
     place_rows((x0, x1, x2, x3), where[1], crossed)
@@ -174,19 +172,11 @@
     first, second = pick_chunks(crossed, where[1])
     block_out[:, 0:LANES] = first
     block_out[:, LANES:] = second
-    for i in range(SIDE):
-        c_out[i * rows : (i + 1) * rows, :] = y_in[i, rows : 2 * rows, :]
-    lane = lax.broadcasted_iota(jnp.int32, (1, c_out.shape[1]), 1)
-    held = jnp.zeros((1, c_out.shape[1]), jnp.int32)
-    for b in range(NBAND):
-        held = jnp.where(lane == b, offsets[0, b], held)
-    c_out[panel:, :] = jnp.broadcast_to(held.astype(F32), (8, c_out.shape[1]))
-    c_out[panel : panel + NBAND, :] = weights[...]
 
 
 def second_gain(
-    where, offsets, weights, gain, x_in, e0, e1, e2, e3, unread,
-    gain_out, x_out, shift_out, rows_out, high_out, low_out, tall,
+    where, offsets, weights, gain, x_in, e0, e1, e2, e3, y_in,
+    gain_out, x_out, shift_out, c_out, high_out, low_out, tall,
 ):
     panel = gain.shape[0]
     at_y = where[0]
@@ -206,14 +196,24 @@
     for i in range(SIDE):
         mine = mine + jnp.where(at_y == i, natural[0:1, i * panel : (i + 1) * panel], 0.0)
     shift_out[...] = jnp.broadcast_to(mine - row_times(forward[0:1], gain_wide), (8, panel))
-    rows_out[0:4, :] = filtered[0:4]
-    rows_out[4:, :] = forward[0:4]
-
-
-def later_inputs(offsets, c_in, own_high, own_low, crossed_high, crossed_low):
+    rows = panel // SIDE
+    for i in range(SIDE):
+        c_out[i * rows : (i + 1) * rows, :] = y_in[i, rows : 2 * rows, :]
+    c_out[panel : panel + NBAND, :] = weights[...]
+    c_out[panel + NBAND : panel + NBAND + 1, :] = filtered[0:1]
+    c_out[panel + NBAND + 1 : panel + NBAND + 2, :] = forward[0:1]
+    lane = lax.broadcasted_iota(jnp.int32, (1, c_out.shape[1]), 1)
+    held = jnp.zeros((1, c_out.shape[1]), jnp.int32)
+    for b in range(NBAND):
+        held = jnp.where(lane == b, offsets[0, b], held)
+    c_out[panel + NBAND + 2 : panel + NBAND + 3, :] = held.astype(F32)
+
+
+def later_inputs(offsets, c_in, rows_out, own_high, own_low, crossed_high, crossed_low):
     panel, columns = own_high.shape
     matrix = c_in[0:panel, :]
     weights = c_in[panel : panel + NBAND, :]
+    rows_out[...] = c_in[panel:, :]
     high, low = halves(matrix)
     reach = 3 * LANES
     ahead = (
@@ -245,8 +245,8 @@
 
 def first_spread(
     where, wide_high, wide_low, gain_2_in, own_high, own_low, crossed_high, crossed_low,
-    later_rows, block, own, e0, e1, e2, e3, shift, gain_2, gain_2_later,
-    part_out, shift_out, pair_out, high_out, low_out, tall,
+    block, own, e0, e1, e2, e3, gain_2, gain_2_later,
+    part_out, pair_out, high_out, low_out, tall,
 ):
     panel = e0.shape[0]
     at_y = where[0]
@@ -260,11 +260,7 @@
     turned = three(gain_wide, (own_high[...], own_low[...]), across) - three(
         gain_2_wide, (crossed_high[...], crossed_low[...]), across
     )
-    moved = row_times(later_rows[0:1, :], gain_wide) - row_times(
-        later_rows[4:5, :], gain_2_wide
-    )
     inside = where[2] == 1
-    shift_out[...] = shift[...] + jnp.where(inside, moved, 0.0)
     turned = halves(jnp.where(inside, turned, 0.0) - block[...])
     place_tall((e0, e1, e2, e3), at_y, tall)
     twice = jnp.concatenate(swap_tiles(tiles(jnp.concatenate([own[...]] * 2, axis=0))), axis=1)
@@ -274,6 +270,13 @@
         part_out[i] = three(halves(tall[i * panel : (i + 1) * panel, :]), turned, across)
         turned_own = twice[:, i * panel : (i + 1) * panel].T
         part_out[i, :, pl.ds(at_x, LANES)] += jnp.where(mine, turned_own, 0.0)
+
+
+def later_shift(where, high, low, high_2, low_2, later_rows, shift, out):
+    moved = row_times(later_rows[NBAND : NBAND + 1, :], (high[...], low[...])) - row_times(
+        later_rows[NBAND + 1 : NBAND + 2, :], (high_2[...], low_2[...])
+    )
+    out[...] = shift[...] + jnp.where(where[2] == 1, moved, 0.0)
 
 
 def join_spread(parts, shift, out):
@@ -418,47 +421,52 @@
     )
     y_in = swap(y_message, "y")
     crossed_pieces = ring(crossed, "x")
-    gain, crossed_block, c_message, x_message = call(
+    gain, crossed_block, x_message = call(
         first_gain,
-        (where, band_offset),
-        (y_in, *far(*crossed_pieces, weights)),
-        ((panel, panel), (panel, panel), (panel + 8, columns), (SIDE, panel + 8, panel)),
+        (where,),
+        (y_in, *far(*crossed_pieces)),
+        ((panel, panel), (panel, panel), (SIDE, panel + 8, panel)),
         ((panel, columns),),
         unit,
     )
     gain_in = swap(x_message, "x")
     later_pieces = ring_shifted(gain, 1)
-    c_in = shifted(c_message, 1)
-    next_offsets = c_in[panel + NBAND, 0:8].astype(jnp.int32)
-    gain_2, x_message, shift, rows_message, wide_high, wide_low = call(
+    gain_2, x_message, shift, c_message, wide_high, wide_low = call(
         second_gain,
         (where, band_offset),
-        (*far(weights, gain), gain_in, *far(*later_pieces)),
-        ((panel, panel), (SIDE, panel, panel), (8, panel), (8, columns)),
+        (*far(weights, gain), gain_in, *far(*later_pieces), y_in),
+        ((panel, panel), (SIDE, panel, panel), (8, panel), (panel + 8, columns)),
         ((columns, panel),),
         unit,
-        unread=(c_in,),
         coarse=((panel, columns),) * 2,
     )
     gain_2_in = swap(x_message, "x")
     gain_pieces = ring(gain, "y")
     gain_2_later = shifted(gain_2, 2)
-    later_rows = shifted(rows_message, 1)
-    later_halves = call(
-        later_inputs, (next_offsets,), far(c_in), (), coarse=((panel, columns),) * 4
-    )
-    part, shift_2, gain_2_pair, wide_high, wide_low = call(
+    c_in = shifted(c_message, 1)
+    next_offsets = c_in[panel + NBAND + 2, 0:8].astype(jnp.int32)
+    later_rows, *later_halves = call(
+        later_inputs, (next_offsets,), far(c_in), ((8, columns),), coarse=((panel, columns),) * 4
+    )
+    part, gain_2_pair, wide_2_high, wide_2_low = call(
         first_spread,
         (where,),
         (
-            *far(wide_high, wide_low), gain_2_in, *far(*later_halves, later_rows, crossed_block),
-            *far(own, gain, *gain_pieces[1:], shift, gain_2, gain_2_later),
+            *far(wide_high, wide_low), gain_2_in, *far(*later_halves, crossed_block),
+            *far(own, gain, *gain_pieces[1:], gain_2, gain_2_later),
         ),
-        ((SIDE, panel, panel), (8, panel), (2 * panel, panel)),
+        ((SIDE, panel, panel), (2 * panel, panel)),
         ((columns, panel),),
         3 * unit,
         coarse=((panel, columns),) * 2,
     )
+    (shift_2,) = call(
+        later_shift,
+        (where,),
+        far(wide_high, wide_low, wide_2_high, wide_2_low, later_rows, shift),
+        ((8, panel),),
+    )
+    wide_high, wide_low = wide_2_high, wide_2_low
     parts = swap(part, "x")
     gain_2_pieces = ring(gain_2_pair, "y")
     (spread_2,) = call(join_spread, (), (parts, *far(shift_2)), ((panel + 8, panel),))

time: 189 us -> 183 us (0.968)
  the two profiles are of different devices: /device:TPU:224 before, /device:TPU:384 now
where the time goes in v8:
time: 183 us; the launch traced here: 182 us
  starting transfers between devices  75.5 us (41%)
  waiting for transfers between devices  48.8 us (27%)
  Pallas kernels  32 us (17%)
  blocking collectives  18.5 us (10%)
  local copies, waits for them, and re-layouts  5.81 us (3%)
    pallas_call x10, Pallas kernels, call(): pl.pallas_call(kernel, out_shape=shapes, in_specs=[SMEM] * len(scalars) +...  32 us
    ppermute x9, starting transfers between devices, ring(): lax.ppermute(block, axis, [(i, (i + step) % SIDE) for i in range(SIDE)])  29.5 us
    all_to_all x5, waiting for transfers between devices, swap(): return lax.all_to_all(message, axis, 0, 0)  24.2 us
    all_to_all x5, starting transfers between devices, swap(): return lax.all_to_all(message, axis, 0, 0)  22.7 us
    all_to_all x1, blocking collectives, swap(): return lax.all_to_all(message, axis, 0, 0)  18.5 us
    ppermute x9, waiting for transfers between devices, ring(): lax.ppermute(block, axis, [(i, (i + step) % SIDE) for i in range(SIDE)])  14.6 us
    ppermute x4, starting transfers between devices, ring_shifted(): pieces.append(lax.ppermute(block, ('tm', 'y'), route))  12.3 us
    ppermute x3, starting transfers between devices, shifted(): lax.ppermute(block, 'tm', [(i + distance, i) for i in range(count - dista...  11 us
  transfers between devices with their start and end apart: 21, of which 10 were waited for; matrix products, arithmetic and copies ran while one was open for 1% of the time, Pallas kernels for 5%

profile of v8, /device:TPU:384, one launch (start us, length us, event | category | flops | bytes accessed | tf_op | source)
XLA Modules:
  0.0 181.6 jit_solution(5706668607527016184)
XLA Ops:
  2.6 3.4 %shard_map.94 = (f32[64,1024]{1,0:T(8,128)}, f32[4,136,1024]{2,1,0:T(8,128)}) custom-call(s32[1,5]{1,0:T(1,128)S(1)} %copy-done.3, f32[64,1024]{1,0:T(8,128)} %bitcast.13, f32[64,1024]{1,0:T(8,128)} %bitcast.17, f32[5,1024]{1,0:T(8,128)} %bitcast.15, f32[1,64]{1,0:T(1,128)} %prior.1, f32[1,128]{1,0:T(1,128)} %innovation.1, s32[1,128]{1,0:T(1,128)} %sites.1), custom_call_target="tpu_custom_call" | custom-call | bytes 3036416 | tf_op jit(solution)/shard_map/pallas_call | solution.py:357
  6.0 4.6 %all-to-all-start = ((f32[4,136,1024]{2,1,0:T(8,128)}), f32[4,136,1024]{2,1,0:T(8,128)S(1)}, u32[]{:S(2)}, u32[]{:S(2)}) async-start(f32[4,136,1024]{2,1,0:T(8,128)} %get-tuple-element.27), calls=%async_computation | async-start | bytes 4456448 | tf_op jit(solution)/shard_map/all_to_all | solution.py:374
  10.6 3.4 %collective-permute-start = (f32[64,1024]{1,0:T(8,128)S(1)}, f32[64,1024]{1,0:T(8,128)S(1)}, u32[]{:S(2)}, u32[]{:S(2)}) collective-permute-start(f32[64,1024]{1,0:T(8,128)S(1)} %copy-done.15), channel_id=1, source_target_pairs={{0,1},{1,2},{2,3},{3,0},{4,5},{5,6},{6,7},{7,4},{8,9},{9,10},{10,1... | collective-permute-start | bytes 786440 | tf_op jit(solution)/shard_map/ppermute | solution.py:380
  14.0 3.7 %collective-permute-start.1 = (f32[64,1024]{1,0:T(8,128)S(1)}, f32[64,1024]{1,0:T(8,128)S(1)}, u32[]{:S(2)}, u32[]{:S(2)}) collective-permute-start(f32[64,1024]{1,0:T(8,128)S(1)} %copy-done.15), channel_id=1, source_target_pairs={{0,3},{1,0},{2,1},{3,2},{4,7},{5,4},{6,5},{7,6},{8,11},{9,8},{10,9... | collective-permute-start | bytes 786440 | tf_op jit(solution)/shard_map/ppermute | solution.py:380
  17.6 3.7 %collective-permute-start.2 = (f32[64,1024]{1,0:T(8,128)S(1)}, f32[64,1024]{1,0:T(8,128)S(1)}, u32[]{:S(2)}, u32[]{:S(2)}) collective-permute-start(f32[64,1024]{1,0:T(8,128)S(1)} %copy-done.15), channel_id=1, source_target_pairs={{0,2},{1,3},{2,0},{3,1},{4,6},{5,7},{6,4},{7,5},{8,10},{9,11},{10,... | collective-permute-start | bytes 786440 | tf_op jit(solution)/shard_map/ppermute | solution.py:380
  21.5 6.8 %collective-permute-done.1.x2 = f32[64,1024]{1,0:T(8,128)S(1)} collective-permute-done((f32[64,1024]{1,0:T(8,128)S(1)}, f32[64,1024]{1,0:T(8,128)S(1)}, u32[]{:S(2)}, u32[]{:S(2)}) %collective-permute-start.1) | collective-permute-done | bytes 262176 | tf_op jit(solution)/shard_map/ppermute | solution.py:380
  28.3 10.0 %all-to-all-done.y_in = f32[4,136,1024]{2,1,0:T(8,128)S(1)} async-done(((f32[4,136,1024]{2,1,0:T(8,128)}), f32[4,136,1024]{2,1,0:T(8,128)S(1)}, u32[]{:S(2)}, u32[]{:S(2)}) %all-to-all-start) | async-done | bytes 2228256 | tf_op jit(solution)/shard_map/all_to_all | solution.py:374
  38.3 3.1 %shard_map.95 = (f32[256,256]{1,0:T(8,128)}, f32[256,256]{1,0:T(8,128)}, f32[4,264,256]{2,1,0:T(8,128)}) custom-call(s32[4]{0:T(128)S(1)} %pad_add_fusion.where, f32[4,136,1024]{2,1,0:T(8,128)S(1)} %all-to-all-done.y_in, f32[64,1024]{1,0:T(8,128)} %get-tuple-element.28.x0, f32[64,1024]{1,0:T(8,128)} %copy-done.16, f32[64,1024]{1,0:T(8,128)} %copy-done.17, ...), custom_call_target="tpu_custom_call" | custom-call | flops 134217728 | bytes 4882432 | tf_op jit(solution)/shard_map/pallas_call | solution.py:357
  41.4 4.4 %all-to-all-start.1 = ((f32[4,264,256]{2,1,0:T(8,128)}), f32[4,264,256]{2,1,0:T(8,128)S(1)}, u32[]{:S(2)}, u32[]{:S(2)}) async-start(f32[4,264,256]{2,1,0:T(8,128)} %get-tuple-element.30), calls=%async_computation.1 | async-start | bytes 2162688 | tf_op jit(solution)/shard_map/all_to_all | solution.py:374
  45.9 2.1 %collective-permute-start.3 = (f32[256,256]{1,0:T(8,128)}, f32[256,256]{1,0:T(8,128)S(1)}, u32[]{:S(2)}, u32[]{:S(2)}) collective-permute-start(f32[256,256]{1,0:T(8,128)} %get-tuple-element.29.gain.e0), channel_id=1, source_target_pairs={{16,0},{20,4},{24,8},{28,12},{32,16},{36,20},{40,24},{44,28},{48,3... | collective-permute-start | bytes 786440 | tf_op jit(solution)/shard_map/ppermute | solution.py:393
  48.0 4.1 %collective-permute-start.4 = (f32[256,256]{1,0:T(8,128)}, f32[256,256]{1,0:T(8,128)S(1)}, u32[]{:S(2)}, u32[]{:S(2)}) collective-permute-start(f32[256,256]{1,0:T(8,128)} %get-tuple-element.29.gain.e0), channel_id=1, source_target_pairs={{16,4},{20,8},{24,12},{28,0},{32,20},{36,24},{40,28},{44,16},{48,3... | collective-permute-start | bytes 786440 | tf_op jit(solution)/shard_map/ppermute | solution.py:393
  52.0 4.2 %collective-permute-start.5 = (f32[256,256]{1,0:T(8,128)}, f32[256,256]{1,0:T(8,128)S(1)}, u32[]{:S(2)}, u32[]{:S(2)}) collective-permute-start(f32[256,256]{1,0:T(8,128)} %get-tuple-element.29.gain.e0), channel_id=1, source_target_pairs={{16,12},{20,0},{24,4},{28,8},{32,28},{36,16},{40,20},{44,24},{48,4... | collective-permute-start | bytes 786440 | tf_op jit(solution)/shard_map/ppermute | solution.py:393
  59.9 5.3 %collective-permute-done.5.e2 = f32[256,256]{1,0:T(8,128)S(1)} collective-permute-done((f32[256,256]{1,0:T(8,128)}, f32[256,256]{1,0:T(8,128)S(1)}, u32[]{:S(2)}, u32[]{:S(2)}) %collective-permute-start.5) | collective-permute-done | bytes 262176 | tf_op jit(solution)/shard_map/ppermute | solution.py:393
  65.9 2.7 %collective-permute-done.6.e3 = f32[256,256]{1,0:T(8,128)} collective-permute-done((f32[256,256]{1,0:T(8,128)}, f32[256,256]{1,0:T(8,128)}, u32[]{:S(2)}, u32[]{:S(2)}) %collective-permute-start.6) | collective-permute-done | bytes 262176 | tf_op jit(solution)/shard_map/ppermute | solution.py:393
  68.6 4.1 %shard_map.96 = (f32[256,256]{1,0:T(8,128)}, f32[4,256,256]{2,1,0:T(8,128)}, f32[8,256]{1,0:T(8,128)}, f32[264,1024]{1,0:T(8,128)}, bf16[256,1024]{1,0:T(8,128)(2,1)}, /*index=5*/bf16[256,1024]{1,0:T(8,128)(2,1)}) custom-call(s32[4]{0:T(128)S(1)} %pad_add_fusion.where, s32[1,5]{1,0:T(1,128)S(1)} %copy-done.4, f32[5,1024]{1,0:T(8,128)} %bitcast.16, ...), custom_call_target="tpu_custom_call" | custom-call | flops 134217728 | bytes 7041024 | tf_op jit(solution)/shard_map/pallas_call | solution.py:357
  72.6 3.6 %collective-permute-start.7 = (f32[264,1024]{1,0:T(8,128)}, f32[264,1024]{1,0:T(8,128)S(1)}, u32[]{:S(2)}, u32[]{:S(2)}) collective-permute-start(f32[264,1024]{1,0:T(8,128)} %get-tuple-element.35), channel_id=1, source_target_pairs={{16,0},{32,16},{48,32},{64,48},{80,64},{96,80},{112,96},{128,112},... | collective-permute-start | bytes 3244040 | tf_op jit(solution)/shard_map/ppermute | solution.py:370
  76.2 4.8 %all-to-all-start.2 = ((f32[4,256,256]{2,1,0:T(8,128)}), f32[4,256,256]{2,1,0:T(8,128)S(1)}, u32[]{:S(2)}, u32[]{:S(2)}) async-start(f32[4,256,256]{2,1,0:T(8,128)} %get-tuple-element.34), calls=%async_computation.2 | async-start | bytes 2097152 | tf_op jit(solution)/shard_map/all_to_all | solution.py:374
  83.0 5.0 %collective-permute-start.8 = (f32[256,256]{1,0:T(8,128)S(1)}, f32[256,256]{1,0:T(8,128)S(1)}, u32[]{:S(2)}, u32[]{:S(2)}) collective-permute-start(f32[256,256]{1,0:T(8,128)S(1)} %copy-done.7), channel_id=1, source_target_pairs={{0,4},{4,8},{8,12},{12,0},{1,5},{5,9},{9,13},{13,1},{2,6},{6,10},{... | collective-permute-start | bytes 786440 | tf_op jit(solution)/shard_map/ppermute | solution.py:380
  90.1 3.4 %collective-permute-start.11 = (f32[256,256]{1,0:T(8,128)S(1)}, f32[256,256]{1,0:T(8,128)}, u32[]{:S(2)}, u32[]{:S(2)}) collective-permute-start(f32[256,256]{1,0:T(8,128)S(1)} %copy-done.6), channel_id=1, source_target_pairs={{32,0},{48,16},{64,32},{80,48},{96,64},{112,80},{128,96},{144,112}... | collective-permute-start | bytes 786440 | tf_op jit(solution)/shard_map/ppermute | solution.py:370
  94.5 4.2 %shard_map.97 = (f32[8,1024]{1,0:T(8,128)}, bf16[256,1024]{1,0:T(8,128)(2,1)}, bf16[256,1024]{1,0:T(8,128)(2,1)}, bf16[256,1024]{1,0:T(8,128)(2,1)}, bf16[256,1024]{1,0:T(8,128)(2,1)}) custom-call(s32[8]{0:T(128)S(1)} %fusion.offsets, f32[264,1024]{1,0:T(8,128)} %copy-done.5), custom_call_target="tpu_custom_call" | custom-call | bytes 1114112 | tf_op jit(solution)/shard_map/pallas_call | solution.py:357
  99.8 5.5 %shard_map.98 = (f32[4,256,256]{2,1,0:T(8,128)}, f32[512,256]{1,0:T(8,128)}, bf16[256,1024]{1,0:T(8,128)(2,1)}, bf16[256,1024]{1,0:T(8,128)(2,1)}) custom-call(s32[4]{0:T(128)S(1)} %pad_add_fusion.where, bf16[256,1024]{1,0:T(8,128)(2,1)} %get-tuple-element.32.wide_high.high, bf16[256,1024]{1,0:T(8,128)(2,1)} %get-tuple-element.33.wide_low.low, ...), custom_call_target="tpu_custom_call" | custom-call | flops 402653184 | bytes 11010048 | tf_op jit(solution)/shard_map/pallas_call | solution.py:357
  105.3 4.7 %all-to-all-start.3 = ((f32[4,256,256]{2,1,0:T(8,128)}), f32[4,256,256]{2,1,0:T(8,128)S(1)}, u32[]{:S(2)}, u32[]{:S(2)}) async-start(f32[4,256,256]{2,1,0:T(8,128)} %get-tuple-element.43), calls=%async_computation.3 | async-start | bytes 2097152 | tf_op jit(solution)/shard_map/all_to_all | solution.py:374
  110.0 3.9 %collective-permute-start.13 = (f32[512,256]{1,0:T(8,128)S(1)}, f32[512,256]{1,0:T(8,128)S(1)}, u32[]{:S(2)}, u32[]{:S(2)}) collective-permute-start(f32[512,256]{1,0:T(8,128)S(1)} %copy-done.8), channel_id=1, source_target_pairs={{0,4},{4,8},{8,12},{12,0},{1,5},{5,9},{9,13},{13,1},{2,6},{6,10},{... | collective-permute-start | bytes 1572872 | tf_op jit(solution)/shard_map/ppermute | solution.py:380
  113.9 3.1 %collective-permute-start.14 = (f32[512,256]{1,0:T(8,128)S(1)}, f32[512,256]{1,0:T(8,128)S(1)}, u32[]{:S(2)}, u32[]{:S(2)}) collective-permute-start(f32[512,256]{1,0:T(8,128)S(1)} %copy-done.8), channel_id=1, source_target_pairs={{0,12},{4,0},{8,4},{12,8},{1,13},{5,1},{9,5},{13,9},{2,14},{6,2},{... | collective-permute-start | bytes 1572872 | tf_op jit(solution)/shard_map/ppermute | solution.py:380
  117.0 2.8 %collective-permute-start.15 = (f32[512,256]{1,0:T(8,128)S(1)}, f32[512,256]{1,0:T(8,128)S(1)}, u32[]{:S(2)}, u32[]{:S(2)}) collective-permute-start(f32[512,256]{1,0:T(8,128)S(1)} %copy-done.8), channel_id=1, source_target_pairs={{0,8},{4,12},{8,0},{12,4},{1,9},{5,13},{9,1},{13,5},{2,10},{6,14},... | collective-permute-start | bytes 1572872 | tf_op jit(solution)/shard_map/ppermute | solution.py:380
  119.8 3.1 %shard_map.99.shift = f32[8,256]{1,0:T(8,128)} custom-call(s32[4]{0:T(128)S(1)} %pad_add_fusion.where, bf16[256,1024]{1,0:T(8,128)(2,1)} %get-tuple-element.32.wide_high.high, bf16[256,1024]{1,0:T(8,128)(2,1)} %get-tuple-element.33.wide_low.low, bf16[256,1024]{1,0:T(8,128)(2,1)} %get-tuple-element.41.high_2.wide_high, ...), custom_call_target="tpu_custom_call" | custom-call | bytes 4243456 | tf_op jit(solution)/shard_map/pallas_call | solution.py:357
  125.9 4.0 %collective-permute-start.12 = (f32[264,256]{1,0:T(8,128)}, f32[264,256]{1,0:T(8,128)S(1)}, u32[]{:S(2)}, u32[]{:S(2)}) collective-permute-start(f32[264,256]{1,0:T(8,128)} %shard_map.100.spread), channel_id=1, source_target_pairs={{32,0},{48,16},{64,32},{80,48},{96,64},{112,80},{128,96},{144,112}... | collective-permute-start | bytes 811016 | tf_op jit(solution)/shard_map/ppermute | solution.py:370
  130.6 7.1 %collective-permute-done.15.p3.a3 = f32[512,256]{1,0:T(8,128)S(1)} collective-permute-done((f32[512,256]{1,0:T(8,128)S(1)}, f32[512,256]{1,0:T(8,128)S(1)}, u32[]{:S(2)}, u32[]{:S(2)}) %collective-permute-start.15) | collective-permute-done | bytes 524320 | tf_op jit(solution)/shard_map/ppermute | solution.py:380
  138.9 18.5 %all_to_all.30.y_in = f32[4,264,256]{2,1,0:T(8,128)S(1)} all-to-all(f32[4,264,256]{2,1,0:T(8,128)} %shard_map.101), channel_id=1, replica_groups=mesh['tm'=32,'y'=4,'x'=4] {'y'}, dimensions={0} | all-to-all | bytes 2162688 | tf_op jit(solution)/shard_map/all_to_all | solution.py:374
  157.4 5.1 %shard_map.102 = (f32[4,64,1280]{2,1,0:T(8,128)}, f32[8,256]{1,0:T(8,128)}) custom-call(s32[4]{0:T(128)S(1)} %pad_add_fusion.where, f32[256,256]{1,0:T(8,128)} %get-tuple-element.31.gain_2, bf16[256,1024]{1,0:T(8,128)(2,1)} %get-tuple-element.41.high_2.wide_high, bf16[256,1024]{1,0:T(8,128)(2,1)} %get-tuple-element.42.low_2.wide_low, ...), custom_call_target="tpu_custom_call" | custom-call | flops 402653184 | bytes 7127040 | tf_op jit(solution)/shard_map/pallas_call | solution.py:357
  162.5 4.2 %all-to-all-start.5 = ((f32[4,64,1280]{2,1,0:T(8,128)}), f32[4,64,1280]{2,1,0:T(8,128)S(1)}, u32[]{:S(2)}, u32[]{:S(2)}) async-start(f32[4,64,1280]{2,1,0:T(8,128)} %get-tuple-element.47), calls=%async_computation.5 | async-start | bytes 2621440 | tf_op jit(solution)/shard_map/all_to_all | solution.py:374
  168.0 12.7 %all-to-all-done.5.x_in = f32[4,64,1280]{2,1,0:T(8,128)S(1)} async-done(((f32[4,64,1280]{2,1,0:T(8,128)}), f32[4,64,1280]{2,1,0:T(8,128)S(1)}, u32[]{:S(2)}, u32[]{:S(2)}) %all-to-all-start.5) | async-done | bytes 1310752 | tf_op jit(solution)/shard_map/all_to_all | solution.py:374
  (64 shorter events, 19.6 us)
Async XLA Ops:
  6.0 32.3 %all-to-all-start = ((f32[4,136,1024]{2,1,0:T(8,128)}), f32[4,136,1024]{2,1,0:T(8,128)S(1)}, u32[]{:S(2)}, u32[]{:S(2)}) async-start(f32[4,136,1024]{2,1,0:T(8,128)} %get-tuple-element.27), calls=%async_computation | async-start | bytes 4456448 | tf_op jit(solution)/shard_map/all_to_all | solution.py:374
  10.6 10.9 %collective-permute-start = (f32[64,1024]{1,0:T(8,128)S(1)}, f32[64,1024]{1,0:T(8,128)S(1)}, u32[]{:S(2)}, u32[]{:S(2)}) collective-permute-start(f32[64,1024]{1,0:T(8,128)S(1)} %copy-done.15), channel_id=1, source_target_pairs={{0,1},{1,2},{2,3},{3,0},{4,5},{5,6},{6,7},{7,4},{8,9},{9,10},{10,1... | collective-permute-start | bytes 786440 | tf_op jit(solution)/shard_map/ppermute | solution.py:380
  14.0 14.3 %collective-permute-start.1 = (f32[64,1024]{1,0:T(8,128)S(1)}, f32[64,1024]{1,0:T(8,128)S(1)}, u32[]{:S(2)}, u32[]{:S(2)}) collective-permute-start(f32[64,1024]{1,0:T(8,128)S(1)} %copy-done.15), channel_id=1, source_target_pairs={{0,3},{1,0},{2,1},{3,2},{4,7},{5,4},{6,5},{7,6},{8,11},{9,8},{10,9... | collective-permute-start | bytes 786440 | tf_op jit(solution)/shard_map/ppermute | solution.py:380
  17.6 10.6 %collective-permute-start.2 = (f32[64,1024]{1,0:T(8,128)S(1)}, f32[64,1024]{1,0:T(8,128)S(1)}, u32[]{:S(2)}, u32[]{:S(2)}) collective-permute-start(f32[64,1024]{1,0:T(8,128)S(1)} %copy-done.15), channel_id=1, source_target_pairs={{0,2},{1,3},{2,0},{3,1},{4,6},{5,7},{6,4},{7,5},{8,10},{9,11},{10,... | collective-permute-start | bytes 786440 | tf_op jit(solution)/shard_map/ppermute | solution.py:380
  21.5 16.9 %copy-start.16 = (f32[64,1024]{1,0:T(8,128)}, f32[64,1024]{1,0:T(8,128)S(1)}, u32[]{:S(2)}) copy-start(f32[64,1024]{1,0:T(8,128)S(1)} %collective-permute-done.x1) | copy-start | bytes 786436
  28.3 10.1 %copy-start.17 = (f32[64,1024]{1,0:T(8,128)}, f32[64,1024]{1,0:T(8,128)S(1)}, u32[]{:S(2)}) copy-start(f32[64,1024]{1,0:T(8,128)S(1)} %collective-permute-done.1.x2) | copy-start | bytes 786436
  28.3 10.0 %copy-start.18 = (f32[64,1024]{1,0:T(8,128)}, f32[64,1024]{1,0:T(8,128)S(1)}, u32[]{:S(2)}) copy-start(f32[64,1024]{1,0:T(8,128)S(1)} %collective-permute-done.2.x3) | copy-start | bytes 786436
  41.4 27.1 %copy-start.4 = (s32[1,5]{1,0:T(1,128)S(1)}, s32[1,5]{1,0:T(1,128)}, u32[]{:S(2)}) copy-start(s32[1,5]{1,0:T(1,128)} %offsets.3) | copy-start | bytes 64
  41.4 27.1 %all-to-all-start.1 = ((f32[4,264,256]{2,1,0:T(8,128)}), f32[4,264,256]{2,1,0:T(8,128)S(1)}, u32[]{:S(2)}, u32[]{:S(2)}) async-start(f32[4,264,256]{2,1,0:T(8,128)} %get-tuple-element.30), calls=%async_computation.1 | async-start | bytes 2162688 | tf_op jit(solution)/shard_map/all_to_all | solution.py:374
  45.9 12.3 %collective-permute-start.3 = (f32[256,256]{1,0:T(8,128)}, f32[256,256]{1,0:T(8,128)S(1)}, u32[]{:S(2)}, u32[]{:S(2)}) collective-permute-start(f32[256,256]{1,0:T(8,128)} %get-tuple-element.29.gain.e0), channel_id=1, source_target_pairs={{16,0},{20,4},{24,8},{28,12},{32,16},{36,20},{40,24},{44,28},{48,3... | collective-permute-start | bytes 786440 | tf_op jit(solution)/shard_map/ppermute | solution.py:393
  48.0 11.9 %collective-permute-start.4 = (f32[256,256]{1,0:T(8,128)}, f32[256,256]{1,0:T(8,128)S(1)}, u32[]{:S(2)}, u32[]{:S(2)}) collective-permute-start(f32[256,256]{1,0:T(8,128)} %get-tuple-element.29.gain.e0), channel_id=1, source_target_pairs={{16,4},{20,8},{24,12},{28,0},{32,20},{36,24},{40,28},{44,16},{48,3... | collective-permute-start | bytes 786440 | tf_op jit(solution)/shard_map/ppermute | solution.py:393
  52.0 13.1 %collective-permute-start.5 = (f32[256,256]{1,0:T(8,128)}, f32[256,256]{1,0:T(8,128)S(1)}, u32[]{:S(2)}, u32[]{:S(2)}) collective-permute-start(f32[256,256]{1,0:T(8,128)} %get-tuple-element.29.gain.e0), channel_id=1, source_target_pairs={{16,12},{20,0},{24,4},{28,8},{32,28},{36,16},{40,20},{44,24},{48,4... | collective-permute-start | bytes 786440 | tf_op jit(solution)/shard_map/ppermute | solution.py:393
  56.2 12.3 %collective-permute-start.6 = (f32[256,256]{1,0:T(8,128)}, f32[256,256]{1,0:T(8,128)}, u32[]{:S(2)}, u32[]{:S(2)}) collective-permute-start(f32[256,256]{1,0:T(8,128)} %get-tuple-element.29.gain.e0), channel_id=1, source_target_pairs={{16,8},{20,12},{24,0},{28,4},{32,24},{36,28},{40,16},{44,20},{48,4... | collective-permute-start | bytes 786440 | tf_op jit(solution)/shard_map/ppermute | solution.py:393
  58.2 7.0 %copy-start.12 = (f32[256,256]{1,0:T(8,128)}, f32[256,256]{1,0:T(8,128)S(1)}, u32[]{:S(2)}) copy-start(f32[256,256]{1,0:T(8,128)S(1)} %collective-permute-done.3.e0) | copy-start | bytes 786436
  59.9 5.3 %copy-start.13 = (f32[256,256]{1,0:T(8,128)}, f32[256,256]{1,0:T(8,128)S(1)}, u32[]{:S(2)}) copy-start(f32[256,256]{1,0:T(8,128)S(1)} %collective-permute-done.4.e1) | copy-start | bytes 786436
  72.6 8.4 %copy-start.7 = (f32[256,256]{1,0:T(8,128)S(1)}, f32[256,256]{1,0:T(8,128)}, u32[]{:S(2)}) copy-start(f32[256,256]{1,0:T(8,128)} %get-tuple-element.29.gain.e0) | copy-start | bytes 786436
  72.6 17.4 %copy-start.6 = (f32[256,256]{1,0:T(8,128)S(1)}, f32[256,256]{1,0:T(8,128)}, u32[]{:S(2)}) copy-start(f32[256,256]{1,0:T(8,128)} %get-tuple-element.31.gain_2) | copy-start | bytes 786436
  72.6 20.8 %collective-permute-start.7 = (f32[264,1024]{1,0:T(8,128)}, f32[264,1024]{1,0:T(8,128)S(1)}, u32[]{:S(2)}, u32[]{:S(2)}) collective-permute-start(f32[264,1024]{1,0:T(8,128)} %get-tuple-element.35), channel_id=1, source_target_pairs={{16,0},{32,16},{48,32},{64,48},{80,64},{96,80},{112,96},{128,112},... | collective-permute-start | bytes 3244040 | tf_op jit(solution)/shard_map/ppermute | solution.py:370
  76.2 23.6 %all-to-all-start.2 = ((f32[4,256,256]{2,1,0:T(8,128)}), f32[4,256,256]{2,1,0:T(8,128)S(1)}, u32[]{:S(2)}, u32[]{:S(2)}) async-start(f32[4,256,256]{2,1,0:T(8,128)} %get-tuple-element.34), calls=%async_computation.2 | async-start | bytes 2097152 | tf_op jit(solution)/shard_map/all_to_all | solution.py:374
  81.1 17.6 %collective-permute-start.10 = (f32[256,256]{1,0:T(8,128)S(1)}, f32[256,256]{1,0:T(8,128)S(1)}, u32[]{:S(2)}, u32[]{:S(2)}) collective-permute-start(f32[256,256]{1,0:T(8,128)S(1)} %copy-done.7), channel_id=1, source_target_pairs={{0,8},{4,12},{8,0},{12,4},{1,9},{5,13},{9,1},{13,5},{2,10},{6,14},... | collective-permute-start | bytes 786440 | tf_op jit(solution)/shard_map/ppermute | solution.py:380
  83.0 15.7 %collective-permute-start.8 = (f32[256,256]{1,0:T(8,128)S(1)}, f32[256,256]{1,0:T(8,128)S(1)}, u32[]{:S(2)}, u32[]{:S(2)}) collective-permute-start(f32[256,256]{1,0:T(8,128)S(1)} %copy-done.7), channel_id=1, source_target_pairs={{0,4},{4,8},{8,12},{12,0},{1,5},{5,9},{9,13},{13,1},{2,6},{6,10},{... | collective-permute-start | bytes 786440 | tf_op jit(solution)/shard_map/ppermute | solution.py:380
  88.0 10.7 %collective-permute-start.9 = (f32[256,256]{1,0:T(8,128)S(1)}, f32[256,256]{1,0:T(8,128)S(1)}, u32[]{:S(2)}, u32[]{:S(2)}) collective-permute-start(f32[256,256]{1,0:T(8,128)S(1)} %copy-done.7), channel_id=1, source_target_pairs={{0,12},{4,0},{8,4},{12,8},{1,13},{5,1},{9,5},{13,9},{2,14},{6,2},{... | collective-permute-start | bytes 786440 | tf_op jit(solution)/shard_map/ppermute | solution.py:380
  90.1 9.8 %collective-permute-start.11 = (f32[256,256]{1,0:T(8,128)S(1)}, f32[256,256]{1,0:T(8,128)}, u32[]{:S(2)}, u32[]{:S(2)}) collective-permute-start(f32[256,256]{1,0:T(8,128)S(1)} %copy-done.6), channel_id=1, source_target_pairs={{32,0},{48,16},{64,32},{80,48},{96,64},{112,80},{128,96},{144,112}... | collective-permute-start | bytes 786440 | tf_op jit(solution)/shard_map/ppermute | solution.py:370
  105.3 4.7 %copy-start.8 = (f32[512,256]{1,0:T(8,128)S(1)}, f32[512,256]{1,0:T(8,128)}, u32[]{:S(2)}) copy-start(f32[512,256]{1,0:T(8,128)} %get-tuple-element.46.a0) | copy-start | bytes 1572868
  105.3 19.0 %all-to-all-start.3 = ((f32[4,256,256]{2,1,0:T(8,128)}), f32[4,256,256]{2,1,0:T(8,128)S(1)}, u32[]{:S(2)}, u32[]{:S(2)}) async-start(f32[4,256,256]{2,1,0:T(8,128)} %get-tuple-element.43), calls=%async_computation.3 | async-start | bytes 2097152 | tf_op jit(solution)/shard_map/all_to_all | solution.py:374
  110.0 19.9 %collective-permute-start.13 = (f32[512,256]{1,0:T(8,128)S(1)}, f32[512,256]{1,0:T(8,128)S(1)}, u32[]{:S(2)}, u32[]{:S(2)}) collective-permute-start(f32[512,256]{1,0:T(8,128)S(1)} %copy-done.8), channel_id=1, source_target_pairs={{0,4},{4,8},{8,12},{12,0},{1,5},{5,9},{9,13},{13,1},{2,6},{6,10},{... | collective-permute-start | bytes 1572872 | tf_op jit(solution)/shard_map/ppermute | solution.py:380
  113.9 16.8 %collective-permute-start.14 = (f32[512,256]{1,0:T(8,128)S(1)}, f32[512,256]{1,0:T(8,128)S(1)}, u32[]{:S(2)}, u32[]{:S(2)}) collective-permute-start(f32[512,256]{1,0:T(8,128)S(1)} %copy-done.8), channel_id=1, source_target_pairs={{0,12},{4,0},{8,4},{12,8},{1,13},{5,1},{9,5},{13,9},{2,14},{6,2},{... | collective-permute-start | bytes 1572872 | tf_op jit(solution)/shard_map/ppermute | solution.py:380
  117.0 20.7 %collective-permute-start.15 = (f32[512,256]{1,0:T(8,128)S(1)}, f32[512,256]{1,0:T(8,128)S(1)}, u32[]{:S(2)}, u32[]{:S(2)}) collective-permute-start(f32[512,256]{1,0:T(8,128)S(1)} %copy-done.8), channel_id=1, source_target_pairs={{0,8},{4,12},{8,0},{12,4},{1,9},{5,13},{9,1},{13,5},{2,10},{6,14},... | collective-permute-start | bytes 1572872 | tf_op jit(solution)/shard_map/ppermute | solution.py:380
  125.9 11.9 %collective-permute-start.12 = (f32[264,256]{1,0:T(8,128)}, f32[264,256]{1,0:T(8,128)S(1)}, u32[]{:S(2)}, u32[]{:S(2)}) collective-permute-start(f32[264,256]{1,0:T(8,128)} %shard_map.100.spread), channel_id=1, source_target_pairs={{32,0},{48,16},{64,32},{80,48},{96,64},{112,80},{128,96},{144,112}... | collective-permute-start | bytes 811016 | tf_op jit(solution)/shard_map/ppermute | solution.py:370
  129.9 9.0 %copy-start = (f32[512,256]{1,0:T(8,128)}, f32[512,256]{1,0:T(8,128)S(1)}, u32[]{:S(2)}) copy-start(f32[512,256]{1,0:T(8,128)S(1)} %collective-permute-done.13.p1.a1) | copy-start | bytes 1572868
  130.6 8.3 %copy-start.1 = (f32[512,256]{1,0:T(8,128)}, f32[512,256]{1,0:T(8,128)S(1)}, u32[]{:S(2)}) copy-start(f32[512,256]{1,0:T(8,128)S(1)} %collective-permute-done.14.p2.a2) | copy-start | bytes 1572868
  162.5 18.2 %all-to-all-start.5 = ((f32[4,64,1280]{2,1,0:T(8,128)}), f32[4,64,1280]{2,1,0:T(8,128)S(1)}, u32[]{:S(2)}, u32[]{:S(2)}) async-start(f32[4,64,1280]{2,1,0:T(8,128)} %get-tuple-element.47), calls=%async_computation.5 | async-start | bytes 2621440 | tf_op jit(solution)/shard_map/all_to_all | solution.py:374
  (8 other events, 11.2 us)

commit v9 on v8

--- a/solution.py
+++ b/solution.py
@@ -121,10 +121,9 @@
             ]
 
 
-def prepare(offsets, own, inverse, weights, prior, innovation, sites, crossed_out, y_out):
+def first_message(own, inverse, prior, innovation, sites, y_out):
     rows, columns = own.shape
     matrix = own[...]
-    crossed_out[...] = bands(matrix, weights[...], lambda b: offsets[0, b])
     state = lax.broadcasted_iota(jnp.int32, (columns, sites.shape[1]), 0)
     matches = (state == sites[...]).astype(F32)
     pulled = vector_times(innovation[...], matches)
@@ -134,6 +133,10 @@
         y_out[i, rows : 2 * rows, :] = matrix
         y_out[i, 2 * rows :, :] = jnp.zeros((8, columns), F32)
         y_out[i, 2 * rows : 2 * rows + 1, 0:rows] = filtered
+
+
+def cross(offsets, own, weights, crossed_out):
+    crossed_out[...] = bands(own[...], weights[...], lambda b: offsets[0, b])
 
 
 def place_rows(pieces, at, out):
@@ -413,13 +416,14 @@
     )
     unit = 2 * panel * panel * columns
 
-    crossed, y_message = call(
-        prepare,
-        (band_offset,),
-        far(own, inverse, weights, prior_mean, innovation, seen_sites),
-        ((rows, columns), (SIDE, 2 * rows + 8, columns)),
+    (y_message,) = call(
+        first_message,
+        (),
+        far(own, inverse, prior_mean, innovation, seen_sites),
+        ((SIDE, 2 * rows + 8, columns),),
     )
     y_in = swap(y_message, "y")
+    (crossed,) = call(cross, (band_offset,), far(own, weights), ((rows, columns),))
     crossed_pieces = ring(crossed, "x")
     gain, crossed_block, x_message = call(
         first_gain,

time: 183 us -> 181 us (0.989)
  waiting for transfers between devices: 48.8 us -> 46 us
  Pallas kernels: 32 us -> 34 us
    all_to_all x5, waiting for transfers between devices: 24.2 us -> 21.1 us  [swap(): return lax.all_to_all(message, axis, 0, 0)]
    pallas_call x10 -> x11, Pallas kernels: 32 us -> 34 us  [call(): pl.pallas_call(kernel, out_shape=shapes, in_specs=[SMEM] * len(scalars) +...]
    unnamed x39 -> x37, local copies, waits for them, and re-layouts: 4.53 us -> 3.15 us
  transfers between devices with their start and end apart: 21 -> 21, of which waited for: 10 -> 11; matrix products, arithmetic and copies ran while one was open for 1% -> 1% of each run, Pallas kernels for 5% -> 6%
where the time goes in v9:
time: 181 us; the launch traced here: 179 us
  starting transfers between devices  75.4 us (42%)
  waiting for transfers between devices  46 us (25%)
  Pallas kernels  34 us (19%)
  blocking collectives  18.5 us (10%)
  local copies, waits for them, and re-layouts  4.43 us (2%)
    pallas_call x11, Pallas kernels, call(): pl.pallas_call(kernel, out_shape=shapes, in_specs=[SMEM] * len(scalars) +...  34 us
    ppermute x9, starting transfers between devices, ring(): lax.ppermute(block, axis, [(i, (i + step) % SIDE) for i in range(SIDE)])  29.5 us
    all_to_all x5, starting transfers between devices, swap(): return lax.all_to_all(message, axis, 0, 0)  22.6 us
    all_to_all x5, waiting for transfers between devices, swap(): return lax.all_to_all(message, axis, 0, 0)  21.1 us
    all_to_all x1, blocking collectives, swap(): return lax.all_to_all(message, axis, 0, 0)  18.5 us
    ppermute x9, waiting for transfers between devices, ring(): lax.ppermute(block, axis, [(i, (i + step) % SIDE) for i in range(SIDE)])  15 us
    ppermute x4, starting transfers between devices, ring_shifted(): pieces.append(lax.ppermute(block, ('tm', 'y'), route))  12.3 us
    ppermute x3, starting transfers between devices, shifted(): lax.ppermute(block, 'tm', [(i + distance, i) for i in range(count - dista...  11 us
  transfers between devices with their start and end apart: 21, of which 11 were waited for; matrix products, arithmetic and copies ran while one was open for 1% of the time, Pallas kernels for 6%

profile of v9, /device:TPU:384, one launch (start us, length us, event | category | flops | bytes accessed | tf_op | source)
XLA Modules:
  0.0 179.3 jit_solution(4685509734709476468)
XLA Ops:
  0.6 3.2 %shard_map.94 = f32[4,136,1024]{2,1,0:T(8,128)} custom-call(f32[64,1024]{1,0:T(8,128)} %bitcast.13, f32[64,1024]{1,0:T(8,128)} %bitcast.18, f32[1,64]{1,0:T(1,128)} %prior.1, f32[1,128]{1,0:T(1,128)} %innovation.1, s32[1,128]{1,0:T(1,128)} %sites.1), custom_call_target="tpu_custom_call" | custom-call | bytes 2753792 | tf_op jit(solution)/shard_map/pallas_call | solution.py:360
  3.8 4.6 %all-to-all-start = ((f32[4,136,1024]{2,1,0:T(8,128)}), f32[4,136,1024]{2,1,0:T(8,128)S(1)}, u32[]{:S(2)}, u32[]{:S(2)}) async-start(f32[4,136,1024]{2,1,0:T(8,128)} %shard_map.94), calls=%async_computation | async-start | bytes 4456448 | tf_op jit(solution)/shard_map/all_to_all | solution.py:377
  9.0 2.2 %shard_map.95.x0 = f32[64,1024]{1,0:T(8,128)} custom-call(s32[1,5]{1,0:T(1,128)S(1)} %copy-done.3, f32[64,1024]{1,0:T(8,128)} %bitcast.14, f32[5,1024]{1,0:T(8,128)} %bitcast.16), custom_call_target="tpu_custom_call" | custom-call | bytes 544768 | tf_op jit(solution)/shard_map/pallas_call | solution.py:360
  11.2 3.4 %collective-permute-start = (f32[64,1024]{1,0:T(8,128)}, f32[64,1024]{1,0:T(8,128)S(1)}, u32[]{:S(2)}, u32[]{:S(2)}) collective-permute-start(f32[64,1024]{1,0:T(8,128)} %shard_map.95.x0), channel_id=1, source_target_pairs={{0,1},{1,2},{2,3},{3,0},{4,5},{5,6},{6,7},{7,4},{8,9},{9,10},{10,1... | collective-permute-start | bytes 786440 | tf_op jit(solution)/shard_map/ppermute | solution.py:383
  14.6 3.7 %collective-permute-start.1 = (f32[64,1024]{1,0:T(8,128)}, f32[64,1024]{1,0:T(8,128)S(1)}, u32[]{:S(2)}, u32[]{:S(2)}) collective-permute-start(f32[64,1024]{1,0:T(8,128)} %shard_map.95.x0), channel_id=1, source_target_pairs={{0,3},{1,0},{2,1},{3,2},{4,7},{5,4},{6,5},{7,6},{8,11},{9,8},{10,9... | collective-permute-start | bytes 786440 | tf_op jit(solution)/shard_map/ppermute | solution.py:383
  18.3 3.7 %collective-permute-start.2 = (f32[64,1024]{1,0:T(8,128)}, f32[64,1024]{1,0:T(8,128)S(1)}, u32[]{:S(2)}, u32[]{:S(2)}) collective-permute-start(f32[64,1024]{1,0:T(8,128)} %shard_map.95.x0), channel_id=1, source_target_pairs={{0,2},{1,3},{2,0},{3,1},{4,6},{5,7},{6,4},{7,5},{8,10},{9,11},{10,... | collective-permute-start | bytes 786440 | tf_op jit(solution)/shard_map/ppermute | solution.py:383
  22.3 6.9 %collective-permute-done.1.x2 = f32[64,1024]{1,0:T(8,128)S(1)} collective-permute-done((f32[64,1024]{1,0:T(8,128)}, f32[64,1024]{1,0:T(8,128)S(1)}, u32[]{:S(2)}, u32[]{:S(2)}) %collective-permute-start.1) | collective-permute-done | bytes 262176 | tf_op jit(solution)/shard_map/ppermute | solution.py:383
  29.2 6.9 %all-to-all-done.y_in = f32[4,136,1024]{2,1,0:T(8,128)S(1)} async-done(((f32[4,136,1024]{2,1,0:T(8,128)}), f32[4,136,1024]{2,1,0:T(8,128)S(1)}, u32[]{:S(2)}, u32[]{:S(2)}) %all-to-all-start) | async-done | bytes 2228256 | tf_op jit(solution)/shard_map/all_to_all | solution.py:377
  36.2 3.1 %shard_map.96 = (f32[256,256]{1,0:T(8,128)}, f32[256,256]{1,0:T(8,128)}, f32[4,264,256]{2,1,0:T(8,128)}) custom-call(s32[4]{0:T(128)S(1)} %pad_add_fusion.where, f32[4,136,1024]{2,1,0:T(8,128)S(1)} %all-to-all-done.y_in, f32[64,1024]{1,0:T(8,128)} %shard_map.95.x0, f32[64,1024]{1,0:T(8,128)} %copy-done.14, f32[64,1024]{1,0:T(8,128)} %copy-done.15, ...), custom_call_target="tpu_custom_call" | custom-call | flops 134217728 | bytes 4882432 | tf_op jit(solution)/shard_map/pallas_call | solution.py:360
  39.3 4.3 %all-to-all-start.1 = ((f32[4,264,256]{2,1,0:T(8,128)}), f32[4,264,256]{2,1,0:T(8,128)S(1)}, u32[]{:S(2)}, u32[]{:S(2)}) async-start(f32[4,264,256]{2,1,0:T(8,128)} %get-tuple-element.26), calls=%async_computation.1 | async-start | bytes 2162688 | tf_op jit(solution)/shard_map/all_to_all | solution.py:377
  45.6 4.1 %collective-permute-start.4 = (f32[256,256]{1,0:T(8,128)}, f32[256,256]{1,0:T(8,128)S(1)}, u32[]{:S(2)}, u32[]{:S(2)}) collective-permute-start(f32[256,256]{1,0:T(8,128)} %get-tuple-element.25.gain.e0), channel_id=1, source_target_pairs={{16,4},{20,8},{24,12},{28,0},{32,20},{36,24},{40,28},{44,16},{48,3... | collective-permute-start | bytes 786440 | tf_op jit(solution)/shard_map/ppermute | solution.py:396
  49.7 4.2 %collective-permute-start.5 = (f32[256,256]{1,0:T(8,128)}, f32[256,256]{1,0:T(8,128)S(1)}, u32[]{:S(2)}, u32[]{:S(2)}) collective-permute-start(f32[256,256]{1,0:T(8,128)} %get-tuple-element.25.gain.e0), channel_id=1, source_target_pairs={{16,12},{20,0},{24,4},{28,8},{32,28},{36,16},{40,20},{44,24},{48,4... | collective-permute-start | bytes 786440 | tf_op jit(solution)/shard_map/ppermute | solution.py:396
  57.6 5.3 %collective-permute-done.5.e2 = f32[256,256]{1,0:T(8,128)S(1)} collective-permute-done((f32[256,256]{1,0:T(8,128)}, f32[256,256]{1,0:T(8,128)S(1)}, u32[]{:S(2)}, u32[]{:S(2)}) %collective-permute-start.5) | collective-permute-done | bytes 262176 | tf_op jit(solution)/shard_map/ppermute | solution.py:396
  63.5 2.7 %collective-permute-done.6.e3 = f32[256,256]{1,0:T(8,128)} collective-permute-done((f32[256,256]{1,0:T(8,128)}, f32[256,256]{1,0:T(8,128)}, u32[]{:S(2)}, u32[]{:S(2)}) %collective-permute-start.6) | collective-permute-done | bytes 262176 | tf_op jit(solution)/shard_map/ppermute | solution.py:396
  66.2 4.1 %shard_map.97 = (f32[256,256]{1,0:T(8,128)}, f32[4,256,256]{2,1,0:T(8,128)}, f32[8,256]{1,0:T(8,128)}, f32[264,1024]{1,0:T(8,128)}, bf16[256,1024]{1,0:T(8,128)(2,1)}, /*index=5*/bf16[256,1024]{1,0:T(8,128)(2,1)}) custom-call(s32[4]{0:T(128)S(1)} %pad_add_fusion.where, s32[1,5]{1,0:T(1,128)S(1)} %copy-done.3, f32[5,1024]{1,0:T(8,128)} %bitcast.17, ...), custom_call_target="tpu_custom_call" | custom-call | flops 134217728 | bytes 7041024 | tf_op jit(solution)/shard_map/pallas_call | solution.py:360
  70.3 3.6 %collective-permute-start.7 = (f32[264,1024]{1,0:T(8,128)}, f32[264,1024]{1,0:T(8,128)S(1)}, u32[]{:S(2)}, u32[]{:S(2)}) collective-permute-start(f32[264,1024]{1,0:T(8,128)} %get-tuple-element.31), channel_id=1, source_target_pairs={{16,0},{32,16},{48,32},{64,48},{80,64},{96,80},{112,96},{128,112},... | collective-permute-start | bytes 3244040 | tf_op jit(solution)/shard_map/ppermute | solution.py:373
  73.9 4.8 %all-to-all-start.2 = ((f32[4,256,256]{2,1,0:T(8,128)}), f32[4,256,256]{2,1,0:T(8,128)S(1)}, u32[]{:S(2)}, u32[]{:S(2)}) async-start(f32[4,256,256]{2,1,0:T(8,128)} %get-tuple-element.30), calls=%async_computation.2 | async-start | bytes 2097152 | tf_op jit(solution)/shard_map/all_to_all | solution.py:377
  80.7 5.0 %collective-permute-start.8 = (f32[256,256]{1,0:T(8,128)S(1)}, f32[256,256]{1,0:T(8,128)S(1)}, u32[]{:S(2)}, u32[]{:S(2)}) collective-permute-start(f32[256,256]{1,0:T(8,128)S(1)} %copy-done.6), channel_id=1, source_target_pairs={{0,4},{4,8},{8,12},{12,0},{1,5},{5,9},{9,13},{13,1},{2,6},{6,10},{... | collective-permute-start | bytes 786440 | tf_op jit(solution)/shard_map/ppermute | solution.py:383
  87.8 3.4 %collective-permute-start.11 = (f32[256,256]{1,0:T(8,128)S(1)}, f32[256,256]{1,0:T(8,128)}, u32[]{:S(2)}, u32[]{:S(2)}) collective-permute-start(f32[256,256]{1,0:T(8,128)S(1)} %copy-done.5), channel_id=1, source_target_pairs={{32,0},{48,16},{64,32},{80,48},{96,64},{112,80},{128,96},{144,112}... | collective-permute-start | bytes 786440 | tf_op jit(solution)/shard_map/ppermute | solution.py:373
  92.1 4.2 %shard_map.98 = (f32[8,1024]{1,0:T(8,128)}, bf16[256,1024]{1,0:T(8,128)(2,1)}, bf16[256,1024]{1,0:T(8,128)(2,1)}, bf16[256,1024]{1,0:T(8,128)(2,1)}, bf16[256,1024]{1,0:T(8,128)(2,1)}) custom-call(s32[8]{0:T(128)S(1)} %fusion.offsets, f32[264,1024]{1,0:T(8,128)} %copy-done.4), custom_call_target="tpu_custom_call" | custom-call | bytes 1114112 | tf_op jit(solution)/shard_map/pallas_call | solution.py:360
  97.5 5.5 %shard_map.99 = (f32[4,256,256]{2,1,0:T(8,128)}, f32[512,256]{1,0:T(8,128)}, bf16[256,1024]{1,0:T(8,128)(2,1)}, bf16[256,1024]{1,0:T(8,128)(2,1)}) custom-call(s32[4]{0:T(128)S(1)} %pad_add_fusion.where, bf16[256,1024]{1,0:T(8,128)(2,1)} %get-tuple-element.28.wide_high.high, bf16[256,1024]{1,0:T(8,128)(2,1)} %get-tuple-element.29.wide_low.low, ...), custom_call_target="tpu_custom_call" | custom-call | flops 402653184 | bytes 11010048 | tf_op jit(solution)/shard_map/pallas_call | solution.py:360
  103.0 4.7 %all-to-all-start.3 = ((f32[4,256,256]{2,1,0:T(8,128)}), f32[4,256,256]{2,1,0:T(8,128)S(1)}, u32[]{:S(2)}, u32[]{:S(2)}) async-start(f32[4,256,256]{2,1,0:T(8,128)} %get-tuple-element.39), calls=%async_computation.3 | async-start | bytes 2097152 | tf_op jit(solution)/shard_map/all_to_all | solution.py:377
  107.7 3.9 %collective-permute-start.13 = (f32[512,256]{1,0:T(8,128)S(1)}, f32[512,256]{1,0:T(8,128)S(1)}, u32[]{:S(2)}, u32[]{:S(2)}) collective-permute-start(f32[512,256]{1,0:T(8,128)S(1)} %copy-done.7), channel_id=1, source_target_pairs={{0,4},{4,8},{8,12},{12,0},{1,5},{5,9},{9,13},{13,1},{2,6},{6,10},{... | collective-permute-start | bytes 1572872 | tf_op jit(solution)/shard_map/ppermute | solution.py:383
  111.6 3.1 %collective-permute-start.14 = (f32[512,256]{1,0:T(8,128)S(1)}, f32[512,256]{1,0:T(8,128)S(1)}, u32[]{:S(2)}, u32[]{:S(2)}) collective-permute-start(f32[512,256]{1,0:T(8,128)S(1)} %copy-done.7), channel_id=1, source_target_pairs={{0,12},{4,0},{8,4},{12,8},{1,13},{5,1},{9,5},{13,9},{2,14},{6,2},{... | collective-permute-start | bytes 1572872 | tf_op jit(solution)/shard_map/ppermute | solution.py:383
  114.7 2.8 %collective-permute-start.15 = (f32[512,256]{1,0:T(8,128)S(1)}, f32[512,256]{1,0:T(8,128)S(1)}, u32[]{:S(2)}, u32[]{:S(2)}) collective-permute-start(f32[512,256]{1,0:T(8,128)S(1)} %copy-done.7), channel_id=1, source_target_pairs={{0,8},{4,12},{8,0},{12,4},{1,9},{5,13},{9,1},{13,5},{2,10},{6,14},... | collective-permute-start | bytes 1572872 | tf_op jit(solution)/shard_map/ppermute | solution.py:383
  117.5 3.1 %shard_map.100.shift = f32[8,256]{1,0:T(8,128)} custom-call(s32[4]{0:T(128)S(1)} %pad_add_fusion.where, bf16[256,1024]{1,0:T(8,128)(2,1)} %get-tuple-element.28.wide_high.high, bf16[256,1024]{1,0:T(8,128)(2,1)} %get-tuple-element.29.wide_low.low, bf16[256,1024]{1,0:T(8,128)(2,1)} %get-tuple-element.37.high_2.wide_high, ...), custom_call_target="tpu_custom_call" | custom-call | bytes 4243456 | tf_op jit(solution)/shard_map/pallas_call | solution.py:360
  123.6 4.1 %collective-permute-start.12 = (f32[264,256]{1,0:T(8,128)}, f32[264,256]{1,0:T(8,128)S(1)}, u32[]{:S(2)}, u32[]{:S(2)}) collective-permute-start(f32[264,256]{1,0:T(8,128)} %shard_map.101.spread), channel_id=1, source_target_pairs={{32,0},{48,16},{64,32},{80,48},{96,64},{112,80},{128,96},{144,112}... | collective-permute-start | bytes 811016 | tf_op jit(solution)/shard_map/ppermute | solution.py:373
  128.3 7.1 %collective-permute-done.15.p3.a3 = f32[512,256]{1,0:T(8,128)S(1)} collective-permute-done((f32[512,256]{1,0:T(8,128)S(1)}, f32[512,256]{1,0:T(8,128)S(1)}, u32[]{:S(2)}, u32[]{:S(2)}) %collective-permute-start.15) | collective-permute-done | bytes 524320 | tf_op jit(solution)/shard_map/ppermute | solution.py:383
  136.6 18.5 %all_to_all.30.y_in = f32[4,264,256]{2,1,0:T(8,128)S(1)} all-to-all(f32[4,264,256]{2,1,0:T(8,128)} %shard_map.102), channel_id=1, replica_groups=mesh['tm'=32,'y'=4,'x'=4] {'y'}, dimensions={0} | all-to-all | bytes 2162688 | tf_op jit(solution)/shard_map/all_to_all | solution.py:377
  155.1 5.1 %shard_map.103 = (f32[4,64,1280]{2,1,0:T(8,128)}, f32[8,256]{1,0:T(8,128)}) custom-call(s32[4]{0:T(128)S(1)} %pad_add_fusion.where, f32[256,256]{1,0:T(8,128)} %get-tuple-element.27.gain_2, bf16[256,1024]{1,0:T(8,128)(2,1)} %get-tuple-element.37.high_2.wide_high, bf16[256,1024]{1,0:T(8,128)(2,1)} %get-tuple-element.38.low_2.wide_low, ...), custom_call_target="tpu_custom_call" | custom-call | flops 402653184 | bytes 7127040 | tf_op jit(solution)/shard_map/pallas_call | solution.py:360
  160.2 4.2 %all-to-all-start.5 = ((f32[4,64,1280]{2,1,0:T(8,128)}), f32[4,64,1280]{2,1,0:T(8,128)S(1)}, u32[]{:S(2)}, u32[]{:S(2)}) async-start(f32[4,64,1280]{2,1,0:T(8,128)} %get-tuple-element.43), calls=%async_computation.5 | async-start | bytes 2621440 | tf_op jit(solution)/shard_map/all_to_all | solution.py:377
  165.7 12.7 %all-to-all-done.5.x_in = f32[4,64,1280]{2,1,0:T(8,128)S(1)} async-done(((f32[4,64,1280]{2,1,0:T(8,128)}), f32[4,64,1280]{2,1,0:T(8,128)S(1)}, u32[]{:S(2)}, u32[]{:S(2)}) %all-to-all-start.5) | async-done | bytes 1310752 | tf_op jit(solution)/shard_map/all_to_all | solution.py:377
  (63 shorter events, 20.5 us)
Async XLA Ops:
  3.8 5.2 %copy-start.3 = (s32[1,5]{1,0:T(1,128)S(1)}, s32[1,5]{1,0:T(1,128)}, u32[]{:S(2)}) copy-start(s32[1,5]{1,0:T(1,128)} %offsets.3) | copy-start | bytes 64
  3.8 32.3 %all-to-all-start = ((f32[4,136,1024]{2,1,0:T(8,128)}), f32[4,136,1024]{2,1,0:T(8,128)S(1)}, u32[]{:S(2)}, u32[]{:S(2)}) async-start(f32[4,136,1024]{2,1,0:T(8,128)} %shard_map.94), calls=%async_computation | async-start | bytes 4456448 | tf_op jit(solution)/shard_map/all_to_all | solution.py:377
  11.2 11.1 %collective-permute-start = (f32[64,1024]{1,0:T(8,128)}, f32[64,1024]{1,0:T(8,128)S(1)}, u32[]{:S(2)}, u32[]{:S(2)}) collective-permute-start(f32[64,1024]{1,0:T(8,128)} %shard_map.95.x0), channel_id=1, source_target_pairs={{0,1},{1,2},{2,3},{3,0},{4,5},{5,6},{6,7},{7,4},{8,9},{9,10},{10,1... | collective-permute-start | bytes 786440 | tf_op jit(solution)/shard_map/ppermute | solution.py:383
  14.6 14.6 %collective-permute-start.1 = (f32[64,1024]{1,0:T(8,128)}, f32[64,1024]{1,0:T(8,128)S(1)}, u32[]{:S(2)}, u32[]{:S(2)}) collective-permute-start(f32[64,1024]{1,0:T(8,128)} %shard_map.95.x0), channel_id=1, source_target_pairs={{0,3},{1,0},{2,1},{3,2},{4,7},{5,4},{6,5},{7,6},{8,11},{9,8},{10,9... | collective-permute-start | bytes 786440 | tf_op jit(solution)/shard_map/ppermute | solution.py:383
  18.3 10.9 %collective-permute-start.2 = (f32[64,1024]{1,0:T(8,128)}, f32[64,1024]{1,0:T(8,128)S(1)}, u32[]{:S(2)}, u32[]{:S(2)}) collective-permute-start(f32[64,1024]{1,0:T(8,128)} %shard_map.95.x0), channel_id=1, source_target_pairs={{0,2},{1,3},{2,0},{3,1},{4,6},{5,7},{6,4},{7,5},{8,10},{9,11},{10,... | collective-permute-start | bytes 786440 | tf_op jit(solution)/shard_map/ppermute | solution.py:383
  22.3 13.9 %copy-start.14 = (f32[64,1024]{1,0:T(8,128)}, f32[64,1024]{1,0:T(8,128)S(1)}, u32[]{:S(2)}) copy-start(f32[64,1024]{1,0:T(8,128)S(1)} %collective-permute-done.x1) | copy-start | bytes 786436
  29.2 6.9 %copy-start.15 = (f32[64,1024]{1,0:T(8,128)}, f32[64,1024]{1,0:T(8,128)S(1)}, u32[]{:S(2)}) copy-start(f32[64,1024]{1,0:T(8,128)S(1)} %collective-permute-done.1.x2) | copy-start | bytes 786436
  29.2 6.9 %copy-start.16 = (f32[64,1024]{1,0:T(8,128)}, f32[64,1024]{1,0:T(8,128)S(1)}, u32[]{:S(2)}) copy-start(f32[64,1024]{1,0:T(8,128)S(1)} %collective-permute-done.2.x3) | copy-start | bytes 786436
  39.3 27.0 %all-to-all-start.1 = ((f32[4,264,256]{2,1,0:T(8,128)}), f32[4,264,256]{2,1,0:T(8,128)S(1)}, u32[]{:S(2)}, u32[]{:S(2)}) async-start(f32[4,264,256]{2,1,0:T(8,128)} %get-tuple-element.26), calls=%async_computation.1 | async-start | bytes 2162688 | tf_op jit(solution)/shard_map/all_to_all | solution.py:377
  43.5 12.3 %collective-permute-start.3 = (f32[256,256]{1,0:T(8,128)}, f32[256,256]{1,0:T(8,128)S(1)}, u32[]{:S(2)}, u32[]{:S(2)}) collective-permute-start(f32[256,256]{1,0:T(8,128)} %get-tuple-element.25.gain.e0), channel_id=1, source_target_pairs={{16,0},{20,4},{24,8},{28,12},{32,16},{36,20},{40,24},{44,28},{48,3... | collective-permute-start | bytes 786440 | tf_op jit(solution)/shard_map/ppermute | solution.py:396
  45.6 11.9 %collective-permute-start.4 = (f32[256,256]{1,0:T(8,128)}, f32[256,256]{1,0:T(8,128)S(1)}, u32[]{:S(2)}, u32[]{:S(2)}) collective-permute-start(f32[256,256]{1,0:T(8,128)} %get-tuple-element.25.gain.e0), channel_id=1, source_target_pairs={{16,4},{20,8},{24,12},{28,0},{32,20},{36,24},{40,28},{44,16},{48,3... | collective-permute-start | bytes 786440 | tf_op jit(solution)/shard_map/ppermute | solution.py:396
  49.7 13.1 %collective-permute-start.5 = (f32[256,256]{1,0:T(8,128)}, f32[256,256]{1,0:T(8,128)S(1)}, u32[]{:S(2)}, u32[]{:S(2)}) collective-permute-start(f32[256,256]{1,0:T(8,128)} %get-tuple-element.25.gain.e0), channel_id=1, source_target_pairs={{16,12},{20,0},{24,4},{28,8},{32,28},{36,16},{40,20},{44,24},{48,4... | collective-permute-start | bytes 786440 | tf_op jit(solution)/shard_map/ppermute | solution.py:396
  53.9 12.3 %collective-permute-start.6 = (f32[256,256]{1,0:T(8,128)}, f32[256,256]{1,0:T(8,128)}, u32[]{:S(2)}, u32[]{:S(2)}) collective-permute-start(f32[256,256]{1,0:T(8,128)} %get-tuple-element.25.gain.e0), channel_id=1, source_target_pairs={{16,8},{20,12},{24,0},{28,4},{32,24},{36,28},{40,16},{44,20},{48,4... | collective-permute-start | bytes 786440 | tf_op jit(solution)/shard_map/ppermute | solution.py:396
  55.8 7.0 %copy-start.11 = (f32[256,256]{1,0:T(8,128)}, f32[256,256]{1,0:T(8,128)S(1)}, u32[]{:S(2)}) copy-start(f32[256,256]{1,0:T(8,128)S(1)} %collective-permute-done.3.e0) | copy-start | bytes 786436
  57.6 5.3 %copy-start.12 = (f32[256,256]{1,0:T(8,128)}, f32[256,256]{1,0:T(8,128)S(1)}, u32[]{:S(2)}) copy-start(f32[256,256]{1,0:T(8,128)S(1)} %collective-permute-done.4.e1) | copy-start | bytes 786436
  70.3 8.4 %copy-start.6 = (f32[256,256]{1,0:T(8,128)S(1)}, f32[256,256]{1,0:T(8,128)}, u32[]{:S(2)}) copy-start(f32[256,256]{1,0:T(8,128)} %get-tuple-element.25.gain.e0) | copy-start | bytes 786436
  70.3 17.4 %copy-start.5 = (f32[256,256]{1,0:T(8,128)S(1)}, f32[256,256]{1,0:T(8,128)}, u32[]{:S(2)}) copy-start(f32[256,256]{1,0:T(8,128)} %get-tuple-element.27.gain_2) | copy-start | bytes 786436
  70.3 20.8 %collective-permute-start.7 = (f32[264,1024]{1,0:T(8,128)}, f32[264,1024]{1,0:T(8,128)S(1)}, u32[]{:S(2)}, u32[]{:S(2)}) collective-permute-start(f32[264,1024]{1,0:T(8,128)} %get-tuple-element.31), channel_id=1, source_target_pairs={{16,0},{32,16},{48,32},{64,48},{80,64},{96,80},{112,96},{128,112},... | collective-permute-start | bytes 3244040 | tf_op jit(solution)/shard_map/ppermute | solution.py:373
  73.9 23.6 %all-to-all-start.2 = ((f32[4,256,256]{2,1,0:T(8,128)}), f32[4,256,256]{2,1,0:T(8,128)S(1)}, u32[]{:S(2)}, u32[]{:S(2)}) async-start(f32[4,256,256]{2,1,0:T(8,128)} %get-tuple-element.30), calls=%async_computation.2 | async-start | bytes 2097152 | tf_op jit(solution)/shard_map/all_to_all | solution.py:377
  78.8 17.6 %collective-permute-start.10 = (f32[256,256]{1,0:T(8,128)S(1)}, f32[256,256]{1,0:T(8,128)S(1)}, u32[]{:S(2)}, u32[]{:S(2)}) collective-permute-start(f32[256,256]{1,0:T(8,128)S(1)} %copy-done.6), channel_id=1, source_target_pairs={{0,8},{4,12},{8,0},{12,4},{1,9},{5,13},{9,1},{13,5},{2,10},{6,14},... | collective-permute-start | bytes 786440 | tf_op jit(solution)/shard_map/ppermute | solution.py:383
  80.7 15.7 %collective-permute-start.8 = (f32[256,256]{1,0:T(8,128)S(1)}, f32[256,256]{1,0:T(8,128)S(1)}, u32[]{:S(2)}, u32[]{:S(2)}) collective-permute-start(f32[256,256]{1,0:T(8,128)S(1)} %copy-done.6), channel_id=1, source_target_pairs={{0,4},{4,8},{8,12},{12,0},{1,5},{5,9},{9,13},{13,1},{2,6},{6,10},{... | collective-permute-start | bytes 786440 | tf_op jit(solution)/shard_map/ppermute | solution.py:383
  85.7 10.7 %collective-permute-start.9 = (f32[256,256]{1,0:T(8,128)S(1)}, f32[256,256]{1,0:T(8,128)S(1)}, u32[]{:S(2)}, u32[]{:S(2)}) collective-permute-start(f32[256,256]{1,0:T(8,128)S(1)} %copy-done.6), channel_id=1, source_target_pairs={{0,12},{4,0},{8,4},{12,8},{1,13},{5,1},{9,5},{13,9},{2,14},{6,2},{... | collective-permute-start | bytes 786440 | tf_op jit(solution)/shard_map/ppermute | solution.py:383
  87.8 9.8 %collective-permute-start.11 = (f32[256,256]{1,0:T(8,128)S(1)}, f32[256,256]{1,0:T(8,128)}, u32[]{:S(2)}, u32[]{:S(2)}) collective-permute-start(f32[256,256]{1,0:T(8,128)S(1)} %copy-done.5), channel_id=1, source_target_pairs={{32,0},{48,16},{64,32},{80,48},{96,64},{112,80},{128,96},{144,112}... | collective-permute-start | bytes 786440 | tf_op jit(solution)/shard_map/ppermute | solution.py:373
  103.0 4.7 %copy-start.7 = (f32[512,256]{1,0:T(8,128)S(1)}, f32[512,256]{1,0:T(8,128)}, u32[]{:S(2)}) copy-start(f32[512,256]{1,0:T(8,128)} %get-tuple-element.42.a0) | copy-start | bytes 1572868
  103.0 19.0 %all-to-all-start.3 = ((f32[4,256,256]{2,1,0:T(8,128)}), f32[4,256,256]{2,1,0:T(8,128)S(1)}, u32[]{:S(2)}, u32[]{:S(2)}) async-start(f32[4,256,256]{2,1,0:T(8,128)} %get-tuple-element.39), calls=%async_computation.3 | async-start | bytes 2097152 | tf_op jit(solution)/shard_map/all_to_all | solution.py:377
  107.7 19.9 %collective-permute-start.13 = (f32[512,256]{1,0:T(8,128)S(1)}, f32[512,256]{1,0:T(8,128)S(1)}, u32[]{:S(2)}, u32[]{:S(2)}) collective-permute-start(f32[512,256]{1,0:T(8,128)S(1)} %copy-done.7), channel_id=1, source_target_pairs={{0,4},{4,8},{8,12},{12,0},{1,5},{5,9},{9,13},{13,1},{2,6},{6,10},{... | collective-permute-start | bytes 1572872 | tf_op jit(solution)/shard_map/ppermute | solution.py:383
  111.6 16.8 %collective-permute-start.14 = (f32[512,256]{1,0:T(8,128)S(1)}, f32[512,256]{1,0:T(8,128)S(1)}, u32[]{:S(2)}, u32[]{:S(2)}) collective-permute-start(f32[512,256]{1,0:T(8,128)S(1)} %copy-done.7), channel_id=1, source_target_pairs={{0,12},{4,0},{8,4},{12,8},{1,13},{5,1},{9,5},{13,9},{2,14},{6,2},{... | collective-permute-start | bytes 1572872 | tf_op jit(solution)/shard_map/ppermute | solution.py:383
  114.7 20.7 %collective-permute-start.15 = (f32[512,256]{1,0:T(8,128)S(1)}, f32[512,256]{1,0:T(8,128)S(1)}, u32[]{:S(2)}, u32[]{:S(2)}) collective-permute-start(f32[512,256]{1,0:T(8,128)S(1)} %copy-done.7), channel_id=1, source_target_pairs={{0,8},{4,12},{8,0},{12,4},{1,9},{5,13},{9,1},{13,5},{2,10},{6,14},... | collective-permute-start | bytes 1572872 | tf_op jit(solution)/shard_map/ppermute | solution.py:383
  123.6 11.9 %collective-permute-start.12 = (f32[264,256]{1,0:T(8,128)}, f32[264,256]{1,0:T(8,128)S(1)}, u32[]{:S(2)}, u32[]{:S(2)}) collective-permute-start(f32[264,256]{1,0:T(8,128)} %shard_map.101.spread), channel_id=1, source_target_pairs={{32,0},{48,16},{64,32},{80,48},{96,64},{112,80},{128,96},{144,112}... | collective-permute-start | bytes 811016 | tf_op jit(solution)/shard_map/ppermute | solution.py:373
  127.6 9.0 %copy-start = (f32[512,256]{1,0:T(8,128)}, f32[512,256]{1,0:T(8,128)S(1)}, u32[]{:S(2)}) copy-start(f32[512,256]{1,0:T(8,128)S(1)} %collective-permute-done.13.p1.a1) | copy-start | bytes 1572868
  128.3 8.3 %copy-start.1 = (f32[512,256]{1,0:T(8,128)}, f32[512,256]{1,0:T(8,128)S(1)}, u32[]{:S(2)}) copy-start(f32[512,256]{1,0:T(8,128)S(1)} %collective-permute-done.14.p2.a2) | copy-start | bytes 1572868
  160.2 18.2 %all-to-all-start.5 = ((f32[4,64,1280]{2,1,0:T(8,128)}), f32[4,64,1280]{2,1,0:T(8,128)S(1)}, u32[]{:S(2)}, u32[]{:S(2)}) async-start(f32[4,64,1280]{2,1,0:T(8,128)} %get-tuple-element.43), calls=%async_computation.5 | async-start | bytes 2621440 | tf_op jit(solution)/shard_map/all_to_all | solution.py:377
  (7 other events, 10.6 us)

commit v10 on v9

--- a/solution.py
+++ b/solution.py
@@ -293,14 +293,24 @@
         out[i] = block[...]
 
 
+def third_gain(where, gain_2, wide_high, wide_low, a0, a1, a2, a3, gain_out, high_out, low_out, tall):
+    panel = gain_2.shape[0]
+    at_y = where[0]
+    pieces = (a0, a1, a2, a3)
+    place_tall(pieces, at_y, tall, panel)
+    product = three((wide_high[...], wide_low[...]), halves(tall[...]), ((1,), (0,)))
+    gain_out[...] = jnp.where(where[3] == 1, product, gain_2[...])
+    for piece, source in sources(pieces, at_y):
+        at = pl.ds(pl.multiple_of(source * panel, panel), panel)
+        high_out[at, :], low_out[at, :] = halves(piece[0:panel, :])
+
+
 def second_spread(
-    where, gain_2, wide_high, wide_low, spread, y_in, a0, a1, a2, a3,
-    x_out, shift_out, tall, later_tall,
+    where, gain_4, wide_high, wide_low, tall_high, tall_low, spread, y_in, x_out, shift_out, tall
 ):
-    panel = gain_2.shape[0]
+    panel = gain_4.shape[0]
     rows = panel // SIDE
     columns = SIDE * panel
-    at_y = where[0]
     inside = where[3] == 1
     gain_2_wide = (wide_high[...], wide_low[...])
     for i in range(SIDE):
@@ -308,19 +318,14 @@
             tall[b * panel + i * rows : b * panel + (i + 1) * rows, :] = y_in[
                 i, b * rows : (b + 1) * rows, :
             ]
-    along = ((1,), (0,))
-    turned = halves(jnp.where(inside, three(gain_2_wide, halves(tall[...]), along), 0.0))
+    turned = three(gain_2_wide, halves(tall[...]), ((1,), (0,)))
+    turned = halves(jnp.where(inside, turned, 0.0))
     shifts = jnp.concatenate([y_in[i, panel : panel + 8, :] for i in range(SIDE)], axis=1)
     moved = row_times(swap_lanes(shifts)[0:1], gain_2_wide)
     shift_out[...] = spread[panel:, :] + jnp.where(inside, moved, 0.0)
-    pieces = (a0, a1, a2, a3)
-    place_tall(pieces, at_y, later_tall, panel)
-    gain_4 = jnp.where(inside, three(gain_2_wide, halves(later_tall[...]), along), gain_2[...])
-    for i in range(SIDE):
-        x_out[i, :, columns : columns + panel] = gain_4[i * rows : (i + 1) * rows]
-    for piece, source in sources(pieces, at_y):
-        tall[pl.ds(pl.multiple_of(source * panel, panel), panel), :] = piece[0:panel, :]
-    part = three(turned, halves(tall[...]), ((1,), (1,)))
+    for i in range(SIDE):
+        x_out[i, :, columns : columns + panel] = gain_4[i * rows : (i + 1) * rows, :]
+    part = three(turned, (tall_high[...], tall_low[...]), ((1,), (1,)))
     for i in range(SIDE):
         x_out[i, :, 0:columns] = part[i * rows : (i + 1) * rows]
     odd = lax.rem(where[1], 2)
@@ -479,13 +484,22 @@
         four_times, (), (later,), ((SIDE, panel + 8, panel),), unread=gain_2_pieces[1:]
     )
     y_in = swap(y_message, "y")
+    gain_4, tall_high, tall_low = call(
+        third_gain,
+        (where,),
+        far(gain_2, wide_high, wide_low, *gain_2_pieces),
+        ((panel, panel),),
+        ((columns, panel),),
+        unit,
+        coarse=((columns, panel),) * 2,
+    )
     x_message, shift_4 = call(
         second_spread,
         (where,),
-        (*far(gain_2, wide_high, wide_low, spread_2), y_in, *far(*gain_2_pieces)),
+        (*far(gain_4, wide_high, wide_low, tall_high, tall_low, spread_2), y_in),
         ((SIDE, rows, columns + panel), (8, panel)),
-        ((columns, panel), (columns, panel)),
-        3 * unit,
+        ((columns, panel),),
+        2 * unit,
     )
     last_in = swap(x_message, "x")
     final_gain, final_spread = call(finish, (), (last_in,), ((rows, columns), (rows, columns)))

time: 181 us -> 180 us (level)
  blocking collectives: 18.5 us -> 0 us
  waiting for transfers between devices: 46 us -> 55.2 us
  starting transfers between devices: 75.4 us -> 80.7 us
  Pallas kernels: 34 us -> 37 us
    all_to_all x1 -> x0, blocking collectives: 18.5 us -> none  [swap(): return lax.all_to_all(message, axis, 0, 0)]
    all_to_all x5 -> x6, waiting for transfers between devices: 21.1 us -> 30.3 us  [swap(): return lax.all_to_all(message, axis, 0, 0)]
    all_to_all x5 -> x6, starting transfers between devices: 22.6 us -> 27.9 us  [swap(): return lax.all_to_all(message, axis, 0, 0)]
    pallas_call x11 -> x12, Pallas kernels: 34 us -> 37 us  [call(): pl.pallas_call(kernel, out_shape=shapes, in_specs=[SMEM] * len(scalars) +...]
  transfers between devices with their start and end apart: 21 -> 22, of which waited for: 11 -> 12; matrix products, arithmetic and copies ran while one was open for 1% -> 1% of each run, Pallas kernels for 6% -> 8%
where the time goes in v10:
time: 180 us; the launch traced here: 178 us
  starting transfers between devices  80.7 us (45%)
  waiting for transfers between devices  55.2 us (31%)
  Pallas kernels  37 us (21%)
  local copies, waits for them, and re-layouts  4.41 us (2%)
    pallas_call x12, Pallas kernels, call(): pl.pallas_call(kernel, out_shape=shapes, in_specs=[SMEM] * len(scalars) +...  37 us
    all_to_all x6, waiting for transfers between devices, swap(): return lax.all_to_all(message, axis, 0, 0)  30.3 us
    ppermute x9, starting transfers between devices, ring(): lax.ppermute(block, axis, [(i, (i + step) % SIDE) for i in range(SIDE)])  29.5 us
    all_to_all x6, starting transfers between devices, swap(): return lax.all_to_all(message, axis, 0, 0)  27.9 us
    ppermute x9, waiting for transfers between devices, ring(): lax.ppermute(block, axis, [(i, (i + step) % SIDE) for i in range(SIDE)])  15 us
    ppermute x4, starting transfers between devices, ring_shifted(): pieces.append(lax.ppermute(block, ('tm', 'y'), route))  12.3 us
    ppermute x3, starting transfers between devices, shifted(): lax.ppermute(block, 'tm', [(i + distance, i) for i in range(count - dista...  11 us
    ppermute x4, waiting for transfers between devices, ring_shifted(): pieces.append(lax.ppermute(block, ('tm', 'y'), route))  9.67 us
  transfers between devices with their start and end apart: 22, of which 12 were waited for; matrix products, arithmetic and copies ran while one was open for 1% of the time, Pallas kernels for 8%

profile of v10, /device:TPU:384, one launch (start us, length us, event | category | flops | bytes accessed | tf_op | source)
XLA Modules:
  0.0 178.4 jit_solution(11924669227064295815)
XLA Ops:
  0.6 3.2 %shard_map.94 = f32[4,136,1024]{2,1,0:T(8,128)} custom-call(f32[64,1024]{1,0:T(8,128)} %bitcast.13, f32[64,1024]{1,0:T(8,128)} %bitcast.18, f32[1,64]{1,0:T(1,128)} %prior.1, f32[1,128]{1,0:T(1,128)} %innovation.1, s32[1,128]{1,0:T(1,128)} %sites.1), custom_call_target="tpu_custom_call" | custom-call | bytes 2753792 | tf_op jit(solution)/shard_map/pallas_call | solution.py:365
  3.8 4.6 %all-to-all-start = ((f32[4,136,1024]{2,1,0:T(8,128)}), f32[4,136,1024]{2,1,0:T(8,128)S(1)}, u32[]{:S(2)}, u32[]{:S(2)}) async-start(f32[4,136,1024]{2,1,0:T(8,128)} %shard_map.94), calls=%async_computation | async-start | bytes 4456448 | tf_op jit(solution)/shard_map/all_to_all | solution.py:382
  11.2 3.4 %collective-permute-start = (f32[64,1024]{1,0:T(8,128)}, f32[64,1024]{1,0:T(8,128)S(1)}, u32[]{:S(2)}, u32[]{:S(2)}) collective-permute-start(f32[64,1024]{1,0:T(8,128)} %shard_map.95.x0), channel_id=1, source_target_pairs={{0,1},{1,2},{2,3},{3,0},{4,5},{5,6},{6,7},{7,4},{8,9},{9,10},{10,1... | collective-permute-start | bytes 786440 | tf_op jit(solution)/shard_map/ppermute | solution.py:388
  14.6 3.7 %collective-permute-start.1 = (f32[64,1024]{1,0:T(8,128)}, f32[64,1024]{1,0:T(8,128)S(1)}, u32[]{:S(2)}, u32[]{:S(2)}) collective-permute-start(f32[64,1024]{1,0:T(8,128)} %shard_map.95.x0), channel_id=1, source_target_pairs={{0,3},{1,0},{2,1},{3,2},{4,7},{5,4},{6,5},{7,6},{8,11},{9,8},{10,9... | collective-permute-start | bytes 786440 | tf_op jit(solution)/shard_map/ppermute | solution.py:388
  18.3 3.7 %collective-permute-start.2 = (f32[64,1024]{1,0:T(8,128)}, f32[64,1024]{1,0:T(8,128)S(1)}, u32[]{:S(2)}, u32[]{:S(2)}) collective-permute-start(f32[64,1024]{1,0:T(8,128)} %shard_map.95.x0), channel_id=1, source_target_pairs={{0,2},{1,3},{2,0},{3,1},{4,6},{5,7},{6,4},{7,5},{8,10},{9,11},{10,... | collective-permute-start | bytes 786440 | tf_op jit(solution)/shard_map/ppermute | solution.py:388
  22.3 6.9 %collective-permute-done.1.x2 = f32[64,1024]{1,0:T(8,128)S(1)} collective-permute-done((f32[64,1024]{1,0:T(8,128)}, f32[64,1024]{1,0:T(8,128)S(1)}, u32[]{:S(2)}, u32[]{:S(2)}) %collective-permute-start.1) | collective-permute-done | bytes 262176 | tf_op jit(solution)/shard_map/ppermute | solution.py:388
  29.3 6.9 %all-to-all-done.y_in = f32[4,136,1024]{2,1,0:T(8,128)S(1)} async-done(((f32[4,136,1024]{2,1,0:T(8,128)}), f32[4,136,1024]{2,1,0:T(8,128)S(1)}, u32[]{:S(2)}, u32[]{:S(2)}) %all-to-all-start) | async-done | bytes 2228256 | tf_op jit(solution)/shard_map/all_to_all | solution.py:382
  36.2 3.1 %shard_map.96 = (f32[256,256]{1,0:T(8,128)}, f32[256,256]{1,0:T(8,128)}, f32[4,264,256]{2,1,0:T(8,128)}) custom-call(s32[4]{0:T(128)S(1)} %pad_add_fusion.where, f32[4,136,1024]{2,1,0:T(8,128)S(1)} %all-to-all-done.y_in, f32[64,1024]{1,0:T(8,128)} %shard_map.95.x0, f32[64,1024]{1,0:T(8,128)} %copy-done.14, f32[64,1024]{1,0:T(8,128)} %copy-done.15, ...), custom_call_target="tpu_custom_call" | custom-call | flops 134217728 | bytes 4882432 | tf_op jit(solution)/shard_map/pallas_call | solution.py:365
  39.2 4.3 %all-to-all-start.1 = ((f32[4,264,256]{2,1,0:T(8,128)}), f32[4,264,256]{2,1,0:T(8,128)S(1)}, u32[]{:S(2)}, u32[]{:S(2)}) async-start(f32[4,264,256]{2,1,0:T(8,128)} %get-tuple-element.29), calls=%async_computation.1 | async-start | bytes 2162688 | tf_op jit(solution)/shard_map/all_to_all | solution.py:382
  45.6 4.1 %collective-permute-start.4 = (f32[256,256]{1,0:T(8,128)}, f32[256,256]{1,0:T(8,128)S(1)}, u32[]{:S(2)}, u32[]{:S(2)}) collective-permute-start(f32[256,256]{1,0:T(8,128)} %get-tuple-element.28.gain.e0), channel_id=1, source_target_pairs={{16,4},{20,8},{24,12},{28,0},{32,20},{36,24},{40,28},{44,16},{48,3... | collective-permute-start | bytes 786440 | tf_op jit(solution)/shard_map/ppermute | solution.py:401
  49.7 4.2 %collective-permute-start.5 = (f32[256,256]{1,0:T(8,128)}, f32[256,256]{1,0:T(8,128)S(1)}, u32[]{:S(2)}, u32[]{:S(2)}) collective-permute-start(f32[256,256]{1,0:T(8,128)} %get-tuple-element.28.gain.e0), channel_id=1, source_target_pairs={{16,12},{20,0},{24,4},{28,8},{32,28},{36,16},{40,20},{44,24},{48,4... | collective-permute-start | bytes 786440 | tf_op jit(solution)/shard_map/ppermute | solution.py:401
  57.6 5.3 %collective-permute-done.5.e2 = f32[256,256]{1,0:T(8,128)S(1)} collective-permute-done((f32[256,256]{1,0:T(8,128)}, f32[256,256]{1,0:T(8,128)S(1)}, u32[]{:S(2)}, u32[]{:S(2)}) %collective-permute-start.5) | collective-permute-done | bytes 262176 | tf_op jit(solution)/shard_map/ppermute | solution.py:401
  66.2 4.1 %shard_map.97 = (f32[256,256]{1,0:T(8,128)}, f32[4,256,256]{2,1,0:T(8,128)}, f32[8,256]{1,0:T(8,128)}, f32[264,1024]{1,0:T(8,128)}, bf16[256,1024]{1,0:T(8,128)(2,1)}, /*index=5*/bf16[256,1024]{1,0:T(8,128)(2,1)}) custom-call(s32[4]{0:T(128)S(1)} %pad_add_fusion.where, s32[1,5]{1,0:T(1,128)S(1)} %copy-done.3, f32[5,1024]{1,0:T(8,128)} %bitcast.17, ...), custom_call_target="tpu_custom_call" | custom-call | flops 134217728 | bytes 7041024 | tf_op jit(solution)/shard_map/pallas_call | solution.py:365
  70.3 3.6 %collective-permute-start.7 = (f32[264,1024]{1,0:T(8,128)}, f32[264,1024]{1,0:T(8,128)S(1)}, u32[]{:S(2)}, u32[]{:S(2)}) collective-permute-start(f32[264,1024]{1,0:T(8,128)} %get-tuple-element.34), channel_id=1, source_target_pairs={{16,0},{32,16},{48,32},{64,48},{80,64},{96,80},{112,96},{128,112},... | collective-permute-start | bytes 3244040 | tf_op jit(solution)/shard_map/ppermute | solution.py:378
  73.9 4.8 %all-to-all-start.2 = ((f32[4,256,256]{2,1,0:T(8,128)}), f32[4,256,256]{2,1,0:T(8,128)S(1)}, u32[]{:S(2)}, u32[]{:S(2)}) async-start(f32[4,256,256]{2,1,0:T(8,128)} %get-tuple-element.33), calls=%async_computation.2 | async-start | bytes 2097152 | tf_op jit(solution)/shard_map/all_to_all | solution.py:382
  80.6 5.0 %collective-permute-start.8 = (f32[256,256]{1,0:T(8,128)S(1)}, f32[256,256]{1,0:T(8,128)S(1)}, u32[]{:S(2)}, u32[]{:S(2)}) collective-permute-start(f32[256,256]{1,0:T(8,128)S(1)} %copy-done.6), channel_id=1, source_target_pairs={{0,4},{4,8},{8,12},{12,0},{1,5},{5,9},{9,13},{13,1},{2,6},{6,10},{... | collective-permute-start | bytes 786440 | tf_op jit(solution)/shard_map/ppermute | solution.py:388
  87.7 3.4 %collective-permute-start.11 = (f32[256,256]{1,0:T(8,128)S(1)}, f32[256,256]{1,0:T(8,128)}, u32[]{:S(2)}, u32[]{:S(2)}) collective-permute-start(f32[256,256]{1,0:T(8,128)S(1)} %copy-done.5), channel_id=1, source_target_pairs={{32,0},{48,16},{64,32},{80,48},{96,64},{112,80},{128,96},{144,112}... | collective-permute-start | bytes 786440 | tf_op jit(solution)/shard_map/ppermute | solution.py:378
  92.1 4.2 %shard_map.98 = (f32[8,1024]{1,0:T(8,128)}, bf16[256,1024]{1,0:T(8,128)(2,1)}, bf16[256,1024]{1,0:T(8,128)(2,1)}, bf16[256,1024]{1,0:T(8,128)(2,1)}, bf16[256,1024]{1,0:T(8,128)(2,1)}) custom-call(s32[8]{0:T(128)S(1)} %fusion.offsets, f32[264,1024]{1,0:T(8,128)} %copy-done.4), custom_call_target="tpu_custom_call" | custom-call | bytes 1114112 | tf_op jit(solution)/shard_map/pallas_call | solution.py:365
  97.5 5.5 %shard_map.99 = (f32[4,256,256]{2,1,0:T(8,128)}, f32[512,256]{1,0:T(8,128)}, bf16[256,1024]{1,0:T(8,128)(2,1)}, bf16[256,1024]{1,0:T(8,128)(2,1)}) custom-call(s32[4]{0:T(128)S(1)} %pad_add_fusion.where, bf16[256,1024]{1,0:T(8,128)(2,1)} %get-tuple-element.31.wide_high.high, bf16[256,1024]{1,0:T(8,128)(2,1)} %get-tuple-element.32.wide_low.low, ...), custom_call_target="tpu_custom_call" | custom-call | flops 402653184 | bytes 11010048 | tf_op jit(solution)/shard_map/pallas_call | solution.py:365
  103.0 4.7 %all-to-all-start.3 = ((f32[4,256,256]{2,1,0:T(8,128)}), f32[4,256,256]{2,1,0:T(8,128)S(1)}, u32[]{:S(2)}, u32[]{:S(2)}) async-start(f32[4,256,256]{2,1,0:T(8,128)} %get-tuple-element.46), calls=%async_computation.3 | async-start | bytes 2097152 | tf_op jit(solution)/shard_map/all_to_all | solution.py:382
  107.6 3.9 %collective-permute-start.12 = (f32[512,256]{1,0:T(8,128)S(1)}, f32[512,256]{1,0:T(8,128)S(1)}, u32[]{:S(2)}, u32[]{:S(2)}) collective-permute-start(f32[512,256]{1,0:T(8,128)S(1)} %copy-done.7), channel_id=1, source_target_pairs={{0,4},{4,8},{8,12},{12,0},{1,5},{5,9},{9,13},{13,1},{2,6},{6,10},{... | collective-permute-start | bytes 1572872 | tf_op jit(solution)/shard_map/ppermute | solution.py:388
  111.6 3.1 %collective-permute-start.13 = (f32[512,256]{1,0:T(8,128)S(1)}, f32[512,256]{1,0:T(8,128)S(1)}, u32[]{:S(2)}, u32[]{:S(2)}) collective-permute-start(f32[512,256]{1,0:T(8,128)S(1)} %copy-done.7), channel_id=1, source_target_pairs={{0,12},{4,0},{8,4},{12,8},{1,13},{5,1},{9,5},{13,9},{2,14},{6,2},{... | collective-permute-start | bytes 1572872 | tf_op jit(solution)/shard_map/ppermute | solution.py:388
  114.7 2.8 %collective-permute-start.14 = (f32[512,256]{1,0:T(8,128)S(1)}, f32[512,256]{1,0:T(8,128)S(1)}, u32[]{:S(2)}, u32[]{:S(2)}) collective-permute-start(f32[512,256]{1,0:T(8,128)S(1)} %copy-done.7), channel_id=1, source_target_pairs={{0,8},{4,12},{8,0},{12,4},{1,9},{5,13},{9,1},{13,5},{2,10},{6,14},... | collective-permute-start | bytes 1572872 | tf_op jit(solution)/shard_map/ppermute | solution.py:388
  117.5 3.1 %shard_map.101.shift = f32[8,256]{1,0:T(8,128)} custom-call(s32[4]{0:T(128)S(1)} %pad_add_fusion.where, bf16[256,1024]{1,0:T(8,128)(2,1)} %get-tuple-element.31.wide_high.high, bf16[256,1024]{1,0:T(8,128)(2,1)} %get-tuple-element.32.wide_low.low, bf16[256,1024]{1,0:T(8,128)(2,1)} %get-tuple-element.40.wide_high.high_2, ...), custom_call_target="tpu_custom_call" | custom-call | bytes 4243456 | tf_op jit(solution)/shard_map/pallas_call | solution.py:365
  123.5 4.0 %collective-permute-start.15 = (f32[264,256]{1,0:T(8,128)}, f32[264,256]{1,0:T(8,128)S(1)}, u32[]{:S(2)}, u32[]{:S(2)}) collective-permute-start(f32[264,256]{1,0:T(8,128)} %shard_map.102.spread), channel_id=1, source_target_pairs={{32,0},{48,16},{64,32},{80,48},{96,64},{112,80},{128,96},{144,112}... | collective-permute-start | bytes 811016 | tf_op jit(solution)/shard_map/ppermute | solution.py:378
  128.3 7.1 %collective-permute-done.14.a3.p3 = f32[512,256]{1,0:T(8,128)S(1)} collective-permute-done((f32[512,256]{1,0:T(8,128)S(1)}, f32[512,256]{1,0:T(8,128)S(1)}, u32[]{:S(2)}, u32[]{:S(2)}) %collective-permute-start.14) | collective-permute-done | bytes 524320 | tf_op jit(solution)/shard_map/ppermute | solution.py:388
  136.6 5.3 %all-to-all-start.4 = ((f32[4,264,256]{2,1,0:T(8,128)}), f32[4,264,256]{2,1,0:T(8,128)S(1)}, u32[]{:S(2)}, u32[]{:S(2)}) async-start(f32[4,264,256]{2,1,0:T(8,128)} %shard_map.103), calls=%async_computation.4 | async-start | bytes 2162688 | tf_op jit(solution)/shard_map/all_to_all | solution.py:382
  141.9 3.8 %shard_map.100 = (f32[256,256]{1,0:T(8,128)}, bf16[1024,256]{1,0:T(8,128)(2,1)}, bf16[1024,256]{1,0:T(8,128)(2,1)}) custom-call(s32[4]{0:T(128)S(1)} %pad_add_fusion.where, f32[256,256]{1,0:T(8,128)} %get-tuple-element.30.gain_2, bf16[256,1024]{1,0:T(8,128)(2,1)} %get-tuple-element.40.wide_high.high_2, bf16[256,1024]{1,0:T(8,128)(2,1)} %get-tuple-element.41.wide_low.low_2, ...), custom_call_target="tpu_custom_call" | custom-call | flops 134217728 | bytes 4718592 | tf_op jit(solution)/shard_map/pallas_call | solution.py:365
  145.7 9.4 %all-to-all-done.4.y_in = f32[4,264,256]{2,1,0:T(8,128)S(1)} async-done(((f32[4,264,256]{2,1,0:T(8,128)}), f32[4,264,256]{2,1,0:T(8,128)S(1)}, u32[]{:S(2)}, u32[]{:S(2)}) %all-to-all-start.4) | async-done | bytes 1081376 | tf_op jit(solution)/shard_map/all_to_all | solution.py:382
  155.1 4.3 %shard_map.104 = (f32[4,64,1280]{2,1,0:T(8,128)}, f32[8,256]{1,0:T(8,128)}) custom-call(s32[4]{0:T(128)S(1)} %pad_add_fusion.where, f32[256,256]{1,0:T(8,128)} %get-tuple-element.43.gain_4, bf16[256,1024]{1,0:T(8,128)(2,1)} %get-tuple-element.40.wide_high.high_2, bf16[256,1024]{1,0:T(8,128)(2,1)} %get-tuple-element.41.wide_low.low_2, ...), custom_call_target="tpu_custom_call" | custom-call | flops 268435456 | bytes 7127040 | tf_op jit(solution)/shard_map/pallas_call | solution.py:365
  159.4 4.2 %all-to-all-start.5 = ((f32[4,64,1280]{2,1,0:T(8,128)}), f32[4,64,1280]{2,1,0:T(8,128)S(1)}, u32[]{:S(2)}, u32[]{:S(2)}) async-start(f32[4,64,1280]{2,1,0:T(8,128)} %get-tuple-element.49), calls=%async_computation.5 | async-start | bytes 2621440 | tf_op jit(solution)/shard_map/all_to_all | solution.py:382
  164.9 12.5 %all-to-all-done.5.x_in = f32[4,64,1280]{2,1,0:T(8,128)S(1)} async-done(((f32[4,64,1280]{2,1,0:T(8,128)}), f32[4,64,1280]{2,1,0:T(8,128)S(1)}, u32[]{:S(2)}, u32[]{:S(2)}) %all-to-all-start.5) | async-done | bytes 1310752 | tf_op jit(solution)/shard_map/all_to_all | solution.py:382
  (65 shorter events, 25.4 us)
Async XLA Ops:
  3.8 5.2 %copy-start.3 = (s32[1,5]{1,0:T(1,128)S(1)}, s32[1,5]{1,0:T(1,128)}, u32[]{:S(2)}) copy-start(s32[1,5]{1,0:T(1,128)} %offsets.3) | copy-start | bytes 64
  3.8 32.3 %all-to-all-start = ((f32[4,136,1024]{2,1,0:T(8,128)}), f32[4,136,1024]{2,1,0:T(8,128)S(1)}, u32[]{:S(2)}, u32[]{:S(2)}) async-start(f32[4,136,1024]{2,1,0:T(8,128)} %shard_map.94), calls=%async_computation | async-start | bytes 4456448 | tf_op jit(solution)/shard_map/all_to_all | solution.py:382
  11.2 11.1 %collective-permute-start = (f32[64,1024]{1,0:T(8,128)}, f32[64,1024]{1,0:T(8,128)S(1)}, u32[]{:S(2)}, u32[]{:S(2)}) collective-permute-start(f32[64,1024]{1,0:T(8,128)} %shard_map.95.x0), channel_id=1, source_target_pairs={{0,1},{1,2},{2,3},{3,0},{4,5},{5,6},{6,7},{7,4},{8,9},{9,10},{10,1... | collective-permute-start | bytes 786440 | tf_op jit(solution)/shard_map/ppermute | solution.py:388
  14.6 14.6 %collective-permute-start.1 = (f32[64,1024]{1,0:T(8,128)}, f32[64,1024]{1,0:T(8,128)S(1)}, u32[]{:S(2)}, u32[]{:S(2)}) collective-permute-start(f32[64,1024]{1,0:T(8,128)} %shard_map.95.x0), channel_id=1, source_target_pairs={{0,3},{1,0},{2,1},{3,2},{4,7},{5,4},{6,5},{7,6},{8,11},{9,8},{10,9... | collective-permute-start | bytes 786440 | tf_op jit(solution)/shard_map/ppermute | solution.py:388
  18.3 10.9 %collective-permute-start.2 = (f32[64,1024]{1,0:T(8,128)}, f32[64,1024]{1,0:T(8,128)S(1)}, u32[]{:S(2)}, u32[]{:S(2)}) collective-permute-start(f32[64,1024]{1,0:T(8,128)} %shard_map.95.x0), channel_id=1, source_target_pairs={{0,2},{1,3},{2,0},{3,1},{4,6},{5,7},{6,4},{7,5},{8,10},{9,11},{10,... | collective-permute-start | bytes 786440 | tf_op jit(solution)/shard_map/ppermute | solution.py:388
  22.3 13.9 %copy-start.14 = (f32[64,1024]{1,0:T(8,128)}, f32[64,1024]{1,0:T(8,128)S(1)}, u32[]{:S(2)}) copy-start(f32[64,1024]{1,0:T(8,128)S(1)} %collective-permute-done.x1) | copy-start | bytes 786436
  29.2 6.9 %copy-start.15 = (f32[64,1024]{1,0:T(8,128)}, f32[64,1024]{1,0:T(8,128)S(1)}, u32[]{:S(2)}) copy-start(f32[64,1024]{1,0:T(8,128)S(1)} %collective-permute-done.1.x2) | copy-start | bytes 786436
  29.2 6.9 %copy-start.16 = (f32[64,1024]{1,0:T(8,128)}, f32[64,1024]{1,0:T(8,128)S(1)}, u32[]{:S(2)}) copy-start(f32[64,1024]{1,0:T(8,128)S(1)} %collective-permute-done.2.x3) | copy-start | bytes 786436
  39.2 27.0 %all-to-all-start.1 = ((f32[4,264,256]{2,1,0:T(8,128)}), f32[4,264,256]{2,1,0:T(8,128)S(1)}, u32[]{:S(2)}, u32[]{:S(2)}) async-start(f32[4,264,256]{2,1,0:T(8,128)} %get-tuple-element.29), calls=%async_computation.1 | async-start | bytes 2162688 | tf_op jit(solution)/shard_map/all_to_all | solution.py:382
  43.5 12.3 %collective-permute-start.3 = (f32[256,256]{1,0:T(8,128)}, f32[256,256]{1,0:T(8,128)S(1)}, u32[]{:S(2)}, u32[]{:S(2)}) collective-permute-start(f32[256,256]{1,0:T(8,128)} %get-tuple-element.28.gain.e0), channel_id=1, source_target_pairs={{16,0},{20,4},{24,8},{28,12},{32,16},{36,20},{40,24},{44,28},{48,3... | collective-permute-start | bytes 786440 | tf_op jit(solution)/shard_map/ppermute | solution.py:401
  45.6 11.9 %collective-permute-start.4 = (f32[256,256]{1,0:T(8,128)}, f32[256,256]{1,0:T(8,128)S(1)}, u32[]{:S(2)}, u32[]{:S(2)}) collective-permute-start(f32[256,256]{1,0:T(8,128)} %get-tuple-element.28.gain.e0), channel_id=1, source_target_pairs={{16,4},{20,8},{24,12},{28,0},{32,20},{36,24},{40,28},{44,16},{48,3... | collective-permute-start | bytes 786440 | tf_op jit(solution)/shard_map/ppermute | solution.py:401
  49.7 13.1 %collective-permute-start.5 = (f32[256,256]{1,0:T(8,128)}, f32[256,256]{1,0:T(8,128)S(1)}, u32[]{:S(2)}, u32[]{:S(2)}) collective-permute-start(f32[256,256]{1,0:T(8,128)} %get-tuple-element.28.gain.e0), channel_id=1, source_target_pairs={{16,12},{20,0},{24,4},{28,8},{32,28},{36,16},{40,20},{44,24},{48,4... | collective-permute-start | bytes 786440 | tf_op jit(solution)/shard_map/ppermute | solution.py:401
  53.9 12.3 %collective-permute-start.6 = (f32[256,256]{1,0:T(8,128)}, f32[256,256]{1,0:T(8,128)}, u32[]{:S(2)}, u32[]{:S(2)}) collective-permute-start(f32[256,256]{1,0:T(8,128)} %get-tuple-element.28.gain.e0), channel_id=1, source_target_pairs={{16,8},{20,12},{24,0},{28,4},{32,24},{36,28},{40,16},{44,20},{48,4... | collective-permute-start | bytes 786440 | tf_op jit(solution)/shard_map/ppermute | solution.py:401
  55.8 7.0 %copy-start.11 = (f32[256,256]{1,0:T(8,128)}, f32[256,256]{1,0:T(8,128)S(1)}, u32[]{:S(2)}) copy-start(f32[256,256]{1,0:T(8,128)S(1)} %collective-permute-done.3.e0) | copy-start | bytes 786436
  57.5 5.3 %copy-start.12 = (f32[256,256]{1,0:T(8,128)}, f32[256,256]{1,0:T(8,128)S(1)}, u32[]{:S(2)}) copy-start(f32[256,256]{1,0:T(8,128)S(1)} %collective-permute-done.4.e1) | copy-start | bytes 786436
  70.3 8.4 %copy-start.6 = (f32[256,256]{1,0:T(8,128)S(1)}, f32[256,256]{1,0:T(8,128)}, u32[]{:S(2)}) copy-start(f32[256,256]{1,0:T(8,128)} %get-tuple-element.28.gain.e0) | copy-start | bytes 786436
  70.3 17.4 %copy-start.5 = (f32[256,256]{1,0:T(8,128)S(1)}, f32[256,256]{1,0:T(8,128)}, u32[]{:S(2)}) copy-start(f32[256,256]{1,0:T(8,128)} %get-tuple-element.30.gain_2) | copy-start | bytes 786436
  70.3 20.8 %collective-permute-start.7 = (f32[264,1024]{1,0:T(8,128)}, f32[264,1024]{1,0:T(8,128)S(1)}, u32[]{:S(2)}, u32[]{:S(2)}) collective-permute-start(f32[264,1024]{1,0:T(8,128)} %get-tuple-element.34), channel_id=1, source_target_pairs={{16,0},{32,16},{48,32},{64,48},{80,64},{96,80},{112,96},{128,112},... | collective-permute-start | bytes 3244040 | tf_op jit(solution)/shard_map/ppermute | solution.py:378
  73.9 23.6 %all-to-all-start.2 = ((f32[4,256,256]{2,1,0:T(8,128)}), f32[4,256,256]{2,1,0:T(8,128)S(1)}, u32[]{:S(2)}, u32[]{:S(2)}) async-start(f32[4,256,256]{2,1,0:T(8,128)} %get-tuple-element.33), calls=%async_computation.2 | async-start | bytes 2097152 | tf_op jit(solution)/shard_map/all_to_all | solution.py:382
  78.7 17.6 %collective-permute-start.10 = (f32[256,256]{1,0:T(8,128)S(1)}, f32[256,256]{1,0:T(8,128)S(1)}, u32[]{:S(2)}, u32[]{:S(2)}) collective-permute-start(f32[256,256]{1,0:T(8,128)S(1)} %copy-done.6), channel_id=1, source_target_pairs={{0,8},{4,12},{8,0},{12,4},{1,9},{5,13},{9,1},{13,5},{2,10},{6,14},... | collective-permute-start | bytes 786440 | tf_op jit(solution)/shard_map/ppermute | solution.py:388
  80.6 15.7 %collective-permute-start.8 = (f32[256,256]{1,0:T(8,128)S(1)}, f32[256,256]{1,0:T(8,128)S(1)}, u32[]{:S(2)}, u32[]{:S(2)}) collective-permute-start(f32[256,256]{1,0:T(8,128)S(1)} %copy-done.6), channel_id=1, source_target_pairs={{0,4},{4,8},{8,12},{12,0},{1,5},{5,9},{9,13},{13,1},{2,6},{6,10},{... | collective-permute-start | bytes 786440 | tf_op jit(solution)/shard_map/ppermute | solution.py:388
  85.7 10.7 %collective-permute-start.9 = (f32[256,256]{1,0:T(8,128)S(1)}, f32[256,256]{1,0:T(8,128)S(1)}, u32[]{:S(2)}, u32[]{:S(2)}) collective-permute-start(f32[256,256]{1,0:T(8,128)S(1)} %copy-done.6), channel_id=1, source_target_pairs={{0,12},{4,0},{8,4},{12,8},{1,13},{5,1},{9,5},{13,9},{2,14},{6,2},{... | collective-permute-start | bytes 786440 | tf_op jit(solution)/shard_map/ppermute | solution.py:388
  87.7 9.8 %collective-permute-start.11 = (f32[256,256]{1,0:T(8,128)S(1)}, f32[256,256]{1,0:T(8,128)}, u32[]{:S(2)}, u32[]{:S(2)}) collective-permute-start(f32[256,256]{1,0:T(8,128)S(1)} %copy-done.5), channel_id=1, source_target_pairs={{32,0},{48,16},{64,32},{80,48},{96,64},{112,80},{128,96},{144,112}... | collective-permute-start | bytes 786440 | tf_op jit(solution)/shard_map/ppermute | solution.py:378
  103.0 19.0 %all-to-all-start.3 = ((f32[4,256,256]{2,1,0:T(8,128)}), f32[4,256,256]{2,1,0:T(8,128)S(1)}, u32[]{:S(2)}, u32[]{:S(2)}) async-start(f32[4,256,256]{2,1,0:T(8,128)} %get-tuple-element.46), calls=%async_computation.3 | async-start | bytes 2097152 | tf_op jit(solution)/shard_map/all_to_all | solution.py:382
  107.6 19.9 %collective-permute-start.12 = (f32[512,256]{1,0:T(8,128)S(1)}, f32[512,256]{1,0:T(8,128)S(1)}, u32[]{:S(2)}, u32[]{:S(2)}) collective-permute-start(f32[512,256]{1,0:T(8,128)S(1)} %copy-done.7), channel_id=1, source_target_pairs={{0,4},{4,8},{8,12},{12,0},{1,5},{5,9},{9,13},{13,1},{2,6},{6,10},{... | collective-permute-start | bytes 1572872 | tf_op jit(solution)/shard_map/ppermute | solution.py:388
  111.6 16.8 %collective-permute-start.13 = (f32[512,256]{1,0:T(8,128)S(1)}, f32[512,256]{1,0:T(8,128)S(1)}, u32[]{:S(2)}, u32[]{:S(2)}) collective-permute-start(f32[512,256]{1,0:T(8,128)S(1)} %copy-done.7), channel_id=1, source_target_pairs={{0,12},{4,0},{8,4},{12,8},{1,13},{5,1},{9,5},{13,9},{2,14},{6,2},{... | collective-permute-start | bytes 1572872 | tf_op jit(solution)/shard_map/ppermute | solution.py:388
  114.7 20.7 %collective-permute-start.14 = (f32[512,256]{1,0:T(8,128)S(1)}, f32[512,256]{1,0:T(8,128)S(1)}, u32[]{:S(2)}, u32[]{:S(2)}) collective-permute-start(f32[512,256]{1,0:T(8,128)S(1)} %copy-done.7), channel_id=1, source_target_pairs={{0,8},{4,12},{8,0},{12,4},{1,9},{5,13},{9,1},{13,5},{2,10},{6,14},... | collective-permute-start | bytes 1572872 | tf_op jit(solution)/shard_map/ppermute | solution.py:388
  123.5 11.9 %collective-permute-start.15 = (f32[264,256]{1,0:T(8,128)}, f32[264,256]{1,0:T(8,128)S(1)}, u32[]{:S(2)}, u32[]{:S(2)}) collective-permute-start(f32[264,256]{1,0:T(8,128)} %shard_map.102.spread), channel_id=1, source_target_pairs={{32,0},{48,16},{64,32},{80,48},{96,64},{112,80},{128,96},{144,112}... | collective-permute-start | bytes 811016 | tf_op jit(solution)/shard_map/ppermute | solution.py:378
  127.6 9.0 %copy-start = (f32[512,256]{1,0:T(8,128)}, f32[512,256]{1,0:T(8,128)S(1)}, u32[]{:S(2)}) copy-start(f32[512,256]{1,0:T(8,128)S(1)} %collective-permute-done.12.a1.p1) | copy-start | bytes 1572868
  128.3 8.3 %copy-start.1 = (f32[512,256]{1,0:T(8,128)}, f32[512,256]{1,0:T(8,128)S(1)}, u32[]{:S(2)}) copy-start(f32[512,256]{1,0:T(8,128)S(1)} %collective-permute-done.13.a2.p2) | copy-start | bytes 1572868
  136.6 18.5 %all-to-all-start.4 = ((f32[4,264,256]{2,1,0:T(8,128)}), f32[4,264,256]{2,1,0:T(8,128)S(1)}, u32[]{:S(2)}, u32[]{:S(2)}) async-start(f32[4,264,256]{2,1,0:T(8,128)} %shard_map.103), calls=%async_computation.4 | async-start | bytes 2162688 | tf_op jit(solution)/shard_map/all_to_all | solution.py:382
  159.4 18.0 %all-to-all-start.5 = ((f32[4,64,1280]{2,1,0:T(8,128)}), f32[4,64,1280]{2,1,0:T(8,128)S(1)}, u32[]{:S(2)}, u32[]{:S(2)}) async-start(f32[4,64,1280]{2,1,0:T(8,128)} %get-tuple-element.49), calls=%async_computation.5 | async-start | bytes 2621440 | tf_op jit(solution)/shard_map/all_to_all | solution.py:382
  (8 other events, 15.2 us)

commit v11 on v10

--- a/solution.py
+++ b/solution.py
@@ -455,7 +455,7 @@
     c_in = shifted(c_message, 1)
     next_offsets = c_in[panel + NBAND + 2, 0:8].astype(jnp.int32)
     later_rows, *later_halves = call(
-        later_inputs, (next_offsets,), far(c_in), ((8, columns),), coarse=((panel, columns),) * 4
+        later_inputs, (next_offsets,), (c_in,), ((8, columns),), coarse=((panel, columns),) * 4
     )
     part, gain_2_pair, wide_2_high, wide_2_low = call(
         first_spread,

time: 180 us -> 180 us (level)
  no operation moved by 1% of the time
where the time goes in v11:
time: 180 us; the launch traced here: 179 us
  starting transfers between devices  81.1 us (45%)
  waiting for transfers between devices  56.5 us (31%)
  Pallas kernels  36.6 us (20%)
  local copies, waits for them, and re-layouts  3.51 us (2%)
    pallas_call x12, Pallas kernels, call(): pl.pallas_call(kernel, out_shape=shapes, in_specs=[SMEM] * len(scalars) +...  36.6 us
    all_to_all x6, waiting for transfers between devices, swap(): return lax.all_to_all(message, axis, 0, 0)  29.9 us
    ppermute x9, starting transfers between devices, ring(): lax.ppermute(block, axis, [(i, (i + step) % SIDE) for i in range(SIDE)])  29.5 us
    all_to_all x6, starting transfers between devices, swap(): return lax.all_to_all(message, axis, 0, 0)  27.5 us
    ppermute x9, waiting for transfers between devices, ring(): lax.ppermute(block, axis, [(i, (i + step) % SIDE) for i in range(SIDE)])  15.9 us
    ppermute x4, starting transfers between devices, ring_shifted(): pieces.append(lax.ppermute(block, ('tm', 'y'), route))  12.3 us
    ppermute x3, starting transfers between devices, shifted(): lax.ppermute(block, 'tm', [(i + distance, i) for i in range(count - dista...  11.8 us
    ppermute x4, waiting for transfers between devices, ring_shifted(): pieces.append(lax.ppermute(block, ('tm', 'y'), route))  9.66 us
  transfers between devices with their start and end apart: 22, of which 12 were waited for; matrix products, arithmetic and copies ran while one was open for 1% of the time, Pallas kernels for 8%

profile of v11, /device:TPU:384, one launch (start us, length us, event | category | flops | bytes accessed | tf_op | source)
XLA Modules:
  0.0 178.6 jit_solution(2688731816472580249)
XLA Ops:
  0.6 3.2 %shard_map.94 = f32[4,136,1024]{2,1,0:T(8,128)} custom-call(f32[64,1024]{1,0:T(8,128)} %bitcast.13, f32[64,1024]{1,0:T(8,128)} %bitcast.18, f32[1,64]{1,0:T(1,128)} %prior.1, f32[1,128]{1,0:T(1,128)} %innovation.1, s32[1,128]{1,0:T(1,128)} %sites.1), custom_call_target="tpu_custom_call" | custom-call | bytes 2753792 | tf_op jit(solution)/shard_map/pallas_call | solution.py:365
  3.8 4.6 %all-to-all-start = ((f32[4,136,1024]{2,1,0:T(8,128)}), f32[4,136,1024]{2,1,0:T(8,128)S(1)}, u32[]{:S(2)}, u32[]{:S(2)}) async-start(f32[4,136,1024]{2,1,0:T(8,128)} %shard_map.94), calls=%async_computation | async-start | bytes 4456448 | tf_op jit(solution)/shard_map/all_to_all | solution.py:382
  11.2 3.4 %collective-permute-start = (f32[64,1024]{1,0:T(8,128)}, f32[64,1024]{1,0:T(8,128)S(1)}, u32[]{:S(2)}, u32[]{:S(2)}) collective-permute-start(f32[64,1024]{1,0:T(8,128)} %shard_map.95.x0), channel_id=1, source_target_pairs={{0,1},{1,2},{2,3},{3,0},{4,5},{5,6},{6,7},{7,4},{8,9},{9,10},{10,1... | collective-permute-start | bytes 786440 | tf_op jit(solution)/shard_map/ppermute | solution.py:388
  14.6 3.7 %collective-permute-start.1 = (f32[64,1024]{1,0:T(8,128)}, f32[64,1024]{1,0:T(8,128)S(1)}, u32[]{:S(2)}, u32[]{:S(2)}) collective-permute-start(f32[64,1024]{1,0:T(8,128)} %shard_map.95.x0), channel_id=1, source_target_pairs={{0,3},{1,0},{2,1},{3,2},{4,7},{5,4},{6,5},{7,6},{8,11},{9,8},{10,9... | collective-permute-start | bytes 786440 | tf_op jit(solution)/shard_map/ppermute | solution.py:388
  18.3 3.7 %collective-permute-start.2 = (f32[64,1024]{1,0:T(8,128)}, f32[64,1024]{1,0:T(8,128)S(1)}, u32[]{:S(2)}, u32[]{:S(2)}) collective-permute-start(f32[64,1024]{1,0:T(8,128)} %shard_map.95.x0), channel_id=1, source_target_pairs={{0,2},{1,3},{2,0},{3,1},{4,6},{5,7},{6,4},{7,5},{8,10},{9,11},{10,... | collective-permute-start | bytes 786440 | tf_op jit(solution)/shard_map/ppermute | solution.py:388
  22.3 6.9 %collective-permute-done.1.x2 = f32[64,1024]{1,0:T(8,128)S(1)} collective-permute-done((f32[64,1024]{1,0:T(8,128)}, f32[64,1024]{1,0:T(8,128)S(1)}, u32[]{:S(2)}, u32[]{:S(2)}) %collective-permute-start.1) | collective-permute-done | bytes 262176 | tf_op jit(solution)/shard_map/ppermute | solution.py:388
  29.2 6.9 %all-to-all-done.y_in = f32[4,136,1024]{2,1,0:T(8,128)S(1)} async-done(((f32[4,136,1024]{2,1,0:T(8,128)}), f32[4,136,1024]{2,1,0:T(8,128)S(1)}, u32[]{:S(2)}, u32[]{:S(2)}) %all-to-all-start) | async-done | bytes 2228256 | tf_op jit(solution)/shard_map/all_to_all | solution.py:382
  36.1 3.1 %shard_map.96 = (f32[256,256]{1,0:T(8,128)}, f32[256,256]{1,0:T(8,128)}, f32[4,264,256]{2,1,0:T(8,128)}) custom-call(s32[4]{0:T(128)S(1)} %pad_add_fusion.where, f32[4,136,1024]{2,1,0:T(8,128)S(1)} %all-to-all-done.y_in, f32[64,1024]{1,0:T(8,128)} %shard_map.95.x0, f32[64,1024]{1,0:T(8,128)} %copy-done.13, f32[64,1024]{1,0:T(8,128)} %copy-done.14, ...), custom_call_target="tpu_custom_call" | custom-call | flops 134217728 | bytes 4882432 | tf_op jit(solution)/shard_map/pallas_call | solution.py:365
  39.2 4.3 %all-to-all-start.1 = ((f32[4,264,256]{2,1,0:T(8,128)}), f32[4,264,256]{2,1,0:T(8,128)S(1)}, u32[]{:S(2)}, u32[]{:S(2)}) async-start(f32[4,264,256]{2,1,0:T(8,128)} %get-tuple-element.29), calls=%async_computation.1 | async-start | bytes 2162688 | tf_op jit(solution)/shard_map/all_to_all | solution.py:382
  45.6 4.1 %collective-permute-start.4 = (f32[256,256]{1,0:T(8,128)}, f32[256,256]{1,0:T(8,128)S(1)}, u32[]{:S(2)}, u32[]{:S(2)}) collective-permute-start(f32[256,256]{1,0:T(8,128)} %get-tuple-element.28.gain.e0), channel_id=1, source_target_pairs={{16,4},{20,8},{24,12},{28,0},{32,20},{36,24},{40,28},{44,16},{48,3... | collective-permute-start | bytes 786440 | tf_op jit(solution)/shard_map/ppermute | solution.py:401
  49.7 4.2 %collective-permute-start.5 = (f32[256,256]{1,0:T(8,128)}, f32[256,256]{1,0:T(8,128)S(1)}, u32[]{:S(2)}, u32[]{:S(2)}) collective-permute-start(f32[256,256]{1,0:T(8,128)} %get-tuple-element.28.gain.e0), channel_id=1, source_target_pairs={{16,12},{20,0},{24,4},{28,8},{32,28},{36,16},{40,20},{44,24},{48,4... | collective-permute-start | bytes 786440 | tf_op jit(solution)/shard_map/ppermute | solution.py:401
  57.5 5.3 %collective-permute-done.5.e2 = f32[256,256]{1,0:T(8,128)S(1)} collective-permute-done((f32[256,256]{1,0:T(8,128)}, f32[256,256]{1,0:T(8,128)S(1)}, u32[]{:S(2)}, u32[]{:S(2)}) %collective-permute-start.5) | collective-permute-done | bytes 262176 | tf_op jit(solution)/shard_map/ppermute | solution.py:401
  66.2 4.1 %shard_map.97 = (f32[256,256]{1,0:T(8,128)}, f32[4,256,256]{2,1,0:T(8,128)}, f32[8,256]{1,0:T(8,128)}, f32[264,1024]{1,0:T(8,128)}, bf16[256,1024]{1,0:T(8,128)(2,1)}, /*index=5*/bf16[256,1024]{1,0:T(8,128)(2,1)}) custom-call(s32[4]{0:T(128)S(1)} %pad_add_fusion.where, s32[1,5]{1,0:T(1,128)S(1)} %copy-done.3, f32[5,1024]{1,0:T(8,128)} %bitcast.17, ...), custom_call_target="tpu_custom_call" | custom-call | flops 134217728 | bytes 7041024 | tf_op jit(solution)/shard_map/pallas_call | solution.py:365
  70.3 3.6 %collective-permute-start.7 = (f32[264,1024]{1,0:T(8,128)}, f32[264,1024]{1,0:T(8,128)S(1)}, u32[]{:S(2)}, u32[]{:S(2)}) collective-permute-start(f32[264,1024]{1,0:T(8,128)} %get-tuple-element.34), channel_id=1, source_target_pairs={{16,0},{32,16},{48,32},{64,48},{80,64},{96,80},{112,96},{128,112},... | collective-permute-start | bytes 3244040 | tf_op jit(solution)/shard_map/ppermute | solution.py:378
  74.0 4.8 %all-to-all-start.2 = ((f32[4,256,256]{2,1,0:T(8,128)}), f32[4,256,256]{2,1,0:T(8,128)S(1)}, u32[]{:S(2)}, u32[]{:S(2)}) async-start(f32[4,256,256]{2,1,0:T(8,128)} %get-tuple-element.33), calls=%async_computation.2 | async-start | bytes 2097152 | tf_op jit(solution)/shard_map/all_to_all | solution.py:382
  80.7 5.0 %collective-permute-start.8 = (f32[256,256]{1,0:T(8,128)S(1)}, f32[256,256]{1,0:T(8,128)S(1)}, u32[]{:S(2)}, u32[]{:S(2)}) collective-permute-start(f32[256,256]{1,0:T(8,128)S(1)} %copy-done.5), channel_id=1, source_target_pairs={{0,4},{4,8},{8,12},{12,0},{1,5},{5,9},{9,13},{13,1},{2,6},{6,10},{... | collective-permute-start | bytes 786440 | tf_op jit(solution)/shard_map/ppermute | solution.py:388
  87.8 3.4 %collective-permute-start.11 = (f32[256,256]{1,0:T(8,128)S(1)}, f32[256,256]{1,0:T(8,128)}, u32[]{:S(2)}, u32[]{:S(2)}) collective-permute-start(f32[256,256]{1,0:T(8,128)S(1)} %copy-done.4), channel_id=1, source_target_pairs={{32,0},{48,16},{64,32},{80,48},{96,64},{112,80},{128,96},{144,112}... | collective-permute-start | bytes 786440 | tf_op jit(solution)/shard_map/ppermute | solution.py:378
  91.2 3.7 %shard_map.98 = (f32[8,1024]{1,0:T(8,128)}, bf16[256,1024]{1,0:T(8,128)(2,1)}, bf16[256,1024]{1,0:T(8,128)(2,1)}, bf16[256,1024]{1,0:T(8,128)(2,1)}, bf16[256,1024]{1,0:T(8,128)(2,1)}) custom-call(s32[8]{0:T(128)S(1)} %fusion.offsets, f32[264,1024]{1,0:T(8,128)S(1)} %collective-permute-done.7.c_in), custom_call_target="tpu_custom_call" | custom-call | bytes 1114112 | tf_op jit(solution)/shard_map/pallas_call | solution.py:365
  97.5 5.5 %shard_map.99 = (f32[4,256,256]{2,1,0:T(8,128)}, f32[512,256]{1,0:T(8,128)}, bf16[256,1024]{1,0:T(8,128)(2,1)}, bf16[256,1024]{1,0:T(8,128)(2,1)}) custom-call(s32[4]{0:T(128)S(1)} %pad_add_fusion.where, bf16[256,1024]{1,0:T(8,128)(2,1)} %get-tuple-element.31.wide_high.high, bf16[256,1024]{1,0:T(8,128)(2,1)} %get-tuple-element.32.wide_low.low, ...), custom_call_target="tpu_custom_call" | custom-call | flops 402653184 | bytes 11010048 | tf_op jit(solution)/shard_map/pallas_call | solution.py:365
  103.1 4.7 %all-to-all-start.3 = ((f32[4,256,256]{2,1,0:T(8,128)}), f32[4,256,256]{2,1,0:T(8,128)S(1)}, u32[]{:S(2)}, u32[]{:S(2)}) async-start(f32[4,256,256]{2,1,0:T(8,128)} %get-tuple-element.46), calls=%async_computation.3 | async-start | bytes 2097152 | tf_op jit(solution)/shard_map/all_to_all | solution.py:382
  107.7 3.6 %collective-permute-start.12 = (f32[512,256]{1,0:T(8,128)S(1)}, f32[512,256]{1,0:T(8,128)S(1)}, u32[]{:S(2)}, u32[]{:S(2)}) collective-permute-start(f32[512,256]{1,0:T(8,128)S(1)} %copy-done.6), channel_id=1, source_target_pairs={{0,4},{4,8},{8,12},{12,0},{1,5},{5,9},{9,13},{13,1},{2,6},{6,10},{... | collective-permute-start | bytes 1572872 | tf_op jit(solution)/shard_map/ppermute | solution.py:388
  111.4 3.4 %collective-permute-start.13 = (f32[512,256]{1,0:T(8,128)S(1)}, f32[512,256]{1,0:T(8,128)S(1)}, u32[]{:S(2)}, u32[]{:S(2)}) collective-permute-start(f32[512,256]{1,0:T(8,128)S(1)} %copy-done.6), channel_id=1, source_target_pairs={{0,12},{4,0},{8,4},{12,8},{1,13},{5,1},{9,5},{13,9},{2,14},{6,2},{... | collective-permute-start | bytes 1572872 | tf_op jit(solution)/shard_map/ppermute | solution.py:388
  114.8 2.8 %collective-permute-start.14 = (f32[512,256]{1,0:T(8,128)S(1)}, f32[512,256]{1,0:T(8,128)S(1)}, u32[]{:S(2)}, u32[]{:S(2)}) collective-permute-start(f32[512,256]{1,0:T(8,128)S(1)} %copy-done.6), channel_id=1, source_target_pairs={{0,8},{4,12},{8,0},{12,4},{1,9},{5,13},{9,1},{13,5},{2,10},{6,14},... | collective-permute-start | bytes 1572872 | tf_op jit(solution)/shard_map/ppermute | solution.py:388
  117.6 3.1 %shard_map.101.shift = f32[8,256]{1,0:T(8,128)} custom-call(s32[4]{0:T(128)S(1)} %pad_add_fusion.where, bf16[256,1024]{1,0:T(8,128)(2,1)} %get-tuple-element.31.wide_high.high, bf16[256,1024]{1,0:T(8,128)(2,1)} %get-tuple-element.32.wide_low.low, bf16[256,1024]{1,0:T(8,128)(2,1)} %get-tuple-element.40.wide_high.high_2, ...), custom_call_target="tpu_custom_call" | custom-call | bytes 4243456 | tf_op jit(solution)/shard_map/pallas_call | solution.py:365
  122.9 4.8 %collective-permute-start.15 = (f32[264,256]{1,0:T(8,128)}, f32[264,256]{1,0:T(8,128)S(1)}, u32[]{:S(2)}, u32[]{:S(2)}) collective-permute-start(f32[264,256]{1,0:T(8,128)} %shard_map.102.spread), channel_id=1, source_target_pairs={{32,0},{48,16},{64,32},{80,48},{96,64},{112,80},{128,96},{144,112}... | collective-permute-start | bytes 811016 | tf_op jit(solution)/shard_map/ppermute | solution.py:378
  127.7 7.9 %collective-permute-done.13.a2.p2 = f32[512,256]{1,0:T(8,128)S(1)} collective-permute-done((f32[512,256]{1,0:T(8,128)S(1)}, f32[512,256]{1,0:T(8,128)S(1)}, u32[]{:S(2)}, u32[]{:S(2)}) %collective-permute-start.13) | collective-permute-done | bytes 524320 | tf_op jit(solution)/shard_map/ppermute | solution.py:388
  136.8 4.9 %all-to-all-start.4 = ((f32[4,264,256]{2,1,0:T(8,128)}), f32[4,264,256]{2,1,0:T(8,128)S(1)}, u32[]{:S(2)}, u32[]{:S(2)}) async-start(f32[4,264,256]{2,1,0:T(8,128)} %shard_map.103), calls=%async_computation.4 | async-start | bytes 2162688 | tf_op jit(solution)/shard_map/all_to_all | solution.py:382
  141.8 3.8 %shard_map.100 = (f32[256,256]{1,0:T(8,128)}, bf16[1024,256]{1,0:T(8,128)(2,1)}, bf16[1024,256]{1,0:T(8,128)(2,1)}) custom-call(s32[4]{0:T(128)S(1)} %pad_add_fusion.where, f32[256,256]{1,0:T(8,128)} %get-tuple-element.30.gain_2, bf16[256,1024]{1,0:T(8,128)(2,1)} %get-tuple-element.40.wide_high.high_2, bf16[256,1024]{1,0:T(8,128)(2,1)} %get-tuple-element.41.wide_low.low_2, ...), custom_call_target="tpu_custom_call" | custom-call | flops 134217728 | bytes 4718592 | tf_op jit(solution)/shard_map/pallas_call | solution.py:365
  145.5 9.6 %all-to-all-done.4.y_in = f32[4,264,256]{2,1,0:T(8,128)S(1)} async-done(((f32[4,264,256]{2,1,0:T(8,128)}), f32[4,264,256]{2,1,0:T(8,128)S(1)}, u32[]{:S(2)}, u32[]{:S(2)}) %all-to-all-start.4) | async-done | bytes 1081376 | tf_op jit(solution)/shard_map/all_to_all | solution.py:382
  155.1 4.3 %shard_map.104 = (f32[4,64,1280]{2,1,0:T(8,128)}, f32[8,256]{1,0:T(8,128)}) custom-call(s32[4]{0:T(128)S(1)} %pad_add_fusion.where, f32[256,256]{1,0:T(8,128)} %get-tuple-element.43.gain_4, bf16[256,1024]{1,0:T(8,128)(2,1)} %get-tuple-element.40.wide_high.high_2, bf16[256,1024]{1,0:T(8,128)(2,1)} %get-tuple-element.41.wide_low.low_2, ...), custom_call_target="tpu_custom_call" | custom-call | flops 268435456 | bytes 7127040 | tf_op jit(solution)/shard_map/pallas_call | solution.py:365
  159.4 4.2 %all-to-all-start.5 = ((f32[4,64,1280]{2,1,0:T(8,128)}), f32[4,64,1280]{2,1,0:T(8,128)S(1)}, u32[]{:S(2)}, u32[]{:S(2)}) async-start(f32[4,64,1280]{2,1,0:T(8,128)} %get-tuple-element.49), calls=%async_computation.5 | async-start | bytes 2621440 | tf_op jit(solution)/shard_map/all_to_all | solution.py:382
  164.9 12.7 %all-to-all-done.5.x_in = f32[4,64,1280]{2,1,0:T(8,128)S(1)} async-done(((f32[4,64,1280]{2,1,0:T(8,128)}), f32[4,64,1280]{2,1,0:T(8,128)S(1)}, u32[]{:S(2)}, u32[]{:S(2)}) %all-to-all-start.5) | async-done | bytes 1310752 | tf_op jit(solution)/shard_map/all_to_all | solution.py:382
  (63 shorter events, 24.6 us)
Async XLA Ops:
  3.8 5.2 %copy-start.3 = (s32[1,5]{1,0:T(1,128)S(1)}, s32[1,5]{1,0:T(1,128)}, u32[]{:S(2)}) copy-start(s32[1,5]{1,0:T(1,128)} %offsets.3) | copy-start | bytes 64
  3.8 32.3 %all-to-all-start = ((f32[4,136,1024]{2,1,0:T(8,128)}), f32[4,136,1024]{2,1,0:T(8,128)S(1)}, u32[]{:S(2)}, u32[]{:S(2)}) async-start(f32[4,136,1024]{2,1,0:T(8,128)} %shard_map.94), calls=%async_computation | async-start | bytes 4456448 | tf_op jit(solution)/shard_map/all_to_all | solution.py:382
  11.2 11.1 %collective-permute-start = (f32[64,1024]{1,0:T(8,128)}, f32[64,1024]{1,0:T(8,128)S(1)}, u32[]{:S(2)}, u32[]{:S(2)}) collective-permute-start(f32[64,1024]{1,0:T(8,128)} %shard_map.95.x0), channel_id=1, source_target_pairs={{0,1},{1,2},{2,3},{3,0},{4,5},{5,6},{6,7},{7,4},{8,9},{9,10},{10,1... | collective-permute-start | bytes 786440 | tf_op jit(solution)/shard_map/ppermute | solution.py:388
  14.6 14.6 %collective-permute-start.1 = (f32[64,1024]{1,0:T(8,128)}, f32[64,1024]{1,0:T(8,128)S(1)}, u32[]{:S(2)}, u32[]{:S(2)}) collective-permute-start(f32[64,1024]{1,0:T(8,128)} %shard_map.95.x0), channel_id=1, source_target_pairs={{0,3},{1,0},{2,1},{3,2},{4,7},{5,4},{6,5},{7,6},{8,11},{9,8},{10,9... | collective-permute-start | bytes 786440 | tf_op jit(solution)/shard_map/ppermute | solution.py:388
  18.3 10.9 %collective-permute-start.2 = (f32[64,1024]{1,0:T(8,128)}, f32[64,1024]{1,0:T(8,128)S(1)}, u32[]{:S(2)}, u32[]{:S(2)}) collective-permute-start(f32[64,1024]{1,0:T(8,128)} %shard_map.95.x0), channel_id=1, source_target_pairs={{0,2},{1,3},{2,0},{3,1},{4,6},{5,7},{6,4},{7,5},{8,10},{9,11},{10,... | collective-permute-start | bytes 786440 | tf_op jit(solution)/shard_map/ppermute | solution.py:388
  22.3 13.9 %copy-start.13 = (f32[64,1024]{1,0:T(8,128)}, f32[64,1024]{1,0:T(8,128)S(1)}, u32[]{:S(2)}) copy-start(f32[64,1024]{1,0:T(8,128)S(1)} %collective-permute-done.x1) | copy-start | bytes 786436
  29.2 6.9 %copy-start.14 = (f32[64,1024]{1,0:T(8,128)}, f32[64,1024]{1,0:T(8,128)S(1)}, u32[]{:S(2)}) copy-start(f32[64,1024]{1,0:T(8,128)S(1)} %collective-permute-done.1.x2) | copy-start | bytes 786436
  29.2 6.9 %copy-start.15 = (f32[64,1024]{1,0:T(8,128)}, f32[64,1024]{1,0:T(8,128)S(1)}, u32[]{:S(2)}) copy-start(f32[64,1024]{1,0:T(8,128)S(1)} %collective-permute-done.2.x3) | copy-start | bytes 786436
  39.2 27.0 %all-to-all-start.1 = ((f32[4,264,256]{2,1,0:T(8,128)}), f32[4,264,256]{2,1,0:T(8,128)S(1)}, u32[]{:S(2)}, u32[]{:S(2)}) async-start(f32[4,264,256]{2,1,0:T(8,128)} %get-tuple-element.29), calls=%async_computation.1 | async-start | bytes 2162688 | tf_op jit(solution)/shard_map/all_to_all | solution.py:382
  43.5 12.3 %collective-permute-start.3 = (f32[256,256]{1,0:T(8,128)}, f32[256,256]{1,0:T(8,128)S(1)}, u32[]{:S(2)}, u32[]{:S(2)}) collective-permute-start(f32[256,256]{1,0:T(8,128)} %get-tuple-element.28.gain.e0), channel_id=1, source_target_pairs={{16,0},{20,4},{24,8},{28,12},{32,16},{36,20},{40,24},{44,28},{48,3... | collective-permute-start | bytes 786440 | tf_op jit(solution)/shard_map/ppermute | solution.py:401
  45.6 11.9 %collective-permute-start.4 = (f32[256,256]{1,0:T(8,128)}, f32[256,256]{1,0:T(8,128)S(1)}, u32[]{:S(2)}, u32[]{:S(2)}) collective-permute-start(f32[256,256]{1,0:T(8,128)} %get-tuple-element.28.gain.e0), channel_id=1, source_target_pairs={{16,4},{20,8},{24,12},{28,0},{32,20},{36,24},{40,28},{44,16},{48,3... | collective-permute-start | bytes 786440 | tf_op jit(solution)/shard_map/ppermute | solution.py:401
  49.7 13.1 %collective-permute-start.5 = (f32[256,256]{1,0:T(8,128)}, f32[256,256]{1,0:T(8,128)S(1)}, u32[]{:S(2)}, u32[]{:S(2)}) collective-permute-start(f32[256,256]{1,0:T(8,128)} %get-tuple-element.28.gain.e0), channel_id=1, source_target_pairs={{16,12},{20,0},{24,4},{28,8},{32,28},{36,16},{40,20},{44,24},{48,4... | collective-permute-start | bytes 786440 | tf_op jit(solution)/shard_map/ppermute | solution.py:401
  53.9 12.3 %collective-permute-start.6 = (f32[256,256]{1,0:T(8,128)}, f32[256,256]{1,0:T(8,128)}, u32[]{:S(2)}, u32[]{:S(2)}) collective-permute-start(f32[256,256]{1,0:T(8,128)} %get-tuple-element.28.gain.e0), channel_id=1, source_target_pairs={{16,8},{20,12},{24,0},{28,4},{32,24},{36,28},{40,16},{44,20},{48,4... | collective-permute-start | bytes 786440 | tf_op jit(solution)/shard_map/ppermute | solution.py:401
  55.8 7.0 %copy-start.10 = (f32[256,256]{1,0:T(8,128)}, f32[256,256]{1,0:T(8,128)S(1)}, u32[]{:S(2)}) copy-start(f32[256,256]{1,0:T(8,128)S(1)} %collective-permute-done.3.e0) | copy-start | bytes 786436
  57.5 5.3 %copy-start.11 = (f32[256,256]{1,0:T(8,128)}, f32[256,256]{1,0:T(8,128)S(1)}, u32[]{:S(2)}) copy-start(f32[256,256]{1,0:T(8,128)S(1)} %collective-permute-done.4.e1) | copy-start | bytes 786436
  70.3 8.4 %copy-start.5 = (f32[256,256]{1,0:T(8,128)S(1)}, f32[256,256]{1,0:T(8,128)}, u32[]{:S(2)}) copy-start(f32[256,256]{1,0:T(8,128)} %get-tuple-element.28.gain.e0) | copy-start | bytes 786436
  70.3 17.4 %copy-start.4 = (f32[256,256]{1,0:T(8,128)S(1)}, f32[256,256]{1,0:T(8,128)}, u32[]{:S(2)}) copy-start(f32[256,256]{1,0:T(8,128)} %get-tuple-element.30.gain_2) | copy-start | bytes 786436
  70.3 20.8 %collective-permute-start.7 = (f32[264,1024]{1,0:T(8,128)}, f32[264,1024]{1,0:T(8,128)S(1)}, u32[]{:S(2)}, u32[]{:S(2)}) collective-permute-start(f32[264,1024]{1,0:T(8,128)} %get-tuple-element.34), channel_id=1, source_target_pairs={{16,0},{32,16},{48,32},{64,48},{80,64},{96,80},{112,96},{128,112},... | collective-permute-start | bytes 3244040 | tf_op jit(solution)/shard_map/ppermute | solution.py:378
  74.0 23.6 %all-to-all-start.2 = ((f32[4,256,256]{2,1,0:T(8,128)}), f32[4,256,256]{2,1,0:T(8,128)S(1)}, u32[]{:S(2)}, u32[]{:S(2)}) async-start(f32[4,256,256]{2,1,0:T(8,128)} %get-tuple-element.33), calls=%async_computation.2 | async-start | bytes 2097152 | tf_op jit(solution)/shard_map/all_to_all | solution.py:382
  78.8 16.1 %collective-permute-start.10 = (f32[256,256]{1,0:T(8,128)S(1)}, f32[256,256]{1,0:T(8,128)S(1)}, u32[]{:S(2)}, u32[]{:S(2)}) collective-permute-start(f32[256,256]{1,0:T(8,128)S(1)} %copy-done.5), channel_id=1, source_target_pairs={{0,8},{4,12},{8,0},{12,4},{1,9},{5,13},{9,1},{13,5},{2,10},{6,14},... | collective-permute-start | bytes 786440 | tf_op jit(solution)/shard_map/ppermute | solution.py:388
  80.7 14.2 %collective-permute-start.8 = (f32[256,256]{1,0:T(8,128)S(1)}, f32[256,256]{1,0:T(8,128)S(1)}, u32[]{:S(2)}, u32[]{:S(2)}) collective-permute-start(f32[256,256]{1,0:T(8,128)S(1)} %copy-done.5), channel_id=1, source_target_pairs={{0,4},{4,8},{8,12},{12,0},{1,5},{5,9},{9,13},{13,1},{2,6},{6,10},{... | collective-permute-start | bytes 786440 | tf_op jit(solution)/shard_map/ppermute | solution.py:388
  85.7 10.1 %collective-permute-start.9 = (f32[256,256]{1,0:T(8,128)S(1)}, f32[256,256]{1,0:T(8,128)S(1)}, u32[]{:S(2)}, u32[]{:S(2)}) collective-permute-start(f32[256,256]{1,0:T(8,128)S(1)} %copy-done.5), channel_id=1, source_target_pairs={{0,12},{4,0},{8,4},{12,8},{1,13},{5,1},{9,5},{13,9},{2,14},{6,2},{... | collective-permute-start | bytes 786440 | tf_op jit(solution)/shard_map/ppermute | solution.py:388
  87.8 9.8 %collective-permute-start.11 = (f32[256,256]{1,0:T(8,128)S(1)}, f32[256,256]{1,0:T(8,128)}, u32[]{:S(2)}, u32[]{:S(2)}) collective-permute-start(f32[256,256]{1,0:T(8,128)S(1)} %copy-done.4), channel_id=1, source_target_pairs={{32,0},{48,16},{64,32},{80,48},{96,64},{112,80},{128,96},{144,112}... | collective-permute-start | bytes 786440 | tf_op jit(solution)/shard_map/ppermute | solution.py:378
  103.1 4.7 %copy-start.6 = (f32[512,256]{1,0:T(8,128)S(1)}, f32[512,256]{1,0:T(8,128)}, u32[]{:S(2)}) copy-start(f32[512,256]{1,0:T(8,128)} %get-tuple-element.42.a0) | copy-start | bytes 1572868
  103.1 18.3 %all-to-all-start.3 = ((f32[4,256,256]{2,1,0:T(8,128)}), f32[4,256,256]{2,1,0:T(8,128)S(1)}, u32[]{:S(2)}, u32[]{:S(2)}) async-start(f32[4,256,256]{2,1,0:T(8,128)} %get-tuple-element.46), calls=%async_computation.3 | async-start | bytes 2097152 | tf_op jit(solution)/shard_map/all_to_all | solution.py:382
  107.7 19.9 %collective-permute-start.12 = (f32[512,256]{1,0:T(8,128)S(1)}, f32[512,256]{1,0:T(8,128)S(1)}, u32[]{:S(2)}, u32[]{:S(2)}) collective-permute-start(f32[512,256]{1,0:T(8,128)S(1)} %copy-done.6), channel_id=1, source_target_pairs={{0,4},{4,8},{8,12},{12,0},{1,5},{5,9},{9,13},{13,1},{2,6},{6,10},{... | collective-permute-start | bytes 1572872 | tf_op jit(solution)/shard_map/ppermute | solution.py:388
  111.4 24.2 %collective-permute-start.13 = (f32[512,256]{1,0:T(8,128)S(1)}, f32[512,256]{1,0:T(8,128)S(1)}, u32[]{:S(2)}, u32[]{:S(2)}) collective-permute-start(f32[512,256]{1,0:T(8,128)S(1)} %copy-done.6), channel_id=1, source_target_pairs={{0,12},{4,0},{8,4},{12,8},{1,13},{5,1},{9,5},{13,9},{2,14},{6,2},{... | collective-permute-start | bytes 1572872 | tf_op jit(solution)/shard_map/ppermute | solution.py:388
  114.8 20.8 %collective-permute-start.14 = (f32[512,256]{1,0:T(8,128)S(1)}, f32[512,256]{1,0:T(8,128)S(1)}, u32[]{:S(2)}, u32[]{:S(2)}) collective-permute-start(f32[512,256]{1,0:T(8,128)S(1)} %copy-done.6), channel_id=1, source_target_pairs={{0,8},{4,12},{8,0},{12,4},{1,9},{5,13},{9,1},{13,5},{2,10},{6,14},... | collective-permute-start | bytes 1572872 | tf_op jit(solution)/shard_map/ppermute | solution.py:388
  122.9 12.7 %collective-permute-start.15 = (f32[264,256]{1,0:T(8,128)}, f32[264,256]{1,0:T(8,128)S(1)}, u32[]{:S(2)}, u32[]{:S(2)}) collective-permute-start(f32[264,256]{1,0:T(8,128)} %shard_map.102.spread), channel_id=1, source_target_pairs={{32,0},{48,16},{64,32},{80,48},{96,64},{112,80},{128,96},{144,112}... | collective-permute-start | bytes 811016 | tf_op jit(solution)/shard_map/ppermute | solution.py:378
  127.7 9.0 %copy-start = (f32[512,256]{1,0:T(8,128)}, f32[512,256]{1,0:T(8,128)S(1)}, u32[]{:S(2)}) copy-start(f32[512,256]{1,0:T(8,128)S(1)} %collective-permute-done.12.a1.p1) | copy-start | bytes 1572868
  136.8 18.3 %all-to-all-start.4 = ((f32[4,264,256]{2,1,0:T(8,128)}), f32[4,264,256]{2,1,0:T(8,128)S(1)}, u32[]{:S(2)}, u32[]{:S(2)}) async-start(f32[4,264,256]{2,1,0:T(8,128)} %shard_map.103), calls=%async_computation.4 | async-start | bytes 2162688 | tf_op jit(solution)/shard_map/all_to_all | solution.py:382
  159.4 18.2 %all-to-all-start.5 = ((f32[4,64,1280]{2,1,0:T(8,128)}), f32[4,64,1280]{2,1,0:T(8,128)S(1)}, u32[]{:S(2)}, u32[]{:S(2)}) async-start(f32[4,64,1280]{2,1,0:T(8,128)} %get-tuple-element.49), calls=%async_computation.5 | async-start | bytes 2621440 | tf_op jit(solution)/shard_map/all_to_all | solution.py:382
  (7 other events, 13.7 us)
